TPU v7x, 32 devices: a whole 2x2x4 slice. The times are simulated.
32 devices in a mesh: expert: 8 (over z, y), tensor: 4 (over x, core).
Axes of the slice: x: 2, y: 2, z: 4, core: 2. Of those that a mesh axis runs over, the one named last changes fastest.
Arguments:
- tokens: bfloat16 [4096, 2048], P('expert'), may hold values from -6 to 6
- segment_ids: int32 [4096], replicated, may hold values from 0 to 2, as said below
- attn_routes: int32 [4096, 2], P('expert'), may hold values from 0 to 7, all different within a row; in each aligned block of 512 rows (0 to 511, 512 to 1023, ...) at most 160 rows name the same one
- ffn_routes: int32 [4096, 2], P('expert'), may hold values from 0 to 7, all different within a row; in each aligned block of 512 rows (0 to 511, 512 to 1023, ...) at most 160 rows name the same one
- attn_gain: bfloat16 [2048], replicated, may hold values from 0.099609375 to 1.8984375
- ffn_gain: bfloat16 [2048], replicated, may hold values from 0.099609375 to 1.8984375
- routers: bfloat16 [2048, 16], replicated, may hold values from -0.09375 to 0.09375
- query_weight: bfloat16 [8, 2048, 2048], P(None, 'expert', 'tensor'), may hold values from -0.125 to 0.125
- output_weight: bfloat16 [8, 2048, 2048], P(None, 'expert', 'tensor'), may hold values from -2 to 2
- key_value_weight: bfloat16 [2, 2048, 2048], P(None, 'expert', 'tensor'), may hold values from -0.125 to 0.125
- gate_weight: bfloat16 [8, 2048, 5632], P('expert', None, 'tensor'), may hold values from -0.125 to 0.125
- up_weight: bfloat16 [8, 2048, 5632], P('expert', None, 'tensor'), may hold values from -0.125 to 0.125
- down_weight: bfloat16 [8, 5632, 2048], P('expert', 'tensor'), may hold values from -0.078125 to 0.078125
- cotangent: bfloat16 [4096, 2048], P('expert'), may hold values from -6 to 6
Outputs:
- mixed: bfloat16 [4096, 2048], P('expert', 'tensor')
- tokens_grad: float32 [4096, 2048], P('expert')
- attn_gain_grad: float32 [2048], P('expert')
- ffn_gain_grad: float32 [2048], P('expert')
- routers_grad: float32 [2048, 16], P('expert')
- query_grad: float32 [8, 2048, 2048], P(None, 'expert', 'tensor')
- output_grad: float32 [8, 2048, 2048], P(None, 'expert', 'tensor')
- key_value_grad: float32 [2, 2048, 2048], P(None, 'expert', 'tensor')
- gate_grad: float32 [8, 2048, 5632], P('expert', None, 'tensor')
- up_grad: float32 [8, 2048, 5632], P('expert', None, 'tensor')
- down_grad: float32 [8, 5632, 2048], P('expert', 'tensor')
Inputs may be any that keep to these rules, and one draw needn't show every extreme that they name: `segment_ids`: ids start at 0 and rise by 0 or 1 from one token to the next; there are exactly three documents, the middle one begins among the first 512 tokens and ends among the last 512. `attn_routes`: each row names 2 different experts; among the rows of one device no expert is named more than 160 times, a bound that some block reaches. `ffn_routes`: each row names 2 different experts; among the rows of one device no expert is named more than 160 times, a bound that some block reaches.
All inputs are finite; a program needn't handle non-finite values.
Results may differ from a plain program's by a relative error of at most 0.019.
Values may be sent and summed in bfloat16 or wider, within the bound.
A program may use at most 384 MiB of HBM per device.

v0:
```python
import jax
import jax.numpy as jnp
from jax import lax
from jax.sharding import PartitionSpec as P

D = 2048
HD = 128
EXPERTS = 8
TOPK = 2
WINDOW = 1024
CAP = 160


eps = 1e-06
masked_value = -1e30


def shifted_2(shard, axis, by):
    count = lax.axis_size(axis)
    pairs = [(i, i + by) for i in range(count) if 0 <= i + by < count]
    return lax.ppermute(shard, axis, pairs)


def slot_rows(routes, experts):
    flat_routes = routes.reshape(-1)
    one_hot = (flat_routes[:, None] == jnp.arange(experts, dtype=jnp.int32)[None, :]).astype(
        jnp.int32
    )
    earlier = jnp.cumsum(one_hot, axis=0) - one_hot
    return flat_routes * CAP + jnp.sum(earlier * one_hot, axis=1)


def group_rows(row_data, target, slots_all):
    return jnp.zeros((slots_all, row_data.shape[1]), row_data.dtype).at[target].set(row_data)


def pick_gates(logits, routes):
    chosen = jnp.take_along_axis(logits, routes, axis=1)
    return jax.nn.softmax(chosen, axis=-1)


def gate_back(gating, pulled, routes, experts):
    inner_sum = gating * (pulled - jnp.sum(gating * pulled, axis=1, keepdims=True))
    one_hot = (routes[:, :, None] == jnp.arange(experts, dtype=jnp.int32)[None, None, :]).astype(
        jnp.float32
    )
    return jnp.sum(one_hot * inner_sum[:, :, None], axis=1).astype(jnp.bfloat16)


def norm_back(source, factor, gain_vec, upstream):
    ahead = upstream * gain_vec
    centre = jnp.mean(ahead * source, axis=1, keepdims=True)
    return factor * ahead - source * factor * factor * factor * centre


def score_block(query_block, key_block, allowed):
    scores = jnp.einsum(
        "qkhd,jhd->khqj", query_block, key_block, preferred_element_type=jnp.float32
    ) * HD ** (-0.5)
    return jnp.where(allowed[None, None], scores, masked_value)


def attend(query_block, key_block, value_block, allowed):
    scores = score_block(query_block, key_block, allowed)
    row_max = jnp.max(scores, axis=-1, keepdims=True)
    shifted = jnp.exp(scores - row_max)
    row_total = jnp.sum(shifted, axis=-1, keepdims=True)
    attn_probs = (shifted / row_total).astype(jnp.bfloat16)
    result = jnp.einsum(
        "khqj,jhd->qkhd", attn_probs, value_block, preferred_element_type=jnp.float32
    )
    return (result.astype(jnp.bfloat16), (row_max + jnp.log(row_total))[..., 0])


def attend_back(query_block, key_block, value_block, allowed, log_total, grad_block):
    scores = score_block(query_block, key_block, allowed)
    attn_probs = jnp.exp(scores - log_total[..., None])
    pulled = jnp.einsum(
        "qkhd,jhd->khqj", grad_block, value_block, preferred_element_type=jnp.float32
    )
    row_inner = jnp.sum(attn_probs * pulled, axis=-1, keepdims=True)
    score_back = (attn_probs * (pulled - row_inner)).astype(jnp.bfloat16)
    query_back = jnp.einsum(
        "khqj,jhd->qkhd", score_back, key_block, preferred_element_type=jnp.float32
    ) * HD ** (-0.5)
    key_back = jnp.einsum(
        "khqj,qkhd->jhd", score_back, query_block, preferred_element_type=jnp.float32
    ) * HD ** (-0.5)
    value_back = jnp.einsum(
        "khqj,qkhd->jhd",
        attn_probs.astype(jnp.bfloat16),
        grad_block,
        preferred_element_type=jnp.float32,
    )
    return (query_back, key_back, value_back)


def swiglu(gate_in, up_in):
    return jax.nn.silu(gate_in) * up_in


def per_device(
    tokens,
    segment_ids,
    attn_routes,
    ffn_routes,
    attn_gain,
    ffn_gain,
    routers,
    query_weight,
    output_weight,
    key_value_weight,
    gate_weight,
    up_weight,
    down_weight,
    cotangent,
):
    rows_here = tokens.shape[0]
    expert_count = lax.axis_size("expert")
    tensor_count = lax.axis_size("tensor")
    pieces = expert_count // EXPERTS
    column_count = D // tensor_count
    expert_index = lax.axis_index("expert")
    tensor_index = lax.axis_index("tensor")
    slots_all = EXPERTS * CAP
    block_rows = min(512, rows_here)
    block_count = rows_here // block_rows
    key_span = WINDOW + block_rows
    depth = (WINDOW + rows_here - 1) // rows_here
    state_in = tokens.astype(jnp.float32)
    gain_one = attn_gain.astype(jnp.float32)
    gain_two = ffn_gain.astype(jnp.float32)
    rate_one = lax.rsqrt(jnp.mean(state_in * state_in, axis=1, keepdims=True) + eps)
    normed_one = (state_in * rate_one * gain_one).astype(jnp.bfloat16)
    query_all, output_all, pair_all = (
        lax.all_gather(query_weight, "expert", axis=1, tiled=True),
        lax.all_gather(output_weight, "expert", axis=1, tiled=True),
        lax.all_gather(key_value_weight, "expert", axis=1, tiled=True),
    )
    attn_logits = jnp.dot(normed_one, routers[:, :EXPERTS], preferred_element_type=jnp.float32)
    attn_gates = pick_gates(attn_logits, attn_routes)
    pair = jnp.einsum(
        "td,cdf->ctf", normed_one, pair_all, preferred_element_type=jnp.float32
    ).astype(jnp.bfloat16)
    keys = pair[0]
    values = pair[1]
    attn_slot = slot_rows(attn_routes, EXPERTS)
    spread_one = group_rows(jnp.repeat(normed_one, TOPK, axis=0), attn_slot, slots_all).reshape(
        EXPERTS, CAP, D
    )
    query_rows = jnp.einsum(
        "ecd,edf->ecf", spread_one, query_all, preferred_element_type=jnp.float32
    )
    query_rows = query_rows.reshape(slots_all, -1)[attn_slot].astype(jnp.bfloat16)
    queries = query_rows.reshape(rows_here, TOPK, -1, HD)
    head_count = queries.shape[2]
    earlier_keys = []
    earlier_values = []
    for step in range(depth):
        got_keys, got_values = shifted_2((keys, values), "expert", step + 1)
        earlier_keys.append(got_keys)
        earlier_values.append(got_values)
    key_cat = jnp.concatenate(earlier_keys[::-1] + [keys]).reshape(
        (depth + 1) * rows_here, head_count, HD
    )
    value_cat = jnp.concatenate(earlier_values[::-1] + [values]).reshape(
        (depth + 1) * rows_here, head_count, HD
    )
    padded_segments = jnp.concatenate([jnp.full((depth * rows_here,), -1, jnp.int32), segment_ids])
    segment_cat = lax.dynamic_slice_in_dim(
        padded_segments, expert_index * rows_here, (depth + 1) * rows_here
    )
    own_segments = lax.dynamic_slice_in_dim(segment_ids, expert_index * rows_here, rows_here)

    def keep_mask(row_start):
        query_place = expert_index * rows_here + row_start + jnp.arange(block_rows, dtype=jnp.int32)
        key_first = depth * rows_here + row_start - WINDOW
        key_place = (
            (expert_index - depth) * rows_here + key_first + jnp.arange(key_span, dtype=jnp.int32)
        )
        distance = query_place[:, None] - key_place[None, :]
        allowed = (distance >= 0) & (distance < WINDOW) & (key_place[None, :] >= 0)
        allowed = allowed & (own_segments[:, None] == segment_cat[None, :])
        return (allowed, key_first)

    def forward_block(row_start):
        allowed, key_first = keep_mask(row_start)
        return attend(queries, key_cat, value_cat, allowed)

    row_starts = jnp.arange(block_count, dtype=jnp.int32) * block_rows
    heads_blocks, log_totals = lax.map(forward_block, row_starts)
    heads_out = heads_blocks.reshape(rows_here * TOPK, -1)
    spread_attn = group_rows(heads_out, attn_slot, slots_all).reshape(EXPERTS, CAP, -1)
    attn_rows = jnp.einsum(
        "ecf,edf->ecd", spread_attn, output_all, preferred_element_type=jnp.float32
    )
    attn_rows = attn_rows.reshape(slots_all, D)[attn_slot].reshape(rows_here, TOPK, D)
    attn_part = jnp.sum(attn_gates[:, :, None] * attn_rows, axis=1)
    attn_out = lax.psum(attn_part, "tensor")
    state = state_in + attn_out
    rate_two = lax.rsqrt(jnp.mean(state * state, axis=1, keepdims=True) + eps)
    normed_two = (state * rate_two * gain_two).astype(jnp.bfloat16)
    ffn_logits = jnp.dot(normed_two, routers[:, EXPERTS:], preferred_element_type=jnp.float32)
    ffn_gates = pick_gates(ffn_logits, ffn_routes)
    ffn_slot = slot_rows(ffn_routes, EXPERTS)
    spread_two = group_rows(jnp.repeat(normed_two, TOPK, axis=0), ffn_slot, slots_all).reshape(
        EXPERTS, CAP, D
    )
    spread_rep = jnp.repeat(spread_two, pieces, axis=0)
    arrived = lax.all_to_all(spread_rep, "expert", split_axis=0, concat_axis=0, tiled=True).reshape(
        -1, D
    )
    gate_map, up_map, down_map = (gate_weight[0], up_weight[0], down_weight[0])
    gate_pre = jnp.dot(arrived, gate_map, preferred_element_type=jnp.float32)
    up_pre = jnp.dot(arrived, up_map, preferred_element_type=jnp.float32)
    hidden = swiglu(gate_pre, up_pre).astype(jnp.bfloat16)
    partial_rows = jnp.dot(hidden, down_map, preferred_element_type=jnp.float32)
    back_form = (
        lax.psum_scatter(
            partial_rows.astype(jnp.bfloat16), "tensor", scatter_dimension=1, tiled=True
        )
        .astype(jnp.float32)
        .reshape(expert_count, CAP, column_count)
    )
    returned = lax.all_to_all(
        back_form.astype(jnp.bfloat16), "expert", split_axis=0, concat_axis=0, tiled=True
    ).astype(back_form.dtype)
    returned_sum = jnp.sum(returned.reshape((EXPERTS, pieces) + returned.shape[1:]), axis=1)
    expert_cols = returned_sum.reshape(slots_all, column_count)[ffn_slot].reshape(
        rows_here, TOPK, column_count
    )
    ffn_cols = jnp.sum(ffn_gates[:, :, None] * expert_cols, axis=1)
    state_cols = lax.dynamic_slice_in_dim(state, tensor_index * column_count, column_count, 1)
    mixed = (state_cols + ffn_cols).astype(jnp.bfloat16)
    upstream = cotangent.astype(jnp.float32)
    ffn_row_grad = (
        (ffn_gates[:, :, None] * upstream[:, None, :])
        .reshape(rows_here * TOPK, D)
        .astype(jnp.bfloat16)
    )
    sent_grad = jnp.repeat(
        group_rows(ffn_row_grad, ffn_slot, slots_all).reshape(EXPERTS, CAP, D), pieces, axis=0
    )
    arrived_grad = lax.all_to_all(
        sent_grad, "expert", split_axis=0, concat_axis=0, tiled=True
    ).reshape(-1, D)
    hidden_grad = jnp.einsum(
        "rd,fd->rf", arrived_grad, down_map, preferred_element_type=jnp.float32
    )
    down_part = jnp.einsum("rf,rd->fd", hidden, arrived_grad, preferred_element_type=jnp.float32)
    unused_value, swiglu_pull = jax.vjp(swiglu, gate_pre, up_pre)
    gate_back_rows, up_back_rows = swiglu_pull(hidden_grad)
    gate_low = gate_back_rows.astype(jnp.bfloat16)
    up_low = up_back_rows.astype(jnp.bfloat16)
    gate_part = jnp.einsum("rd,rf->df", arrived, gate_low, preferred_element_type=jnp.float32)
    up_part = jnp.einsum("rd,rf->df", arrived, up_low, preferred_element_type=jnp.float32)
    row_grad = jnp.einsum("rf,df->rd", gate_low, gate_map, preferred_element_type=jnp.float32)
    row_grad = row_grad + jnp.einsum(
        "rf,df->rd", up_low, up_map, preferred_element_type=jnp.float32
    )
    gate_grad, up_grad, down_grad = (gate_part, up_part, down_part)
    row_form = lax.psum_scatter(row_grad, "tensor", scatter_dimension=1, tiled=True).reshape(
        expert_count, CAP, column_count
    )
    row_back = lax.all_to_all(row_form, "expert", split_axis=0, concat_axis=0, tiled=True)
    back_sum = jnp.sum(row_back.reshape((EXPERTS, pieces) + row_back.shape[1:]), axis=1)
    gather_first = jnp.sum(
        back_sum.reshape(slots_all, column_count)[ffn_slot].reshape(rows_here, TOPK, column_count),
        axis=1,
    )
    gather_second = expert_cols.reshape(rows_here * TOPK, column_count)
    first_got, second_got = (
        lax.all_gather(gather_first, "tensor", axis=1, tiled=True),
        lax.all_gather(gather_second, "tensor", axis=1, tiled=True),
    )
    rows_full = second_got.reshape(rows_here, TOPK, D)
    ffn_pull = jnp.sum(upstream[:, None, :] * rows_full, axis=2)
    ffn_logit_grad = gate_back(ffn_gates, ffn_pull, ffn_routes, EXPERTS)
    normed_two_grad = first_got + jnp.einsum(
        "te,de->td", ffn_logit_grad, routers[:, EXPERTS:], preferred_element_type=jnp.float32
    )
    ffn_router_grad = jnp.einsum(
        "td,te->de", normed_two, ffn_logit_grad, preferred_element_type=jnp.float32
    )
    ffn_gain_part = jnp.sum(normed_two_grad * state * rate_two, axis=0)
    state_grad = upstream + norm_back(state, rate_two, gain_two, normed_two_grad)
    attn_pull_part = jnp.sum(attn_rows * state_grad[:, None, :], axis=2)
    attn_row_grad = (
        (attn_gates[:, :, None] * state_grad[:, None, :])
        .reshape(rows_here * TOPK, D)
        .astype(jnp.bfloat16)
    )
    back_spread = group_rows(attn_row_grad, attn_slot, slots_all).reshape(EXPERTS, CAP, D)
    output_part = jnp.einsum(
        "ecd,ecf->edf", back_spread, spread_attn, preferred_element_type=jnp.float32
    )
    heads_grad = jnp.einsum(
        "ecd,edf->ecf", back_spread, output_all, preferred_element_type=jnp.float32
    )
    heads_grad = heads_grad.reshape(slots_all, -1)[attn_slot].astype(jnp.bfloat16)
    heads_grad = heads_grad.reshape(block_count, block_rows, TOPK, head_count, HD)

    def backward_block(carry, block_data):
        key_acc, value_acc = carry
        row_start, log_total, grad_block = block_data
        allowed, key_first = keep_mask(row_start)
        query_back, key_back, value_back = attend_back(
            queries, key_cat, value_cat, allowed, log_total, grad_block
        )
        key_acc = key_acc + key_back
        value_acc = value_acc + value_back
        return ((key_acc, value_acc), query_back)

    zero_keys = jnp.zeros(((depth + 1) * rows_here, head_count, HD), jnp.float32)
    (key_acc, value_acc), query_back_blocks = lax.scan(
        backward_block, (zero_keys, zero_keys), (row_starts, log_totals, heads_grad)
    )
    key_total = key_acc[depth * rows_here :]
    value_total = value_acc[depth * rows_here :]
    for step in range(1, depth + 1):
        lower = (depth - step) * rows_here
        sent_keys, sent_values = (
            shifted_2(
                key_acc[lower : lower + rows_here].astype(jnp.bfloat16), "expert", -step
            ).astype(jnp.float32),
            shifted_2(
                value_acc[lower : lower + rows_here].astype(jnp.bfloat16), "expert", -step
            ).astype(jnp.float32),
        )
        key_total = key_total + sent_keys
        value_total = value_total + sent_values
    keys_grad = key_total.reshape(rows_here, -1).astype(jnp.bfloat16)
    values_grad = value_total.reshape(rows_here, -1).astype(jnp.bfloat16)
    query_rows_grad = query_back_blocks.reshape(rows_here * TOPK, -1).astype(jnp.bfloat16)
    query_spread = group_rows(query_rows_grad, attn_slot, slots_all).reshape(EXPERTS, CAP, -1)
    query_part = jnp.einsum(
        "ecd,ecf->edf", spread_one, query_spread, preferred_element_type=jnp.float32
    )
    normed_one_grad = jnp.einsum(
        "ecf,edf->ecd", query_spread, query_all, preferred_element_type=jnp.float32
    )
    normed_one_grad = jnp.sum(
        normed_one_grad.reshape(slots_all, D)[attn_slot].reshape(rows_here, TOPK, D), axis=1
    )
    pair_grad = jnp.stack([keys_grad, values_grad])
    pair_part = jnp.einsum("td,ctf->cdf", normed_one, pair_grad, preferred_element_type=jnp.float32)
    normed_one_grad = normed_one_grad + jnp.einsum(
        "ctf,cdf->td", pair_grad, pair_all, preferred_element_type=jnp.float32
    )
    normed_one_grad, attn_pull = (
        lax.psum(normed_one_grad.astype(jnp.bfloat16), "tensor").astype(jnp.float32),
        lax.psum(attn_pull_part.astype(jnp.bfloat16), "tensor").astype(jnp.float32),
    )
    attn_logit_grad = gate_back(attn_gates, attn_pull, attn_routes, EXPERTS)
    normed_one_grad = normed_one_grad + jnp.einsum(
        "te,de->td", attn_logit_grad, routers[:, :EXPERTS], preferred_element_type=jnp.float32
    )
    attn_router_grad = jnp.einsum(
        "td,te->de", normed_one, attn_logit_grad, preferred_element_type=jnp.float32
    )
    attn_gain_part = jnp.sum(normed_one_grad * state_in * rate_one, axis=0)
    tokens_grad = state_grad + norm_back(state_in, rate_one, gain_one, normed_one_grad)
    gain_parts = jnp.stack([attn_gain_part, ffn_gain_part])
    router_part = jnp.concatenate([attn_router_grad, ffn_router_grad], axis=1)[None]
    query_grad, output_grad, key_value_grad, gain_grads, routers_grad = (
        lax.psum_scatter(
            query_part.astype(jnp.bfloat16), "expert", scatter_dimension=1, tiled=True
        ).astype(jnp.float32),
        lax.psum_scatter(
            output_part.astype(jnp.bfloat16), "expert", scatter_dimension=1, tiled=True
        ).astype(jnp.float32),
        lax.psum_scatter(
            pair_part.astype(jnp.bfloat16), "expert", scatter_dimension=1, tiled=True
        ).astype(jnp.float32),
        lax.psum_scatter(
            gain_parts.astype(jnp.bfloat16), "expert", scatter_dimension=1, tiled=True
        ).astype(jnp.float32),
        lax.psum_scatter(
            router_part.astype(jnp.bfloat16), "expert", scatter_dimension=1, tiled=True
        ).astype(jnp.float32),
    )
    return (
        mixed,
        tokens_grad,
        gain_grads[0],
        gain_grads[1],
        routers_grad[0],
        query_grad,
        output_grad,
        key_value_grad,
        gate_grad[None],
        up_grad[None],
        down_grad[None],
    )


def solution(mesh):
    in_specs = (
        P("expert", None),
        P(),
        P("expert", None),
        P("expert", None),
        P(),
        P(),
        P(),
        P(None, "expert", "tensor"),
        P(None, "expert", "tensor"),
        P(None, "expert", "tensor"),
        P("expert", None, "tensor"),
        P("expert", None, "tensor"),
        P("expert", "tensor", None),
        P("expert", None),
    )
    out_specs = (
        P("expert", "tensor"),
        P("expert", None),
        P("expert"),
        P("expert"),
        P("expert", None),
        P(None, "expert", "tensor"),
        P(None, "expert", "tensor"),
        P(None, "expert", "tensor"),
        P("expert", None, "tensor"),
        P("expert", None, "tensor"),
        P("expert", "tensor", None),
    )
    return jax.shard_map(
        per_device, mesh=mesh, in_specs=in_specs, out_specs=out_specs, check_vma=False
    )
```

profile of v0, /device:TPU:0, one launch (start us, length us, event | category | flops | bytes accessed | tf_op | source)
XLA Modules:
  0.0 2479.4 jit_solution(9005908194612503224)
XLA Ops:
  18.8 6.5 gather_fusion.6
  26.0 62.4 %all-gather.7.cloned.1.call-done = bf16[2,2048,512]{1,2,0:T(8,128)(2,1)} async-done(((bf16[2,256,512]{1,2,0:T(8,128)(2,1)}), bf16[2,2048,512]{1,2,0:T(8,128)(2,1)}) %all-gather.7.cloned.1.call-update) | async-done | bytes 4194320 | tf_op jit(solution)/shard_map/all_gather | solution.py:138
  103.4 7.2 reshape.523
  111.5 10.6 scatter_custom_fusion
  136.2 219.9 %all-gather.9.cloned.1.call-done = bf16[8,2048,512]{2,1,0:T(8,128)(2,1)} async-done(((bf16[8,256,512]{2,1,0:T(8,128)(2,1)}), bf16[8,2048,512]{2,1,0:T(8,128)(2,1)}) %all-gather.9.cloned.1.call-update) | async-done | bytes 16777232 | tf_op jit(solution)/shard_map/all_gather | solution.py:136
  356.2 10.2 fusion.119
  371.6 12.3 fusion.116
  384.0 10.2 fusion.3
  394.2 11.1 fusion.66
  406.1 5.8 scatter_custom_fusion.1
  411.9 172.3 %all-gather.11.cloned.1.call-done = bf16[8,2048,512]{2,1,0:T(8,128)(2,1)} async-done(((bf16[8,256,512]{2,1,0:T(8,128)(2,1)}), bf16[8,2048,512]{2,1,0:T(8,128)(2,1)}) %all-gather.11.cloned.1.call-update) | async-done | bytes 16777232 | tf_op jit(solution)/shard_map/all_gather | solution.py:137
  584.2 11.5 fusion.120
  595.7 12.8 gather_fusion.1
  608.5 10.6 reshape.439
  619.1 15.5 multiply_reduce_fusion.2
  639.0 79.5 %all-reduce.4.cloned.1.call-done = f32[512,2048]{1,0:T(8,128)} async-done(((f32[512,2048]{1,0:T(8,128)}), f32[512,2048]{1,0:T(8,128)}) %all-reduce.4.cloned.1.call-update) | async-done | bytes 4194320 | tf_op jit(solution)/shard_map/psum | solution.py:199
  728.8 7.2 reshape.539
  735.9 10.9 scatter_custom_fusion.2
  746.9 121.6 %all_to_all.20 = bf16[8,160,2048]{2,1,0:T(8,128)(2,1)S(1)} all-to-all(bf16[8,160,2048]{2,1,0:T(8,128)(2,1)} %bitcast.247), channel_id=1, replica_groups=mesh['expert'=8,'tensor'=4] {'expert'}, dimensions={0} | all-to-all | bytes 10485760 | tf_op jit(solution)/shard_map/all_to_all | solution.py:210
  868.4 10.2 fusion.21
  878.7 12.7 multiply_convert_fusion.3
  893.2 10.1 convolution_convert_fusion.2
  903.3 49.8 %reduce-scatter.10.cloned.1.call-done = bf16[1280,512]{1,0:T(8,128)(2,1)} async-done(((bf16[1280,2048]{1,0:T(8,128)(2,1)}), bf16[1280,512]{1,0:T(8,128)(2,1)}) %reduce-scatter.10.cloned.1.call-update) | async-done | bytes 1310736 | tf_op jit(solution)/shard_map/reduce_scatter | solution.py:219
  958.6 31.4 %all-to-all-done.1 = bf16[8,160,512]{2,1,0:T(8,128)(2,1)} async-done(((bf16[8,160,512]{2,1,0:T(8,128)(2,1)}), bf16[8,160,512]{2,1,0:T(8,128)(2,1)}, u32[]{:S(2)}, u32[]{:S(2)}) %all-to-all-start.1) | async-done | bytes 1310752 | tf_op jit(solution)/shard_map/all_to_all | solution.py:225
  997.1 8.4 mul.369
  1005.6 11.3 mul.370
  1017.8 6.5 gather_fusion.7
  1024.8 28.5 %all-gather.15.cloned.1.call-done = f32[1024,2048]{1,0:T(8,128)} async-done(((f32[1024,512]{1,0:T(8,128)}), f32[1024,2048]{1,0:T(8,128)}) %all-gather.15.cloned.1.call-update) | async-done | bytes 8388624 | tf_op jit(solution)/shard_map/all_gather | solution.py:274
  1053.2 6.6 multiply_reduce_fusion.1
  1060.5 11.6 scatter_custom_fusion.3
  1072.1 121.7 %all_to_all.21 = bf16[8,160,2048]{2,1,0:T(8,128)(2,1)S(1)} all-to-all(bf16[8,160,2048]{2,1,0:T(8,128)(2,1)} %bitcast.246), channel_id=1, replica_groups=mesh['expert'=8,'tensor'=4] {'expert'}, dimensions={0} | all-to-all | bytes 10485760 | tf_op jit(solution)/shard_map/all_to_all | solution.py:244
  1193.8 18.2 multiply_convert_fusion.2
  1212.0 11.5 fusion.19
  1223.5 13.8 convolution_add_fusion
  1237.4 83.5 %reduce-scatter.12.cloned.1.call-done = f32[1280,512]{1,0:T(8,128)} async-done(((f32[1280,2048]{1,0:T(8,128)}), f32[1280,512]{1,0:T(8,128)}) %reduce-scatter.12.cloned.1.call-update) | async-done | bytes 2621456 | tf_op jit(solution)/shard_map/reduce_scatter | solution.py:262
  1320.9 65.0 %all_to_all.22 = f32[8,160,512]{2,1,0:T(8,128)S(1)} all-to-all(f32[8,160,512]{2,1,0:T(8,128)} %bitcast.262), channel_id=1, replica_groups=mesh['expert'=8,'tensor'=4] {'expert'}, dimensions={0} | all-to-all | bytes 5242880 | tf_op jit(solution)/shard_map/all_to_all | solution.py:265
  1401.0 31.2 %all-gather.13.cloned.1.call-done = f32[512,2048]{1,0:T(8,128)} async-done(((f32[512,512]{1,0:T(8,128)}), f32[512,2048]{1,0:T(8,128)}) %all-gather.13.cloned.1.call-update) | async-done | bytes 4194320 | tf_op jit(solution)/shard_map/all_gather | solution.py:273
  1441.2 5.8 mul.392
  1447.0 10.9 mul.393
  1457.8 11.9 scatter_custom_fusion.4
  1469.8 10.2 fusion.121
  1485.3 15.9 fusion
  1501.2 14.7 fusion.117
  1515.9 17.5 fusion.2
  1539.9 11.0 fusion.118
  1552.4 6.1 scatter_custom_fusion.5
  1567.0 11.7 fusion.122
  1578.7 12.8 gather_fusion.5
  1591.6 10.5 reshape.454
  1602.1 13.3 reduce_sum.232
  1619.9 7.3 fusion.36
  1627.3 8.8 multiply_reduce_fusion
  1637.5 6.5 psum.23
  1647.3 37.2 %all-reduce.6.cloned.1.call-done = bf16[512,2048]{1,0:T(8,128)(2,1)} async-done(((bf16[512,2048]{1,0:T(8,128)(2,1)}), bf16[512,2048]{1,0:T(8,128)(2,1)}) %all-reduce.6.cloned.1.call-update) | async-done | bytes 2097168 | tf_op jit(solution)/shard_map/psum | solution.py:351
  1697.5 11.5 convolution_convert_fusion.1
  1710.3 11.4 convolution_convert_fusion
  1732.3 13.4 convolution_bitcast_fusion
  1745.8 11.5 convolution_bitcast_fusion.2
  1757.3 11.3 convolution_bitcast_fusion.1
  1770.0 7.0 fusion.29
  1776.9 29.9 %reduce-scatter.22.cloned.1.call-done = bf16[256,2]{1,0:T(8,128)(2,1)} async-done(((bf16[2048,2]{1,0:T(8,128)(2,1)}), bf16[256,2]{1,0:T(8,128)(2,1)}) %reduce-scatter.22.cloned.1.call-update) | async-done | bytes 1040
  1808.3 89.5 %reduce-scatter.20.cloned.1.call-done = bf16[2,256,512]{1,2,0:T(8,128)(2,1)} async-done(((bf16[2,2048,512]{1,2,0:T(8,128)(2,1)}), bf16[2,256,512]{1,2,0:T(8,128)(2,1)}) %reduce-scatter.20.cloned.1.call-update) | async-done | bytes 524304 | tf_op jit(solution)/shard_map/reduce_scatter | solution.py:372
  1900.0 283.9 %reduce-scatter.16.cloned.1.call-done = bf16[8,256,512]{2,1,0:T(8,128)(2,1)} async-done(((bf16[8,2048,512]{2,1,0:T(8,128)(2,1)}), bf16[8,256,512]{2,1,0:T(8,128)(2,1)}) %reduce-scatter.16.cloned.1.call-update) | async-done | bytes 2097168 | tf_op jit(solution)/shard_map/reduce_scatter | solution.py:366
  2188.0 280.5 %reduce-scatter.18.cloned.1.call-done = bf16[8,256,512]{2,1,0:T(8,128)(2,1)} async-done(((bf16[8,2048,512]{2,1,0:T(8,128)(2,1)}), bf16[8,256,512]{2,1,0:T(8,128)(2,1)}) %reduce-scatter.18.cloned.1.call-update) | async-done | bytes 2097168 | tf_op jit(solution)/shard_map/reduce_scatter | solution.py:369
  (318 shorter events, 172.0 us)
Async XLA Ops:
  7.2 81.2 %all-gather.7.cloned.1.call-start = ((), (), s32[]{:S(2)}) async-start(), calls=%async_computation.11 | async-start | bytes 4718592 | tf_op jit(solution)/shard_map/all_gather | solution.py:138
  9.5 346.7 %all-gather.9.cloned.1.call-start = ((), (), s32[]{:S(2)}) async-start(), calls=%async_computation.12 | async-start | bytes 18874368 | tf_op jit(solution)/shard_map/all_gather | solution.py:136
  10.2 573.9 %all-gather.11.cloned.1.call-start = ((), (), s32[]{:S(2)}) async-start(), calls=%async_computation.13 | async-start | bytes 18874368 | tf_op jit(solution)/shard_map/all_gather | solution.py:137
  11.0 707.6 %all-reduce.4.cloned.1.call-start = ((), (), s32[]{:S(2)}) async-start(), calls=%async_computation.14 | async-start | bytes 8388608 | tf_op jit(solution)/shard_map/psum | solution.py:199
  18.2 81.5 %copy-start.7 = (bf16[512,2048]{1,0:T(8,128)(2,1)}, bf16[512,2048]{1,0:T(8,128)(2,1)S(1)}, u32[]{:S(2)}) copy-start(bf16[512,2048]{1,0:T(8,128)(2,1)S(1)} %fusion.25) | copy-start | bytes 6291460
  25.8 62.6 %copy-start.42 = (f32[512,2]{0,1:T(2,128)}, f32[512,2]{0,1:T(2,128)S(1)}, u32[]{:S(2)}) copy-start(f32[512,2]{0,1:T(2,128)S(1)} %get-tuple-element.152) | copy-start | bytes 12292
  25.8 62.6 %copy-start.50 = (f32[512]{0:T(512)}, f32[512]{0:T(512)S(1)}, u32[]{:S(2)}) copy-start(f32[512]{0:T(512)S(1)} %get-tuple-element.151) | copy-start | bytes 6148
  25.9 67.1 %copy-start.53 = (f32[512]{0:T(512)}, f32[512]{0:T(512)S(1)}, u32[]{:S(2)}) copy-start(f32[512]{0:T(512)S(1)} %fusion.101) | copy-start | bytes 6148
  26.0 380.1 %copy-start.59 = (s32[1024,1]{0,1:T(1,128)}, s32[1024,1]{0,1:T(1,128)S(1)}, u32[]{:S(2)}) copy-start(s32[1024,1]{0,1:T(1,128)S(1)} %compare_select_fusion.1) | copy-start | bytes 12292
  26.0 569.7 %copy-start.37 = (s32[1024]{0:T(1024)}, s32[1024]{0:T(1024)S(1)}, u32[]{:S(2)}) copy-start(s32[1024]{0:T(1024)S(1)} %broadcast_clamp_fusion.1) | copy-start | bytes 12292
  94.2 38.9 %collective-permute-start.3 = (bf16[512,512]{0,1:T(8,128)(2,1)}, bf16[512,512]{0,1:T(8,128)(2,1)}, u32[]{:S(2)}, u32[]{:S(2)}) collective-permute-start(bf16[512,512]{0,1:T(8,128)(2,1)} %get-tuple-element.160), channel_id=1, source_target_pairs={{0,4},{4,8},{8,12},{12,16},{16,20},{20,24},{24,28},{1,5},{5,9},{9,... | collective-permute-start | bytes 1572872 | tf_op jit(solution)/shard_map/ppermute | solution.py:21
  98.4 36.9 %collective-permute-start.2 = (bf16[512,512]{0,1:T(8,128)(2,1)}, bf16[512,512]{0,1:T(8,128)(2,1)S(1)}, u32[]{:S(2)}, u32[]{:S(2)}) collective-permute-start(bf16[512,512]{0,1:T(8,128)(2,1)} %get-tuple-element.160), channel_id=1, source_target_pairs={{0,8},{4,12},{8,16},{12,20},{16,24},{20,28},{1,9},{5,13},{9,17},{1... | collective-permute-start | bytes 1572872 | tf_op jit(solution)/shard_map/ppermute | solution.py:21
  124.7 269.5 %collective-permute-start.1 = (bf16[512,512]{0,1:T(8,128)(2,1)}, bf16[512,512]{0,1:T(8,128)(2,1)}, u32[]{:S(2)}, u32[]{:S(2)}) collective-permute-start(bf16[512,512]{0,1:T(8,128)(2,1)} %get-tuple-element.159), channel_id=1, source_target_pairs={{0,4},{4,8},{8,12},{12,16},{16,20},{20,24},{24,28},{1,5},{5,9},{9,... | collective-permute-start | bytes 1572872 | tf_op jit(solution)/shard_map/ppermute | solution.py:21
  129.3 264.9 %collective-permute-start = (bf16[512,512]{0,1:T(8,128)(2,1)}, bf16[512,512]{0,1:T(8,128)(2,1)}, u32[]{:S(2)}, u32[]{:S(2)}) collective-permute-start(bf16[512,512]{0,1:T(8,128)(2,1)} %get-tuple-element.159), channel_id=1, source_target_pairs={{0,8},{4,12},{8,16},{12,20},{16,24},{20,28},{1,9},{5,13},{9,17},{1... | collective-permute-start | bytes 1572872 | tf_op jit(solution)/shard_map/ppermute | solution.py:21
  371.6 12.3 copy-start.19
  383.9 10.3 copy-start.46
  394.2 11.1 copy-start.48
  411.9 183.8 %copy-start.13 = (bf16[1280,512]{1,0:T(8,128)(2,1)}, bf16[1280,512]{1,0:T(8,128)(2,1)S(1)}, u32[]{:S(2)}) copy-start(bf16[1280,512]{1,0:T(8,128)(2,1)S(1)} %scatter_custom_fusion.1) | copy-start | bytes 3932164
  608.5 10.6 copy-start.21
  634.6 83.9 %copy-start.10 = (bf16[512,2048]{1,0:T(8,128)(2,1)S(1)}, bf16[512,2048]{1,0:T(8,128)(2,1)}, u32[]{:S(2)}) copy-start(bf16[512,2048]{1,0:T(8,128)(2,1)} %param.16) | copy-start | bytes 6291460
  634.6 318.4 %reduce-scatter.10.cloned.1.call-start = ((), (), s32[]{:S(2)}) async-start(), calls=%async_computation.15 | async-start | bytes 6553600 | tf_op jit(solution)/shard_map/reduce_scatter | solution.py:219
  638.9 82.5 %copy-start.35 = (f32[2048]{0:T(1024)}, f32[2048]{0:T(1024)S(1)}, u32[]{:S(2)}) copy-start(f32[2048]{0:T(1024)S(1)} %convert_element_type.216) | copy-start | bytes 24580
  735.9 132.5 %slice-start.4 = ((s8[5767168]{0:T(1024)(128)(4,1)}), s8[1572864]{0:T(1024)(128)(4,1)S(1)}, s32[]{:S(2)}) async-start(s8[5767168]{0:T(1024)(128)(4,1)} %bitcast.293), calls=%async_computation.29 | async-start | bytes 3145728
  746.8 121.6 %slice-start.5 = ((s8[5767168]{0:T(1024)(128)(4,1)}), s8[4194304]{0:T(1024)(128)(4,1)S(1)}, s32[]{:S(2)}) async-start(s8[5767168]{0:T(1024)(128)(4,1)} %bitcast.293), calls=%async_computation.30 | async-start | bytes 8388608
  746.8 131.9 %slice-start.6 = ((s8[5767168]{0:T(1024)(128)(4,1)}), s8[4194304]{0:T(1024)(128)(4,1)S(1)}, s32[]{:S(2)}) async-start(s8[5767168]{0:T(1024)(128)(4,1)} %bitcast.295), calls=%async_computation.31 | async-start | bytes 8388608
  868.4 24.7 slice-start.2
  878.7 14.5 slice-start.3
  953.1 37.0 %all-to-all-start.1 = ((bf16[8,160,512]{2,1,0:T(8,128)(2,1)}), bf16[8,160,512]{2,1,0:T(8,128)(2,1)}, u32[]{:S(2)}, u32[]{:S(2)}) async-start(bf16[8,160,512]{2,1,0:T(8,128)(2,1)} %bitcast.269), calls=%async_computation.2 | async-start | bytes 2621440 | tf_op jit(solution)/shard_map/all_to_all | solution.py:225
  958.6 94.7 %all-gather.15.cloned.1.call-start = ((), (), s32[]{:S(2)}) async-start(), calls=%async_computation.23 | async-start | bytes 10485760 | tf_op jit(solution)/shard_map/all_gather | solution.py:274
  958.6 38.0 %copy-start.51 = (s32[1024]{0:T(1024)}, s32[1024]{0:T(1024)S(1)}, u32[]{:S(2)}) copy-start(s32[1024]{0:T(1024)S(1)} %broadcast_clamp_fusion) | copy-start | bytes 12292
  996.7 324.2 %reduce-scatter.12.cloned.1.call-start = ((), (), s32[]{:S(2)}) async-start(), calls=%async_computation.16 | async-start | bytes 13107200 | tf_op jit(solution)/shard_map/reduce_scatter | solution.py:262
  1005.6 11.6 copy-start.5
  1005.6 11.6 copy-start.33
  1060.3 11.8 copy-start.23
  1193.8 18.2 copy-start.17
  1237.3 148.6 %copy-start.52 = (s32[1024]{0:T(1024)S(1)}, s32[1024]{0:T(1024)}, u32[]{:S(2)}) copy-start(s32[1024]{0:T(1024)} %copy-done.51) | copy-start | bytes 12292
  1237.3 194.9 %all-gather.13.cloned.1.call-start = ((), (), s32[]{:S(2)}) async-start(), calls=%async_computation.17 | async-start | bytes 5242880 | tf_op jit(solution)/shard_map/all_gather | solution.py:273
  1394.4 37.8 %copy-start.34 = (bf16[2048,16]{0,1:T(8,128)(2,1)S(1)}, bf16[2048,16]{0,1:T(8,128)(2,1)}, u32[]{:S(2)}) copy-start(bf16[2048,16]{0,1:T(8,128)(2,1)} %param.22) | copy-start | bytes 196612
  1394.4 37.8 %copy-start.36 = (f32[2048]{0:T(1024)S(1)}, f32[2048]{0:T(1024)}, u32[]{:S(2)}) copy-start(f32[2048]{0:T(1024)} %copy-done.35) | copy-start | bytes 24580
  1394.4 37.8 %copy-start.55 = (f32[512]{0:T(512)S(1)}, f32[512]{0:T(512)}, u32[]{:S(2)}) copy-start(f32[512]{0:T(512)} %copy-done.54) | copy-start | bytes 6148
  1399.5 285.0 %all-reduce.6.cloned.1.call-start = ((), (), s32[]{:S(2)}) async-start(), calls=%async_computation.18 | async-start | bytes 4194304 | tf_op jit(solution)/shard_map/psum | solution.py:351
  1401.0 36.8 %copy-start.15 = (bf16[512,2048]{1,0:T(8,128)(2,1)S(1)}, bf16[512,2048]{1,0:T(8,128)(2,1)}, u32[]{:S(2)}) copy-start(bf16[512,2048]{1,0:T(8,128)(2,1)} %param.29) | copy-start | bytes 6291460
  1515.8 22.1 copy-start.27
  1515.9 22.1 copy-start.28
  1515.9 22.1 copy-start.29
  1559.5 55.9 %collective-permute-start.7 = (bf16[512,4,128]{0,2,1:T(8,128)(2,1)}, bf16[512,4,128]{0,2,1:T(8,128)(2,1)S(1)}, u32[]{:S(2)}, u32[]{:S(2)}) collective-permute-start(bf16[512,4,128]{0,2,1:T(8,128)(2,1)} %get-tuple-element.158), channel_id=1, source_target_pairs={{8,0},{12,4},{16,8},{20,12},{24,16},{28,20},{9,1},{13,5},{17,9},{2... | collective-permute-start | bytes 1572872 | tf_op jit(solution)/shard_map/ppermute | solution.py:21
  1560.8 54.6 %collective-permute-start.6 = (bf16[512,4,128]{0,2,1:T(8,128)(2,1)}, bf16[512,4,128]{0,2,1:T(8,128)(2,1)S(1)}, u32[]{:S(2)}, u32[]{:S(2)}) collective-permute-start(bf16[512,4,128]{0,2,1:T(8,128)(2,1)} %get-tuple-element.157), channel_id=1, source_target_pairs={{4,0},{8,4},{12,8},{16,12},{20,16},{24,20},{28,24},{5,1},{9,5},{13... | collective-permute-start | bytes 1572872 | tf_op jit(solution)/shard_map/ppermute | solution.py:21
  1564.4 53.6 %collective-permute-start.5 = (bf16[512,4,128]{0,2,1:T(8,128)(2,1)}, bf16[512,4,128]{0,2,1:T(8,128)(2,1)S(1)}, u32[]{:S(2)}, u32[]{:S(2)}) collective-permute-start(bf16[512,4,128]{0,2,1:T(8,128)(2,1)} %get-tuple-element.156), channel_id=1, source_target_pairs={{8,0},{12,4},{16,8},{20,12},{24,16},{28,20},{9,1},{13,5},{17,9},{2... | collective-permute-start | bytes 1572872 | tf_op jit(solution)/shard_map/ppermute | solution.py:21
  1565.7 52.3 %collective-permute-start.4 = (bf16[512,4,128]{0,2,1:T(8,128)(2,1)}, bf16[512,4,128]{0,2,1:T(8,128)(2,1)S(1)}, u32[]{:S(2)}, u32[]{:S(2)}) collective-permute-start(bf16[512,4,128]{0,2,1:T(8,128)(2,1)} %get-tuple-element.155), channel_id=1, source_target_pairs={{4,0},{8,4},{12,8},{16,12},{20,16},{24,20},{28,24},{5,1},{9,5},{13... | collective-permute-start | bytes 1572872 | tf_op jit(solution)/shard_map/ppermute | solution.py:21
  1627.2 16.8 copy-start.43
  1627.2 18.2 copy-start.41
  1627.2 18.2 copy-start.8
  1627.2 57.2 %copy-start.45 = (f32[2048]{0:T(1024)S(1)}, f32[2048]{0:T(1024)}, u32[]{:S(2)}) copy-start(f32[2048]{0:T(1024)} %copy-done.44) | copy-start | bytes 24580
  1627.3 141.4 %reduce-scatter.14.cloned.1.call-start = ((), (), s32[]{:S(2)}) async-start(), calls=%async_computation.19 | async-start | bytes 73728 | tf_op jit(solution)/shard_map/reduce_scatter | solution.py:378
  1647.2 159.6 %reduce-scatter.22.cloned.1.call-start = ((), (), s32[]{:S(2)}) async-start(), calls=%async_computation.24 | async-start | bytes 589824
  1691.4 206.4 %reduce-scatter.20.cloned.1.call-start = ((), (), s32[]{:S(2)}) async-start(), calls=%async_computation.22 | async-start | bytes 4718592 | tf_op jit(solution)/shard_map/reduce_scatter | solution.py:372
  1697.5 486.4 %reduce-scatter.16.cloned.1.call-start = ((), (), s32[]{:S(2)}) async-start(), calls=%async_computation.20 | async-start | bytes 18874368 | tf_op jit(solution)/shard_map/reduce_scatter | solution.py:366
  1709.0 759.5 %reduce-scatter.18.cloned.1.call-start = ((), (), s32[]{:S(2)}) async-start(), calls=%async_computation.21 | async-start | bytes 18874368 | tf_op jit(solution)/shard_map/reduce_scatter | solution.py:369
  1725.6 20.2 slice-start
  1732.3 13.4 slice-start.1
  1732.3 13.4 copy-start.64
  1745.8 11.5 copy-start.63
  1757.3 12.7 copy-start.11
  1757.3 12.7 copy-start.58
  (32 other events, 175.1 us)
Sparse Core Ops, SparseCore 0:
  10.7 77.7 all-gather.6
  90.6 265.5 all-gather.8
  358.3 225.7 all-gather.10
  634.8 83.7 all-reduce.3
  903.4 49.6 reduce-scatter.9
  996.8 56.4 all-gather.14
  1237.4 83.4 reduce-scatter.11
  1399.6 32.5 all-gather.12
  1627.3 57.1 all-reduce.5
  1687.8 53.6 reduce-scatter.13
  1745.8 60.9 reduce-scatter.21
  1810.3 87.4 reduce-scatter.19
  1902.0 281.7 reduce-scatter.15
  2187.5 281.0 reduce-scatter.17
where the time goes:
time: 2490 us; the launch traced here: 2480 us
  waiting for transfers between devices  1480 us (59%)
  blocking collectives  315 us (13%)
  matrix products  278 us (11%)
  local copies, waits for them, and re-layouts  219 us (9%)
  other arithmetic  147 us (6%)
  starting transfers between devices  25.2 us (1%)
    reduce_scatter x1, waiting for transfers between devices, per_device(): lax.psum_scatter(query_part.astype(jnp.bfloat16), 'expert', scatter_dimen...  284 us
    reduce_scatter x1, waiting for transfers between devices, per_device(): lax.psum_scatter(output_part.astype(jnp.bfloat16), 'expert', scatter_dime...  281 us
    all_gather x1, waiting for transfers between devices, per_device(): lax.all_gather(query_weight, 'expert', axis=1, tiled=True)  220 us
    all_gather x1, waiting for transfers between devices, per_device(): lax.all_gather(output_weight, 'expert', axis=1, tiled=True)  172 us
    all_to_all x1, blocking collectives, per_device(): lax.all_to_all(sent_grad, 'expert', split_axis=0, concat_axis=0, tiled=True)  122 us
    all_to_all x1, blocking collectives, per_device(): lax.all_to_all(spread_rep, 'expert', split_axis=0, concat_axis=0, tiled=T...  122 us
    reduce_scatter x1, waiting for transfers between devices, per_device(): lax.psum_scatter(pair_part.astype(jnp.bfloat16), 'expert', scatter_dimens...  89.5 us
    reduce_scatter x1, waiting for transfers between devices, per_device(): lax.psum_scatter(row_grad, 'tensor', scatter_dimension=1, tiled=True)  83.5 us
  transfers between devices with their start and end apart: 23, of which 14 were waited for; matrix products, arithmetic and copies ran while one was open for 12% of the time, Pallas kernels for 0%

commit v1 on v0

v1 whole, which is shorter than its diff:
```python
import jax
import jax.numpy as jnp
from jax import lax
from jax.sharding import PartitionSpec as P

D = 2048
HD = 128
EXPERTS = 8
TOPK = 2
WINDOW = 1024
CAP = 160
SLOTS = EXPERTS * CAP

eps = 1e-06
masked_value = -1e30
F32 = jnp.float32
BF16 = jnp.bfloat16


def dot(left, right, dims):
    return lax.dot_general(left, right, ((dims[0], dims[1]), ((), ())), preferred_element_type=F32)


def mm(left, right):
    return dot(left, right, ((1,), (0,)))


def mm_nt(left, right):
    return dot(left, right, ((1,), (1,)))


def mm_tn(left, right):
    return dot(left, right, ((0,), (0,)))


def shifted_by(shard, axis, by):
    count = lax.axis_size(axis)
    pairs = [(i, i + by) for i in range(count) if 0 <= i + by < count]
    return lax.ppermute(shard, axis, pairs)


def swap(blocks):
    return lax.all_to_all(blocks, "expert", split_axis=0, concat_axis=0, tiled=True)


def columns_together(rows):
    return lax.all_gather(rows, "tensor", axis=1, tiled=True)


def columns_summed(rows):
    return lax.psum_scatter(rows, "tensor", scatter_dimension=1, tiled=True)


def slot_places(routes):
    flat = routes.T.reshape(-1)
    one_hot = (flat[:, None] == jnp.arange(EXPERTS, dtype=jnp.int32)[None, :]).astype(jnp.int32)
    earlier = jnp.cumsum(one_hot, axis=0) - one_hot
    slots = flat * CAP + jnp.sum(earlier * one_hot, axis=1)
    return (jnp.arange(SLOTS, dtype=jnp.int32)[:, None] == slots[None, :]).astype(BF16)


def to_pieces(rows, pieces):
    if pieces == 1:
        return rows
    experts, r, c = rows.shape
    return rows.reshape(experts, r, pieces, c // pieces).transpose(0, 2, 1, 3).reshape(experts * pieces, r, -1)


def from_pieces(rows, pieces):
    if pieces == 1:
        return rows
    both, r, c = rows.shape
    return rows.reshape(both // pieces, pieces, r, c).transpose(0, 2, 1, 3).reshape(both // pieces, r, -1)


def for_pieces(rows, pieces):
    return jnp.repeat(rows, pieces, axis=0) if pieces > 1 else rows


def own_gate(logits, own, other):
    places = jnp.arange(EXPERTS, dtype=F32)[None, :]
    mine = jnp.sum(jnp.where(places == own, logits, 0.0), axis=1)
    rival = jnp.sum(jnp.where(places == other[:, None], logits, 0.0), axis=1)
    top = jnp.maximum(mine, rival)
    mine, rival = jnp.exp(mine - top), jnp.exp(rival - top)
    return (mine / (mine + rival))[:, None]


def pick_gates(logits, routes):
    one_hot = (routes[:, :, None] == jnp.arange(EXPERTS, dtype=jnp.int32)[None, None, :]).astype(F32)
    return jax.nn.softmax(jnp.sum(one_hot * logits[:, None, :], axis=2), axis=-1)


def gate_back(gating, pulled, routes):
    inner_sum = gating * (pulled - jnp.sum(gating * pulled, axis=1, keepdims=True))
    one_hot = (routes[:, :, None] == jnp.arange(EXPERTS, dtype=jnp.int32)[None, None, :]).astype(F32)
    return jnp.sum(one_hot * inner_sum[:, :, None], axis=1).astype(BF16)


def score_block(query_block, key_block, allowed):
    scores = jnp.einsum(
        "kqhd,jhd->khqj", query_block, key_block, preferred_element_type=F32
    ) * HD ** (-0.5)
    return jnp.where(allowed[None, None], scores, masked_value)


def attend(query_block, key_block, value_block, allowed):
    scores = score_block(query_block, key_block, allowed)
    row_max = jnp.max(scores, axis=-1, keepdims=True)
    shifted = jnp.exp(scores - row_max)
    row_total = jnp.sum(shifted, axis=-1, keepdims=True)
    attn_probs = (shifted / row_total).astype(BF16)
    result = jnp.einsum("khqj,jhd->kqhd", attn_probs, value_block, preferred_element_type=F32)
    return (result.astype(BF16), (row_max + jnp.log(row_total))[..., 0])


def attend_back(query_block, key_block, value_block, allowed, log_total, grad_block):
    scores = score_block(query_block, key_block, allowed)
    attn_probs = jnp.exp(scores - log_total[..., None])
    pulled = jnp.einsum("kqhd,jhd->khqj", grad_block, value_block, preferred_element_type=F32)
    row_inner = jnp.sum(attn_probs * pulled, axis=-1, keepdims=True)
    score_back = (attn_probs * (pulled - row_inner)).astype(BF16)
    query_back = jnp.einsum(
        "khqj,jhd->kqhd", score_back, key_block, preferred_element_type=F32
    ) * HD ** (-0.5)
    key_back = jnp.einsum(
        "khqj,kqhd->jhd", score_back, query_block, preferred_element_type=F32
    ) * HD ** (-0.5)
    value_back = jnp.einsum(
        "khqj,kqhd->jhd", attn_probs.astype(BF16), grad_block, preferred_element_type=F32
    )
    return (query_back, key_back, value_back)


def per_device(
    tokens,
    segment_ids,
    attn_routes,
    ffn_routes,
    attn_gain,
    ffn_gain,
    routers,
    query_weight,
    output_weight,
    key_value_weight,
    gate_weight,
    up_weight,
    down_weight,
    cotangent,
):
    rows_here = tokens.shape[0]
    expert_count = lax.axis_size("expert")
    tensor_count = lax.axis_size("tensor")
    pieces = expert_count // EXPERTS
    column_count = D // tensor_count
    expert_index = lax.axis_index("expert")
    tensor_index = lax.axis_index("tensor")
    own = (expert_index // pieces).astype(F32)
    head_width = query_weight.shape[2]
    head_count = head_width // HD
    depth = (WINDOW + rows_here - 1) // rows_here

    def cols(whole):
        return lax.dynamic_slice_in_dim(whole, tensor_index * column_count, column_count, whole.ndim - 1)

    def tokens_to_experts(token_cols, places):
        grouped = mm(places, token_cols).astype(BF16).reshape(EXPERTS, CAP, -1)
        return columns_together(swap(for_pieces(grouped, pieces)).reshape(-1, column_count))

    def choices_to_experts(choice_rows, places):
        grouped = mm(places, choice_rows).astype(BF16).reshape(EXPERTS, CAP, -1)
        out = swap(to_pieces(grouped, pieces))
        return out.reshape(-1, out.shape[2])

    def choices_from_experts(rows, places):
        back = from_pieces(swap(rows.reshape(expert_count, CAP, -1)), pieces)
        return mm_tn(places, back.reshape(SLOTS, -1)).astype(BF16)

    def sums_from_experts(part_rows, places):
        back = swap(columns_summed(part_rows.astype(BF16)).reshape(expert_count, CAP, column_count))
        back = back.reshape(EXPERTS, pieces, CAP, column_count)
        if pieces > 1:
            total = sum(mm_tn(places, back[:, p].reshape(SLOTS, -1)) for p in range(pieces))
        else:
            total = mm_tn(places, back.reshape(SLOTS, -1))
        return total

    def scalars_from_experts(scalars, places):
        n = scalars.shape[1]
        back = swap(lax.psum(scalars, "tensor").reshape(expert_count, CAP, n))
        back = back.reshape(EXPERTS, pieces, CAP, n).sum(1).reshape(SLOTS, n)
        got = lax.dot_general(
            places.astype(F32), back, (((0,), (0,)), ((), ())), precision=lax.Precision.HIGHEST,
            preferred_element_type=F32)
        return got.reshape(TOPK, rows_here, n)

    state_in = tokens.astype(F32)
    gain_one = attn_gain.astype(F32)
    gain_two = cols(ffn_gain.astype(F32))
    routers_one, routers_two = routers[:, :EXPERTS], routers[:, EXPERTS:]
    dy_cols = cols(cotangent)
    token_cols = cols(tokens).astype(F32)

    attn_places = slot_places(attn_routes)
    ffn_places = slot_places(ffn_routes)
    attn_tokens = attn_places[:, :rows_here] + attn_places[:, rows_here:]
    ffn_tokens = ffn_places[:, :rows_here] + ffn_places[:, rows_here:]
    others = jnp.stack([
        mm(attn_places, attn_routes[:, ::-1].T.reshape(-1, 1).astype(BF16)),
        mm(ffn_places, ffn_routes[:, ::-1].T.reshape(-1, 1).astype(BF16)),
    ]).reshape(2, EXPERTS, CAP).transpose(1, 0, 2)
    others = swap(for_pieces(others, pieces)).transpose(1, 0, 2).reshape(2, -1)

    rate_one = lax.rsqrt(jnp.mean(state_in * state_in, axis=1, keepdims=True) + eps)
    normed_one = (state_in * rate_one * gain_one).astype(BF16)

    query_map = swap(to_pieces(query_weight, pieces)).reshape(D, -1)
    output_map = swap(to_pieces(output_weight, pieces)).reshape(D, -1)
    pair_map = lax.all_gather(key_value_weight, "expert", axis=1, tiled=True)

    pair = jnp.einsum("td,cdf->ctf", normed_one, pair_map, preferred_element_type=F32).astype(BF16)
    keys, values = pair[0], pair[1]
    rows_one = tokens_to_experts(cols(normed_one), attn_tokens)
    query_rows = mm(rows_one, query_map).astype(BF16)
    queries = choices_from_experts(query_rows, attn_places).reshape(TOPK, rows_here, head_count, HD)
    earlier_keys, earlier_values = [], []
    for step in range(depth):
        got_keys, got_values = shifted_by((keys, values), "expert", step + 1)
        earlier_keys.append(got_keys)
        earlier_values.append(got_values)
    span = (depth + 1) * rows_here
    key_cat = jnp.concatenate(earlier_keys[::-1] + [keys]).reshape(span, head_count, HD)
    value_cat = jnp.concatenate(earlier_values[::-1] + [values]).reshape(span, head_count, HD)
    padded_segments = jnp.concatenate([jnp.full((depth * rows_here,), -1, jnp.int32), segment_ids])
    segment_cat = lax.dynamic_slice_in_dim(padded_segments, expert_index * rows_here, span)
    own_segments = lax.dynamic_slice_in_dim(segment_ids, expert_index * rows_here, rows_here)
    distance = jnp.arange(rows_here)[:, None] + depth * rows_here - jnp.arange(span)[None, :]
    allowed = (distance >= 0) & (distance < WINDOW) & (own_segments[:, None] == segment_cat[None, :])
    heads, log_total = attend(queries, key_cat, value_cat, allowed)
    heads_rows = choices_to_experts(heads.reshape(TOPK * rows_here, head_width), attn_places)

    attn_logits_there = mm(rows_one, routers_one)
    attn_gate_rows = own_gate(attn_logits_there, own, others[0])
    attn_back = attn_gate_rows * mm_nt(heads_rows, output_map)
    state = token_cols + sums_from_experts(attn_back, attn_tokens)

    mean_two = lax.psum(jnp.sum(state * state, axis=1, keepdims=True), "tensor") / D
    rate_two = lax.rsqrt(mean_two + eps)
    normed_two = (state * rate_two * gain_two).astype(BF16)
    rows_dy = tokens_to_experts(dy_cols, ffn_tokens)
    rows_two = tokens_to_experts(normed_two, ffn_tokens)
    gate_map, up_map, down_map = gate_weight[0], up_weight[0], down_weight[0]
    ffn_gate_rows = own_gate(mm(rows_two, routers_two), own, others[1])
    hidden_grad = mm_nt(rows_dy, down_map)
    gate_pre = mm(rows_two, gate_map)
    up_pre = mm(rows_two, up_map)
    sigma = 1.0 / (1.0 + jnp.exp(-gate_pre))
    silu = gate_pre * sigma
    hidden = (silu * up_pre).astype(BF16)
    scaled_grad = hidden_grad * ffn_gate_rows
    gate_low = (scaled_grad * up_pre * (sigma * (1.0 + gate_pre * (1.0 - sigma)))).astype(BF16)
    up_low = (scaled_grad * silu).astype(BF16)
    ffn_pull_part = jnp.sum(hidden.astype(F32) * hidden_grad, axis=1, keepdims=True)
    gate_part = ffn_gate_rows / tensor_count
    ffn_scalars = scalars_from_experts(jnp.concatenate([ffn_pull_part, gate_part / pieces], axis=1), ffn_places)
    row_grad = mm_nt(gate_low, gate_map) + mm_nt(up_low, up_map)
    normed_two_grad = sums_from_experts(row_grad, ffn_tokens)
    ffn_pull, ffn_gates = ffn_scalars[:, :, 0].T, ffn_scalars[:, :, 1].T
    ffn_logit_grad = gate_back(ffn_gates, ffn_pull, ffn_routes)
    normed_two_grad = normed_two_grad + mm_nt(
        ffn_logit_grad, lax.dynamic_slice_in_dim(routers_two, tensor_index * column_count, column_count, 0))
    ffn_router_cols = mm_tn(normed_two, ffn_logit_grad)
    ffn_gain_cols = jnp.sum(normed_two_grad * state * rate_two, axis=0)
    ahead = normed_two_grad * gain_two
    centre = lax.psum(jnp.sum(ahead * state, axis=1, keepdims=True), "tensor") / D
    state_grad = dy_cols.astype(F32) + rate_two * ahead - state * rate_two * rate_two * rate_two * centre

    rows_state = tokens_to_experts(state_grad.astype(BF16), attn_tokens)
    heads_grad_rows = mm(rows_state, output_map)
    attn_pull_part = jnp.sum(heads_grad_rows * heads_rows.astype(F32), axis=1, keepdims=True)
    heads_grad = choices_from_experts((heads_grad_rows * attn_gate_rows).astype(BF16), attn_places)
    output_part = mm_tn((rows_state.astype(F32) * attn_gate_rows).astype(BF16), heads_rows)
    attn_pull = scalars_from_experts(attn_pull_part, attn_places)[:, :, 0].T

    query_back, key_back, value_back = attend_back(
        queries, key_cat, value_cat, allowed, log_total, heads_grad.reshape(TOPK, rows_here, head_count, HD))
    key_back = key_back.reshape(span, head_width)
    value_back = value_back.reshape(span, head_width)
    key_total, value_total = key_back[depth * rows_here:], value_back[depth * rows_here:]
    for step in range(1, depth + 1):
        lower = (depth - step) * rows_here
        key_total = key_total + shifted_by(
            key_back[lower : lower + rows_here].astype(BF16), "expert", -step).astype(F32)
        value_total = value_total + shifted_by(
            value_back[lower : lower + rows_here].astype(BF16), "expert", -step).astype(F32)
    keys_grad, values_grad = key_total.astype(BF16), value_total.astype(BF16)
    query_grad_rows = choices_to_experts(
        query_back.reshape(TOPK * rows_here, head_width).astype(BF16), attn_places)
    query_part = mm_tn(rows_one, query_grad_rows)
    normed_grad = sums_from_experts(mm_nt(query_grad_rows, query_map), attn_tokens)
    pair_grad = jnp.stack([keys_grad, values_grad])
    pair_part = jnp.einsum("td,ctf->cdf", normed_one, pair_grad, preferred_element_type=F32)
    pair_back = jnp.einsum("ctf,cdf->td", pair_grad, pair_map, preferred_element_type=F32)
    normed_grad = normed_grad + columns_summed(pair_back.astype(BF16)).astype(F32)
    attn_gates = pick_gates(mm(normed_one, routers_one), attn_routes)
    attn_logit_grad = gate_back(attn_gates, attn_pull, attn_routes)
    normed_grad = normed_grad + mm_nt(
        attn_logit_grad, lax.dynamic_slice_in_dim(routers_one, tensor_index * column_count, column_count, 0))
    attn_router_cols = mm_tn(cols(normed_one), attn_logit_grad)
    attn_gain_cols = jnp.sum(normed_grad * token_cols * rate_one, axis=0)
    ahead_one = normed_grad * cols(gain_one)
    centre_one = lax.psum(jnp.sum(ahead_one * token_cols, axis=1, keepdims=True), "tensor") / D
    tokens_grad = state_grad + rate_one * ahead_one - token_cols * rate_one * rate_one * rate_one * centre_one
    tokens_grad = columns_together(tokens_grad)

    def from_maps(part):
        got = swap(part.astype(BF16).reshape(expert_count, D // expert_count, -1))
        return from_pieces(got, pieces).astype(F32)

    query_grad, output_grad = from_maps(query_part), from_maps(output_part)
    key_value_grad = lax.psum_scatter(
        pair_part.astype(BF16), "expert", scatter_dimension=1, tiled=True).astype(F32)
    small = jnp.concatenate(
        [attn_router_cols, ffn_router_cols, attn_gain_cols[:, None], ffn_gain_cols[:, None]], axis=1)
    small = lax.all_gather(small, "tensor", axis=0, tiled=True)
    small = lax.psum_scatter(small, "expert", scatter_dimension=0, tiled=True)

    scaled_dy = (rows_dy.astype(F32) * ffn_gate_rows).astype(BF16)
    gate_grad = mm_tn(rows_two, gate_low)
    up_grad = mm_tn(rows_two, up_low)
    down_grad = mm_tn(hidden, scaled_dy)
    ffn_back = sums_from_experts(mm(hidden, down_map) * ffn_gate_rows, ffn_tokens)
    mixed = (state + ffn_back).astype(BF16)
    return (
        mixed,
        tokens_grad,
        small[:, 2 * EXPERTS],
        small[:, 2 * EXPERTS + 1],
        small[:, : 2 * EXPERTS],
        query_grad,
        output_grad,
        key_value_grad,
        gate_grad[None],
        up_grad[None],
        down_grad[None],
    )


def solution(mesh):
    in_specs = (
        P("expert", None),
        P(),
        P("expert", None),
        P("expert", None),
        P(),
        P(),
        P(),
        P(None, "expert", "tensor"),
        P(None, "expert", "tensor"),
        P(None, "expert", "tensor"),
        P("expert", None, "tensor"),
        P("expert", None, "tensor"),
        P("expert", "tensor", None),
        P("expert", None),
    )
    out_specs = (
        P("expert", "tensor"),
        P("expert", None),
        P("expert"),
        P("expert"),
        P("expert", None),
        P(None, "expert", "tensor"),
        P(None, "expert", "tensor"),
        P(None, "expert", "tensor"),
        P("expert", None, "tensor"),
        P("expert", None, "tensor"),
        P("expert", "tensor", None),
    )
    return jax.shard_map(
        per_device, mesh=mesh, in_specs=in_specs, out_specs=out_specs, check_vma=False
    )
```

time: 2490 us -> 1360 us (0.55)
  waiting for transfers between devices: 1480 us -> 571 us
  local copies, waits for them, and re-layouts: 219 us -> 52.4 us
  other arithmetic: 147 us -> 60.8 us
  starting transfers between devices: 25.2 us -> 95.9 us
  blocking collectives: 315 us -> 250 us
    reduce_scatter x6 -> x7, waiting for transfers between devices: 787 us -> 120 us  [the longest x5 79.6 us: columns_summed(): return lax.psum_scatter(rows, 'tensor', scatter_dimension=1, tiled=True)]
    all_gather x5 -> x6, waiting for transfers between devices: 514 us -> 147 us  [the longest x5 77.5 us: columns_together(): return lax.all_gather(rows, 'tensor', axis=1, tiled=True)]
    all_to_all x1 -> x12, waiting for transfers between devices: 31.4 us -> 293 us  [swap(): lax.all_to_all(blocks, 'expert', split_axis=0, concat_axis=0, tiled=True)]
    psum x2 -> x0, waiting for transfers between devices: 117 us -> none  [the longest x1 79.5 us: per_device(): attn_out = lax.psum(attn_part, 'tensor')]
    all_to_all x3 -> x7, blocking collectives: 308 us -> 209 us  [swap(): lax.all_to_all(blocks, 'expert', split_axis=0, concat_axis=0, tiled=True)]
    all_to_all x1 -> x12, starting transfers between devices: 5.51 us -> 67 us  [swap(): lax.all_to_all(blocks, 'expert', split_axis=0, concat_axis=0, tiled=True)]
    gather x16 -> x0, local copies, waits for them, and re-layouts: 57.7 us -> none  [the longest x10 14.3 us: pick_gates(): chosen = jnp.take_along_axis(logits, routes, axis=1)]
    reduce_sum x13 -> x6, other arithmetic: 56.7 us -> 0.13 us  [the longest x2 0.05 us: slot_places(): slots = flat * CAP + jnp.sum(earlier * one_hot, axis=1)]
  transfers between devices with their start and end apart: 23 -> 33, of which waited for: 14 -> 18; matrix products, arithmetic and copies ran while one was open for 12% -> 20% of each run, Pallas kernels for 0% -> 0%
where the time goes in v1:
time: 1360 us; the launch traced here: 1340 us
  waiting for transfers between devices  571 us (42%)
  matrix products  298 us (22%)
  blocking collectives  250 us (18%)
  starting transfers between devices  95.9 us (7%)
  other arithmetic  60.8 us (4%)
  local copies, waits for them, and re-layouts  52.4 us (4%)
  between operations  15.1 us (1%)
    all_to_all x12, waiting for transfers between devices, swap(): lax.all_to_all(blocks, 'expert', split_axis=0, concat_axis=0, tiled=True)  293 us
    dot_general x36, matrix products, dot(): lax.dot_general(left, right, ((dims[0], dims[1]), ((), ())), preferred_el...  209 us
    all_to_all x7, blocking collectives, swap(): lax.all_to_all(blocks, 'expert', split_axis=0, concat_axis=0, tiled=True)  209 us
    reduce_scatter x5, waiting for transfers between devices, columns_summed(): return lax.psum_scatter(rows, 'tensor', scatter_dimension=1, tiled=True)  79.6 us
    all_gather x5, waiting for transfers between devices, columns_together(): return lax.all_gather(rows, 'tensor', axis=1, tiled=True)  77.5 us
    all_gather x1, waiting for transfers between devices, per_device(): pair_map = lax.all_gather(key_value_weight, 'expert', axis=1, tiled=True)  70 us
    all_to_all x12, starting transfers between devices, swap(): lax.all_to_all(blocks, 'expert', split_axis=0, concat_axis=0, tiled=True)  67 us
    reduce_scatter x1, waiting for transfers between devices, per_device(): small = lax.psum_scatter(small, 'expert', scatter_dimension=0, tiled=True)  40.1 us
  transfers between devices with their start and end apart: 33, of which 18 were waited for; matrix products, arithmetic and copies ran while one was open for 20% of the time, Pallas kernels for 0%

profile of v1, /device:TPU:0, one launch (start us, length us, event | category | flops | bytes accessed | tf_op | source)
XLA Modules:
  0.0 1343.6 jit_solution(2160749130347236074)
XLA Ops:
  19.3 38.7 %all_to_all.95 = bf16[8,160,512]{2,1,0:T(8,128)(2,1)} all-to-all(bf16[8,160,512]{2,1,0:T(8,128)(2,1)S(1)} %bitcast.337), channel_id=1, replica_groups=mesh['expert'=8,'tensor'=4] {'expert'}, dimensions={0} | all-to-all | bytes 2621440 | tf_op jit(solution)/shard_map/all_to_all | solution.py:43
  66.5 44.3 %all-to-all-done.2 = bf16[8,256,512]{2,1,0:T(8,128)(2,1)} async-done(((bf16[8,256,512]{2,1,0:T(8,128)(2,1)}), bf16[8,256,512]{2,1,0:T(8,128)(2,1)}, u32[]{:S(2)}, u32[]{:S(2)}) %all-to-all-start.2) | async-done | bytes 2097184 | tf_op jit(solution)/shard_map/all_to_all | solution.py:43
  110.8 7.1 convolution_convert_fusion.5
  125.2 70.0 %all-gather.9.cloned.1.call-done = bf16[2,2048,512]{1,2,0:T(8,128)(2,1)} async-done(((bf16[2,256,512]{1,2,0:T(8,128)(2,1)}), bf16[2,2048,512]{1,2,0:T(8,128)(2,1)}) %all-gather.9.cloned.1.call-update) | async-done | bytes 4194320 | tf_op jit(solution)/shard_map/all_gather | solution.py:219
  195.1 5.2 fusion.65
  212.8 5.3 collective-permute-start
  222.2 13.9 %all-to-all-start.1 = ((f32[8,2,160]{2,1,0:T(2,128)}), f32[8,2,160]{2,1,0:T(2,128)S(1)}, u32[]{:S(2)}, u32[]{:S(2)}) async-start(f32[8,2,160]{2,1,0:T(2,128)} %maximum_bitcast_fusion.6), calls=%async_computation.1 | async-start | bytes 32768 | tf_op jit(solution)/shard_map/all_to_all | solution.py:43
  241.7 12.2 fusion.139
  253.9 10.1 fusion.3
  264.1 6.1 all-to-all-start.5
  270.3 11.9 fusion.69
  286.5 30.2 %all-to-all-done.5 = bf16[8,256,512]{2,1,0:T(8,128)(2,1)} async-done(((bf16[8,256,512]{2,1,0:T(8,128)(2,1)}), bf16[8,256,512]{2,1,0:T(8,128)(2,1)}, u32[]{:S(2)}, u32[]{:S(2)}) %all-to-all-start.5) | async-done | bytes 2097184 | tf_op jit(solution)/shard_map/all_to_all | solution.py:43
  325.0 26.7 %all-to-all-done.4 = bf16[8,160,512]{2,1,0:T(8,128)(2,1)S(1)} async-done(((bf16[8,160,512]{2,1,0:T(8,128)(2,1)}), bf16[8,160,512]{2,1,0:T(8,128)(2,1)S(1)}, u32[]{:S(2)}, u32[]{:S(2)}) %all-to-all-start.4) | async-done | bytes 1310752 | tf_op jit(solution)/shard_map/all_to_all | solution.py:43
  351.7 6.7 multiply_convert_fusion.3
  358.4 50.6 %reduce-scatter.8.cloned.1.call-done = bf16[1280,512]{1,0:T(8,128)(2,1)} async-done(((bf16[1280,2048]{1,0:T(8,128)(2,1)}), bf16[1280,512]{1,0:T(8,128)(2,1)}) %reduce-scatter.8.cloned.1.call-update) | async-done | bytes 1310736 | tf_op jit(solution)/shard_map/reduce_scatter | solution.py:51
  408.9 5.5 all-to-all-start.6
  419.8 26.2 %all-to-all-done.6 = bf16[8,160,512]{2,1,0:T(8,128)(2,1)} async-done(((bf16[8,160,512]{2,1,0:T(8,128)(2,1)}), bf16[8,160,512]{2,1,0:T(8,128)(2,1)}, u32[]{:S(2)}, u32[]{:S(2)}) %all-to-all-start.6) | async-done | bytes 1310752 | tf_op jit(solution)/shard_map/all_to_all | solution.py:43
  448.7 5.9 psum.35
  456.9 34.7 %all_to_all.96 = bf16[8,160,512]{2,1,0:T(8,128)(2,1)} all-to-all(bf16[8,160,512]{2,1,0:T(8,128)(2,1)S(1)} %bitcast.338), channel_id=1, replica_groups=mesh['expert'=8,'tensor'=4] {'expert'}, dimensions={0} | all-to-all | bytes 2621440 | tf_op jit(solution)/shard_map/all_to_all | solution.py:43
  494.2 34.5 %all_to_all.97 = bf16[8,160,512]{2,1,0:T(8,128)(2,1)} all-to-all(bf16[8,160,512]{2,1,0:T(8,128)(2,1)S(1)} %bitcast.339), channel_id=1, replica_groups=mesh['expert'=8,'tensor'=4] {'expert'}, dimensions={0} | all-to-all | bytes 2621440 | tf_op jit(solution)/shard_map/all_to_all | solution.py:43
  528.7 8.6 reduce-scatter.12.cloned.1.call-start
  537.4 4.7 select_reduce_fusion
  542.9 12.5 fusion.14
  555.4 10.3 fusion.18
  565.7 6.5 all-gather.13.cloned.1.call-done
  572.3 19.1 %multiply_reduce_fusion = (f32[1280]{0:T(1024)S(1)}, bf16[1280,1408]{1,0:T(8,128)(2,1)}, bf16[1280,1408]{1,0:T(8,128)(2,1)}, bf16[1280,1408]{1,0:T(8,128)(2,1)}) fusion(f32[1280,1408]{1,0:T(8,128)} %fusion.14, f32[1280,1408]{1,0:T(8,128)} %fusion.18, f32[1280]{0:T(1024)S(1)} %add_divide_fusion.1, bf16[1280,2048]{1,0:T(8,128)(2,1)} %all-gather.13.cloned.1.call-done, ...), kind=kOutput, calls=%fused_computation.23 | convolution fusion | flops 7416216576 | bytes 36251648 | tf_op jit(solution)/shard_map/dot_general | solution.py:21
  591.3 11.7 fusion.16
  603.0 13.2 add_convert_fusion
  616.4 10.2 psum.36
  626.6 12.0 all_to_all.98
  638.7 29.1 %reduce-scatter.12.cloned.1.call-done = bf16[1280,512]{1,0:T(8,128)(2,1)} async-done(((bf16[1280,2048]{1,0:T(8,128)(2,1)}), bf16[1280,512]{1,0:T(8,128)(2,1)}) %reduce-scatter.12.cloned.1.call-update) | async-done | bytes 1310736 | tf_op jit(solution)/shard_map/reduce_scatter | solution.py:51
  667.8 5.6 all-to-all-start.10
  676.8 28.1 %all-to-all-done.10 = bf16[8,160,512]{2,1,0:T(8,128)(2,1)} async-done(((bf16[8,160,512]{2,1,0:T(8,128)(2,1)}), bf16[8,160,512]{2,1,0:T(8,128)(2,1)}, u32[]{:S(2)}, u32[]{:S(2)}) %all-to-all-start.10) | async-done | bytes 1310752 | tf_op jit(solution)/shard_map/all_to_all | solution.py:43
  708.1 5.9 psum.37
  716.5 35.1 %all_to_all.99 = bf16[8,160,512]{2,1,0:T(8,128)(2,1)} all-to-all(bf16[8,160,512]{2,1,0:T(8,128)(2,1)S(1)} %bitcast.340), channel_id=1, replica_groups=mesh['expert'=8,'tensor'=4] {'expert'}, dimensions={0} | all-to-all | bytes 2621440 | tf_op jit(solution)/shard_map/all_to_all | solution.py:43
  751.6 38.6 %all-gather.15.cloned.1.call-done = bf16[1280,2048]{1,0:T(8,128)(2,1)} async-done(((bf16[1280,512]{1,0:T(8,128)(2,1)}), bf16[1280,2048]{1,0:T(8,128)(2,1)}) %all-gather.15.cloned.1.call-update) | async-done | bytes 5242896 | tf_op jit(solution)/shard_map/all_gather | solution.py:47
  790.2 7.5 multiply_reduce_fusion.1
  797.7 5.5 all-to-all-start.13
  803.3 31.7 %all-to-all-done.13 = bf16[8,160,512]{2,1,0:T(8,128)(2,1)S(1)} async-done(((bf16[8,160,512]{2,1,0:T(8,128)(2,1)}), bf16[8,160,512]{2,1,0:T(8,128)(2,1)S(1)}, u32[]{:S(2)}, u32[]{:S(2)}) %all-to-all-start.13) | async-done | bytes 1310752 | tf_op jit(solution)/shard_map/all_to_all | solution.py:43
  839.6 15.9 %fusion = (f32[2,4,512]{2,0,1:T(2,128)S(1)}, f32[4,1536,2,512]{3,1,2,0:T(8,128)}) fusion(f32[2,4,512,1536]{2,3,0,1:T(8,128)} %get-tuple-element.99, f32[2,4,512]{2,0,1:T(2,128)S(1)} %bitcast.344, bf16[2,512,4,128]{1,3,0,2:T(8,128)(2,1)S(1)} %copy.213, bf16[512,4,128]{0,2,1:T(8,128)(2,1)} %bitcast.316, bf16[512,4,128]{0,2,1:T(8,128)(2,1)} %bitcast.16, ...), kind=kOutput, calls=%fused_computation.2 | convolution fusion | flops 1634201600 | bytes 52985856 | tf_op jit(solution)/shard_map/kqhd,jhd->khqj/dot_general | solution.py:120
  855.6 17.3 %fusion.2 = bf16[2,4,512,1536]{2,3,0,1:T(8,128)(2,1)S(1)} fusion(f32[4,1536,2,512]{3,1,2,0:T(8,128)} %get-tuple-element.104, f32[2,4,512,1536]{2,3,0,1:T(8,128)} %get-tuple-element.99, f32[2,4,512]{2,0,1:T(2,128)S(1)} %get-tuple-element.103, f32[2,4,512]{2,0,1:T(2,128)S(1)} %bitcast.345), kind=kLoop, calls=%fused_computation.4 | loop fusion | flops 25165824 | bytes 62947328 | tf_op jit(solution)/shard_map/convert_element_type | solution.py:122
  883.6 35.0 %all_to_all.100 = bf16[8,160,512]{2,1,0:T(8,128)(2,1)S(1)} all-to-all(bf16[8,160,512]{2,1,0:T(8,128)(2,1)S(1)} %bitcast.336), channel_id=1, replica_groups=mesh['expert'=8,'tensor'=4] {'expert'}, dimensions={0} | all-to-all | bytes 2621440 | tf_op jit(solution)/shard_map/all_to_all | solution.py:43
  919.7 6.2 convolution_convert_fusion
  925.9 13.2 multiply_convert_fusion.2
  939.2 15.5 %fusion.140 = (bf16[1536,4,128]{0,2,1:T(8,128)(2,1)}, f32[1536,4,128]{0,2,1:T(8,128)}) fusion(bf16[2,512,4,128]{1,3,0,2:T(8,128)(2,1)S(1)} %copy.213, f32[2,4,512,1536]{2,3,0,1:T(8,128)} %get-tuple-element.99, f32[2,4,512]{2,0,1:T(2,128)S(1)} %bitcast.346), kind=kOutput, calls=%fused_computation.252 | convolution fusion | flops 1623982080 | bytes 30949376 | tf_op jit(solution)/shard_map/khqj,kqhd->jhd/dot_general | solution.py:129
  960.6 10.8 fusion.141
  985.6 11.0 collective-permute-done.5
  1002.6 5.6 convert_bitcast_fusion
  1008.3 6.5 psum.38
  1014.9 18.6 %all_to_all.101 = f32[8,160,1]{1,2,0:T(1,128)S(1)} all-to-all(f32[8,160,1]{1,2,0:T(1,128)S(1)} %copy.221), channel_id=1, replica_groups=mesh['expert'=8,'tensor'=4] {'expert'}, dimensions={0} | all-to-all | bytes 10240 | tf_op jit(solution)/shard_map/all_to_all | solution.py:43
  1040.4 27.2 %all-to-all-done.15 = bf16[8,160,512]{2,1,0:T(8,128)(2,1)} async-done(((bf16[8,160,512]{2,1,0:T(8,128)(2,1)}), bf16[8,160,512]{2,1,0:T(8,128)(2,1)}, u32[]{:S(2)}, u32[]{:S(2)}) %all-to-all-start.15) | async-done | bytes 1310752 | tf_op jit(solution)/shard_map/all_to_all | solution.py:43
  1072.4 7.4 fusion.47
  1087.4 41.7 %all-to-all-done.8 = bf16[8,160,512]{2,1,0:T(8,128)(2,1)} async-done(((bf16[8,160,512]{2,1,0:T(8,128)(2,1)}), bf16[8,160,512]{2,1,0:T(8,128)(2,1)}, u32[]{:S(2)}, u32[]{:S(2)}) %all-to-all-start.8) | async-done | bytes 1310752 | tf_op jit(solution)/shard_map/all_to_all | solution.py:43
  1136.6 6.1 all_gather.27
  1142.7 6.9 psum.39
  1153.1 14.1 %convolution_bitcast_fusion.2 = f32[1,2048,1408]{2,1,0:T(8,128)} fusion(bf16[1280,2048]{1,0:T(8,128)(2,1)} %all-gather.11.cloned.1.call-done, bf16[1280,1408]{1,0:T(8,128)(2,1)} %get-tuple-element.80), kind=kOutput, calls=%fused_computation.21 | convolution fusion | flops 7381975040 | bytes 20381696 | tf_op jit(solution)/shard_map/dot_general | solution.py:21
  1167.2 6.7 convolution_convert_fusion.1
  1173.9 7.9 all-to-all-done.18
  1186.4 13.7 %convolution_bitcast_fusion = f32[1,1408,2048]{2,1,0:T(8,128)} fusion(bf16[1280,1408]{1,0:T(8,128)(2,1)} %get-tuple-element.79, bf16[1280,2048]{1,0:T(8,128)(2,1)} %all-gather.13.cloned.1.call-done, f32[1280]{0:T(1024)S(1)} %add_divide_fusion.1), kind=kOutput, calls=%fused_computation.19 | convolution fusion | flops 7389839360 | bytes 20386816 | tf_op jit(solution)/shard_map/dot_general | solution.py:21
  1200.1 13.1 convolution_bitcast_fusion.1
  1220.9 29.0 %all-to-all-done.17 = bf16[8,256,512]{2,1,0:T(8,128)(2,1)} async-done(((bf16[8,256,512]{2,1,0:T(8,128)(2,1)}), bf16[8,256,512]{2,1,0:T(8,128)(2,1)}, u32[]{:S(2)}, u32[]{:S(2)}) %all-to-all-start.17) | async-done | bytes 2097184 | tf_op jit(solution)/shard_map/all_to_all | solution.py:43
  1256.3 40.1 %reduce-scatter.18.cloned.1.call-done = f32[256,18]{0,1:T(8,128)} async-done(((f32[2048,18]{0,1:T(8,128)}), f32[256,18]{0,1:T(8,128)}) %reduce-scatter.18.cloned.1.call-update) | async-done | bytes 18448 | tf_op jit(solution)/shard_map/reduce_scatter | solution.py:326
  1299.2 32.4 %all-gather.17.cloned.1.call-done = f32[512,2048]{0,1:T(8,128)} async-done(((f32[512,512]{0,1:T(8,128)}), f32[512,2048]{0,1:T(8,128)}) %all-gather.17.cloned.1.call-update) | async-done | bytes 4194320 | tf_op jit(solution)/shard_map/all_gather | solution.py:47
  1331.5 5.3 copy.225
  (268 shorter events, 179.4 us)
Async XLA Ops:
  7.2 484.6 %copy-start = (bf16[512,2048]{1,0:T(8,128)(2,1)S(1)}, bf16[512,2048]{1,0:T(8,128)(2,1)}, u32[]{:S(2)}) copy-start(bf16[512,2048]{1,0:T(8,128)(2,1)} %param.27) | copy-start | bytes 6291460
  7.2 103.6 %all-gather.7.cloned.1.call-start = ((), (), s32[]{:S(2)}) async-start(), calls=%async_computation.26 | async-start | bytes 6553600 | tf_op jit(solution)/shard_map/all_gather | solution.py:47
  13.7 5.5 copy-start.28
  19.2 38.8 %copy-start.19 = (bf16[2,256,512]{2,1,0:T(8,128)(2,1)S(1)}, bf16[2,256,512]{2,1,0:T(8,128)(2,1)}, u32[]{:S(2)}) copy-start(bf16[2,256,512]{2,1,0:T(8,128)(2,1)} %param.23) | copy-start | bytes 1572868
  58.0 5.5 copy-start.26
  58.0 137.1 %all-gather.9.cloned.1.call-start = ((), (), s32[]{:S(2)}) async-start(), calls=%async_computation.27 | async-start | bytes 4718592 | tf_op jit(solution)/shard_map/all_gather | solution.py:219
  59.1 51.8 %all-to-all-start.2 = ((bf16[8,256,512]{2,1,0:T(8,128)(2,1)}), bf16[8,256,512]{2,1,0:T(8,128)(2,1)}, u32[]{:S(2)}, u32[]{:S(2)}) async-start(bf16[8,256,512]{2,1,0:T(8,128)(2,1)} %param.21), calls=%async_computation.2 | async-start | bytes 4194304 | tf_op jit(solution)/shard_map/all_to_all | solution.py:43
  118.0 5.4 copy-start.24
  118.0 6.5 copy-start.30
  118.0 104.3 %all-to-all-start.3 = ((bf16[8,160,512]{2,1,0:T(8,128)(2,1)}), bf16[8,160,512]{2,1,0:T(8,128)(2,1)}, u32[]{:S(2)}, u32[]{:S(2)}) async-start(bf16[8,160,512]{2,1,0:T(8,128)(2,1)} %bitcast.27), calls=%async_computation.3 | async-start | bytes 2621440 | tf_op jit(solution)/shard_map/all_to_all | solution.py:43
  201.5 17.6 %collective-permute-start.3 = (bf16[512,512]{0,1:T(8,128)(2,1)}, bf16[512,512]{0,1:T(8,128)(2,1)}, u32[]{:S(2)}, u32[]{:S(2)}) collective-permute-start(bf16[512,512]{0,1:T(8,128)(2,1)} %get-tuple-element.89), channel_id=1, source_target_pairs={{0,4},{4,8},{8,12},{12,16},{16,20},{20,24},{24,28},{1,5},{5,9},{9,... | collective-permute-start | bytes 1572872 | tf_op jit(solution)/shard_map/ppermute | solution.py:39
  204.4 16.9 %collective-permute-start.2 = (bf16[512,512]{0,1:T(8,128)(2,1)}, bf16[512,512]{0,1:T(8,128)(2,1)S(1)}, u32[]{:S(2)}, u32[]{:S(2)}) collective-permute-start(bf16[512,512]{0,1:T(8,128)(2,1)} %get-tuple-element.89), channel_id=1, source_target_pairs={{0,8},{4,12},{8,16},{12,20},{16,24},{20,28},{1,9},{5,13},{9,17},{1... | collective-permute-start | bytes 1572872 | tf_op jit(solution)/shard_map/ppermute | solution.py:39
  209.6 60.7 %collective-permute-start.1 = (bf16[512,512]{0,1:T(8,128)(2,1)}, bf16[512,512]{0,1:T(8,128)(2,1)}, u32[]{:S(2)}, u32[]{:S(2)}) collective-permute-start(bf16[512,512]{0,1:T(8,128)(2,1)} %get-tuple-element.88), channel_id=1, source_target_pairs={{0,4},{4,8},{8,12},{12,16},{16,20},{20,24},{24,28},{1,5},{5,9},{9,... | collective-permute-start | bytes 1572872 | tf_op jit(solution)/shard_map/ppermute | solution.py:39
  212.8 57.4 %collective-permute-start = (bf16[512,512]{0,1:T(8,128)(2,1)}, bf16[512,512]{0,1:T(8,128)(2,1)}, u32[]{:S(2)}, u32[]{:S(2)}) collective-permute-start(bf16[512,512]{0,1:T(8,128)(2,1)} %get-tuple-element.88), channel_id=1, source_target_pairs={{0,8},{4,12},{8,16},{12,20},{16,24},{20,28},{1,9},{5,13},{9,17},{1... | collective-permute-start | bytes 1572872 | tf_op jit(solution)/shard_map/ppermute | solution.py:39
  222.2 41.8 %all-to-all-start.1 = ((f32[8,2,160]{2,1,0:T(2,128)}), f32[8,2,160]{2,1,0:T(2,128)S(1)}, u32[]{:S(2)}, u32[]{:S(2)}) async-start(f32[8,2,160]{2,1,0:T(2,128)} %maximum_bitcast_fusion.6), calls=%async_computation.1 | async-start | bytes 32768 | tf_op jit(solution)/shard_map/all_to_all | solution.py:43
  241.7 12.2 copy-start.6
  264.1 6.2 copy-start.8
  264.1 52.6 %all-to-all-start.5 = ((bf16[8,256,512]{2,1,0:T(8,128)(2,1)}), bf16[8,256,512]{2,1,0:T(8,128)(2,1)}, u32[]{:S(2)}, u32[]{:S(2)}) async-start(bf16[8,256,512]{2,1,0:T(8,128)(2,1)} %param.22), calls=%async_computation.5 | async-start | bytes 4194304 | tf_op jit(solution)/shard_map/all_to_all | solution.py:43
  283.9 37.1 %copy-start.23 = (bf16[2048,16]{0,1:T(8,128)(2,1)S(1)}, bf16[2048,16]{0,1:T(8,128)(2,1)}, u32[]{:S(2)}) copy-start(bf16[2048,16]{0,1:T(8,128)(2,1)} %param.20) | copy-start | bytes 196612
  316.7 34.9 %all-to-all-start.4 = ((bf16[8,160,512]{2,1,0:T(8,128)(2,1)}), bf16[8,160,512]{2,1,0:T(8,128)(2,1)S(1)}, u32[]{:S(2)}, u32[]{:S(2)}) async-start(bf16[8,160,512]{2,1,0:T(8,128)(2,1)} %bitcast.332), calls=%async_computation.4 | async-start | bytes 2621440 | tf_op jit(solution)/shard_map/all_to_all | solution.py:43
  320.3 88.6 %reduce-scatter.8.cloned.1.call-start = ((), (), s32[]{:S(2)}) async-start(), calls=%async_computation.28 | async-start | bytes 6553600 | tf_op jit(solution)/shard_map/reduce_scatter | solution.py:51
  351.7 6.7 copy-start.12
  408.9 37.0 %all-to-all-start.6 = ((bf16[8,160,512]{2,1,0:T(8,128)(2,1)}), bf16[8,160,512]{2,1,0:T(8,128)(2,1)}, u32[]{:S(2)}, u32[]{:S(2)}) async-start(bf16[8,160,512]{2,1,0:T(8,128)(2,1)} %bitcast.333), calls=%async_computation.7 | async-start | bytes 2621440 | tf_op jit(solution)/shard_map/all_to_all | solution.py:43
  414.5 122.9 %all-gather.11.cloned.1.call-start = ((), (), s32[]{:S(2)}) async-start(), calls=%async_computation.29 | async-start | bytes 6553600 | tf_op jit(solution)/shard_map/all_gather | solution.py:47
  491.7 80.6 %all-gather.13.cloned.1.call-start = ((), (), s32[]{:S(2)}) async-start(), calls=%async_computation.31 | async-start | bytes 6553600 | tf_op jit(solution)/shard_map/all_gather | solution.py:47
  491.8 36.9 %copy-start.10 = (bf16[512,512]{1,0:T(8,128)(2,1)}, bf16[512,512]{1,0:T(8,128)(2,1)S(1)}, u32[]{:S(2)}) copy-start(bf16[512,512]{1,0:T(8,128)(2,1)S(1)} %constant_dynamic-slice_fusion) | copy-start | bytes 1572868
  491.8 45.6 %copy-start.33 = (pred[8]{0:T(512)(128)(4,1)S(1)}, pred[8]{0:T(512)(128)(4,1)}, u32[]{:S(2)}) copy-start(pred[8]{0:T(512)(128)(4,1)} %iota_compare_fusion.24) | copy-start | bytes 28
  528.7 139.1 %reduce-scatter.12.cloned.1.call-start = ((), (), s32[]{:S(2)}) async-start(), calls=%async_computation.32 | async-start | bytes 6553600 | tf_op jit(solution)/shard_map/reduce_scatter | solution.py:51
  537.4 5.6 copy-start.5
  537.4 18.0 %slice-start = ((s8[5767168]{0:T(1024)(128)(4,1)}), s8[4194304]{0:T(1024)(128)(4,1)S(1)}, s32[]{:S(2)}) async-start(s8[5767168]{0:T(1024)(128)(4,1)} %bitcast.377), calls=%async_computation.39 | async-start | bytes 8388608
  542.9 12.5 slice-start.1
  616.2 57.2 %copy-start.11 = (bf16[512,512]{1,0:T(8,128)(2,1)S(1)}, bf16[512,512]{1,0:T(8,128)(2,1)}, u32[]{:S(2)}) copy-start(bf16[512,512]{1,0:T(8,128)(2,1)} %copy-done.10) | copy-start | bytes 1572868
  667.8 9.0 copy-start.27
  667.8 37.1 %all-to-all-start.10 = ((bf16[8,160,512]{2,1,0:T(8,128)(2,1)}), bf16[8,160,512]{2,1,0:T(8,128)(2,1)}, u32[]{:S(2)}, u32[]{:S(2)}) async-start(bf16[8,160,512]{2,1,0:T(8,128)(2,1)} %bitcast.331), calls=%async_computation.13 | async-start | bytes 2621440 | tf_op jit(solution)/shard_map/all_to_all | solution.py:43
  673.4 116.8 %all-gather.15.cloned.1.call-start = ((), (), s32[]{:S(2)}) async-start(), calls=%async_computation.33 | async-start | bytes 6553600 | tf_op jit(solution)/shard_map/all_gather | solution.py:47
  673.7 40.4 %copy-start.9 = (bf16[512,512]{0,1:T(8,128)(2,1)}, bf16[512,512]{0,1:T(8,128)(2,1)S(1)}, u32[]{:S(2)}) copy-start(bf16[512,512]{0,1:T(8,128)(2,1)S(1)} %copy.255) | copy-start | bytes 1572868
  708.1 43.5 %copy-start.7 = (f32[512,512]{0,1:T(8,128)}, f32[512,512]{0,1:T(8,128)S(1)}, u32[]{:S(2)}) copy-start(f32[512,512]{0,1:T(8,128)S(1)} %get-tuple-element.102) | copy-start | bytes 3145732
  797.7 37.3 %all-to-all-start.13 = ((bf16[8,160,512]{2,1,0:T(8,128)(2,1)}), bf16[8,160,512]{2,1,0:T(8,128)(2,1)S(1)}, u32[]{:S(2)}, u32[]{:S(2)}) async-start(bf16[8,160,512]{2,1,0:T(8,128)(2,1)} %bitcast.335), calls=%async_computation.16 | async-start | bytes 2621440 | tf_op jit(solution)/shard_map/all_to_all | solution.py:43
  803.2 230.2 %reduce-scatter.14.cloned.1.call-start = ((), (), s32[]{:S(2)}) async-start(), calls=%async_computation.34 | async-start | bytes 6553600 | tf_op jit(solution)/shard_map/reduce_scatter | solution.py:51
  855.5 21.9 %copy-start.20 = (bf16[512,4,128]{2,0,1:T(8,128)(2,1)S(1)}, bf16[512,4,128]{2,0,1:T(8,128)(2,1)}, u32[]{:S(2)}) copy-start(bf16[512,4,128]{2,0,1:T(8,128)(2,1)} %copy.192) | copy-start | bytes 1572868
  855.5 21.9 %copy-start.21 = (bf16[512,4,128]{2,0,1:T(8,128)(2,1)S(1)}, bf16[512,4,128]{2,0,1:T(8,128)(2,1)}, u32[]{:S(2)}) copy-start(bf16[512,4,128]{2,0,1:T(8,128)(2,1)} %copy.191) | copy-start | bytes 1572868
  855.6 21.9 %copy-start.22 = (bf16[512,4,128]{2,0,1:T(8,128)(2,1)S(1)}, bf16[512,4,128]{2,0,1:T(8,128)(2,1)}, u32[]{:S(2)}) copy-start(bf16[512,4,128]{2,0,1:T(8,128)(2,1)} %copy.190) | copy-start | bytes 1572868
  925.9 114.5 %reduce-scatter.10.cloned.1.call-start = ((), (), s32[]{:S(2)}) async-start(), calls=%async_computation.30 | async-start | bytes 6553600 | tf_op jit(solution)/shard_map/reduce_scatter | solution.py:51
  939.1 144.5 %reduce-scatter.16.cloned.1.call-start = ((), (), s32[]{:S(2)}) async-start(), calls=%async_computation.35 | async-start | bytes 2621440 | tf_op jit(solution)/shard_map/reduce_scatter | solution.py:51
  957.0 26.7 %collective-permute-start.7 = (bf16[512,512]{1,0:T(8,128)(2,1)}, bf16[512,512]{1,0:T(8,128)(2,1)}, u32[]{:S(2)}, u32[]{:S(2)}) collective-permute-start(bf16[512,512]{1,0:T(8,128)(2,1)} %copy.217), channel_id=1, source_target_pairs={{8,0},{12,4},{16,8},{20,12},{24,16},{28,20},{9,1},{13,5},{17,9},{2... | collective-permute-start | bytes 1572872 | tf_op jit(solution)/shard_map/ppermute | solution.py:39
  959.3 24.4 %collective-permute-start.6 = (bf16[512,512]{1,0:T(8,128)(2,1)}, bf16[512,512]{1,0:T(8,128)(2,1)}, u32[]{:S(2)}, u32[]{:S(2)}) collective-permute-start(bf16[512,512]{1,0:T(8,128)(2,1)} %copy.215), channel_id=1, source_target_pairs={{4,0},{8,4},{12,8},{16,12},{20,16},{24,20},{28,24},{5,1},{9,5},{13... | collective-permute-start | bytes 1572872 | tf_op jit(solution)/shard_map/ppermute | solution.py:39
  974.4 22.2 %collective-permute-start.5 = (bf16[512,512]{1,0:T(8,128)(2,1)}, bf16[512,512]{1,0:T(8,128)(2,1)}, u32[]{:S(2)}, u32[]{:S(2)}) collective-permute-start(bf16[512,512]{1,0:T(8,128)(2,1)} %copy.212), channel_id=1, source_target_pairs={{8,0},{12,4},{16,8},{20,12},{24,16},{28,20},{9,1},{13,5},{17,9},{2... | collective-permute-start | bytes 1572872 | tf_op jit(solution)/shard_map/ppermute | solution.py:39
  976.7 19.9 %collective-permute-start.4 = (bf16[512,512]{1,0:T(8,128)(2,1)}, bf16[512,512]{1,0:T(8,128)(2,1)}, u32[]{:S(2)}, u32[]{:S(2)}) collective-permute-start(bf16[512,512]{1,0:T(8,128)(2,1)} %copy.210), channel_id=1, source_target_pairs={{4,0},{8,4},{12,8},{16,12},{20,16},{24,20},{28,24},{5,1},{9,5},{13... | collective-permute-start | bytes 1572872 | tf_op jit(solution)/shard_map/ppermute | solution.py:39
  983.7 15.1 %copy-start.34 = (bf16[2,2048,512]{1,2,0:T(8,128)(2,1)S(1)}, bf16[2,2048,512]{1,2,0:T(8,128)(2,1)}, u32[]{:S(2)}) copy-start(bf16[2,2048,512]{1,2,0:T(8,128)(2,1)} %all-gather.9.cloned.1.call-done) | copy-start | bytes 12582916
  985.6 12.4 copy-start.17
  1002.6 251.5 %reduce-scatter.20.cloned.1.call-start = ((), (), s32[]{:S(2)}) async-start(), calls=%async_computation.38 | async-start | bytes 4718592 | tf_op jit(solution)/shard_map/reduce_scatter | solution.py:321
  1008.2 29.5 %copy-start.32 = (bf16[2048]{0:T(1024)(128)(2,1)S(1)}, bf16[2048]{0:T(1024)(128)(2,1)}, u32[]{:S(2)}) copy-start(bf16[2048]{0:T(1024)(128)(2,1)} %param.18) | copy-start | bytes 12292
  1008.2 30.2 %copy-start.25 = (s32[512,2]{0,1:T(2,128)S(1)}, s32[512,2]{0,1:T(2,128)}, u32[]{:S(2)}) copy-start(s32[512,2]{0,1:T(2,128)} %param.16) | copy-start | bytes 12292
  1033.5 34.1 %all-to-all-start.15 = ((bf16[8,160,512]{2,1,0:T(8,128)(2,1)}), bf16[8,160,512]{2,1,0:T(8,128)(2,1)}, u32[]{:S(2)}, u32[]{:S(2)}) async-start(bf16[8,160,512]{2,1,0:T(8,128)(2,1)} %bitcast.330), calls=%async_computation.19 | async-start | bytes 2621440 | tf_op jit(solution)/shard_map/all_to_all | solution.py:43
  1067.6 61.5 %all-to-all-start.8 = ((bf16[8,160,512]{2,1,0:T(8,128)(2,1)}), bf16[8,160,512]{2,1,0:T(8,128)(2,1)}, u32[]{:S(2)}, u32[]{:S(2)}) async-start(bf16[8,160,512]{2,1,0:T(8,128)(2,1)} %bitcast.329), calls=%async_computation.10 | async-start | bytes 2621440 | tf_op jit(solution)/shard_map/all_to_all | solution.py:43
  1087.4 46.3 %copy-start.29 = (f32[512]{0:T(512)S(1)}, f32[512]{0:T(512)}, u32[]{:S(2)}) copy-start(f32[512]{0:T(512)} %copy-done.28) | copy-start | bytes 6148
  1129.1 52.7 %all-to-all-start.18 = ((bf16[8,256,512]{2,1,0:T(8,128)(2,1)}), bf16[8,256,512]{2,1,0:T(8,128)(2,1)S(1)}, u32[]{:S(2)}, u32[]{:S(2)}) async-start(bf16[8,256,512]{2,1,0:T(8,128)(2,1)} %bitcast.318), calls=%async_computation.24 | async-start | bytes 4194304 | tf_op jit(solution)/shard_map/all_to_all | solution.py:43
  1133.6 162.8 %reduce-scatter.18.cloned.1.call-start = ((), (), s32[]{:S(2)}) async-start(), calls=%async_computation.37 | async-start | bytes 221184 | tf_op jit(solution)/shard_map/reduce_scatter | solution.py:326
  1142.7 188.8 %all-gather.17.cloned.1.call-start = ((), (), s32[]{:S(2)}) async-start(), calls=%async_computation.36 | async-start | bytes 5242880 | tf_op jit(solution)/shard_map/all_gather | solution.py:47
  1153.1 14.1 %copy-start.14 = (bf16[8,160,512]{2,1,0:T(8,128)(2,1)S(1)}, bf16[8,160,512]{2,1,0:T(8,128)(2,1)}, u32[]{:S(2)}) copy-start(bf16[8,160,512]{2,1,0:T(8,128)(2,1)} %copy-done.13) | copy-start | bytes 3932164
  1181.8 68.1 %all-to-all-start.17 = ((bf16[8,256,512]{2,1,0:T(8,128)(2,1)}), bf16[8,256,512]{2,1,0:T(8,128)(2,1)}, u32[]{:S(2)}, u32[]{:S(2)}) async-start(bf16[8,256,512]{2,1,0:T(8,128)(2,1)} %bitcast.319), calls=%async_computation.23 | async-start | bytes 4194304 | tf_op jit(solution)/shard_map/all_to_all | solution.py:43
  1186.4 13.7 %copy-start.35 = (bf16[1280,1408]{1,0:T(8,128)(2,1)S(1)}, bf16[1280,1408]{1,0:T(8,128)(2,1)}, u32[]{:S(2)}) copy-start(bf16[1280,1408]{1,0:T(8,128)(2,1)} %get-tuple-element.81) | copy-start | bytes 10813444
  1200.1 13.1 copy-start.16
  1297.7 39.1 %copy-start.1 = (bf16[512,2048]{1,0:T(8,128)(2,1)S(1)}, bf16[512,2048]{1,0:T(8,128)(2,1)}, u32[]{:S(2)}) copy-start(bf16[512,2048]{1,0:T(8,128)(2,1)} %param.27) | copy-start | bytes 6291460
  (7 other events, 17.6 us)
Sparse Core Ops, SparseCore 0:
  58.1 39.4 all-gather.6
  100.2 94.9 all-gather.8
  358.5 50.3 reduce-scatter.7
  491.8 38.4 all-gather.10
  531.8 40.4 all-gather.12
  616.4 51.3 reduce-scatter.11
  751.7 38.4 all-gather.14
  926.0 49.5 reduce-scatter.13
  978.9 51.6 reduce-scatter.9
  1033.5 31.4 reduce-scatter.15
  1069.6 151.5 reduce-scatter.19
  1224.4 71.9 reduce-scatter.17
  1298.0 33.5 all-gather.16

commit v2 on v1

v2 whole, which is shorter than its diff:
```python
import functools
import math

import jax
import jax.numpy as jnp
from jax import lax
from jax.experimental import pallas as pl
from jax.experimental.pallas import tpu as pltpu
from jax.sharding import PartitionSpec as P

D = 2048
HD = 128
EXPERTS = 8
TOPK = 2
WINDOW = 1024
CAP = 160
SLOTS = EXPERTS * CAP

eps = 1e-06
masked_value = -1e30
SCALE = HD ** (-0.5)
LOG2E = math.log2(math.e)
Q_ROWS = 256
NOTES = 16
WINDOW_ORDER = (1, 0, 2)
F32 = jnp.float32
BF16 = jnp.bfloat16
MESH = pl.DeviceIdType.MESH
VMEM = pl.BlockSpec(memory_space=pltpu.VMEM)
ANY = pl.BlockSpec(memory_space=pl.ANY)


def remote(src, dst, send, recv, **device):
    return pltpu.make_async_remote_copy(
        src_ref=src, dst_ref=dst, send_sem=send, recv_sem=recv, device_id=device, device_id_type=MESH)


def meet(experts, bits):
    e, t = lax.axis_index("expert"), lax.axis_index("tensor")
    barrier = pltpu.get_barrier_semaphore()

    @pl.loop(1, experts)
    def _(s):
        pl.semaphore_signal(barrier, inc=1, device_id={"expert": e ^ s}, device_id_type=MESH)

    for b in range(bits):
        pl.semaphore_signal(barrier, inc=1, device_id={"tensor": t ^ (1 << b)}, device_id_type=MESH)
    pl.semaphore_wait(barrier, experts - 1 + bits)


def partners(e, experts, near):
    if near:
        return lambda s: e ^ s
    return lambda s: e ^ ((experts - s) & (experts - 1))


def low_bit(d):
    return (d & -d).bit_length() - 1


def gather_kernel(experts, bits, near, multiply, scale, *refs):
    refs = list(refs)
    x = refs.pop(0)
    w = refs.pop(0) if multiply else None
    gate = refs.pop(0) if scale else None
    rows = refs.pop(0)
    back = refs.pop(0) if multiply else None
    product = refs.pop(0) if scale else None
    y = refs.pop(0) if multiply else None
    z_send, z_recv, t_send, t_recv = refs[:4]
    refs = refs[4:]
    if multiply:
        y_send, y_recv = refs[:2]
    e, t = lax.axis_index("expert"), lax.axis_index("tensor")
    partner = partners(e, experts, near)
    width = x.shape[2]
    tensor = 1 << bits

    def cols(d):
        return pl.ds(pl.multiple_of((t ^ d) * width, 128), width)

    def arrive(j):
        return remote(x.at[j], rows.at[e, :, cols(0)], z_send.at[j], z_recv.at[e], expert=j)

    def arrived(j):
        return remote(x.at[j], rows.at[j, :, cols(0)], z_send.at[j], z_recv.at[j], expert=j)

    def pass_on(j, d, b):
        place = rows.at[j, :, cols(d)]
        far = d | (1 << b)
        return remote(place, place, t_send.at[j, far], t_recv.at[j, far], tensor=t ^ (1 << b))

    def passed(j, d):
        place = rows.at[j, :, cols(d)]
        return remote(place, place, t_send.at[j, d], t_recv.at[j, d], tensor=t ^ (1 << low_bit(d)))

    def hand_back(j):
        return remote(y.at[j], back.at[e], y_send.at[j], y_recv.at[e], expert=j)

    def handed(j):
        return remote(y.at[j], back.at[j], y_send.at[j], y_recv.at[j], expert=j)

    meet(experts, bits)

    @pl.loop(1, experts)
    def _(s):
        arrive(partner(s)).start()

    rows[e, :, cols(0)] = x[e]

    @pl.loop(0, experts + bits)
    def _(i):
        @pl.when(i < experts)
        def _():
            j = partner(i)

            @pl.when(i > 0)
            def _():
                arrived(j).wait_recv()

            for b in reversed(range(bits)):
                pass_on(j, 0, b).start()

        for k in range(1, bits + 1):
            @pl.when((i >= k) & (i < experts + k))
            def _():
                m = i - k
                j = partner(m)
                bit = bits - k
                for d in range(1, tensor):
                    if low_bit(d) == bit:
                        passed(j, d).wait_recv()
                        for b in reversed(range(bit)):
                            pass_on(j, d, b).start()
                if k == bits and multiply:
                    out = jnp.dot(rows[j], w[...], preferred_element_type=F32)
                    if scale:
                        product[j] = out.astype(BF16)
                        out = out * gate[j]
                    y[j] = out.astype(BF16)

                    @pl.when(m == 0)
                    def _():
                        back[e] = y[e]

                    @pl.when(m > 0)
                    def _():
                        hand_back(j).start()

    @pl.loop(1, experts)
    def _(s):
        j = partner(s)
        arrived(j).wait_send()
        if multiply:
            handed(j).wait_recv()
            handed(j).wait_send()

    @pl.loop(0, experts)
    def _(j):
        for d in range(1, tensor):
            passed(j, d).wait_send()


def gather_rows(x, w=None, gate=None, near=True, collective_id=0):
    experts, tensor = lax.axis_size("expert"), lax.axis_size("tensor")
    bits = tensor.bit_length() - 1
    cap, width = x.shape[1], x.shape[2]
    multiply = w is not None
    f = w.shape[-1] if multiply else 0
    ins, specs = [x], [VMEM]
    outs = [jax.ShapeDtypeStruct((experts, cap, width * tensor), BF16)]
    scratch = []
    if multiply:
        ins.append(w)
        specs.append(VMEM)
        outs.append(jax.ShapeDtypeStruct((experts, cap, f), BF16))
    if gate is not None:
        ins.append(gate)
        specs.append(VMEM)
        outs.append(jax.ShapeDtypeStruct((experts, cap, f), BF16))
    if multiply:
        scratch.append(pltpu.VMEM((experts, cap, f), BF16))
    scratch += [pltpu.SemaphoreType.DMA((experts,))] * 2 + [pltpu.SemaphoreType.DMA((experts, tensor))] * 2
    if multiply:
        scratch += [pltpu.SemaphoreType.DMA((experts,))] * 2
    return pl.pallas_call(
        functools.partial(gather_kernel, experts, bits, near, multiply, gate is not None),
        out_shape=outs,
        in_specs=specs,
        out_specs=[VMEM] * len(outs),
        scratch_shapes=scratch,
        compiler_params=pltpu.CompilerParams(
            collective_id=collective_id, has_side_effects=True, vmem_limit_bytes=48 * 2**20),
    )(*ins)


def front_kernel(experts, bits, *refs):
    (tokens, gain, slots, w_in, kv_in, rows, back, w, window, kv, keys, values, x, y,
     z_send, z_recv, t_send, t_recv, y_send, y_recv, w_send, w_recv, k_send, k_recv, n_send, n_recv, own_sem) = refs
    e, t = lax.axis_index("expert"), lax.axis_index("tensor")
    partner = partners(e, experts, True)
    width = x.shape[1]
    cap = rows.shape[1]
    here = tokens.shape[0]
    tensor = 1 << bits
    expert_bits = experts.bit_length() - 1
    pieces = experts * cap // x.shape[0]

    def x_part(j):
        return pl.ds(pl.multiple_of((j // pieces) * cap, cap), cap)

    def cols(d):
        return pl.ds(pl.multiple_of((t ^ d) * width, 128), width)

    def part(j):
        return pl.ds(j * (w.shape[0] // experts), w.shape[0] // experts)

    def block(q, d):
        if isinstance(q, int):
            return window.at[q - experts, :, cols(d)]
        return rows.at[q, :, cols(d)]

    def pass_on(q, d, b):
        far = d | (1 << b)
        return remote(block(q, d), block(q, d), t_send.at[q, far], t_recv.at[q, far], tensor=t ^ (1 << b))

    def passed(q, d):
        return remote(block(q, d), block(q, d), t_send.at[q, d], t_recv.at[q, d], tensor=t ^ (1 << low_bit(d)))

    def stage(q, k):
        bit = bits - k
        for d in range(1, tensor):
            if low_bit(d) == bit:
                passed(q, d).wait_recv()
                for b in reversed(range(bit)):
                    pass_on(q, d, b).start()

    def arrived(j):
        return remote(x.at[x_part(j)], rows.at[j, :, cols(0)], z_send.at[j], z_recv.at[j], expert=j)

    def handed(j):
        return remote(y.at[j], back.at[j], y_send.at[j], y_recv.at[j], expert=j)

    def chunk(d):
        return kv.at[:, part(e ^ d), :]

    def pass_chunk(d, b):
        far = d | (1 << b)
        return remote(chunk(d), chunk(d), k_send.at[far], k_recv.at[far], expert=e ^ (1 << b))

    def passed_chunk(d):
        return remote(chunk(d), chunk(d), k_send.at[d], k_recv.at[d], expert=e ^ (1 << low_bit(d)))

    def chunks(bit):
        for d in range(1, experts):
            if low_bit(d) == bit:
                passed_chunk(d).wait_recv()
                for b in reversed(range(bit)):
                    pass_chunk(d, b).start()

    def two_on(way):
        return remote(window.at[2, :, cols(0)], window.at[0, :, cols(0)], n_send.at[0], n_recv.at[0],
                      expert=lax.rem(e + experts + 2 * way, experts))

    def across():
        return remote(window.at[2 - 2 * (e & 1), :, cols(0)], window.at[1, :, cols(0)], n_send.at[1], n_recv.at[1],
                      expert=e ^ 1)

    own_kv = pltpu.make_async_copy(kv_in, chunk(0), own_sem.at[0])
    own_w = pltpu.make_async_copy(w_in.at[e], w.at[part(e)], own_sem.at[1])
    own_kv.start()
    own_w.start()
    meet(experts, bits)
    for b in reversed(range(expert_bits)):
        remote(kv_in, chunk(0), k_send.at[1 << b], k_recv.at[1 << b], expert=e ^ (1 << b)).start()

    state = tokens[...].astype(F32)
    rate = lax.rsqrt(jnp.mean(state * state, axis=1, keepdims=True) + eps)
    window[2] = (state * rate * gain[...]).astype(BF16)
    two_on(1).start()
    place = lax.broadcasted_iota(jnp.int32, (x.shape[0], here), 0)
    chosen = (place == slots[:, pl.ds(0, here)]) | (place == slots[:, pl.ds(here, here)])
    x[...] = jnp.dot(chosen.astype(F32).astype(BF16), window[2, :, cols(0)], preferred_element_type=F32).astype(BF16)

    @pl.loop(1, experts)
    def _(s):
        j = partner(s)
        remote(x.at[x_part(j)], rows.at[e, :, cols(0)], z_send.at[j], z_recv.at[e], expert=j).start()

    @pl.loop(1, experts)
    def _(s):
        j = partner(s)
        remote(w_in.at[j], w.at[part(e)], w_send.at[j], w_recv.at[e], expert=j).start()

    rows[e, :, cols(0)] = x[x_part(e), :]
    chunks(expert_bits - 1)

    @pl.loop(0, experts + bits)
    def _(i):
        @pl.when(i < experts)
        def _():
            j = partner(i)

            @pl.when(i > 0)
            def _():
                arrived(j).wait_recv()

            for b in reversed(range(bits)):
                pass_on(j, 0, b).start()

        for k in range(1, bits + 1):
            @pl.when((i >= k) & (i < experts + k))
            def _():
                stage(partner(i - k), k)

        @pl.when(i == experts // 2)
        def _():
            two_on(-1).wait_recv()
            across().start()
            for b in reversed(range(bits)):
                pass_on(experts, 0, b).start()

    for bit in reversed(range(1, expert_bits - 1)):
        chunks(bit)
    across().wait_recv()
    for b in reversed(range(bits)):
        pass_on(experts + 1, 0, b).start()
    own_w.wait()

    @pl.loop(1, experts)
    def _(s):
        q = partner(s)
        remote(w_in.at[q], w.at[part(q)], w_send.at[q], w_recv.at[q], expert=q).wait_recv()

    @pl.loop(0, experts)
    def _(i):
        j = partner(lax.rem(i + 1, experts))
        y[j] = jnp.dot(rows[j], w[...], preferred_element_type=F32).astype(BF16)

        @pl.when(i < experts - 1)
        def _():
            remote(y.at[j], back.at[e], y_send.at[j], y_recv.at[e], expert=j).start()

    back[e] = y[e]
    for k in range(1, bits + 1):
        for q in range(2):
            stage(experts + q, k)
    chunks(0)
    own_kv.wait()
    for q in range(3):
        for c, out in enumerate((keys, values)):
            out[pl.ds(q * here, here), :] = jnp.dot(window[q], kv[c], preferred_element_type=F32).astype(BF16)

    @pl.loop(1, experts)
    def _(s):
        j = partner(s)
        arrived(j).wait_send()
        handed(j).wait_recv()
        handed(j).wait_send()
        remote(w_in.at[j], w.at[part(j)], w_send.at[j], w_recv.at[j], expert=j).wait_send()

    for d in range(1, experts):
        passed_chunk(d).wait_send()
    two_on(1).wait_send()
    across().wait_send()
    for q in range(2):
        for d in range(1, tensor):
            passed(experts + q, d).wait_send()

    @pl.loop(0, experts)
    def _(j):
        for d in range(1, tensor):
            passed(j, d).wait_send()


def front(tokens, gain, slots, w, kv, collective_id):
    experts, tensor = lax.axis_size("expert"), lax.axis_size("tensor")
    bits = tensor.bit_length() - 1
    here = tokens.shape[0]
    f, f_kv = w.shape[2], kv.shape[2]
    dma = pltpu.SemaphoreType.DMA
    return pl.pallas_call(
        functools.partial(front_kernel, experts, bits),
        out_shape=[
            jax.ShapeDtypeStruct((experts, CAP, D), BF16),
            jax.ShapeDtypeStruct((experts, CAP, f), BF16),
            jax.ShapeDtypeStruct((D, f), BF16),
            jax.ShapeDtypeStruct((3, here, D), BF16),
            jax.ShapeDtypeStruct((2, D, f_kv), BF16),
            jax.ShapeDtypeStruct((3 * here, f_kv), BF16),
            jax.ShapeDtypeStruct((3 * here, f_kv), BF16),
        ],
        in_specs=[VMEM, VMEM, VMEM, ANY, ANY],
        out_specs=[VMEM] * 7,
        scratch_shapes=[pltpu.VMEM((SLOTS, D // tensor), BF16), pltpu.VMEM((experts, CAP, f), BF16)]
        + [dma((experts,))] * 2 + [dma((experts + 2, tensor))] * 2 + [dma((experts,))] * 6
        + [dma((2,))] * 3,
        compiler_params=pltpu.CompilerParams(
            collective_id=collective_id, has_side_effects=True, vmem_limit_bytes=56 * 2**20),
    )(tokens, gain, slots, w, kv)


def scatter_kernel(experts, bits, depth, near, multiply, terms, scale, noted, *refs):
    refs = list(refs)
    h_in = refs.pop(0) if multiply else None
    w = refs.pop(0) if multiply else None
    factors = [(refs.pop(0), refs.pop(0)) for _ in range(terms)]
    gate = refs.pop(0) if scale else None
    notes = refs.pop(0) if noted else None
    if depth:
        key_grad, value_grad, kv = refs[:3]
        refs = refs[3:]
    back = refs.pop(0)
    h = refs.pop(0) if multiply else None
    if multiply:
        factors = [(h, w)]
    owed = refs.pop(0) if depth else None
    keep, sent, got, y, t_send, t_recv, y_send, y_recv = refs[:8]
    refs = refs[8:]
    if multiply:
        h_send, h_recv = refs[:2]
        refs = refs[2:]
    if depth:
        n_keep, n_sent, n_got, n_y, n_in, n_send, n_recv, o_send, o_recv = refs
    e, t = lax.axis_index("expert"), lax.axis_index("tensor")
    partner = partners(e, experts, near)
    tensor = 1 << bits
    cap, width = factors[0][0].shape[1], y.shape[2]
    body = pl.ds(0, cap)
    foot = pl.ds(cap, NOTES)

    def slice_at(d):
        return pl.ds(pl.multiple_of((t ^ d) * width, 128), width)

    def handed(j):
        return remote(y.at[j], back.at[j], y_send.at[j], y_recv.at[j], expert=j)

    def give(j, d):
        return remote(sent.at[j, d], got.at[j, d], t_send.at[j, d], t_recv.at[j, d], tensor=t ^ (1 << low_bit(d)))

    def owe(q, d):
        return remote(n_sent.at[q, d], n_got.at[q, d], n_send.at[q, d], n_recv.at[q, d], tensor=t ^ (1 << low_bit(d)))

    def across():
        return remote(n_y.at[1], n_in, o_send.at[1], o_recv.at[1], expert=e ^ 1)

    def two_back(way):
        return remote(n_y.at[0], owed.at[1], o_send.at[0], o_recv.at[0],
                      expert=lax.rem(e + experts - 2 * way, experts))

    def window_stage(k):
        for q in WINDOW_ORDER:
            for d in range(tensor - 1, -1, -1):
                if d % (1 << k) == 0:
                    came = d | (1 << (k - 1))
                    owe(q, came).wait_recv()
                    total = n_keep[q, d // 2] + n_got[q, came].astype(F32)
                    if k == bits:
                        if q == 1:
                            n_y[1] = total.astype(BF16)
                            across().start()
                        else:
                            n_keep[q, 0] = total
                    elif d & (1 << k):
                        n_sent[q, d] = total.astype(BF16)
                        owe(q, d).start()
                    else:
                        n_keep[q, d // 2] = total

    meet(experts, bits)
    if multiply:
        @pl.loop(1, experts)
        def _(s):
            j = partner(s)
            remote(h_in.at[j], h.at[e], h_send.at[j], h_recv.at[e], expert=j).start()

        h[e] = h_in[e]
    if depth:
        here = key_grad.shape[0] // 3
        for q in WINDOW_ORDER:
            place = pl.ds(q * here, here)
            for d in range(tensor - 1, -1, -1):
                part = lax.dot_general(
                    key_grad[place, :], kv[0, slice_at(d), :], (((1,), (1,)), ((), ())), preferred_element_type=F32)
                part += lax.dot_general(
                    value_grad[place, :], kv[1, slice_at(d), :], (((1,), (1,)), ((), ())), preferred_element_type=F32)
                if d & 1:
                    n_sent[q, d] = part.astype(BF16)
                    owe(q, d).start()
                else:
                    n_keep[q, d // 2] = part
        window_stage(1)

    @pl.loop(0, experts + bits)
    def _(i):
        @pl.when(i < experts)
        def _():
            j = partner(i)
            slot = lax.rem(i, bits + 1)
            if multiply:
                @pl.when(i > 0)
                def _():
                    remote(h_in.at[j], h.at[j], h_send.at[j], h_recv.at[j], expert=j).wait_recv()
            for d in range(tensor - 1, -1, -1):
                part = None
                for left, right in factors:
                    term = lax.dot_general(
                        left[j], right[slice_at(d), :], (((1,), (1,)), ((), ())), preferred_element_type=F32)
                    part = term if part is None else part + term
                if scale:
                    part = part * gate[j]
                if d & 1:
                    sent[j, d, body, :] = part.astype(BF16)
                    if noted:
                        sent[j, d, foot, :] = notes[j].astype(BF16)
                    give(j, d).start()
                else:
                    keep[slot, d // 2, body, :] = part
                    if noted:
                        keep[slot, d // 2, foot, :] = notes[j]

        for k in range(1, bits + 1):
            @pl.when((i >= k) & (i < experts + k))
            def _():
                m = i - k
                slot = lax.rem(m, bits + 1)
                j = partner(m)
                for d in range(tensor - 1, -1, -1):
                    if d % (1 << k) == 0:
                        came = d | (1 << (k - 1))
                        give(j, came).wait_recv()
                        total = keep[slot, d // 2] + got[j, came].astype(F32)
                        if k == bits:
                            y[j] = total.astype(BF16)
                        elif d & (1 << k):
                            sent[j, d] = total.astype(BF16)
                            give(j, d).start()
                        else:
                            keep[slot, d // 2] = total
                if k == bits:
                    @pl.when(m == 0)
                    def _():
                        back[e] = y[e]

                    @pl.when(m > 0)
                    def _():
                        remote(y.at[j], back.at[e], y_send.at[j], y_recv.at[e], expert=j).start()

        if depth:
            for k in range(2, bits + 1):
                @pl.when(i == 2 * (k - 1))
                def _():
                    window_stage(k)

            @pl.when(i == 2 * bits)
            def _():
                across().wait_recv()
                passing = (e & 1).astype(F32)
                came = n_in[...].astype(F32)
                n_y[0] = (n_keep[0, 0] + passing * came).astype(BF16)
                owed[0] = (n_keep[2, 0] + (1.0 - passing) * came).astype(BF16)
                two_back(1).start()

    @pl.loop(1, experts)
    def _(s):
        j = partner(s)
        if multiply:
            remote(h_in.at[j], h.at[j], h_send.at[j], h_recv.at[j], expert=j).wait_send()
        handed(j).wait_recv()
        handed(j).wait_send()

    @pl.loop(0, experts)
    def _(j):
        for d in range(1, tensor):
            give(j, d).wait_send()

    if depth:
        for q in range(3):
            for d in range(1, tensor):
                owe(q, d).wait_send()
        across().wait_send()
        two_back(-1).wait_recv()
        two_back(1).wait_send()


def scatter_rows(h=None, w=None, gate=None, notes=None, products=(), windows=None, near=True, collective_id=0):
    experts, tensor = lax.axis_size("expert"), lax.axis_size("tensor")
    bits = tensor.bit_length() - 1
    multiply = w is not None
    high = CAP + (NOTES if notes is not None else 0)
    width = D // tensor
    dma = pltpu.SemaphoreType.DMA
    ins = [a for a in (h, w) if a is not None] + [a for pair in products for a in pair]
    ins += [a for a in (gate, notes) if a is not None]
    outs = [jax.ShapeDtypeStruct((experts, high, width), BF16)]
    scratch = [
        pltpu.VMEM((bits + 1, tensor // 2, high, width), F32),
        pltpu.VMEM((experts, tensor, high, width), BF16),
        pltpu.VMEM((experts, tensor, high, width), BF16),
        pltpu.VMEM((experts, high, width), BF16),
    ]
    scratch += [dma((experts, tensor))] * 2 + [dma((experts,))] * 2
    if multiply:
        outs.append(jax.ShapeDtypeStruct(h.shape, BF16))
        scratch += [dma((experts,))] * 2
    if windows is not None:
        ins += windows
        here = windows[0].shape[0] // 3
        outs.append(jax.ShapeDtypeStruct((2, here, width), BF16))
        scratch += [
            pltpu.VMEM((3, tensor // 2, here, width), F32),
            pltpu.VMEM((3, tensor, here, width), BF16),
            pltpu.VMEM((3, tensor, here, width), BF16),
            pltpu.VMEM((2, here, width), BF16),
            pltpu.VMEM((here, width), BF16),
        ] + [dma((3, tensor))] * 2 + [dma((2,))] * 2
    return pl.pallas_call(
        functools.partial(
            scatter_kernel, experts, bits, windows is not None, near, multiply, len(products), gate is not None,
            notes is not None),
        out_shape=outs,
        in_specs=[VMEM] * len(ins),
        out_specs=[VMEM] * len(outs),
        scratch_shapes=scratch,
        compiler_params=pltpu.CompilerParams(
            collective_id=collective_id, has_side_effects=True, vmem_limit_bytes=60 * 2**20),
    )(*ins)


def dot(left, right, dims):
    return lax.dot_general(left, right, ((dims[0], dims[1]), ((), ())), preferred_element_type=F32)


def mm(left, right):
    return dot(left, right, ((1,), (0,)))


def mm_nt(left, right):
    return dot(left, right, ((1,), (1,)))


def mm_tn(left, right):
    return dot(left, right, ((0,), (0,)))


def swap(blocks):
    return lax.all_to_all(blocks, "expert", split_axis=0, concat_axis=0, tiled=True)


def columns_together(rows):
    return lax.all_gather(rows, "tensor", axis=1, tiled=True)


def columns_summed(rows):
    return lax.psum_scatter(rows, "tensor", scatter_dimension=1, tiled=True)


def slot_numbers(routes):
    flat = routes.T.reshape(-1)
    place = jnp.arange(flat.shape[0], dtype=jnp.int32)
    earlier = (flat[:, None] == flat[None, :]) & (place[None, :] < place[:, None])
    return flat * CAP + jnp.sum(earlier.astype(jnp.int32), axis=1)


def place_matrix(slots, stride=CAP):
    wide = slots + (slots // CAP) * (stride - CAP)
    return (jnp.arange(EXPERTS * stride, dtype=jnp.int32)[:, None] == wide[None, :]).astype(BF16)


def to_pieces(rows, pieces):
    if pieces == 1:
        return rows
    experts, r, c = rows.shape
    return rows.reshape(experts, r, pieces, c // pieces).transpose(0, 2, 1, 3).reshape(experts * pieces, r, -1)


def from_pieces(rows, pieces):
    if pieces == 1:
        return rows
    both, r, c = rows.shape
    return rows.reshape(both // pieces, pieces, r, c).transpose(0, 2, 1, 3).reshape(both // pieces, r, -1)


def for_pieces(rows, pieces):
    return jnp.repeat(rows, pieces, axis=0) if pieces > 1 else rows


def own_gate(logits, own, other):
    places = jnp.arange(EXPERTS, dtype=F32)[None, :]
    mine = jnp.sum(jnp.where(places == own, logits, 0.0), axis=1)
    rival = jnp.sum(jnp.where(places == other[:, None], logits, 0.0), axis=1)
    top = jnp.maximum(mine, rival)
    mine, rival = jnp.exp(mine - top), jnp.exp(rival - top)
    return (mine / (mine + rival))[:, None]


def pick_gates(logits, routes):
    one_hot = (routes[:, :, None] == jnp.arange(EXPERTS, dtype=jnp.int32)[None, None, :]).astype(F32)
    return jax.nn.softmax(jnp.sum(one_hot * logits[:, None, :], axis=2), axis=-1)


def gate_back(gating, pulled, routes):
    inner_sum = gating * (pulled - jnp.sum(gating * pulled, axis=1, keepdims=True))
    one_hot = (routes[:, :, None] == jnp.arange(EXPERTS, dtype=jnp.int32)[None, None, :]).astype(F32)
    return jnp.sum(one_hot * inner_sum[:, :, None], axis=1).astype(BF16)


def place_matrices(slots_ref, spread, gathered):
    count, choices = spread.shape
    spread[...] = (lax.broadcasted_iota(jnp.int32, (count, choices), 0) == slots_ref[...]).astype(F32).astype(BF16)
    gathered[...] = spread[...].T


def mask_bias(query_ids, key_ids, bias):
    blocks, span, _ = bias.shape

    for block in range(blocks):
        first = block * Q_ROWS
        query_place = lax.broadcasted_iota(jnp.int32, (span, Q_ROWS), 1) + WINDOW
        distance = query_place - lax.broadcasted_iota(jnp.int32, (span, Q_ROWS), 0)
        same = key_ids[pl.ds(first, span), :] == query_ids[:, pl.ds(first, Q_ROWS)]
        allowed = (distance >= 0) & (distance < WINDOW) & same
        part = jnp.where(allowed, 0.0, masked_value)
        for k in range(TOPK):
            bias[block, :, pl.ds(k * Q_ROWS, Q_ROWS)] = part


def of_block(choices, block):
    rows = choices.shape[0] // TOPK
    return jnp.concatenate([choices[pl.ds(k * rows + block * Q_ROWS, Q_ROWS), :] for k in range(TOPK)], axis=0)


def attend_kernel(slots_ref, back_ref, key_ref, value_ref, query_ids, key_ids, grouped_ref, query_ref, lse_ref,
                  spread, gathered, bias, heads):
    @pl.when(pl.program_id(0) == 0)
    def _():
        place_matrices(slots_ref, spread, gathered)
        mask_bias(query_ids, key_ids, bias)

    query_ref[...] = jnp.dot(gathered[...], back_ref[...], preferred_element_type=F32).astype(BF16)
    blocks, span, _ = bias.shape
    rows = query_ref.shape[0] // TOPK
    for block in range(blocks):
        queries = of_block(query_ref, block)
        keys = key_ref[pl.ds(block * Q_ROWS, span), :]
        values = value_ref[pl.ds(block * Q_ROWS, span), :]
        scores = lax.dot_general(keys, queries, (((1,), (1,)), ((), ())), preferred_element_type=F32)
        scores = scores * (SCALE * LOG2E) + bias[block]
        top = jnp.max(scores, axis=0, keepdims=True)
        probs = jnp.exp2(scores - top)
        total = jnp.sum(probs, axis=0, keepdims=True)
        out = lax.dot_general(values, probs.astype(BF16), (((0,), (0,)), ((), ())), preferred_element_type=F32)
        out = (out * (1.0 / total)).T.astype(BF16)
        for k in range(TOPK):
            heads[pl.ds(k * rows + block * Q_ROWS, Q_ROWS), :] = out[k * Q_ROWS : (k + 1) * Q_ROWS]
        lse_ref[0, :, pl.ds(block * TOPK * Q_ROWS, TOPK * Q_ROWS)] = top + jnp.log2(total)
    grouped_ref[...] = jnp.dot(spread[...], heads[...], preferred_element_type=F32).astype(BF16)


def attend(slots, back, keys, values, query_ids, key_ids):
    choices, (count, width), span = slots.shape[1], back.shape, keys.shape[0]
    blocks = choices // TOPK // Q_ROWS
    head = lambda rows: pl.BlockSpec((rows, HD), lambda h: (0, h))
    whole = lambda a: pl.BlockSpec(a.shape, lambda h: (0, 0))
    return pl.pallas_call(
        attend_kernel,
        grid=(width // HD,),
        out_shape=[
            jax.ShapeDtypeStruct((count, width), BF16),
            jax.ShapeDtypeStruct((choices, width), BF16),
            jax.ShapeDtypeStruct((width // HD, 1, choices), F32),
        ],
        in_specs=[whole(slots), head(count), head(span), head(span), whole(query_ids), whole(key_ids)],
        out_specs=[head(count), head(choices), pl.BlockSpec((1, 1, choices), lambda h: (h, 0, 0))],
        scratch_shapes=[
            pltpu.VMEM((count, choices), BF16),
            pltpu.VMEM((choices, count), BF16),
            pltpu.VMEM((blocks, WINDOW + Q_ROWS, TOPK * Q_ROWS), F32),
            pltpu.VMEM((choices, HD), BF16),
        ],
        compiler_params=pltpu.CompilerParams(vmem_limit_bytes=48 * 2**20),
        cost_estimate=pl.CostEstimate(flops=16 * 10**9, bytes_accessed=10**7, transcendentals=10**7),
    )(slots, back, keys, values, query_ids, key_ids)


def attend_back_kernel(slots_ref, back_ref, query_ref, key_ref, value_ref, lse_ref, query_ids, key_ids,
                       grouped_ref, key_grad_ref, value_grad_ref,
                       spread, gathered, bias, key_acc, value_acc, query_grad, head_grad):
    @pl.when(pl.program_id(0) == 0)
    def _():
        place_matrices(slots_ref, spread, gathered)
        mask_bias(query_ids, key_ids, bias)

    head_grad[...] = jnp.dot(gathered[...], back_ref[...], preferred_element_type=F32).astype(BF16)
    key_acc[...] = jnp.zeros_like(key_acc)
    value_acc[...] = jnp.zeros_like(value_acc)
    blocks, span, _ = bias.shape
    rows = query_ref.shape[0] // TOPK
    for block in range(blocks):
        queries = of_block(query_ref, block)
        grads = of_block(head_grad, block)
        place = pl.ds(block * Q_ROWS, span)
        keys, values = key_ref[place, :], value_ref[place, :]
        scores = lax.dot_general(keys, queries, (((1,), (1,)), ((), ())), preferred_element_type=F32)
        lse = lse_ref[0, :, pl.ds(block * TOPK * Q_ROWS, TOPK * Q_ROWS)]
        probs = jnp.exp2(scores * (SCALE * LOG2E) + bias[block] - lse)
        pulled = lax.dot_general(values, grads, (((1,), (1,)), ((), ())), preferred_element_type=F32)
        pulled = probs * pulled
        inner = jnp.sum(pulled, axis=0, keepdims=True)
        score_grad = (pulled - probs * inner).astype(BF16)
        value_acc[place, :] += jnp.dot(probs.astype(BF16), grads, preferred_element_type=F32)
        key_acc[place, :] += jnp.dot(score_grad, queries, preferred_element_type=F32)
        out = lax.dot_general(keys, score_grad, (((0,), (0,)), ((), ())), preferred_element_type=F32)
        out = (out * SCALE).T.astype(BF16)
        for k in range(TOPK):
            query_grad[pl.ds(k * rows + block * Q_ROWS, Q_ROWS), :] = out[k * Q_ROWS : (k + 1) * Q_ROWS]
    grouped_ref[...] = jnp.dot(spread[...], query_grad[...], preferred_element_type=F32).astype(BF16)
    key_grad_ref[...] = (key_acc[...] * SCALE).astype(BF16)
    value_grad_ref[...] = value_acc[...].astype(BF16)


def attend_back(slots, back, queries, keys, values, lse, query_ids, key_ids):
    choices, (count, width), span = slots.shape[1], back.shape, keys.shape[0]
    blocks = choices // TOPK // Q_ROWS
    head = lambda rows: pl.BlockSpec((rows, HD), lambda h: (0, h))
    whole = lambda a: pl.BlockSpec(a.shape, lambda h: (0, 0))
    return pl.pallas_call(
        attend_back_kernel,
        grid=(width // HD,),
        out_shape=[jax.ShapeDtypeStruct((count, width), BF16)] + [jax.ShapeDtypeStruct((span, width), BF16)] * 2,
        in_specs=[
            whole(slots), head(count), head(choices), head(span), head(span),
            pl.BlockSpec((1, 1, choices), lambda h: (h, 0, 0)), whole(query_ids), whole(key_ids),
        ],
        out_specs=[head(count), head(span), head(span)],
        scratch_shapes=[
            pltpu.VMEM((count, choices), BF16),
            pltpu.VMEM((choices, count), BF16),
            pltpu.VMEM((blocks, WINDOW + Q_ROWS, TOPK * Q_ROWS), F32),
            pltpu.VMEM((span, HD), F32),
            pltpu.VMEM((span, HD), F32),
            pltpu.VMEM((choices, HD), BF16),
            pltpu.VMEM((choices, HD), BF16),
        ],
        compiler_params=pltpu.CompilerParams(vmem_limit_bytes=56 * 2**20),
        cost_estimate=pl.CostEstimate(flops=30 * 10**9, bytes_accessed=10**7, transcendentals=10**7),
    )(slots, back, queries, keys, values, lse, query_ids, key_ids)


def per_device(
    tokens,
    segment_ids,
    attn_routes,
    ffn_routes,
    attn_gain,
    ffn_gain,
    routers,
    query_weight,
    output_weight,
    key_value_weight,
    gate_weight,
    up_weight,
    down_weight,
    cotangent,
):
    rows_here = tokens.shape[0]
    expert_count = lax.axis_size("expert")
    tensor_count = lax.axis_size("tensor")
    pieces = expert_count // EXPERTS
    column_count = D // tensor_count
    expert_index = lax.axis_index("expert")
    tensor_index = lax.axis_index("tensor")
    own = (expert_index // pieces).astype(F32)
    head_width = query_weight.shape[2]
    head_count = head_width // HD

    def cols(whole):
        return lax.dynamic_slice_in_dim(whole, tensor_index * column_count, column_count, whole.ndim - 1)

    def group_tokens(token_cols, places):
        return for_pieces(mm(places, token_cols).astype(BF16).reshape(EXPERTS, CAP, -1), pieces)

    def tokens_to_experts(token_cols, places):
        return columns_together(swap(group_tokens(token_cols, places)).reshape(-1, column_count))

    def group_choices(choice_rows, places):
        return to_pieces(mm(places, choice_rows).astype(BF16).reshape(EXPERTS, CAP, -1), pieces)

    def choices_of(back, places):
        return mm_tn(places, from_pieces(back, pieces).reshape(SLOTS, -1)).astype(BF16)

    def sums_from_experts(part_rows, places):
        back = swap(columns_summed(part_rows.astype(BF16)).reshape(expert_count, CAP, column_count))
        return sums_of(back, places)

    def sums_of(back, places):
        stride = back.shape[1]
        back = back.reshape(EXPERTS, pieces, stride, column_count)
        if pieces > 1:
            total = sum(mm_tn(places, back[:, p].reshape(EXPERTS * stride, -1)) for p in range(pieces))
        else:
            total = mm_tn(places, back.reshape(EXPERTS * stride, -1))
        return total

    def notes_of(*scalars):
        rows = jnp.stack([v.reshape(expert_count, CAP) for v in scalars], axis=1)
        return jnp.pad(rows, ((0, 0), (0, NOTES - len(scalars)), (0, column_count - CAP)))

    def read_notes(back, places, count):
        noted = back[:, CAP : CAP + count, :CAP].astype(F32)
        noted = noted.reshape(EXPERTS, pieces, count, CAP).sum(1).transpose(0, 2, 1).reshape(SLOTS, count)
        return mm_tn(places, noted.astype(BF16)).reshape(TOPK, rows_here, count)

    state_in = tokens.astype(F32)
    gain_one = attn_gain.astype(F32)
    gain_two = cols(ffn_gain.astype(F32))
    routers_one, routers_two = routers[:, :EXPERTS], routers[:, EXPERTS:]
    dy_cols = cols(cotangent)
    token_cols = cols(tokens).astype(F32)

    def by_token(choices):
        return choices[:, :rows_here] + choices[:, rows_here:]

    attn_slots, ffn_slots = slot_numbers(attn_routes), slot_numbers(ffn_routes)
    attn_places, ffn_places = place_matrix(attn_slots), place_matrix(ffn_slots)
    attn_tokens, ffn_tokens = by_token(attn_places), by_token(ffn_places)
    attn_noted = by_token(place_matrix(attn_slots, CAP + NOTES))
    ffn_noted = by_token(place_matrix(ffn_slots, CAP + NOTES))
    others = jnp.stack([
        mm(attn_places, attn_routes[:, ::-1].T.reshape(-1, 1).astype(BF16)),
        mm(ffn_places, ffn_routes[:, ::-1].T.reshape(-1, 1).astype(BF16)),
    ]).reshape(2, EXPERTS, CAP).transpose(1, 0, 2)


    rows_one, query_rows, query_map, window, pair_map, keys, values = front(
        tokens, gain_one[None], attn_slots[None], to_pieces(query_weight, pieces), key_value_weight, collective_id=0)
    output_weight, others, rows_one = lax.optimization_barrier((output_weight, others, rows_one))
    rows_one = rows_one.reshape(-1, D)
    output_map = swap(to_pieces(output_weight, pieces)).reshape(D, -1)
    others = swap(for_pieces(others, pieces)).transpose(1, 0, 2).reshape(2, -1)
    normed_one = window[2]
    window = window.reshape(-1, D)
    padded_segments = jnp.concatenate([jnp.full((WINDOW,), -1, jnp.int32), segment_ids])
    key_ids = lax.dynamic_slice_in_dim(padded_segments, expert_index * rows_here, WINDOW + rows_here)
    query_ids = key_ids[None, WINDOW:]
    key_ids = key_ids[:, None]
    heads, queries, log_total = attend(
        attn_slots[None], from_pieces(query_rows, pieces).reshape(SLOTS, -1), keys, values, query_ids, key_ids)
    attn_gate_rows = own_gate(mm(rows_one, routers_one), own, others[0])
    attn_gate_blocks = attn_gate_rows.reshape(expert_count, CAP, 1)
    attn_back, heads_rows = scatter_rows(
        to_pieces(heads.reshape(EXPERTS, CAP, -1), pieces), output_map, attn_gate_blocks, collective_id=1)
    heads_rows = heads_rows.reshape(expert_count * CAP, -1)
    dy_cols, attn_back = lax.optimization_barrier((dy_cols, attn_back))
    state = token_cols + sums_of(attn_back, attn_tokens)

    mean_two = lax.psum(jnp.sum(state * state, axis=1, keepdims=True), "tensor") / D
    rate_two = lax.rsqrt(mean_two + eps)
    normed_two = (state * rate_two * gain_two).astype(BF16)
    rows_dy = tokens_to_experts(dy_cols, ffn_tokens)
    (rows_two,) = gather_rows(group_tokens(normed_two, ffn_tokens), collective_id=2)
    rows_two = rows_two.reshape(-1, D)
    gate_map, up_map, down_map = gate_weight[0], up_weight[0], down_weight[0]
    ffn_gate_rows = own_gate(mm(rows_two, routers_two), own, others[1])
    hidden_grad = mm_nt(rows_dy, down_map)
    gate_pre = mm(rows_two, gate_map)
    up_pre = mm(rows_two, up_map)
    sigma = 1.0 / (1.0 + jnp.exp(-gate_pre))
    silu = gate_pre * sigma
    hidden = (silu * up_pre).astype(BF16)
    scaled_grad = hidden_grad * ffn_gate_rows
    gate_low = (scaled_grad * up_pre * (sigma * (1.0 + gate_pre * (1.0 - sigma)))).astype(BF16)
    up_low = (scaled_grad * silu).astype(BF16)
    ffn_notes = notes_of(
        jnp.sum(hidden.astype(F32) * hidden_grad, axis=1), ffn_gate_rows[:, 0] / (tensor_count * pieces))
    (rows_back,) = scatter_rows(
        products=[(gate_low.reshape(expert_count, CAP, -1), gate_map), (up_low.reshape(expert_count, CAP, -1), up_map)],
        notes=ffn_notes, near=False, collective_id=3)
    normed_two_grad = sums_of(rows_back, ffn_noted)
    noted = read_notes(rows_back, ffn_places, 2)
    ffn_pull, ffn_gates = noted[:, :, 0].T, noted[:, :, 1].T
    ffn_logit_grad = gate_back(ffn_gates, ffn_pull, ffn_routes)
    normed_two_grad = normed_two_grad + mm_nt(
        ffn_logit_grad, lax.dynamic_slice_in_dim(routers_two, tensor_index * column_count, column_count, 0))
    ffn_router_cols = mm_tn(normed_two, ffn_logit_grad)
    ffn_gain_cols = jnp.sum(normed_two_grad * state * rate_two, axis=0)
    ahead = normed_two_grad * gain_two
    centre = lax.psum(jnp.sum(ahead * state, axis=1, keepdims=True), "tensor") / D
    state_grad = dy_cols.astype(F32) + rate_two * ahead - state * rate_two * rate_two * rate_two * centre

    rows_state, heads_grad, heads_grad_rows = gather_rows(
        group_tokens(state_grad.astype(BF16), attn_tokens), output_map, gate=attn_gate_blocks, collective_id=4)
    rows_state = rows_state.reshape(-1, D)
    heads_grad_rows = heads_grad_rows.reshape(expert_count * CAP, -1)
    attn_notes = notes_of(jnp.sum(heads_grad_rows.astype(F32) * heads_rows.astype(F32), axis=1))
    output_part = mm_tn((rows_state.astype(F32) * attn_gate_rows).astype(BF16), heads_rows).astype(BF16)
    heads_grad, output_part = lax.optimization_barrier((heads_grad, output_part))

    query_back, key_back, value_back = attend_back(
        attn_slots[None], from_pieces(heads_grad, pieces).reshape(SLOTS, -1), queries, keys, values, log_total,
        query_ids, key_ids)
    output_grad = swap(output_part.reshape(expert_count, D // expert_count, -1))
    query_back, output_grad = lax.optimization_barrier((query_back, output_grad))
    output_grad = from_pieces(output_grad, pieces).astype(F32)
    normed_back, query_grad_rows, owed = scatter_rows(
        to_pieces(query_back.reshape(EXPERTS, CAP, -1), pieces), query_map, notes=attn_notes,
        windows=[key_back, value_back, pair_map], collective_id=5)
    query_grad_rows = query_grad_rows.reshape(expert_count * CAP, -1)
    query_part = mm_tn(rows_one, query_grad_rows)
    normed_grad = sums_of(normed_back, attn_noted) + jnp.sum(owed.astype(F32), axis=0)
    attn_pull = read_notes(normed_back, attn_places, 1)[:, :, 0].T
    pair_grad = jnp.stack([key_back, value_back])
    pair_part = jnp.einsum("td,ctf->cdf", window, pair_grad, preferred_element_type=F32)
    attn_gates = pick_gates(mm(normed_one, routers_one), attn_routes)
    attn_logit_grad = gate_back(attn_gates, attn_pull, attn_routes)
    normed_grad = normed_grad + mm_nt(
        attn_logit_grad, lax.dynamic_slice_in_dim(routers_one, tensor_index * column_count, column_count, 0))
    attn_router_cols = mm_tn(cols(normed_one), attn_logit_grad)
    rate_one = lax.rsqrt(jnp.mean(state_in * state_in, axis=1, keepdims=True) + eps)
    attn_gain_cols = jnp.sum(normed_grad * token_cols * rate_one, axis=0)
    ahead_one = normed_grad * cols(gain_one)
    centre_one = lax.psum(jnp.sum(ahead_one * token_cols, axis=1, keepdims=True), "tensor") / D
    tokens_grad = state_grad + rate_one * ahead_one - token_cols * rate_one * rate_one * rate_one * centre_one
    tokens_grad = columns_together(tokens_grad.astype(BF16)).astype(F32)

    def from_maps(part):
        got = swap(part.astype(BF16).reshape(expert_count, D // expert_count, -1))
        return from_pieces(got, pieces).astype(F32)

    query_grad = from_maps(query_part)
    key_value_grad = lax.psum_scatter(
        pair_part.astype(BF16), "expert", scatter_dimension=1, tiled=True).astype(F32)
    small = jnp.concatenate(
        [attn_router_cols, ffn_router_cols, attn_gain_cols[:, None], ffn_gain_cols[:, None]], axis=1)
    small = lax.all_gather(small, "tensor", axis=0, tiled=True)
    small = lax.psum_scatter(small, "expert", scatter_dimension=0, tiled=True)

    scaled_dy = (rows_dy.astype(F32) * ffn_gate_rows).astype(BF16)
    gate_grad = mm_tn(rows_two, gate_low)
    up_grad = mm_tn(rows_two, up_low)
    down_grad = mm_tn(hidden, scaled_dy)
    ffn_back = sums_from_experts(mm(hidden, down_map) * ffn_gate_rows, ffn_tokens)
    mixed = (state + ffn_back).astype(BF16)
    return (
        mixed,
        tokens_grad,
        small[:, 2 * EXPERTS],
        small[:, 2 * EXPERTS + 1],
        small[:, : 2 * EXPERTS],
        query_grad,
        output_grad,
        key_value_grad,
        gate_grad[None],
        up_grad[None],
        down_grad[None],
    )


def solution(mesh):
    in_specs = (
        P("expert", None),
        P(),
        P("expert", None),
        P("expert", None),
        P(),
        P(),
        P(),
        P(None, "expert", "tensor"),
        P(None, "expert", "tensor"),
        P(None, "expert", "tensor"),
        P("expert", None, "tensor"),
        P("expert", None, "tensor"),
        P("expert", "tensor", None),
        P("expert", None),
    )
    out_specs = (
        P("expert", "tensor"),
        P("expert", None),
        P("expert"),
        P("expert"),
        P("expert", None),
        P(None, "expert", "tensor"),
        P(None, "expert", "tensor"),
        P(None, "expert", "tensor"),
        P("expert", None, "tensor"),
        P("expert", None, "tensor"),
        P("expert", "tensor", None),
    )
    return jax.shard_map(
        per_device, mesh=mesh, in_specs=in_specs, out_specs=out_specs, check_vma=False
    )
```

time: 1360 us -> 1040 us (0.76)
  Pallas kernels: 0 us -> 562 us
  waiting for transfers between devices: 571 us -> 151 us
  blocking collectives: 250 us -> 37.7 us
  matrix products: 298 us -> 161 us
  starting transfers between devices: 95.9 us -> 40 us
  other arithmetic: 60.8 us -> 33.9 us
  local copies, waits for them, and re-layouts: 52.4 us -> 35.9 us
    pallas_call x0 -> x8, Pallas kernels: none -> 562 us  [the longest x3 250 us: scatter_rows(): pl.pallas_call(functools.partial(scatter_kernel, experts, bits, windows i...]
    all_to_all x12 -> x5, waiting for transfers between devices: 293 us -> 69.4 us  [swap(): lax.all_to_all(blocks, 'expert', split_axis=0, concat_axis=0, tiled=True)]
    all_to_all x7 -> x1, blocking collectives: 209 us -> 13.9 us  [swap(): lax.all_to_all(blocks, 'expert', split_axis=0, concat_axis=0, tiled=True)]
    reduce_scatter x1, waiting for transfers between devices: 0.01 us -> 81.5 us  [per_device(): lax.psum_scatter(pair_part.astype(BF16), 'expert', scatter_dimension=1, t...]
    reduce_scatter x5 -> x1, waiting for transfers between devices: 79.6 us -> 0.01 us  [columns_summed(): return lax.psum_scatter(rows, 'tensor', scatter_dimension=1, tiled=True)]
    all_gather x5 -> x2, waiting for transfers between devices: 77.5 us -> 0.01 us  [columns_together(): return lax.all_gather(rows, 'tensor', axis=1, tiled=True)]
    dot_general x11 -> x1, matrix products: 88.4 us -> 11.7 us  [per_device(): jnp.einsum('td,ctf->cdf', window, pair_grad, preferred_element_type=F32)]
    all_gather x1 -> x0, waiting for transfers between devices: 70 us -> none  [per_device(): pair_map = lax.all_gather(key_value_weight, 'expert', axis=1, tiled=True)]
  transfers between devices with their start and end apart: 33 -> 10, of which waited for: 18 -> 5; matrix products, arithmetic and copies ran while one was open for 20% -> 17% of each run, Pallas kernels for 0% -> 34%
where the time goes in v2:
time: 1040 us
  Pallas kernels  562 us (54%)
  matrix products  161 us (15%)
  waiting for transfers between devices  151 us (15%)
  starting transfers between devices  40 us (4%)
  blocking collectives  37.7 us (4%)
  local copies, waits for them, and re-layouts  35.9 us (3%)
  other arithmetic  33.9 us (3%)
  between operations  14.7 us (1%)
    pallas_call x3, Pallas kernels, scatter_rows(): pl.pallas_call(functools.partial(scatter_kernel, experts, bits, windows i...  250 us
    pallas_call x1, Pallas kernels, front(): pl.pallas_call(functools.partial(front_kernel, experts, bits), out_shape=...  152 us
    dot_general x27, matrix products, dot(): lax.dot_general(left, right, ((dims[0], dims[1]), ((), ())), preferred_el...  149 us
    pallas_call x2, Pallas kernels, gather_rows(): pl.pallas_call(functools.partial(gather_kernel, experts, bits, near, mult...  109 us
    reduce_scatter x1, waiting for transfers between devices, per_device(): lax.psum_scatter(pair_part.astype(BF16), 'expert', scatter_dimension=1, t...  81.5 us
    all_to_all x5, waiting for transfers between devices, swap(): lax.all_to_all(blocks, 'expert', split_axis=0, concat_axis=0, tiled=True)  69.4 us
    all_to_all x5, starting transfers between devices, swap(): lax.all_to_all(blocks, 'expert', split_axis=0, concat_axis=0, tiled=True)  39.6 us
    pallas_call x1, Pallas kernels, attend_back(): pl.pallas_call(attend_back_kernel, grid=(width // HD,), out_shape=[jax.Sh...  27.8 us
  transfers between devices with their start and end apart: 10, of which 5 were waited for; matrix products, arithmetic and copies ran while one was open for 17% of the time, Pallas kernels for 34%

profile of v2, /device:TPU:0, one launch (start us, length us, event | category | flops | bytes accessed | tf_op | source)
XLA Modules:
  0.0 1035.7 jit_solution(14098954318466881339)
XLA Ops:
  8.0 1.4 rev.6
  12.0 1.4 rev.7
  17.3 151.6 %shard_map.221 = (bf16[8,160,2048]{2,1,0:T(8,128)(2,1)}, bf16[8,160,512]{2,1,0:T(8,128)(2,1)}, bf16[2048,512]{1,0:T(8,128)(2,1)}, bf16[3,512,2048]{2,1,0:T(8,128...) custom-call(bf16[512,2048]{1,0:T(8,128)(2,1)} %refs_0_.1, ...), custom_call_target="tpu_custom_call" | custom-call | tf_op jit(solution)/shard_map/pallas_call | solution.py:382
  168.9 13.9 %all_to_all.30 = f32[8,2,160]{2,1,0:T(2,128)S(1)} all-to-all(f32[8,2,160]{2,1,0:T(2,128)S(1)} %maximum_bitcast_fusion), channel_id=1, replica_groups=mesh['expert'=8,'tensor'=4] {'expert'}, dimensions={0} | all-to-all | bytes 20480 | tf_op jit(solution)/shard_map/all_to_all | solution.py:647
  182.8 5.0 all-to-all-start
  188.7 2.1 copy.138
  191.2 2.7 fusion.10
  193.9 23.1 %shard_map.222 = (bf16[1280,512]{1,0:T(8,128)(2,1)S(1)}, bf16[1024,512]{1,0:T(8,128)(2,1)S(1)}, f32[4,1,1024]{2,1,0:T(1,128)S(1)}) custom-call(s32[1,1024]{1,0:T(1,128)S(1)} %copy-done.5, bf16[1280,512]{1,0:T(8,128)(2,1)S(1)} %bitcast.162, bf16[1536,512]{1,0:T(8,128)(2,1)S(1)} %copy-done.7, bf16[1536,512]{1,0:T(8,128)(2,1)} %get-tuple-element.43.value_ref, ...), custom_call_target="tpu_custom_call" | custom-call | flops 16000000000 | bytes 10000000 | tf_op jit(solution)/shard_map/pallas_call | solution.py:765
  219.7 4.0 select_reduce_fusion.3
  225.9 9.2 all-to-all-done
  235.1 58.5 %shard_map.223 = (bf16[8,160,512]{2,1,0:T(8,128)(2,1)}, bf16[8,160,512]{2,1,0:T(8,128)(2,1)}) custom-call(bf16[8,160,512]{2,1,0:T(8,128)(2,1)} %bitcast.157, bf16[2048,512]{1,0:T(8,128)(2,1)} %bitcast.12.refs_1_, f32[8,160,1]{2,1,0:T(8,128)} %add_divide_fusion.1.refs_2_), custom_call_target="tpu_custom_call" | custom-call | tf_op jit(solution)/shard_map/pallas_call | solution.py:617
  293.6 3.8 convolution_convert_fusion.1
  297.4 9.8 all-to-all-start.3
  308.3 2.0 copy.139
  310.8 2.7 fusion.9
  313.5 2.9 fusion.4
  316.4 21.4 %all-to-all-done.3 = bf16[8,160,512]{2,1,0:T(8,128)(2,1)S(1)} async-done(((bf16[8,160,512]{2,1,0:T(8,128)(2,1)}), bf16[8,160,512]{2,1,0:T(8,128)(2,1)S(1)}, u32[]{:S(2)}, u32[]{:S(2)}) %all-to-all-start.3) | async-done | bytes 1310752 | tf_op jit(solution)/shard_map/all_to_all | solution.py:647
  339.8 2.2 fusion.24
  342.0 2.9 fusion.5
  345.7 1.9 iota_compare_fusion.2
  347.7 3.1 multiply_reduce_fusion.5
  350.9 6.4 psum.21
  357.3 2.8 convolution_convert_fusion.2
  360.1 48.8 %shard_map.224 = bf16[8,160,2048]{2,1,0:T(8,128)(2,1)} custom-call(bf16[8,160,512]{2,1,0:T(8,128)(2,1)S(1)} %bitcast.159), custom_call_target="tpu_custom_call" | custom-call | tf_op jit(solution)/shard_map/pallas_call | solution.py:186
  409.0 4.1 select_reduce_fusion
  413.2 10.3 fusion.75
  423.5 10.3 fusion.77
  433.8 19.1 %multiply_reduce_fusion = (f32[1280]{0:T(1024)S(1)}, bf16[1280,1408]{1,0:T(8,128)(2,1)}, bf16[1280,1408]{1,0:T(8,128)(2,1)}, bf16[1280,1408]{1,0:T(8,128)(2,1)}) fusion(f32[1280,1408]{1,0:T(8,128)} %fusion.75, f32[1280,1408]{1,0:T(8,128)} %fusion.77, f32[1280]{0:T(1024)S(1)} %add_divide_fusion.4, bf16[1280,2048]{1,0:T(8,128)(2,1)} %all-gather.3.cloned.1.call-done, ...), kind=kOutput, calls=%fused_computation.6 | convolution fusion | flops 7416216576 | bytes 36251648 | tf_op jit(solution)/shard_map/dot_general | solution.py:631
  452.9 13.6 %multiply_convert_fusion.2 = bf16[1280,2048]{1,0:T(8,128)(2,1)} fusion(bf16[1280,1408]{1,0:T(8,128)(2,1)} %get-tuple-element.143, bf16[1,1408,2048]{2,1,0:T(8,128)(2,1)} %param.26, f32[1280]{0:T(1024)S(1)} %add_divide_fusion.4), kind=kOutput, calls=%fused_computation.2 | convolution fusion | flops 7387217920 | bytes 14619648 | tf_op jit(solution)/shard_map/dot_general | solution.py:631
  468.4 87.2 %shard_map.225 = bf16[8,176,512]{2,1,0:T(8,128)(2,1)} custom-call(bf16[8,160,1408]{2,1,0:T(8,128)(2,1)} %bitcast.182, bf16[2048,1408]{1,0:T(8,128)(2,1)} %bitcast.175, bf16[8,160,1408]{2,1,0:T(8,128)(2,1)} %bitcast.181, bf16[2048,1408]{1,0:T(8,128)(2,1)} %bitcast.172, f32[8,16,512]{2,1,0:T(8,128)} %select_maximum_fusion.refs_4_), custom_call_target="tpu_custom_call" | custom-call | tf_op jit(solution)/shard_map/pallas_call | solution.py:617
  557.3 3.3 fusion.28
  561.8 5.7 psum.22
  567.5 3.0 convolution_convert_fusion
  570.5 59.9 %shard_map.226 = (bf16[8,160,2048]{2,1,0:T(8,128)(2,1)}, bf16[8,160,512]{2,1,0:T(8,128)(2,1)S(1)}, bf16[8,160,512]{2,1,0:T(8,128)(2,1)S(1)}) custom-call(bf16[8,160,512]{2,1,0:T(8,128)(2,1)S(1)} %bitcast.158, bf16[2048,512]{1,0:T(8,128)(2,1)} %bitcast.12.refs_1_, f32[8,160,1]{2,1,0:T(8,128)S(1)} %copy-done.2), custom_call_target="tpu_custom_call" | custom-call | tf_op jit(solution)/shard_map/pallas_call | solution.py:186
  630.5 8.1 bitcast_convert_fusion.1
  638.6 9.0 all-to-all-start.4
  647.7 3.2 slice.81
  650.9 1.7 multiply_reduce_fusion.2
  653.7 27.8 %shard_map.227 = (bf16[1280,512]{1,0:T(8,128)(2,1)}, bf16[1536,512]{1,0:T(8,128)(2,1)}, bf16[1536,512]{1,0:T(8,128)(2,1)}) custom-call(s32[1,1024]{1,0:T(1,128)} %add.171.refs_2_.slots_ref, bf16[1280,512]{1,0:T(8,128)(2,1)} %bitcast.163, bf16[1024,512]{1,0:T(8,128)(2,1)} %copy-done.10, bf16[1536,512]{1,0:T(8,128)(2,1)} %get-tuple-element.42.key_ref, ...), custom_call_target="tpu_custom_call" | custom-call | flops 30000001024 | bytes 10000000 | tf_op jit(solution)/shard_map/pallas_call | solution.py:827
  681.5 14.5 %all-to-all-done.4 = bf16[8,256,512]{2,1,0:T(8,128)(2,1)} async-done(((bf16[8,256,512]{2,1,0:T(8,128)(2,1)}), bf16[8,256,512]{2,1,0:T(8,128)(2,1)}, u32[]{:S(2)}, u32[]{:S(2)}) %all-to-all-start.4) | async-done | bytes 2097184 | tf_op jit(solution)/shard_map/all_to_all | solution.py:647
  696.1 104.6 %shard_map.228 = (bf16[8,176,512]{2,1,0:T(8,128)(2,1)}, bf16[8,160,512]{2,1,0:T(8,128)(2,1)}, bf16[2,512,512]{2,1,0:T(8,128)(2,1)}) custom-call(bf16[8,160,512]{2,1,0:T(8,128)(2,1)} %bitcast.190, bf16[2048,512]{1,0:T(8,128)(2,1)} %get-tuple-element.61.refs_1_, f32[8,16,512]{2,1,0:T(8,128)} %pad.10.refs_2_, bf16[1536,512]{1,0:T(8,128)(2,1)} %get-tuple-element.63.refs_3_, ...), custom_call_target="tpu_custom_call" | custom-call | tf_op jit(solution)/shard_map/pallas_call | solution.py:617
  800.6 1.6 convert_reduce_fusion.2
  805.3 3.6 fusion.30
  809.0 1.5 fusion.39
  810.4 5.6 psum.23
  817.3 6.1 all_gather.11
  823.5 2.7 fusion.36
  826.3 11.7 %convert_bitcast_fusion = bf16[2,2048,512]{1,2,0:T(8,128)(2,1)} fusion(bf16[1536,2048,1]{1,0,2:T(8,128)(2,1)} %bitcast.191, bf16[1,1536,512]{2,1,0:T(8,128)(2,1)} %bitcast.186, bf16[1,1536,512]{2,1,0:T(8,128)(2,1)} %bitcast.185), kind=kOutput, calls=%fused_computation.34 | convolution fusion | flops 6446120960 | bytes 13631488 | tf_op jit(solution)/shard_map/td,ctf->cdf/dot_general | solution.py:1013
  839.3 6.8 bitcast_convert_fusion
  846.1 11.4 %all-to-all-start.5 = ((bf16[8,256,512]{2,1,0:T(8,128)(2,1)}), bf16[8,256,512]{2,1,0:T(8,128)(2,1)S(1)}, u32[]{:S(2)}, u32[]{:S(2)}) async-start(bf16[8,256,512]{2,1,0:T(8,128)(2,1)} %bitcast.184), calls=%async_computation.7 | async-start | bytes 4194304 | tf_op jit(solution)/shard_map/all_to_all | solution.py:647
  857.5 14.1 %convolution_bitcast_fusion.2 = f32[1,2048,1408]{2,1,0:T(8,128)} fusion(bf16[1280,2048]{1,0:T(8,128)(2,1)} %bitcast.165, bf16[1280,1408]{1,0:T(8,128)(2,1)} %get-tuple-element.144), kind=kOutput, calls=%fused_computation.5 | convolution fusion | flops 7381975040 | bytes 20381696 | tf_op jit(solution)/shard_map/dot_general | solution.py:631
  871.7 11.3 %convolution_bitcast_fusion.1 = f32[1,2048,1408]{2,1,0:T(8,128)} fusion(bf16[1280,2048]{1,0:T(8,128)(2,1)S(1)} %bitcast.170, bf16[1280,1408]{1,0:T(8,128)(2,1)S(1)} %copy-done.22), kind=kOutput, calls=%fused_computation.4 | convolution fusion | flops 7381975040 | bytes 20381696 | tf_op jit(solution)/shard_map/dot_general | solution.py:631
  883.0 24.2 %all-to-all-done.5 = bf16[8,256,512]{2,1,0:T(8,128)(2,1)S(1)} async-done(((bf16[8,256,512]{2,1,0:T(8,128)(2,1)}), bf16[8,256,512]{2,1,0:T(8,128)(2,1)S(1)}, u32[]{:S(2)}, u32[]{:S(2)}) %all-to-all-start.5) | async-done | bytes 2097184 | tf_op jit(solution)/shard_map/all_to_all | solution.py:647
  907.2 4.4 all-to-all-start.2
  911.6 14.1 %convolution_bitcast_fusion = f32[1,1408,2048]{2,1,0:T(8,128)} fusion(bf16[1280,1408]{1,0:T(8,128)(2,1)} %get-tuple-element.143, bf16[1280,2048]{1,0:T(8,128)(2,1)} %all-gather.3.cloned.1.call-done, f32[1280]{0:T(1024)S(1)} %copy-done.32), kind=kOutput, calls=%fused_computation.3 | convolution fusion | flops 7389839360 | bytes 20386816 | tf_op jit(solution)/shard_map/dot_general | solution.py:631
  925.7 4.2 convert_element_type.222
  929.9 1.3 slice.100
  931.2 1.3 fusion.87
  932.6 4.1 copy.126
  936.7 2.6 convert_element_type.221
  939.2 81.5 %reduce-scatter.8.cloned.1.call-done = bf16[2,256,512]{1,2,0:T(8,128)(2,1)} async-done(((bf16[2,2048,512]{1,2,0:T(8,128)(2,1)}), bf16[2,256,512]{1,2,0:T(8,128)(2,1)}) %reduce-scatter.8.cloned.1.call-update) | async-done | bytes 524304 | tf_op jit(solution)/shard_map/reduce_scatter | solution.py:1031
  1020.8 2.2 copy.127
  1023.0 4.0 fusion.31
  1027.0 2.0 copy.125
  (178 shorter events, 29.5 us)
Async XLA Ops:
  7.2 180.7 %copy-start = (bf16[512,2048]{1,0:T(8,128)(2,1)S(1)}, bf16[512,2048]{1,0:T(8,128)(2,1)}, u32[]{:S(2)}) copy-start(bf16[512,2048]{1,0:T(8,128)(2,1)} %param.27) | copy-start | bytes 6291460
  182.8 7.9 copy-start.28
  182.8 52.3 %all-to-all-start = ((bf16[8,256,512]{2,1,0:T(8,128)(2,1)}), bf16[8,256,512]{2,1,0:T(8,128)(2,1)}, u32[]{:S(2)}, u32[]{:S(2)}) async-start(bf16[8,256,512]{2,1,0:T(8,128)(2,1)} %param.22), calls=%async_computation | async-start | bytes 4194304 | tf_op jit(solution)/shard_map/all_to_all | solution.py:647
  187.8 6.0 copy-start.5
  187.8 6.0 copy-start.8
  190.8 3.1 copy-start.7
  191.1 25.8 %copy-start.4 = (s32[1536,1]{1,0:T(8,128)}, s32[1536,1]{1,0:T(8,128)S(1)}, u32[]{:S(2)}) copy-start(s32[1536,1]{1,0:T(8,128)S(1)} %broadcast_in_dim.54.key_ids) | copy-start | bytes 18436
  191.2 25.7 %copy-start.6 = (s32[512]{0:T(512)}, s32[512]{0:T(512)S(1)}, u32[]{:S(2)}) copy-start(s32[512]{0:T(512)S(1)} %pad_dynamic-slice_fusion) | copy-start | bytes 6148
  193.9 25.8 %copy-start.26 = (bf16[2048,16]{0,1:T(8,128)(2,1)S(1)}, bf16[2048,16]{0,1:T(8,128)(2,1)}, u32[]{:S(2)}) copy-start(bf16[2048,16]{0,1:T(8,128)(2,1)} %param.20) | copy-start | bytes 196612
  217.0 1.1 copy-start.3
  218.0 1.0 copy-start.10
  219.0 0.6 copy-start.11
  224.7 68.9 %copy-start.23 = (bf16[512,512]{0,1:T(8,128)(2,1)S(1)}, bf16[512,512]{0,1:T(8,128)(2,1)}, u32[]{:S(2)}) copy-start(bf16[512,512]{0,1:T(8,128)(2,1)} %copy.138) | copy-start | bytes 1572868
  293.6 13.8 %copy-start.13 = (bf16[512,2048]{1,0:T(8,128)(2,1)S(1)}, bf16[512,2048]{1,0:T(8,128)(2,1)}, u32[]{:S(2)}) copy-start(bf16[512,2048]{1,0:T(8,128)(2,1)} %refs_0_.1) | copy-start | bytes 6291460
  297.4 40.5 %all-to-all-start.3 = ((bf16[8,160,512]{2,1,0:T(8,128)(2,1)}), bf16[8,160,512]{2,1,0:T(8,128)(2,1)S(1)}, u32[]{:S(2)}, u32[]{:S(2)}) async-start(bf16[8,160,512]{2,1,0:T(8,128)(2,1)} %bitcast.189), calls=%async_computation.4 | async-start | bytes 2621440 | tf_op jit(solution)/shard_map/all_to_all | solution.py:647
  307.2 126.6 %all-gather.3.cloned.1.call-start = ((), (), s32[]{:S(2)}) async-start(), calls=%async_computation.10 | async-start | bytes 6553600 | tf_op jit(solution)/shard_map/all_gather | solution.py:651
  337.9 1.1 copy-start.17
  339.0 568.2 %reduce-scatter.4.cloned.1.call-start = ((), (), s32[]{:S(2)}) async-start(), calls=%async_computation.9 | async-start | bytes 6553600 | tf_op jit(solution)/shard_map/reduce_scatter | solution.py:655
  342.0 5.7 copy-start.18
  350.8 472.6 %copy-start.14 = (f32[512,512]{0,1:T(8,128)}, f32[512,512]{0,1:T(8,128)S(1)}, u32[]{:S(2)}) copy-start(f32[512,512]{0,1:T(8,128)S(1)} %get-tuple-element.153) | copy-start | bytes 3145732
  357.2 55.9 %slice-start.2 = ((s8[5767168]{0:T(1024)(128)(4,1)}), s8[4194304]{0:T(1024)(128)(4,1)S(1)}, s32[]{:S(2)}) async-start(s8[5767168]{0:T(1024)(128)(4,1)} %bitcast.173), calls=%async_computation.16 | async-start | bytes 8388608
  360.1 53.0 %slice-start.3 = ((s8[5767168]{0:T(1024)(128)(4,1)}), s8[1572864]{0:T(1024)(128)(4,1)S(1)}, s32[]{:S(2)}) async-start(s8[5767168]{0:T(1024)(128)(4,1)} %bitcast.173), calls=%async_computation.17 | async-start | bytes 3145728
  409.0 4.2 copy-start.12
  409.0 14.5 %slice-start.4 = ((s8[5767168]{0:T(1024)(128)(4,1)}), s8[4194304]{0:T(1024)(128)(4,1)S(1)}, s32[]{:S(2)}) async-start(s8[5767168]{0:T(1024)(128)(4,1)} %bitcast.176), calls=%async_computation.18 | async-start | bytes 8388608
  413.2 39.8 %copy-start.31 = (f32[1280]{0:T(1024)}, f32[1280]{0:T(1024)S(1)}, u32[]{:S(2)}) copy-start(f32[1280]{0:T(1024)S(1)} %add_divide_fusion.4) | copy-start | bytes 15364
  413.2 10.3 slice-start.5
  468.4 88.9 %copy-start.29 = (s32[512,2]{0,1:T(2,128)S(1)}, s32[512,2]{0,1:T(2,128)}, u32[]{:S(2)}) copy-start(s32[512,2]{0,1:T(2,128)} %param.17) | copy-start | bytes 12292
  561.8 8.7 copy-start.20
  567.5 3.0 copy-start.2
  570.5 60.0 %copy-start.25 = (bf16[8,160,512]{2,1,0:T(8,128)(2,1)S(1)}, bf16[8,160,512]{2,1,0:T(8,128)(2,1)}, u32[]{:S(2)}) copy-start(bf16[8,160,512]{2,1,0:T(8,128)(2,1)} %get-tuple-element.54) | copy-start | bytes 3932164
  630.5 8.1 copy-start.9
  638.6 9.0 copy-start.27
  638.6 9.1 copy-start.30
  638.6 57.5 %all-to-all-start.4 = ((bf16[8,256,512]{2,1,0:T(8,128)(2,1)}), bf16[8,256,512]{2,1,0:T(8,128)(2,1)}, u32[]{:S(2)}, u32[]{:S(2)}) async-start(bf16[8,256,512]{2,1,0:T(8,128)(2,1)} %bitcast.183), calls=%async_computation.5 | async-start | bytes 4194304 | tf_op jit(solution)/shard_map/all_to_all | solution.py:647
  647.6 282.3 %reduce-scatter.6.cloned.1.call-start = ((), (), s32[]{:S(2)}) async-start(), calls=%async_computation.12 | async-start | bytes 221184 | tf_op jit(solution)/shard_map/reduce_scatter | solution.py:1036
  800.6 3.8 copy-start.16
  805.3 3.6 copy-start.19
  808.9 14.6 %copy-start.21 = (f32[512,512]{0,1:T(8,128)S(1)}, f32[512,512]{0,1:T(8,128)}, u32[]{:S(2)}) copy-start(f32[512,512]{0,1:T(8,128)} %copy-done.20) | copy-start | bytes 3145732
  808.9 14.6 %copy-start.24 = (bf16[512,512]{0,1:T(8,128)(2,1)S(1)}, bf16[512,512]{0,1:T(8,128)(2,1)}, u32[]{:S(2)}) copy-start(bf16[512,512]{0,1:T(8,128)(2,1)} %copy.138) | copy-start | bytes 1572868
  823.4 109.1 %all-gather.5.cloned.1.call-start = ((), (), s32[]{:S(2)}) async-start(), calls=%async_computation.11 | async-start | bytes 2621440 | tf_op jit(solution)/shard_map/all_gather | solution.py:651
  826.2 194.5 %reduce-scatter.8.cloned.1.call-start = ((), (), s32[]{:S(2)}) async-start(), calls=%async_computation.13 | async-start | bytes 4718592 | tf_op jit(solution)/shard_map/reduce_scatter | solution.py:1031
  838.0 1.3 copy-start.33
  839.3 32.4 %slice-start = ((s8[5242880]{0:T(1024)(128)(4,1)}), s8[1048576]{0:T(1024)(128)(4,1)S(1)}, s32[]{:S(2)}) async-start(s8[5242880]{0:T(1024)(128)(4,1)} %bitcast.168), calls=%async_computation.14 | async-start | bytes 2097152
  846.1 61.1 %all-to-all-start.5 = ((bf16[8,256,512]{2,1,0:T(8,128)(2,1)}), bf16[8,256,512]{2,1,0:T(8,128)(2,1)S(1)}, u32[]{:S(2)}, u32[]{:S(2)}) async-start(bf16[8,256,512]{2,1,0:T(8,128)(2,1)} %bitcast.184), calls=%async_computation.7 | async-start | bytes 4194304 | tf_op jit(solution)/shard_map/all_to_all | solution.py:647
  857.5 14.2 %slice-start.1 = ((s8[5242880]{0:T(1024)(128)(4,1)}), s8[4194304]{0:T(1024)(128)(4,1)S(1)}, s32[]{:S(2)}) async-start(s8[5242880]{0:T(1024)(128)(4,1)} %bitcast.168), calls=%async_computation.15 | async-start | bytes 8388608
  857.5 14.2 %copy-start.22 = (bf16[1280,1408]{1,0:T(8,128)(2,1)S(1)}, bf16[1280,1408]{1,0:T(8,128)(2,1)}, u32[]{:S(2)}) copy-start(bf16[1280,1408]{1,0:T(8,128)(2,1)} %get-tuple-element.145) | copy-start | bytes 10813444
  871.7 39.9 %copy-start.32 = (f32[1280]{0:T(1024)S(1)}, f32[1280]{0:T(1024)}, u32[]{:S(2)}) copy-start(f32[1280]{0:T(1024)} %copy-done.31) | copy-start | bytes 15364
  907.2 115.8 %all-to-all-start.2 = ((bf16[8,160,512]{2,1,0:T(8,128)(2,1)}), bf16[8,160,512]{2,1,0:T(8,128)(2,1)}, u32[]{:S(2)}, u32[]{:S(2)}) async-start(bf16[8,160,512]{2,1,0:T(8,128)(2,1)} %bitcast.188), calls=%async_computation.3 | async-start | bytes 2621440 | tf_op jit(solution)/shard_map/all_to_all | solution.py:647
  936.7 86.3 %copy-start.15 = (f32[512,512]{0,1:T(8,128)S(1)}, f32[512,512]{0,1:T(8,128)}, u32[]{:S(2)}) copy-start(f32[512,512]{0,1:T(8,128)} %copy-done.14) | copy-start | bytes 3145732
  1023.0 6.0 copy-start.1
Sparse Core Ops, SparseCore 0:
  339.1 51.6 all-gather.2
  466.6 78.3 reduce-scatter.3
  823.5 81.6 reduce-scatter.5
  907.3 20.9 all-gather.4
  932.3 88.4 reduce-scatter.7

commit v3 on v2

--- a/solution.py
+++ b/solution.py
@@ -191,12 +191,14 @@
         scratch_shapes=scratch,
         compiler_params=pltpu.CompilerParams(
             collective_id=collective_id, has_side_effects=True, vmem_limit_bytes=48 * 2**20),
+        cost_estimate=pl.CostEstimate(flops=10**11, bytes_accessed=10**7, transcendentals=0),
     )(*ins)
 
 
 def front_kernel(experts, bits, *refs):
-    (tokens, gain, slots, w_in, kv_in, rows, back, w, window, kv, keys, values, x, y,
-     z_send, z_recv, t_send, t_recv, y_send, y_recv, w_send, w_recv, k_send, k_recv, n_send, n_recv, own_sem) = refs
+    (tokens, gain, slots, wide, routes, routers, w_in, kv_in,
+     rows, back, w, window, kv, keys, values, gates, rivals, x, y, facts, facts_in,
+     f_send, f_recv, z_send, z_recv, t_send, t_recv, y_send, y_recv, w_send, w_recv, k_send, k_recv, n_send, n_recv, own_sem) = refs
     e, t = lax.axis_index("expert"), lax.axis_index("tensor")
     partner = partners(e, experts, True)
     width = x.shape[1]
@@ -293,6 +295,34 @@
         remote(w_in.at[j], w.at[part(e)], w_send.at[j], w_recv.at[e], expert=j).start()
 
     rows[e, :, cols(0)] = x[x_part(e), :]
+
+    logits = jnp.dot(window[2], routers[...], preferred_element_type=F32)
+    lane = lax.broadcasted_iota(jnp.int32, logits.shape, 1)
+    first, second = (jnp.sum(jnp.where(lane == routes[:, k : k + 1], logits, 0.0), axis=1, keepdims=True) for k in (0, 1))
+    top = jnp.maximum(first, second)
+    first, second = jnp.exp(first - top), jnp.exp(second - top)
+    gate = jnp.concatenate([first, second], axis=0) / jnp.concatenate([first + second] * 2, axis=0)
+    other = jnp.concatenate([routes[:, 3:4], routes[:, 2:3]], axis=0).astype(F32)
+    high = gate.astype(BF16).astype(F32)
+    middle = (gate - high).astype(BF16).astype(F32)
+    lane = lax.broadcasted_iota(jnp.int32, (2 * here, 128), 1)
+    table = jnp.where(lane == 0, high, jnp.where(lane == 1, middle, jnp.where(lane == 2, gate - high - middle, 0.0)))
+    fact = []
+    for k, values_of in enumerate((table, jnp.where(lane == 0, other, 0.0))):
+        spot = lax.broadcasted_iota(jnp.int32, (2 * here, EXPERTS * 256), 1) == wide[:, k : k + 1]
+        fact.append(jnp.dot(values_of.T[:16].astype(BF16), spot.astype(F32).astype(BF16), preferred_element_type=F32))
+    gate_row = fact[0][0:1] + fact[0][1:2] + fact[0][2:3]
+    row = lax.broadcasted_iota(jnp.int32, (8, EXPERTS * 256), 0)
+    fact = jnp.where(row == 0, gate_row, jnp.where(row == 1, fact[1][0:1], 0.0))
+    for q in range(EXPERTS):
+        facts[q] = fact[:, q * 256 : (q + 1) * 256]
+
+    @pl.loop(1, experts)
+    def _(s):
+        j = partner(s)
+        remote(facts.at[j // pieces], facts_in.at[e], f_send.at[j], f_recv.at[e], expert=j).start()
+
+    facts_in[e] = facts[e // pieces]
     chunks(expert_bits - 1)
 
     @pl.loop(0, experts + bits)
@@ -354,6 +384,19 @@
     @pl.loop(1, experts)
     def _(s):
         j = partner(s)
+        fact_from = remote(facts.at[j // pieces], facts_in.at[j], f_send.at[j], f_recv.at[j], expert=j)
+        fact_from.wait_recv()
+        fact_from.wait_send()
+
+    @pl.loop(0, experts)
+    def _(j):
+        column = jnp.concatenate([facts_in[j], jnp.zeros((120, 256), F32)], axis=0).T[:cap]
+        gates[j] = column[:, 0:1]
+        rivals[j] = column[:, 1:2]
+
+    @pl.loop(1, experts)
+    def _(s):
+        j = partner(s)
         arrived(j).wait_send()
         handed(j).wait_recv()
         handed(j).wait_send()
@@ -373,7 +416,7 @@
             passed(j, d).wait_send()
 
 
-def front(tokens, gain, slots, w, kv, collective_id):
+def front(tokens, gain, slots, wide, routes, routers, w, kv, collective_id):
     experts, tensor = lax.axis_size("expert"), lax.axis_size("tensor")
     bits = tensor.bit_length() - 1
     here = tokens.shape[0]
@@ -389,43 +432,45 @@
             jax.ShapeDtypeStruct((2, D, f_kv), BF16),
             jax.ShapeDtypeStruct((3 * here, f_kv), BF16),
             jax.ShapeDtypeStruct((3 * here, f_kv), BF16),
+            jax.ShapeDtypeStruct((experts, CAP, 1), F32),
+            jax.ShapeDtypeStruct((experts, CAP, 1), F32),
         ],
-        in_specs=[VMEM, VMEM, VMEM, ANY, ANY],
-        out_specs=[VMEM] * 7,
-        scratch_shapes=[pltpu.VMEM((SLOTS, D // tensor), BF16), pltpu.VMEM((experts, CAP, f), BF16)]
-        + [dma((experts,))] * 2 + [dma((experts + 2, tensor))] * 2 + [dma((experts,))] * 6
+        in_specs=[VMEM] * 6 + [ANY, ANY],
+        out_specs=[VMEM] * 9,
+        scratch_shapes=[
+            pltpu.VMEM((SLOTS, D // tensor), BF16),
+            pltpu.VMEM((experts, CAP, f), BF16),
+            pltpu.VMEM((EXPERTS, 8, 256), F32),
+            pltpu.VMEM((experts, 8, 256), F32),
+        ] + [dma((experts,))] * 2 + [dma((experts,))] * 2 + [dma((experts + 2, tensor))] * 2 + [dma((experts,))] * 6
         + [dma((2,))] * 3,
         compiler_params=pltpu.CompilerParams(
             collective_id=collective_id, has_side_effects=True, vmem_limit_bytes=56 * 2**20),
-    )(tokens, gain, slots, w, kv)
-
-
-def scatter_kernel(experts, bits, depth, near, multiply, terms, scale, noted, *refs):
+        cost_estimate=pl.CostEstimate(flops=10**11, bytes_accessed=10**7, transcendentals=0),
+    )(tokens, gain, slots, wide, routes, routers, w, kv)
+
+
+def scatter_kernel(experts, bits, depth, near, scale, noted, *refs):
     refs = list(refs)
-    h_in = refs.pop(0) if multiply else None
-    w = refs.pop(0) if multiply else None
-    factors = [(refs.pop(0), refs.pop(0)) for _ in range(terms)]
+    h_in, w = refs[:2]
+    refs = refs[2:]
     gate = refs.pop(0) if scale else None
     notes = refs.pop(0) if noted else None
     if depth:
-        key_grad, value_grad, kv = refs[:3]
+        key_grad, value_grad, kv, rows, pair_part = refs[:5]
+        refs = refs[5:]
+    back, h = refs[:2]
+    refs = refs[2:]
+    if depth:
+        owed, map_grad, pair_came = refs[:3]
         refs = refs[3:]
-    back = refs.pop(0)
-    h = refs.pop(0) if multiply else None
-    if multiply:
-        factors = [(h, w)]
-    owed = refs.pop(0) if depth else None
-    keep, sent, got, y, t_send, t_recv, y_send, y_recv = refs[:8]
-    refs = refs[8:]
-    if multiply:
-        h_send, h_recv = refs[:2]
-        refs = refs[2:]
+    keep, sent, got, y, t_send, t_recv, y_send, y_recv, h_send, h_recv = refs[:10]
     if depth:
-        n_keep, n_sent, n_got, n_y, n_in, n_send, n_recv, o_send, o_recv = refs
+        n_keep, n_sent, n_got, n_y, n_in, part_grad, n_send, n_recv, o_send, o_recv, g_send, g_recv, p_sem = refs[10:]
     e, t = lax.axis_index("expert"), lax.axis_index("tensor")
     partner = partners(e, experts, near)
     tensor = 1 << bits
-    cap, width = factors[0][0].shape[1], y.shape[2]
+    cap, width = h.shape[1], y.shape[2]
     body = pl.ds(0, cap)
     foot = pl.ds(cap, NOTES)
 
@@ -436,10 +481,17 @@
         return remote(y.at[j], back.at[j], y_send.at[j], y_recv.at[j], expert=j)
 
     def give(j, d):
-        return remote(sent.at[j, d], got.at[j, d], t_send.at[j, d], t_recv.at[j, d], tensor=t ^ (1 << low_bit(d)))
+        return remote(sent.at[j, d - 1], got.at[j, d - 1], t_send.at[j, d], t_recv.at[j, d], tensor=t ^ (1 << low_bit(d)))
 
     def owe(q, d):
-        return remote(n_sent.at[q, d], n_got.at[q, d], n_send.at[q, d], n_recv.at[q, d], tensor=t ^ (1 << low_bit(d)))
+        return remote(n_sent.at[q, d - 1], n_got.at[q, d - 1], n_send.at[q, d], n_recv.at[q, d],
+                      tensor=t ^ (1 << low_bit(d)))
+
+    def grad_to(j):
+        return remote(part_grad.at[j], map_grad.at[e], g_send.at[j], g_recv.at[e], expert=j)
+
+    def grad_from(j):
+        return remote(part_grad.at[j], map_grad.at[j], g_send.at[j], g_recv.at[j], expert=j)
 
     def across():
         return remote(n_y.at[1], n_in, o_send.at[1], o_recv.at[1], expert=e ^ 1)
@@ -454,7 +506,7 @@
                 if d % (1 << k) == 0:
                     came = d | (1 << (k - 1))
                     owe(q, came).wait_recv()
-                    total = n_keep[q, d // 2] + n_got[q, came].astype(F32)
+                    total = n_keep[q, d // 2] + n_got[q, came - 1].astype(F32)
                     if k == bits:
                         if q == 1:
                             n_y[1] = total.astype(BF16)
@@ -462,20 +514,28 @@
                         else:
                             n_keep[q, 0] = total
                     elif d & (1 << k):
-                        n_sent[q, d] = total.astype(BF16)
+                        n_sent[q, d - 1] = total.astype(BF16)
                         owe(q, d).start()
                     else:
                         n_keep[q, d // 2] = total
 
+    def pair_half():
+        half = pair_part.shape[0] // 2
+        return remote(pair_part.at[pl.ds(half, half)], pair_came, p_sem.at[0], p_sem.at[1], expert=e ^ 1)
+
+    def row_from(j):
+        return remote(h_in.at[j], h.at[j], h_send.at[j], h_recv.at[j], expert=j)
+
     meet(experts, bits)
-    if multiply:
-        @pl.loop(1, experts)
-        def _(s):
-            j = partner(s)
-            remote(h_in.at[j], h.at[e], h_send.at[j], h_recv.at[e], expert=j).start()
-
-        h[e] = h_in[e]
+
+    @pl.loop(1, experts)
+    def _(s):
+        j = partner(s)
+        remote(h_in.at[j], h.at[e], h_send.at[j], h_recv.at[e], expert=j).start()
+
+    h[e] = h_in[e]
     if depth:
+        pair_half().start()
         here = key_grad.shape[0] // 3
         for q in WINDOW_ORDER:
             place = pl.ds(q * here, here)
@@ -485,11 +545,30 @@
                 part += lax.dot_general(
                     value_grad[place, :], kv[1, slice_at(d), :], (((1,), (1,)), ((), ())), preferred_element_type=F32)
                 if d & 1:
-                    n_sent[q, d] = part.astype(BF16)
+                    n_sent[q, d - 1] = part.astype(BF16)
                     owe(q, d).start()
                 else:
                     n_keep[q, d // 2] = part
         window_stage(1)
+
+        @pl.loop(1, experts)
+        def _(s):
+            row_from(partner(s)).wait_recv()
+
+        @pl.loop(0, experts)
+        def _(i):
+            j = partner(lax.rem(i + 1, experts))
+            share = part_grad.shape[1]
+            some = rows[:, pl.ds(pl.multiple_of(j * share, share), share)]
+            part_grad[j] = lax.dot_general(
+                some, h[...].reshape(experts * cap, h.shape[2]), (((0,), (0,)), ((), ())),
+                preferred_element_type=F32).astype(BF16)
+
+            @pl.when(i < experts - 1)
+            def _():
+                grad_to(j).start()
+
+        map_grad[e] = part_grad[e]
 
     @pl.loop(0, experts + bits)
     def _(i):
@@ -497,22 +576,19 @@
         def _():
             j = partner(i)
             slot = lax.rem(i, bits + 1)
-            if multiply:
+            if not depth:
                 @pl.when(i > 0)
                 def _():
-                    remote(h_in.at[j], h.at[j], h_send.at[j], h_recv.at[j], expert=j).wait_recv()
+                    row_from(j).wait_recv()
             for d in range(tensor - 1, -1, -1):
-                part = None
-                for left, right in factors:
-                    term = lax.dot_general(
-                        left[j], right[slice_at(d), :], (((1,), (1,)), ((), ())), preferred_element_type=F32)
-                    part = term if part is None else part + term
+                part = lax.dot_general(
+                    h[j], w[slice_at(d), :], (((1,), (1,)), ((), ())), preferred_element_type=F32)
                 if scale:
                     part = part * gate[j]
                 if d & 1:
-                    sent[j, d, body, :] = part.astype(BF16)
+                    sent[j, d - 1, body, :] = part.astype(BF16)
                     if noted:
-                        sent[j, d, foot, :] = notes[j].astype(BF16)
+                        sent[j, d - 1, foot, :] = notes[j].astype(BF16)
                     give(j, d).start()
                 else:
                     keep[slot, d // 2, body, :] = part
@@ -529,11 +605,11 @@
                     if d % (1 << k) == 0:
                         came = d | (1 << (k - 1))
                         give(j, came).wait_recv()
-                        total = keep[slot, d // 2] + got[j, came].astype(F32)
+                        total = keep[slot, d // 2] + got[j, came - 1].astype(F32)
                         if k == bits:
                             y[j] = total.astype(BF16)
                         elif d & (1 << k):
-                            sent[j, d] = total.astype(BF16)
+                            sent[j, d - 1] = total.astype(BF16)
                             give(j, d).start()
                         else:
                             keep[slot, d // 2] = total
@@ -564,10 +640,12 @@
     @pl.loop(1, experts)
     def _(s):
         j = partner(s)
-        if multiply:
-            remote(h_in.at[j], h.at[j], h_send.at[j], h_recv.at[j], expert=j).wait_send()
+        row_from(j).wait_send()
         handed(j).wait_recv()
         handed(j).wait_send()
+        if depth:
+            grad_from(j).wait_recv()
+            grad_from(j).wait_send()
 
     @pl.loop(0, experts)
     def _(j):
@@ -578,53 +656,466 @@
         for q in range(3):
             for d in range(1, tensor):
                 owe(q, d).wait_send()
+        pair_half().wait_recv()
+        pair_half().wait_send()
         across().wait_send()
         two_back(-1).wait_recv()
         two_back(1).wait_send()
 
 
-def scatter_rows(h=None, w=None, gate=None, notes=None, products=(), windows=None, near=True, collective_id=0):
+def scatter_rows(h, w, gate=None, notes=None, windows=None, near=True, collective_id=0):
     experts, tensor = lax.axis_size("expert"), lax.axis_size("tensor")
     bits = tensor.bit_length() - 1
-    multiply = w is not None
     high = CAP + (NOTES if notes is not None else 0)
-    width = D // tensor
+    width, f = D // tensor, w.shape[1]
     dma = pltpu.SemaphoreType.DMA
-    ins = [a for a in (h, w) if a is not None] + [a for pair in products for a in pair]
-    ins += [a for a in (gate, notes) if a is not None]
-    outs = [jax.ShapeDtypeStruct((experts, high, width), BF16)]
+    ins = [a for a in (h, w, gate, notes) if a is not None]
+    outs = [jax.ShapeDtypeStruct((experts, high, width), BF16), jax.ShapeDtypeStruct(h.shape, BF16)]
     scratch = [
         pltpu.VMEM((bits + 1, tensor // 2, high, width), F32),
-        pltpu.VMEM((experts, tensor, high, width), BF16),
-        pltpu.VMEM((experts, tensor, high, width), BF16),
+        pltpu.VMEM((experts, tensor - 1, high, width), BF16),
+        pltpu.VMEM((experts, tensor - 1, high, width), BF16),
         pltpu.VMEM((experts, high, width), BF16),
-    ]
-    scratch += [dma((experts, tensor))] * 2 + [dma((experts,))] * 2
-    if multiply:
-        outs.append(jax.ShapeDtypeStruct(h.shape, BF16))
-        scratch += [dma((experts,))] * 2
+    ] + [dma((experts, tensor))] * 2 + [dma((experts,))] * 4
     if windows is not None:
         ins += windows
         here = windows[0].shape[0] // 3
         outs.append(jax.ShapeDtypeStruct((2, here, width), BF16))
+        outs.append(jax.ShapeDtypeStruct((experts, D // experts, f), BF16))
+        outs.append(jax.ShapeDtypeStruct((windows[4].shape[0] // 2, windows[4].shape[1]), BF16))
         scratch += [
             pltpu.VMEM((3, tensor // 2, here, width), F32),
-            pltpu.VMEM((3, tensor, here, width), BF16),
-            pltpu.VMEM((3, tensor, here, width), BF16),
+            pltpu.VMEM((3, tensor - 1, here, width), BF16),
+            pltpu.VMEM((3, tensor - 1, here, width), BF16),
             pltpu.VMEM((2, here, width), BF16),
             pltpu.VMEM((here, width), BF16),
-        ] + [dma((3, tensor))] * 2 + [dma((2,))] * 2
+            pltpu.VMEM((experts, D // experts, f), BF16),
+        ] + [dma((3, tensor))] * 2 + [dma((2,))] * 2 + [dma((experts,))] * 2 + [dma((2,))]
     return pl.pallas_call(
-        functools.partial(
-            scatter_kernel, experts, bits, windows is not None, near, multiply, len(products), gate is not None,
-            notes is not None),
+        functools.partial(scatter_kernel, experts, bits, windows is not None, near, gate is not None, notes is not None),
         out_shape=outs,
-        in_specs=[VMEM] * len(ins),
-        out_specs=[VMEM] * len(outs),
+        in_specs=[VMEM] * (len(ins) - 1) + [VMEM if windows is None else ANY],
+        out_specs=[VMEM] * (len(outs) - 1) + [VMEM if windows is None else ANY],
         scratch_shapes=scratch,
         compiler_params=pltpu.CompilerParams(
-            collective_id=collective_id, has_side_effects=True, vmem_limit_bytes=60 * 2**20),
+            collective_id=collective_id, has_side_effects=True, vmem_limit_bytes=63 * 2**20),
+        cost_estimate=pl.CostEstimate(flops=10**11, bytes_accessed=10**7, transcendentals=0),
     )(*ins)
+
+
+def ffn_kernel(experts, bits, pieces, *refs):
+    (x_cols, dy_cols, slots, others, routers, gate_in, up_in, down_in,
+     back, rows_out, dys_out, hidden_out, gate_out, up_out,
+     x, dy, land, gate_map, up_map, down_map, gate_pre, up_pre, hidden_grad, gates, pulls, low, sent, got, keep, y,
+     z_send, z_recv, t_send, t_recv, r_send, r_recv, y_send, y_recv, w_sem, o_sem) = refs
+    e, t = lax.axis_index("expert"), lax.axis_index("tensor")
+    tensor = 1 << bits
+    pairs = experts // 2
+    width = x.shape[1]
+    pair_rows = 2 * CAP
+    sources = (x, dy)
+    results = ((low.at[0], hidden_out), (low.at[1], gate_out), (low.at[2], up_out))
+
+    def first_block(u):
+        return ((e >> 1) ^ u) * 2
+
+    def block(j):
+        return pl.ds(pl.multiple_of(j * CAP, CAP), CAP)
+
+    def pair(j):
+        return pl.ds(pl.multiple_of(j * CAP, pair_rows), pair_rows)
+
+    def cols(d):
+        return pl.ds(pl.multiple_of((t ^ d) * width, 128), width)
+
+    def arrive(a, j):
+        return remote(sources[a].at[block(j // pieces)], land.at[a, block(e), cols(0)], z_send.at[a, j], z_recv.at[a, e],
+                      expert=j)
+
+    def arrived(a, j):
+        return remote(sources[a].at[block(j // pieces)], land.at[a, block(j), cols(0)], z_send.at[a, j], z_recv.at[a, j],
+                      expert=j)
+
+    def pass_on(a, j, d, b):
+        place, far = land.at[a, block(j), cols(d)], d | (1 << b)
+        return remote(place, place, t_send.at[a, j, far], t_recv.at[a, j, far], tensor=t ^ (1 << b))
+
+    def passed(a, j, d):
+        place = land.at[a, block(j), cols(d)]
+        return remote(place, place, t_send.at[a, j, d], t_recv.at[a, j, d], tensor=t ^ (1 << low_bit(d)))
+
+    def stage(j, k):
+        for q in range(2):
+            for a in range(2):
+                for d in range(1, tensor):
+                    if low_bit(d) == bits - k:
+                        passed(a, j + q, d).wait_recv()
+                        for b in reversed(range(bits - k)):
+                            pass_on(a, j + q, d, b).start()
+
+    def place_of(u, q):
+        return 2 * (u & 1) + q
+
+    def give(u, q, d):
+        j = first_block(u) + q
+        return remote(sent.at[place_of(u, q), d - 1], got.at[j, d - 1], r_send.at[place_of(u, q), d - 1],
+                      r_recv.at[j, d - 1], tensor=t ^ (1 << low_bit(d)))
+
+    def hand_back(j):
+        return remote(y.at[j], back.at[e], y_send.at[j], y_recv.at[e], expert=j)
+
+    def handed(j):
+        return remote(y.at[j], back.at[j], y_send.at[j], y_recv.at[j], expert=j)
+
+    def sum_stage(u, k):
+        j = first_block(u)
+        for q in range(2):
+            for d in range(tensor - 1, -1, -1):
+                if d % (1 << k) == 0:
+                    came = d | (1 << (k - 1))
+                    give(u, q, came).wait_recv()
+                    total = keep[q, d // 2] + got[j + q, came - 1].astype(F32)
+                    if k == bits:
+                        y[j + q] = total.astype(BF16)
+                    elif d & (1 << k):
+                        sent[place_of(u, q), d - 1] = total.astype(BF16)
+                        give(u, q, d).start()
+                    else:
+                        keep[q, d // 2] = total
+
+    def finish(u):
+        j = first_block(u)
+        for k in range(2, bits + 1):
+            sum_stage(u, k)
+        for q in range(2):
+            @pl.when(j + q == e)
+            def _():
+                back[e] = y[e]
+
+            @pl.when(j + q != e)
+            def _():
+                hand_back(j + q).start()
+
+    def to_memory(j):
+        copies = [pltpu.make_async_copy(land.at[a, pair(j)], out.at[pair(j)], o_sem.at[a])
+                  for a, out in enumerate((rows_out, dys_out))]
+        return copies
+
+    def results_to_memory(j):
+        return [pltpu.make_async_copy(source, out.at[pair(j)], o_sem.at[2 + i])
+                for i, (source, out) in enumerate(results)]
+
+    weights = [pltpu.make_async_copy(a, b, w_sem.at[i])
+               for i, (a, b) in enumerate(((gate_in, gate_map), (up_in, up_map), (down_in, down_map)))]
+    for copy in weights:
+        copy.start()
+    here = x_cols.shape[0]
+    place = lax.broadcasted_iota(jnp.int32, (x.shape[0], here), 0)
+    chosen = (place == slots[:, pl.ds(0, here)]) | (place == slots[:, pl.ds(here, here)])
+    chosen = chosen.astype(F32).astype(BF16)
+    x[...] = jnp.dot(chosen, x_cols[...], preferred_element_type=F32).astype(BF16)
+    dy[...] = jnp.dot(chosen, dy_cols[...], preferred_element_type=F32).astype(BF16)
+    meet(experts, bits)
+    for a in range(2):
+        arrive(a, e ^ 1).start()
+
+    def send_pair(u):
+        for q in range(2):
+            for a in range(2):
+                arrive(a, first_block(u) + q).start()
+
+    def forward_pair(u):
+        for q in range(2):
+            for a in range(2):
+                arrived(a, first_block(u) + q).wait_recv()
+                for b in reversed(range(bits)):
+                    pass_on(a, first_block(u) + q, 0, b).start()
+
+    send_pair(1)
+    if pairs > 2:
+        send_pair(2)
+    own = first_block(0)
+    for a in range(2):
+        land[a, block(e), cols(0)] = sources[a][block(e // pieces), :]
+        for b in reversed(range(bits)):
+            pass_on(a, e, 0, b).start()
+    foot = pl.ds(pair_rows, NOTES)
+    for d in range(tensor):
+        for q in range(4):
+            if d:
+                sent[q, d - 1, foot, :] = jnp.zeros((NOTES, width), BF16)
+        for q in range(2):
+            if d % 2 == 0:
+                keep[q, d // 2, foot, :] = jnp.zeros((NOTES, width), F32)
+    for a in range(2):
+        arrived(a, e ^ 1).wait_recv()
+        for b in reversed(range(bits)):
+            pass_on(a, e ^ 1, 0, b).start()
+    for k in range(1, bits):
+        stage(own, k)
+    forward_pair(1)
+    for copy in weights:
+        copy.wait()
+
+    @pl.loop(0, pairs)
+    def _(u):
+        j = first_block(u)
+        stage(j, bits)
+        for copy in to_memory(j):
+            copy.start()
+        rows = land[0, pair(j), :]
+        gate_pre[...] = jnp.dot(rows, gate_map[...], preferred_element_type=F32)
+        up_pre[...] = jnp.dot(rows, up_map[...], preferred_element_type=F32)
+        logits = jnp.dot(rows, routers[...], preferred_element_type=F32)
+        lane = lax.broadcasted_iota(jnp.int32, logits.shape, 1)
+        mine = jnp.sum(jnp.where(lane == EXPERTS + e // pieces, logits, 0.0), axis=1, keepdims=True)
+        other = others[pair(j), :] + EXPERTS
+        rival = jnp.sum(jnp.where(lane.astype(F32) == other, logits, 0.0), axis=1, keepdims=True)
+        top = jnp.maximum(mine, rival)
+        mine, rival = jnp.exp(mine - top), jnp.exp(rival - top)
+        gates[...] = mine / (mine + rival)
+
+        @pl.when(u < pairs - 1)
+        def _():
+            for k in range(1, bits):
+                stage(first_block(u + 1), k)
+
+        hidden_grad[...] = lax.dot_general(
+            land[1, pair(j), :], down_map[...], (((1,), (1,)), ((), ())), preferred_element_type=F32)
+
+        @pl.when(u > 0)
+        def _():
+            for copy in results_to_memory(j):
+                copy.wait()
+
+        @pl.loop(0, pair_rows // 16)
+        def _(r):
+            some = pl.ds(pl.multiple_of(r * 16, 16), 16)
+            gate_here, up_here = gate_pre[some, :], up_pre[some, :]
+            weight = gates[some, :]
+            sigma = 1.0 / (1.0 + jnp.exp(-gate_here))
+            silu = gate_here * sigma
+            hidden = silu * up_here
+            grad = hidden_grad[some, :]
+            pulls[some, :] = jnp.sum(hidden * grad, axis=1, keepdims=True)
+            grad = grad * weight
+            low[0, some, :] = (hidden * weight).astype(BF16)
+            low[1, some, :] = (grad * up_here * (sigma * (1.0 + gate_here * (1.0 - sigma)))).astype(BF16)
+            low[2, some, :] = (grad * silu).astype(BF16)
+
+        for copy in results_to_memory(j):
+            copy.start()
+
+        @pl.when(u < pairs - 2)
+        def _():
+            forward_pair(u + 2)
+
+            @pl.when(u < pairs - 3)
+            def _():
+                send_pair(u + 3)
+
+        @pl.when(u > 0)
+        def _():
+            finish(u - 1)
+
+        @pl.when(u > 1)
+        def _():
+            for q in range(2):
+                for d in range(1, tensor):
+                    give(u - 2, q, d).wait_send()
+
+        noted = []
+        for q in range(2):
+            some = pl.ds(q * CAP, CAP)
+            lane = lax.broadcasted_iota(jnp.int32, (CAP, 128), 1)
+            column = jnp.where(lane == 0, pulls[some, :], jnp.where(lane == 1, gates[some, :] / (tensor * pieces), 0.0))
+            column = jnp.concatenate([column, jnp.zeros((256 - CAP, 128), F32)], axis=0)
+            noted.append(column.T[:NOTES])
+        for d in range(tensor - 1, -1, -1):
+            grad = lax.dot_general(low[1], gate_map[cols(d), :], (((1,), (1,)), ((), ())), preferred_element_type=F32)
+            grad += lax.dot_general(low[2], up_map[cols(d), :], (((1,), (1,)), ((), ())), preferred_element_type=F32)
+            out = jnp.dot(low[0], down_map[:, cols(d)], preferred_element_type=F32)
+            for q in range(2):
+                part = pl.ds(q * CAP, CAP)
+                parts = [(pl.ds(0, CAP), slice(None), grad[q * CAP : (q + 1) * CAP]),
+                         (pl.ds(CAP, CAP), slice(None), out[q * CAP : (q + 1) * CAP]),
+                         (foot, pl.ds(0, 256), noted[q])]
+                for place, lanes, value in parts:
+                    if d & 1:
+                        sent[place_of(u, q), d - 1, place, lanes] = value.astype(BF16)
+                    else:
+                        keep[q, d // 2, place, lanes] = value
+                if d & 1:
+                    give(u, q, d).start()
+        sum_stage(u, 1)
+        for copy in to_memory(j):
+            copy.wait()
+
+    finish(pairs - 1)
+    for copy in results_to_memory(0):
+        copy.wait()
+    for u in range(max(pairs - 2, 0), pairs):
+        for q in range(2):
+            for d in range(1, tensor):
+                give(u, q, d).wait_send()
+
+    @pl.loop(1, experts)
+    def _(s):
+        j = e ^ s
+        for a in range(2):
+            arrived(a, j).wait_send()
+        handed(j).wait_recv()
+        handed(j).wait_send()
+
+    @pl.loop(0, experts)
+    def _(j):
+        for a in range(2):
+            for d in range(1, tensor):
+                passed(a, j, d).wait_send()
+
+
+def feed_forward(x, dy, slots, others, routers, gate_map, up_map, down_map, collective_id):
+    experts, tensor = lax.axis_size("expert"), lax.axis_size("tensor")
+    bits = tensor.bit_length() - 1
+    width, hidden = x.shape[1], gate_map.shape[1]
+    high = 2 * CAP + NOTES
+    count = experts * CAP
+    dma = pltpu.SemaphoreType.DMA
+    return pl.pallas_call(
+        functools.partial(ffn_kernel, experts, bits, experts // EXPERTS),
+        out_shape=[jax.ShapeDtypeStruct((experts, high, width), BF16)]
+        + [jax.ShapeDtypeStruct((count, D), BF16)] * 2 + [jax.ShapeDtypeStruct((count, hidden), BF16)] * 3,
+        in_specs=[VMEM] * 5 + [ANY] * 3,
+        out_specs=[VMEM] + [ANY] * 5,
+        scratch_shapes=[
+            pltpu.VMEM((SLOTS, width), BF16),
+            pltpu.VMEM((SLOTS, width), BF16),
+            pltpu.VMEM((2, count, D), BF16),
+            pltpu.VMEM((D, hidden), BF16),
+            pltpu.VMEM((D, hidden), BF16),
+            pltpu.VMEM((hidden, D), BF16),
+            pltpu.VMEM((2 * CAP, hidden), F32),
+            pltpu.VMEM((2 * CAP, hidden), F32),
+            pltpu.VMEM((2 * CAP, hidden), F32),
+            pltpu.VMEM((2 * CAP, 1), F32),
+            pltpu.VMEM((2 * CAP, 1), F32),
+            pltpu.VMEM((3, 2 * CAP, hidden), BF16),
+            pltpu.VMEM((4, tensor - 1, high, width), BF16),
+            pltpu.VMEM((experts, tensor - 1, high, width), BF16),
+            pltpu.VMEM((2, tensor // 2, high, width), F32),
+            pltpu.VMEM((experts, high, width), BF16),
+        ] + [dma((2, experts))] * 2 + [dma((2, experts, tensor))] * 2
+        + [dma((4, tensor - 1)), dma((experts, tensor - 1))] + [dma((experts,))] * 2 + [dma((3,)), dma((5,))],
+        compiler_params=pltpu.CompilerParams(
+            collective_id=collective_id, has_side_effects=True, vmem_limit_bytes=63 * 2**20),
+        cost_estimate=pl.CostEstimate(flops=10**11, bytes_accessed=10**7, transcendentals=0),
+    )(x, dy, slots, others, routers, gate_map, up_map, down_map)
+
+
+def share_kernel(me, left_ref, right_ref, out_ref):
+    out_ref[...] = lax.dot_general(
+        left_ref[...], right_ref[...], (((0,), (0,)), ((), ())), preferred_element_type=F32).astype(BF16)
+
+
+def share_products(left, right, expert_index, experts):
+    share, f = D // experts, right.shape[1]
+
+    def share_at(p, me):
+        distance, last = 0, experts // 2
+        for b in range(experts.bit_length() - 1):
+            distance += ((p >> b) & 1) * (last >> b)
+        return me[0] ^ distance
+
+    return pl.pallas_call(
+        share_kernel,
+        grid_spec=pltpu.PrefetchScalarGridSpec(
+            num_scalar_prefetch=1,
+            grid=(experts,),
+            in_specs=[
+                pl.BlockSpec((left.shape[0], share), lambda p, me: (0, share_at(p, me))),
+                pl.BlockSpec(right.shape, lambda p, me: (0, 0)),
+            ],
+            out_specs=pl.BlockSpec((share, f), lambda p, me: (p, 0)),
+        ),
+        out_shape=jax.ShapeDtypeStruct((D, f), BF16),
+        compiler_params=pltpu.CompilerParams(vmem_limit_bytes=32 * 2**20),
+        cost_estimate=pl.CostEstimate(flops=10**10, bytes_accessed=2 * 10**7, transcendentals=0),
+    )(expert_index[None], left, right)
+
+
+def small_kernel(experts, tensor, part, out, came, s_send, s_recv, b_send, b_recv):
+    e, t = lax.axis_index("expert"), lax.axis_index("tensor")
+    owners = experts // tensor
+    width = out.shape[1]
+    place = t * owners
+
+    def to_owner(c):
+        return remote(part.at[:, pl.ds(c * width, width)], came.at[e], s_send.at[c], s_recv.at[e], expert=place + c)
+
+    barrier = pltpu.get_barrier_semaphore()
+
+    @pl.loop(1, experts)
+    def _(s):
+        pl.semaphore_signal(barrier, inc=1, device_id={"expert": e ^ s}, device_id_type=MESH)
+
+    @pl.loop(1, tensor)
+    def _(s):
+        pl.semaphore_signal(barrier, inc=1, device_id={"tensor": t ^ s}, device_id_type=MESH)
+
+    pl.semaphore_wait(barrier, experts + tensor - 2)
+    for c in range(owners):
+        @pl.when(e != place + c)
+        def _():
+            to_owner(c).start()
+
+        @pl.when(e == place + c)
+        def _():
+            came[e] = part[:, c * width : (c + 1) * width]
+
+    @pl.when(e // owners == t)
+    def _():
+        @pl.loop(1, experts)
+        def _(s):
+            j = e ^ s
+            remote(came.at[j], came.at[j], s_send.at[0], s_recv.at[j], expert=j).wait_recv()
+
+        total = came[0]
+        for j in range(1, experts):
+            total += came[j]
+        out[...] = total
+
+        @pl.loop(1, tensor)
+        def _(s):
+            remote(out, out, b_send.at[s], b_recv, tensor=t ^ s).start()
+
+        @pl.loop(1, tensor)
+        def _(s):
+            remote(out, out, b_send.at[s], b_recv, tensor=t ^ s).wait_send()
+
+    @pl.when(e // owners != t)
+    def _():
+        remote(out, out, b_send.at[0], b_recv, tensor=e // owners).wait_recv()
+
+    for c in range(owners):
+        @pl.when(e != place + c)
+        def _():
+            to_owner(c).wait_send()
+
+
+def small_sums(part, collective_id):
+    experts, tensor = lax.axis_size("expert"), lax.axis_size("tensor")
+    n, width = part.shape[0], D // experts
+    dma = pltpu.SemaphoreType.DMA
+    return pl.pallas_call(
+        functools.partial(small_kernel, experts, tensor),
+        out_shape=jax.ShapeDtypeStruct((n, width), F32),
+        in_specs=[VMEM],
+        out_specs=VMEM,
+        scratch_shapes=[pltpu.VMEM((experts, n, width), F32), dma((experts // tensor,)), dma((experts,)), dma((tensor,)),
+                        dma],
+        compiler_params=pltpu.CompilerParams(collective_id=collective_id, has_side_effects=True),
+        cost_estimate=pl.CostEstimate(flops=10**10, bytes_accessed=10**5, transcendentals=0),
+    )(part)
 
 
 def dot(left, right, dims):
@@ -662,9 +1153,18 @@
     return flat * CAP + jnp.sum(earlier.astype(jnp.int32), axis=1)
 
 
-def place_matrix(slots, stride=CAP):
-    wide = slots + (slots // CAP) * (stride - CAP)
-    return (jnp.arange(EXPERTS * stride, dtype=jnp.int32)[:, None] == wide[None, :]).astype(BF16)
+def spaced(slots, stride):
+    return slots + (slots // CAP) * (stride - CAP)
+
+
+def place_matrix(slots):
+    return (jnp.arange(SLOTS, dtype=jnp.int32)[:, None] == slots[None, :]).astype(BF16)
+
+
+def token_matrix(slots, stride=CAP, first=0):
+    wide = (spaced(slots, stride) + first).reshape(TOPK, -1)
+    place = jnp.arange(EXPERTS * stride, dtype=jnp.int32)[:, None]
+    return ((place == wide[0][None, :]) | (place == wide[1][None, :])).astype(BF16)
 
 
 def to_pieces(rows, pieces):
@@ -683,15 +1183,6 @@
 
 def for_pieces(rows, pieces):
     return jnp.repeat(rows, pieces, axis=0) if pieces > 1 else rows
-
-
-def own_gate(logits, own, other):
-    places = jnp.arange(EXPERTS, dtype=F32)[None, :]
-    mine = jnp.sum(jnp.where(places == own, logits, 0.0), axis=1)
-    rival = jnp.sum(jnp.where(places == other[:, None], logits, 0.0), axis=1)
-    top = jnp.maximum(mine, rival)
-    mine, rival = jnp.exp(mine - top), jnp.exp(rival - top)
-    return (mine / (mine + rival))[:, None]
 
 
 def pick_gates(logits, routes):
@@ -880,18 +1371,11 @@
     def group_tokens(token_cols, places):
         return for_pieces(mm(places, token_cols).astype(BF16).reshape(EXPERTS, CAP, -1), pieces)
 
-    def tokens_to_experts(token_cols, places):
-        return columns_together(swap(group_tokens(token_cols, places)).reshape(-1, column_count))
-
     def group_choices(choice_rows, places):
         return to_pieces(mm(places, choice_rows).astype(BF16).reshape(EXPERTS, CAP, -1), pieces)
 
     def choices_of(back, places):
         return mm_tn(places, from_pieces(back, pieces).reshape(SLOTS, -1)).astype(BF16)
-
-    def sums_from_experts(part_rows, places):
-        back = swap(columns_summed(part_rows.astype(BF16)).reshape(expert_count, CAP, column_count))
-        return sums_of(back, places)
 
     def sums_of(back, places):
         stride = back.shape[1]
@@ -906,10 +1390,13 @@
         rows = jnp.stack([v.reshape(expert_count, CAP) for v in scalars], axis=1)
         return jnp.pad(rows, ((0, 0), (0, NOTES - len(scalars)), (0, column_count - CAP)))
 
-    def read_notes(back, places, count):
-        noted = back[:, CAP : CAP + count, :CAP].astype(F32)
+    def read_notes(back, places, count, first=CAP):
+        noted = back[:, first : first + count, :CAP].astype(F32)
         noted = noted.reshape(EXPERTS, pieces, count, CAP).sum(1).transpose(0, 2, 1).reshape(SLOTS, count)
         return mm_tn(places, noted.astype(BF16)).reshape(TOPK, rows_here, count)
+
+    def exchange(away, b):
+        return lax.ppermute(away, "expert", [(i, i ^ (1 << b)) for i in range(expert_count)])
 
     state_in = tokens.astype(F32)
     gain_one = attn_gain.astype(F32)
@@ -918,26 +1405,17 @@
     dy_cols = cols(cotangent)
     token_cols = cols(tokens).astype(F32)
 
-    def by_token(choices):
-        return choices[:, :rows_here] + choices[:, rows_here:]
-
     attn_slots, ffn_slots = slot_numbers(attn_routes), slot_numbers(ffn_routes)
     attn_places, ffn_places = place_matrix(attn_slots), place_matrix(ffn_slots)
-    attn_tokens, ffn_tokens = by_token(attn_places), by_token(ffn_places)
-    attn_noted = by_token(place_matrix(attn_slots, CAP + NOTES))
-    ffn_noted = by_token(place_matrix(ffn_slots, CAP + NOTES))
-    others = jnp.stack([
-        mm(attn_places, attn_routes[:, ::-1].T.reshape(-1, 1).astype(BF16)),
-        mm(ffn_places, ffn_routes[:, ::-1].T.reshape(-1, 1).astype(BF16)),
-    ]).reshape(2, EXPERTS, CAP).transpose(1, 0, 2)
-
-
-    rows_one, query_rows, query_map, window, pair_map, keys, values = front(
-        tokens, gain_one[None], attn_slots[None], to_pieces(query_weight, pieces), key_value_weight, collective_id=0)
-    output_weight, others, rows_one = lax.optimization_barrier((output_weight, others, rows_one))
+
+
+    wide_slots = jnp.stack([spaced(attn_slots, 256), spaced(ffn_slots, 256)], axis=1)
+    rows_one, query_rows, query_map, window, pair_map, keys, values, attn_gate_blocks, rivals = front(
+        tokens, gain_one[None], attn_slots[None], wide_slots, jnp.concatenate([attn_routes, ffn_routes], axis=1), routers,
+        to_pieces(query_weight, pieces), key_value_weight, collective_id=0)
+    output_weight, keys = lax.optimization_barrier((output_weight, keys))
     rows_one = rows_one.reshape(-1, D)
     output_map = swap(to_pieces(output_weight, pieces)).reshape(D, -1)
-    others = swap(for_pieces(others, pieces)).transpose(1, 0, 2).reshape(2, -1)
     normed_one = window[2]
     window = window.reshape(-1, D)
     padded_segments = jnp.concatenate([jnp.full((WINDOW,), -1, jnp.int32), segment_ids])
@@ -946,38 +1424,19 @@
     key_ids = key_ids[:, None]
     heads, queries, log_total = attend(
         attn_slots[None], from_pieces(query_rows, pieces).reshape(SLOTS, -1), keys, values, query_ids, key_ids)
-    attn_gate_rows = own_gate(mm(rows_one, routers_one), own, others[0])
-    attn_gate_blocks = attn_gate_rows.reshape(expert_count, CAP, 1)
     attn_back, heads_rows = scatter_rows(
         to_pieces(heads.reshape(EXPERTS, CAP, -1), pieces), output_map, attn_gate_blocks, collective_id=1)
     heads_rows = heads_rows.reshape(expert_count * CAP, -1)
-    dy_cols, attn_back = lax.optimization_barrier((dy_cols, attn_back))
-    state = token_cols + sums_of(attn_back, attn_tokens)
+    state = token_cols + sums_of(attn_back, token_matrix(attn_slots))
 
     mean_two = lax.psum(jnp.sum(state * state, axis=1, keepdims=True), "tensor") / D
     rate_two = lax.rsqrt(mean_two + eps)
     normed_two = (state * rate_two * gain_two).astype(BF16)
-    rows_dy = tokens_to_experts(dy_cols, ffn_tokens)
-    (rows_two,) = gather_rows(group_tokens(normed_two, ffn_tokens), collective_id=2)
-    rows_two = rows_two.reshape(-1, D)
     gate_map, up_map, down_map = gate_weight[0], up_weight[0], down_weight[0]
-    ffn_gate_rows = own_gate(mm(rows_two, routers_two), own, others[1])
-    hidden_grad = mm_nt(rows_dy, down_map)
-    gate_pre = mm(rows_two, gate_map)
-    up_pre = mm(rows_two, up_map)
-    sigma = 1.0 / (1.0 + jnp.exp(-gate_pre))
-    silu = gate_pre * sigma
-    hidden = (silu * up_pre).astype(BF16)
-    scaled_grad = hidden_grad * ffn_gate_rows
-    gate_low = (scaled_grad * up_pre * (sigma * (1.0 + gate_pre * (1.0 - sigma)))).astype(BF16)
-    up_low = (scaled_grad * silu).astype(BF16)
-    ffn_notes = notes_of(
-        jnp.sum(hidden.astype(F32) * hidden_grad, axis=1), ffn_gate_rows[:, 0] / (tensor_count * pieces))
-    (rows_back,) = scatter_rows(
-        products=[(gate_low.reshape(expert_count, CAP, -1), gate_map), (up_low.reshape(expert_count, CAP, -1), up_map)],
-        notes=ffn_notes, near=False, collective_id=3)
-    normed_two_grad = sums_of(rows_back, ffn_noted)
-    noted = read_notes(rows_back, ffn_places, 2)
+    ffn_back, rows_two, rows_dy, hidden, gate_low, up_low = feed_forward(
+        normed_two, dy_cols, ffn_slots[None], rivals.reshape(-1, 1), routers, gate_map, up_map, down_map, collective_id=2)
+    normed_two_grad = sums_of(ffn_back, token_matrix(ffn_slots, 2 * CAP + NOTES))
+    noted = read_notes(ffn_back, ffn_places, 2, 2 * CAP)
     ffn_pull, ffn_gates = noted[:, :, 0].T, noted[:, :, 1].T
     ffn_logit_grad = gate_back(ffn_gates, ffn_pull, ffn_routes)
     normed_two_grad = normed_two_grad + mm_nt(
@@ -989,28 +1448,27 @@
     state_grad = dy_cols.astype(F32) + rate_two * ahead - state * rate_two * rate_two * rate_two * centre
 
     rows_state, heads_grad, heads_grad_rows = gather_rows(
-        group_tokens(state_grad.astype(BF16), attn_tokens), output_map, gate=attn_gate_blocks, collective_id=4)
+        group_tokens(state_grad.astype(BF16), token_matrix(attn_slots)), output_map, gate=attn_gate_blocks, collective_id=4)
     rows_state = rows_state.reshape(-1, D)
     heads_grad_rows = heads_grad_rows.reshape(expert_count * CAP, -1)
     attn_notes = notes_of(jnp.sum(heads_grad_rows.astype(F32) * heads_rows.astype(F32), axis=1))
-    output_part = mm_tn((rows_state.astype(F32) * attn_gate_rows).astype(BF16), heads_rows).astype(BF16)
+    output_part = mm_tn((rows_state.astype(F32) * attn_gate_blocks.reshape(-1, 1)).astype(BF16), heads_rows).astype(BF16)
     heads_grad, output_part = lax.optimization_barrier((heads_grad, output_part))
 
     query_back, key_back, value_back = attend_back(
         attn_slots[None], from_pieces(heads_grad, pieces).reshape(SLOTS, -1), queries, keys, values, log_total,
         query_ids, key_ids)
     output_grad = swap(output_part.reshape(expert_count, D // expert_count, -1))
+    pair_part = share_products(window, jnp.concatenate([key_back, value_back], axis=1), expert_index, expert_count)
     query_back, output_grad = lax.optimization_barrier((query_back, output_grad))
     output_grad = from_pieces(output_grad, pieces).astype(F32)
-    normed_back, query_grad_rows, owed = scatter_rows(
+    normed_back, unused_rows, owed, query_grad, pair_came = scatter_rows(
         to_pieces(query_back.reshape(EXPERTS, CAP, -1), pieces), query_map, notes=attn_notes,
-        windows=[key_back, value_back, pair_map], collective_id=5)
-    query_grad_rows = query_grad_rows.reshape(expert_count * CAP, -1)
-    query_part = mm_tn(rows_one, query_grad_rows)
-    normed_grad = sums_of(normed_back, attn_noted) + jnp.sum(owed.astype(F32), axis=0)
+        windows=[key_back, value_back, pair_map, rows_one, pair_part], collective_id=5)
+    query_grad = from_pieces(query_grad, pieces).astype(F32)
+    normed_grad = sums_of(normed_back, token_matrix(attn_slots, CAP + NOTES)) + jnp.sum(owed.astype(F32), axis=0)
+    rows_two, rows_dy, normed_back = lax.optimization_barrier((rows_two, rows_dy, normed_back))
     attn_pull = read_notes(normed_back, attn_places, 1)[:, :, 0].T
-    pair_grad = jnp.stack([key_back, value_back])
-    pair_part = jnp.einsum("td,ctf->cdf", window, pair_grad, preferred_element_type=F32)
     attn_gates = pick_gates(mm(normed_one, routers_one), attn_routes)
     attn_logit_grad = gate_back(attn_gates, attn_pull, attn_routes)
     normed_grad = normed_grad + mm_nt(
@@ -1023,24 +1481,24 @@
     tokens_grad = state_grad + rate_one * ahead_one - token_cols * rate_one * rate_one * rate_one * centre_one
     tokens_grad = columns_together(tokens_grad.astype(BF16)).astype(F32)
 
-    def from_maps(part):
-        got = swap(part.astype(BF16).reshape(expert_count, D // expert_count, -1))
-        return from_pieces(got, pieces).astype(F32)
-
-    query_grad = from_maps(query_part)
-    key_value_grad = lax.psum_scatter(
-        pair_part.astype(BF16), "expert", scatter_dimension=1, tiled=True).astype(F32)
     small = jnp.concatenate(
-        [attn_router_cols, ffn_router_cols, attn_gain_cols[:, None], ffn_gain_cols[:, None]], axis=1)
-    small = lax.all_gather(small, "tensor", axis=0, tiled=True)
-    small = lax.psum_scatter(small, "expert", scatter_dimension=0, tiled=True)
-
-    scaled_dy = (rows_dy.astype(F32) * ffn_gate_rows).astype(BF16)
+        [attn_router_cols.T, ffn_router_cols.T, attn_gain_cols[None], ffn_gain_cols[None],
+         jnp.zeros((6, column_count), F32)], axis=0)
+    small = small_sums(small, collective_id=3)
+    small, pair_came = lax.optimization_barrier((small, pair_came))
+    small = small.T
+    for b in range(1, expert_count.bit_length()):
+        pair_part = pair_part[: pair_came.shape[0]].astype(F32) + pair_came.astype(F32)
+        if b < expert_count.bit_length() - 1:
+            pair_part = pair_part.astype(BF16)
+            pair_came = exchange(pair_part[pair_part.shape[0] // 2 :], b)
+    key_value_grad = pair_part.reshape(D // expert_count, 2, -1).transpose(1, 0, 2)
+
     gate_grad = mm_tn(rows_two, gate_low)
     up_grad = mm_tn(rows_two, up_low)
-    down_grad = mm_tn(hidden, scaled_dy)
-    ffn_back = sums_from_experts(mm(hidden, down_map) * ffn_gate_rows, ffn_tokens)
-    mixed = (state + ffn_back).astype(BF16)
+    down_grad = mm_tn(hidden, rows_dy)
+    ffn_out = sums_of(ffn_back, token_matrix(ffn_slots, 2 * CAP + NOTES, CAP))
+    mixed = (state + ffn_out).astype(BF16)
     return (
         mixed,
         tokens_grad,

time: 1040 us -> 887 us (0.85)
  waiting for transfers between devices: 151 us -> 11.1 us
  Pallas kernels: 562 us -> 684 us
  matrix products: 161 us -> 67.1 us
  blocking collectives: 37.7 us -> 17.1 us
  starting transfers between devices: 40 us -> 20.3 us
  local copies, waits for them, and re-layouts: 35.9 us -> 24.8 us
    pallas_call x0 -> x3, Pallas kernels: none -> 199 us  [the longest x1 175 us: feed_forward(): pl.pallas_call(functools.partial(ffn_kernel, experts, bits, experts // EX...]
    dot_general x27 -> x16, matrix products: 149 us -> 67.1 us  [dot(): lax.dot_general(left, right, ((dims[0], dims[1]), ((), ())), preferred_el...]
    reduce_scatter x3 -> x0, waiting for transfers between devices: 81.5 us -> none  [the longest x1 81.5 us: per_device(): lax.psum_scatter(pair_part.astype(BF16), 'expert', scatter_dimension=1, t...]
    all_to_all x5 -> x2, waiting for transfers between devices: 69.4 us -> 6.37 us  [swap(): lax.all_to_all(blocks, 'expert', split_axis=0, concat_axis=0, tiled=True)]
    pallas_call x3 -> x2, Pallas kernels: 250 us -> 203 us  [scatter_rows(): pl.pallas_call(functools.partial(scatter_kernel, experts, bits, windows i...]
    pallas_call x2 -> x1, Pallas kernels: 109 us -> 77.3 us  [gather_rows(): pl.pallas_call(functools.partial(gather_kernel, experts, bits, near, mult...]
    all_to_all x5 -> x2, starting transfers between devices: 39.6 us -> 17.5 us  [swap(): lax.all_to_all(blocks, 'expert', split_axis=0, concat_axis=0, tiled=True)]
    all_to_all x1 -> x0, blocking collectives: 13.9 us -> none  [swap(): lax.all_to_all(blocks, 'expert', split_axis=0, concat_axis=0, tiled=True)]
  transfers between devices with their start and end apart: 10 -> 5, of which waited for: 5 -> 3; matrix products, arithmetic and copies ran while one was open for 17% -> 9% of each run, Pallas kernels for 34% -> 9%
where the time goes in v3:
time: 887 us; the launch traced here: 878 us
  Pallas kernels  684 us (77%)
  matrix products  67.1 us (8%)
  other arithmetic  38.1 us (4%)
  local copies, waits for them, and re-layouts  24.8 us (3%)
  starting transfers between devices  20.3 us (2%)
  blocking collectives  17.1 us (2%)
  between operations  15.1 us (2%)
  waiting for transfers between devices  11.1 us (1%)
    pallas_call x2, Pallas kernels, scatter_rows(): pl.pallas_call(functools.partial(scatter_kernel, experts, bits, windows i...  203 us
    pallas_call x1, Pallas kernels, feed_forward(): pl.pallas_call(functools.partial(ffn_kernel, experts, bits, experts // EX...  175 us
    pallas_call x1, Pallas kernels, front(): pl.pallas_call(functools.partial(front_kernel, experts, bits), out_shape=...  153 us
    pallas_call x1, Pallas kernels, gather_rows(): pl.pallas_call(functools.partial(gather_kernel, experts, bits, near, mult...  77.3 us
    dot_general x16, matrix products, dot(): lax.dot_general(left, right, ((dims[0], dims[1]), ((), ())), preferred_el...  67.1 us
    pallas_call x1, Pallas kernels, attend_back(): pl.pallas_call(attend_back_kernel, grid=(width // HD,), out_shape=[jax.Sh...  27.9 us
    pallas_call x1, Pallas kernels, attend(): pl.pallas_call(attend_kernel, grid=(width // HD,), out_shape=[jax.ShapeDt...  23.1 us
  transfers between devices with their start and end apart: 5, of which 3 were waited for; matrix products, arithmetic and copies ran while one was open for 9% of the time, Pallas kernels for 9%

profile of v3, /device:TPU:0, one launch (start us, length us, event | category | flops | bytes accessed | tf_op | source)
XLA Modules:
  0.0 877.7 jit_solution(6142037641752291212)
XLA Ops:
  7.2 0.7 fusion.63
  8.6 0.7 pad_add_fusion.1
  9.3 0.7 copy.83
  10.5 1.3 convert_element_type.131
  13.1 1.0 copy.68.refs_3_
  14.1 0.9 copy.69.refs_4_
  15.0 1.8 copy.70.refs_5_.refs_4_
  17.4 153.2 %shard_map.221 = (bf16[8,160,2048]{2,1,0:T(8,128)(2,1)}, bf16[8,160,512]{2,1,0:T(8,128)(2,1)}, bf16[2048,512]{1,0:T(8,128)(2,1)}, bf16[3,512,2048]{2,1,0:T(8,128...) custom-call(bf16[512,2048]{1,0:T(8,128)(2,1)} %refs_0_.1, ...), custom_call_target="tpu_custom_call" | custom-call | flops 99999997952 | bytes 10000000 | tf_op jit(solution)/shard_map/pallas_call | solution.py:425
  170.6 8.1 all-to-all-start
  180.1 2.2 fusion.18
  183.5 0.8 dynamic-slice_convert_fusion
  185.0 3.2 slice.95
  189.0 0.9 reduce.1
  189.9 2.0 constant_dynamic-slice_fusion.refs_1_
  193.2 1.9 iota_compare_fusion.6
  195.1 1.9 iota_compare_fusion.7
  196.9 23.1 %shard_map.222 = (bf16[1280,512]{1,0:T(8,128)(2,1)S(1)}, bf16[1024,512]{1,0:T(8,128)(2,1)S(1)}, f32[4,1,1024]{2,1,0:T(1,128)S(1)}) custom-call(s32[1,1024]{1,0:T(1,128)S(1)} %copy-done.4, bf16[1280,512]{1,0:T(8,128)(2,1)S(1)} %bitcast.140, bf16[1536,512]{1,0:T(8,128)(2,1)S(1)} %copy-done.9, bf16[1536,512]{1,0:T(8,128)(2,1)} %get-tuple-element.55.value_ref, ...), custom_call_target="tpu_custom_call" | custom-call | flops 16000000000 | bytes 10000000 | tf_op jit(solution)/shard_map/pallas_call | solution.py:1256
  220.0 1.0 copy-done.8
  221.1 1.0 copy-done.10
  222.7 5.4 all-to-all-done
  228.1 58.9 %shard_map.223 = (bf16[8,160,512]{2,1,0:T(8,128)(2,1)}, bf16[8,160,512]{2,1,0:T(8,128)(2,1)}) custom-call(bf16[8,160,512]{2,1,0:T(8,128)(2,1)} %bitcast.142, bf16[2048,512]{1,0:T(8,128)(2,1)} %bitcast.9.refs_1_, f32[8,160,1]{2,1,0:T(8,128)} %get-tuple-element.58.refs_2_), custom_call_target="tpu_custom_call" | custom-call | flops 99999997952 | bytes 10000000 | tf_op jit(solution)/shard_map/pallas_call | solution.py:694
  287.1 2.4 multiply_reduce_fusion.4
  289.5 5.7 psum.21
  295.2 1.0 multiply_convert_fusion.4.refs_0_
  296.2 174.8 %shard_map.224 = (bf16[8,336,512]{2,1,0:T(8,128)(2,1)}, bf16[1280,2048]{1,0:T(8,128)(2,1)}, bf16[1280,2048]{1,0:T(8,128)(2,1)}, bf16[1280,1408]{1,0:T(8,128)(2,1...) custom-call(bf16[512,512]{1,0:T(8,128)(2,1)} %multiply_convert_fusion.4.refs_0_, ...), custom_call_target="tpu_custom_call" | custom-call | flops 99999997952 | bytes 10000000 | tf_op jit(solution)/shard_map/pallas_call | solution.py:984
  471.0 0.8 slice_bitcast_fusion
  471.9 2.1 fusion.87
  474.1 0.8 fusion.89
  474.9 3.6 fusion.4
  478.5 1.8 multiply_reduce_fusion.2
  480.3 5.7 psum.22
  486.1 1.1 convolution_convert_fusion
  487.2 77.3 %shard_map.225 = (bf16[8,160,2048]{2,1,0:T(8,128)(2,1)}, bf16[8,160,512]{2,1,0:T(8,128)(2,1)S(1)}, bf16[8,160,512]{2,1,0:T(8,128)(2,1)S(1)}) custom-call(bf16[8,160,512]{2,1,0:T(8,128)(2,1)S(1)} %bitcast.143, bf16[2048,512]{1,0:T(8,128)(2,1)} %bitcast.9.refs_1_, f32[8,160,1]{2,1,0:T(8,128)S(1)} %copy-done.3), custom_call_target="tpu_custom_call" | custom-call | flops 99999997952 | bytes 10000000 | tf_op jit(solution)/shard_map/pallas_call | solution.py:186
  564.6 8.1 bitcast_convert_fusion
  572.6 9.4 %all-to-all-start.1 = ((bf16[8,256,512]{2,1,0:T(8,128)(2,1)}), bf16[8,256,512]{2,1,0:T(8,128)(2,1)}, u32[]{:S(2)}, u32[]{:S(2)}) async-start(bf16[8,256,512]{2,1,0:T(8,128)(2,1)} %bitcast.147), calls=%async_computation.1 | async-start | bytes 4194304 | tf_op jit(solution)/shard_map/all_to_all | solution.py:1138
  582.1 1.7 multiply_reduce_fusion.1
  583.8 0.7 pad.5.refs_2_
  584.6 27.9 %shard_map.226 = (bf16[1280,512]{1,0:T(8,128)(2,1)}, bf16[1536,512]{1,0:T(8,128)(2,1)}, bf16[1536,512]{1,0:T(8,128)(2,1)}) custom-call(s32[1,1024]{1,0:T(1,128)} %add.155.refs_2_.slots_ref, bf16[1280,512]{1,0:T(8,128)(2,1)} %bitcast.141, bf16[1024,512]{1,0:T(8,128)(2,1)} %copy-done.10, bf16[1536,512]{1,0:T(8,128)(2,1)} %get-tuple-element.54.key_ref, ...), custom_call_target="tpu_custom_call" | custom-call | flops 30000001024 | bytes 10000000 | tf_op jit(solution)/shard_map/pallas_call | solution.py:1318
  612.5 2.5 pad_maximum_fusion.right_ref
  615.0 2.5 fusion.37
  617.5 9.1 %shard_map.227.refs_7_ = bf16[2048,1024]{1,0:T(8,128)(2,1)S(1)} custom-call(s32[1]{0:T(128)} %bitcast.33.me, bf16[1536,2048]{1,0:T(8,128)(2,1)S(1)} %bitcast.137, bf16[1536,1024]{1,0:T(8,128)(2,1)S(1)} %pad_maximum_fusion.right_ref), custom_call_target="tpu_custom_call" | custom-call | flops 10000000000 | bytes 20000000 | tf_op jit(solution)/shard_map/pallas_call | solution.py:1029
  626.6 2.0 copy-done
  628.6 0.9 all-to-all-done.1
  629.6 144.3 %shard_map.228 = (bf16[8,176,512]{2,1,0:T(8,128)(2,1)}, bf16[8,160,512]{2,1,0:T(8,128)(2,1)}, bf16[2,512,512]{2,1,0:T(8,128)(2,1)}, bf16[8,256,512]{2,1,0:T(8,128)(2,1)}, bf16[1024,1024]{1,0:T(8,128)(2,1)}) custom-call(bf16[8,160,512]{2,1,0:T(8,128)(2,1)} %bitcast.187, bf16[2048,512]{1,0:T(8,128)(2,1)} %get-tuple-element.71.refs_1_, ...), custom_call_target="tpu_custom_call" | custom-call | flops 99999997952 | bytes 10000000 | tf_op jit(solution)/shard_map/pallas_call | solution.py:694
  774.0 2.5 convert_reduce_fusion.2
  776.5 0.8 slice_reduce_fusion
  777.4 0.8 fusion.88
  778.4 2.8 fusion.27
  781.3 2.3 fusion.47
  783.5 5.7 psum.23
  789.3 3.2 fusion.44
  792.5 1.2 fusion.48
  793.8 1.8 concatenate.15.part
  795.6 15.4 %shard_map.229 = f32[24,256]{1,0:T(8,128)} custom-call(f32[24,512]{1,0:T(8,128)} %concatenate.15.part), custom_call_target="tpu_custom_call" | custom-call | flops 10000000000 | bytes 100000 | tf_op jit(solution)/shard_map/pallas_call | solution.py:1109
  811.0 2.7 add_convert_fusion
  814.0 13.4 %convolution_bitcast_fusion.2 = f32[1,2048,1408]{2,1,0:T(8,128)} fusion(bf16[1280,2048]{1,0:T(8,128)(2,1)} %get-tuple-element.88, bf16[1280,1408]{1,0:T(8,128)(2,1)S(1)} %copy-done.56), kind=kOutput, calls=%fused_computation.3 | convolution fusion | flops 7381975040 | bytes 20381696 | tf_op jit(solution)/shard_map/dot_general | solution.py:1122
  827.4 11.3 %convolution_bitcast_fusion.1 = f32[1,2048,1408]{2,1,0:T(8,128)} fusion(bf16[1280,2048]{1,0:T(8,128)(2,1)S(1)} %bitcast.193, bf16[1280,1408]{1,0:T(8,128)(2,1)S(1)} %copy-done.55), kind=kOutput, calls=%fused_computation.2 | convolution fusion | flops 7381975040 | bytes 20381696 | tf_op jit(solution)/shard_map/dot_general | solution.py:1122
  839.2 2.7 collective-permute-start.1
  841.9 10.7 %convolution_bitcast_fusion = f32[1,1408,2048]{2,1,0:T(8,128)} fusion(bf16[1280,1408]{1,0:T(8,128)(2,1)S(1)} %copy-done.54, bf16[1280,2048]{1,0:T(8,128)(2,1)S(1)} %bitcast.191), kind=kOutput, calls=%fused_computation.1 | convolution fusion | flops 7381975040 | bytes 20381696 | tf_op jit(solution)/shard_map/dot_general | solution.py:1122
  853.2 2.6 convert_element_type.153
  855.8 4.2 convert_element_type.154
  860.5 4.8 collective-permute-done.1
  865.4 1.1 copy.99
  866.5 4.1 convert_element_type.152
  (176 shorter events, 11.5 us)
Async XLA Ops:
  170.6 8.2 copy-start.16
  170.6 8.7 copy-start.28
  170.6 9.4 %copy-start.24 = (bf16[2048,16]{0,1:T(8,128)(2,1)S(1)}, bf16[2048,16]{0,1:T(8,128)(2,1)}, u32[]{:S(2)}) copy-start(bf16[2048,16]{0,1:T(8,128)(2,1)} %param.20) | copy-start | bytes 196612
  170.6 57.5 %all-to-all-start = ((bf16[8,256,512]{2,1,0:T(8,128)(2,1)}), bf16[8,256,512]{2,1,0:T(8,128)(2,1)}, u32[]{:S(2)}, u32[]{:S(2)}) async-start(bf16[8,256,512]{2,1,0:T(8,128)(2,1)} %param.22), calls=%async_computation | async-start | bytes 4194304 | tf_op jit(solution)/shard_map/all_to_all | solution.py:1138
  178.8 3.5 copy-start.25
  178.8 5.5 copy-start.41
  179.5 17.4 %copy-start.5 = (s32[512]{0:T(512)}, s32[512]{0:T(512)S(1)}, u32[]{:S(2)}) copy-start(s32[512]{0:T(512)S(1)} %pad_dynamic-slice_fusion) | copy-start | bytes 6148
  182.3 6.7 copy-start.2
  182.4 2.6 copy-start.30
  182.4 2.6 copy-start.38
  184.3 301.7 %copy-start.32 = (f32[512]{0:T(512)}, f32[512]{0:T(512)S(1)}, u32[]{:S(2)}) copy-start(f32[512]{0:T(512)S(1)} %dynamic-slice_convert_fusion) | copy-start | bytes 6148
  188.1 8.8 %copy-start.4 = (s32[1,1024]{1,0:T(1,128)S(1)}, s32[1,1024]{1,0:T(1,128)}, u32[]{:S(2)}) copy-start(s32[1,1024]{1,0:T(1,128)} %add.155.refs_2_.slots_ref) | copy-start | bytes 12292
  188.1 8.8 %copy-start.6 = (bf16[8,160,512]{2,1,0:T(8,128)(2,1)S(1)}, bf16[8,160,512]{2,1,0:T(8,128)(2,1)}, u32[]{:S(2)}) copy-start(bf16[8,160,512]{2,1,0:T(8,128)(2,1)} %get-tuple-element.52) | copy-start | bytes 3932164
  188.4 31.6 %copy-start.1 = (s32[1536,1]{1,0:T(8,128)}, s32[1536,1]{1,0:T(8,128)S(1)}, u32[]{:S(2)}) copy-start(s32[1536,1]{1,0:T(8,128)S(1)} %broadcast_in_dim.39.key_ids) | copy-start | bytes 18436
  189.9 7.0 copy-start.9
  289.5 5.7 copy-start.12
  295.2 190.9 %copy-start.34 = (f32[512,1]{0,1:T(1,128)}, f32[512,1]{0,1:T(1,128)S(1)}, u32[]{:S(2)}) copy-start(f32[512,1]{0,1:T(1,128)S(1)} %add_rsqrt_fusion.1) | copy-start | bytes 6148
  296.1 177.9 %copy-start.29 = (s32[512,2]{0,1:T(2,128)S(1)}, s32[512,2]{0,1:T(2,128)}, u32[]{:S(2)}) copy-start(s32[512,2]{0,1:T(2,128)} %param.17) | copy-start | bytes 12292
  296.2 177.9 %copy-start.21 = (bf16[512,512]{1,0:T(8,128)(2,1)S(1)}, bf16[512,512]{1,0:T(8,128)(2,1)}, u32[]{:S(2)}) copy-start(bf16[512,512]{1,0:T(8,128)(2,1)} %multiply_convert_fusion.4.refs_0_) | copy-start | bytes 1572868
  296.2 178.7 %copy-start.51 = (s32[512]{0:T(512)S(1)}, s32[512]{0:T(512)}, u32[]{:S(2)}) copy-start(s32[512]{0:T(512)} %get-tuple-element.112) | copy-start | bytes 6148
  296.2 178.7 %copy-start.52 = (s32[512]{0:T(512)S(1)}, s32[512]{0:T(512)}, u32[]{:S(2)}) copy-start(s32[512]{0:T(512)} %get-tuple-element.113) | copy-start | bytes 6148
  474.9 3.6 copy-start.13
  478.4 7.6 copy-start.23
  480.3 6.9 copy-start.18
  486.0 1.2 copy-start.43
  487.2 77.4 %copy-start.22 = (bf16[8,160,512]{2,1,0:T(8,128)(2,1)S(1)}, bf16[8,160,512]{2,1,0:T(8,128)(2,1)}, u32[]{:S(2)}) copy-start(bf16[8,160,512]{2,1,0:T(8,128)(2,1)} %get-tuple-element.64) | copy-start | bytes 3932164
  487.2 77.4 %copy-start.42 = (f32[8,160]{1,0:T(8,128)S(1)}, f32[8,160]{1,0:T(8,128)}, u32[]{:S(2)}) copy-start(f32[8,160]{1,0:T(8,128)} %reduce.1) | copy-start | bytes 15364
  564.6 8.1 copy-start.7
  572.6 56.9 %all-to-all-start.1 = ((bf16[8,256,512]{2,1,0:T(8,128)(2,1)}), bf16[8,256,512]{2,1,0:T(8,128)(2,1)}, u32[]{:S(2)}, u32[]{:S(2)}) async-start(bf16[8,256,512]{2,1,0:T(8,128)(2,1)} %bitcast.147), calls=%async_computation.1 | async-start | bytes 4194304 | tf_op jit(solution)/shard_map/all_to_all | solution.py:1138
  582.0 284.5 %all-gather.2.cloned.1.call-start = ((), (), s32[]{:S(2)}) async-start(), calls=%async_computation.2 | async-start | bytes 2621440 | tf_op jit(solution)/shard_map/all_gather | solution.py:1142
  584.6 30.4 %copy-start.53 = (bf16[8,336,512]{2,1,0:T(8,128)(2,1)S(1)}, bf16[8,336,512]{2,1,0:T(8,128)(2,1)}, u32[]{:S(2)}) copy-start(bf16[8,336,512]{2,1,0:T(8,128)(2,1)} %get-tuple-element.61) | copy-start | bytes 8257540
  612.5 2.5 copy-start.49
  612.5 2.5 copy-start.50
  612.5 5.0 slice-start
  615.0 2.5 slice-start.1
  626.6 2.0 copy-start
  773.9 3.5 copy-start.15
  773.9 4.3 copy-start.31
  773.9 4.3 copy-start.39
  773.9 4.3 copy-start.45
  774.0 4.3 copy-start.26
  774.0 4.3 copy-start.47
  774.0 4.3 copy-start.48
  778.3 2.9 copy-start.17
  778.3 2.9 copy-start.36
  778.4 2.9 copy-start.37
  781.2 8.1 copy-start.14
  781.2 8.1 copy-start.33
  781.2 8.1 copy-start.35
  781.2 8.1 copy-start.44
  789.3 4.5 copy-start.27
  789.3 4.5 copy-start.46
  795.6 15.4 %copy-start.20 = (bf16[1024,1024]{1,0:T(8,128)(2,1)S(1)}, bf16[1024,1024]{1,0:T(8,128)(2,1)}, u32[]{:S(2)}) copy-start(bf16[1024,1024]{1,0:T(8,128)(2,1)} %get-tuple-element.87) | copy-start | bytes 6291460
  811.0 2.9 copy-start.56
  811.0 16.3 %slice-start.4 = ((s8[5242880]{0:T(1024)(128)(4,1)}), s8[4194304]{0:T(1024)(128)(4,1)S(1)}, s32[]{:S(2)}) async-start(s8[5242880]{0:T(1024)(128)(4,1)} %bitcast.192), calls=%async_computation.7 | async-start | bytes 8388608
  813.9 24.9 %collective-permute-start = (bf16[512,1024]{1,0:T(8,128)(2,1)S(1)}, bf16[512,1024]{1,0:T(8,128)(2,1)S(1)}, u32[]{:S(2)}, u32[]{:S(2)}) collective-permute-start(bf16[512,1024]{1,0:T(8,128)(2,1)S(1)} %slice.113), channel_id=1, source_target_pairs={{0,8},{4,12},{8,0},{12,4},{16,24},{20,28},{24,16},{28,20},{1,9},{5... | collective-permute-start | bytes 3145736 | tf_op jit(solution)/shard_map/ppermute | solution.py:1399
  813.9 13.4 %slice-start.5 = ((s8[5242880]{0:T(1024)(128)(4,1)}), s8[1048576]{0:T(1024)(128)(4,1)S(1)}, s32[]{:S(2)}) async-start(s8[5242880]{0:T(1024)(128)(4,1)} %bitcast.192), calls=%async_computation.8 | async-start | bytes 2097152
  814.0 13.4 %copy-start.55 = (bf16[1280,1408]{1,0:T(8,128)(2,1)S(1)}, bf16[1280,1408]{1,0:T(8,128)(2,1)}, u32[]{:S(2)}) copy-start(bf16[1280,1408]{1,0:T(8,128)(2,1)} %get-tuple-element.90) | copy-start | bytes 10813444
  814.0 27.9 %slice-start.2 = ((s8[5242880]{0:T(1024)(128)(4,1)}), s8[4194304]{0:T(1024)(128)(4,1)S(1)}, s32[]{:S(2)}) async-start(s8[5242880]{0:T(1024)(128)(4,1)} %bitcast.190), calls=%async_computation.5 | async-start | bytes 8388608
  827.4 14.5 %slice-start.3 = ((s8[5242880]{0:T(1024)(128)(4,1)}), s8[1048576]{0:T(1024)(128)(4,1)S(1)}, s32[]{:S(2)}) async-start(s8[5242880]{0:T(1024)(128)(4,1)} %bitcast.190), calls=%async_computation.6 | async-start | bytes 2097152
  838.7 3.1 copy-start.54
  839.2 26.1 %collective-permute-start.1 = (bf16[256,1024]{1,0:T(8,128)(2,1)S(1)}, bf16[256,1024]{1,0:T(8,128)(2,1)S(1)}, u32[]{:S(2)}, u32[]{:S(2)}) collective-permute-start(bf16[256,1024]{1,0:T(8,128)(2,1)S(1)} %slice.115), channel_id=1, source_target_pairs={{0,16},{4,20},{8,24},{12,28},{16,0},{20,4},{24,8},{28,12},{1,17},{... | collective-permute-start | bytes 1572872 | tf_op jit(solution)/shard_map/ppermute | solution.py:1399
  841.8 10.7 %copy-start.40 = (f32[24,256]{1,0:T(8,128)S(1)}, f32[24,256]{1,0:T(8,128)}, u32[]{:S(2)}) copy-start(f32[24,256]{1,0:T(8,128)} %shard_map.229) | copy-start | bytes 73732
  841.9 11.3 %copy-start.19 = (bf16[8,256,512]{2,1,0:T(8,128)(2,1)S(1)}, bf16[8,256,512]{2,1,0:T(8,128)(2,1)}, u32[]{:S(2)}) copy-start(bf16[8,256,512]{2,1,0:T(8,128)(2,1)} %get-tuple-element.85) | copy-start | bytes 6291460
  (4 other events, 3.8 us)
Sparse Core Ops, SparseCore 0:
  792.6 25.3 all-gather.1

commit v4 on v3

--- a/solution.py
+++ b/solution.py
@@ -22,7 +22,6 @@
 LOG2E = math.log2(math.e)
 Q_ROWS = 256
 NOTES = 16
-WINDOW_ORDER = (1, 0, 2)
 F32 = jnp.float32
 BF16 = jnp.bfloat16
 MESH = pl.DeviceIdType.MESH
@@ -195,10 +194,181 @@
     )(*ins)
 
 
+def place_matrices(slots_ref, spread, gathered):
+    count, choices = spread.shape
+    spread[...] = (lax.broadcasted_iota(jnp.int32, (count, choices), 0) == slots_ref[0:1, :]).astype(F32).astype(BF16)
+    gathered[...] = spread[...].T
+
+
+def mask_bias(segments, bias):
+    blocks, span, _ = bias.shape
+    here = blocks * Q_ROWS
+    e = lax.axis_index("expert")
+    query_ids = segments[:, pl.ds(pl.multiple_of(e * here + WINDOW, 128), here)]
+    key_row = segments[:, pl.ds(pl.multiple_of(e * here, 128), WINDOW + here)].astype(F32)
+    key_ids = jnp.concatenate([key_row, jnp.zeros((7, WINDOW + here), F32)], axis=0).T[:, 0:1].astype(jnp.int32)
+
+    for block in range(blocks):
+        first = block * Q_ROWS
+        query_place = lax.broadcasted_iota(jnp.int32, (span, Q_ROWS), 1) + WINDOW
+        distance = query_place - lax.broadcasted_iota(jnp.int32, (span, Q_ROWS), 0)
+        same = key_ids[first : first + span] == query_ids[:, first : first + Q_ROWS]
+        allowed = (distance >= 0) & (distance < WINDOW) & same
+        part = jnp.where(allowed, 0.0, masked_value)
+        for k in range(TOPK):
+            bias[block, :, pl.ds(k * Q_ROWS, Q_ROWS)] = part
+
+
+def of_block(choices, block, lanes):
+    rows = choices.shape[0] // TOPK
+    return jnp.concatenate([choices[pl.ds(k * rows + block * Q_ROWS, Q_ROWS), lanes] for k in range(TOPK)], axis=0)
+
+
+def attend(back, keys_ref, values_ref, grouped, queries_ref, lse, spread, gathered, bias, packed, heads):
+    blocks, span, _ = bias.shape
+    rows = queries_ref.shape[0] // TOPK
+    pieces, of_piece = back.shape[0] // EXPERTS, back.shape[2] // HD
+
+    @pl.loop(0, queries_ref.shape[1] // HD)
+    def _(head):
+        lanes = pl.ds(pl.multiple_of(head * HD, HD), HD)
+        inner = pl.ds(pl.multiple_of(lax.rem(head, of_piece) * HD, HD), HD)
+        for q in range(EXPERTS):
+            packed[pl.ds(q * CAP, CAP), :] = back[q * pieces + lax.div(head, of_piece), :, inner]
+        queries_ref[:, lanes] = jnp.dot(gathered[...], packed[...], preferred_element_type=F32).astype(BF16)
+        for block in range(blocks):
+            place = pl.ds(block * Q_ROWS, span)
+            queries = of_block(queries_ref, block, lanes)
+            scores = lax.dot_general(
+                keys_ref[place, lanes], queries, (((1,), (1,)), ((), ())), preferred_element_type=F32)
+            scores = scores * (SCALE * LOG2E) + bias[block]
+            top = jnp.max(scores, axis=0, keepdims=True)
+            probs = jnp.exp2(scores - top)
+            total = jnp.sum(probs, axis=0, keepdims=True)
+            out = lax.dot_general(
+                values_ref[place, lanes], probs.astype(BF16), (((0,), (0,)), ((), ())), preferred_element_type=F32)
+            out = (out * (1.0 / total)).T.astype(BF16)
+            for k in range(TOPK):
+                heads[pl.ds(k * rows + block * Q_ROWS, Q_ROWS), :] = out[k * Q_ROWS : (k + 1) * Q_ROWS]
+            lse[head, :, pl.ds(block * TOPK * Q_ROWS, TOPK * Q_ROWS)] = top + jnp.log2(total)
+        grouped[:, lanes] = jnp.dot(spread[...], heads[...], preferred_element_type=F32).astype(BF16)
+
+
+def attend_back_kernel(experts, *refs):
+    (slots, back, queries_ref, keys_ref, values_ref, lse, segments, rows, heads_rows, gates,
+     grouped, key_grad, value_grad, map_grad,
+     spread, gathered, bias, key_acc, value_acc, query_grad, head_grad, scaled, part_grad,
+     g_send, g_recv) = refs
+    e = lax.axis_index("expert")
+    blocks, span, _ = bias.shape
+    here = queries_ref.shape[0] // TOPK
+    share = part_grad.shape[1]
+
+    def shares(q):
+        return pl.ds(pl.multiple_of(q * share, share), share)
+
+    def grad_from(j):
+        return remote(part_grad.at[j], map_grad.at[j], g_send.at[j], g_recv.at[j], expert=j)
+
+    barrier = pltpu.get_barrier_semaphore()
+
+    @pl.loop(1, experts)
+    def _(s):
+        pl.semaphore_signal(barrier, inc=1, device_id={"expert": e ^ s}, device_id_type=MESH)
+
+    scaled[...] = (heads_rows[...].astype(F32) * gates[...]).astype(BF16)
+    pl.semaphore_wait(barrier, experts - 1)
+
+    @pl.loop(0, experts)
+    def _(s):
+        j = e ^ lax.rem(s + 1, experts)
+        part_grad[j] = lax.dot_general(
+            rows[:, shares(j)], scaled[...], (((0,), (0,)), ((), ())), preferred_element_type=F32).astype(BF16)
+
+        @pl.when(s < experts - 1)
+        def _():
+            remote(part_grad.at[j], map_grad.at[e], g_send.at[j], g_recv.at[e], expert=j).start()
+
+    map_grad[e] = part_grad[e]
+    place_matrices(slots, spread, gathered)
+    mask_bias(segments, bias)
+
+    @pl.loop(0, queries_ref.shape[1] // HD)
+    def _(head):
+        lanes = pl.ds(pl.multiple_of(head * HD, HD), HD)
+        head_grad[...] = jnp.dot(gathered[...], back[:, lanes], preferred_element_type=F32).astype(BF16)
+        key_acc[...] = jnp.zeros_like(key_acc)
+        value_acc[...] = jnp.zeros_like(value_acc)
+        for block in range(blocks):
+            queries = of_block(queries_ref, block, lanes)
+            grads = of_block(head_grad, block, slice(None))
+            place = pl.ds(block * Q_ROWS, span)
+            keys, values = keys_ref[place, lanes], values_ref[place, lanes]
+            scores = lax.dot_general(keys, queries, (((1,), (1,)), ((), ())), preferred_element_type=F32)
+            probs = jnp.exp2(scores * (SCALE * LOG2E) + bias[block]
+                             - lse[head, :, pl.ds(block * TOPK * Q_ROWS, TOPK * Q_ROWS)])
+            pulled = lax.dot_general(values, grads, (((1,), (1,)), ((), ())), preferred_element_type=F32)
+            pulled = probs * pulled
+            inner = jnp.sum(pulled, axis=0, keepdims=True)
+            score_grad = (pulled - probs * inner).astype(BF16)
+            value_acc[place, :] += jnp.dot(probs.astype(BF16), grads, preferred_element_type=F32)
+            key_acc[place, :] += jnp.dot(score_grad, queries, preferred_element_type=F32)
+            out = lax.dot_general(keys, score_grad, (((0,), (0,)), ((), ())), preferred_element_type=F32)
+            out = (out * SCALE).T.astype(BF16)
+            for k in range(TOPK):
+                query_grad[pl.ds(k * here + block * Q_ROWS, Q_ROWS), :] = out[k * Q_ROWS : (k + 1) * Q_ROWS]
+        grouped[:, lanes] = jnp.dot(spread[...], query_grad[...], preferred_element_type=F32).astype(BF16)
+        key_grad[:, lanes] = (key_acc[...] * SCALE).astype(BF16)
+        value_grad[:, lanes] = value_acc[...].astype(BF16)
+
+    @pl.loop(1, experts)
+    def _(s):
+        grad_from(e ^ s).wait_recv()
+        grad_from(e ^ s).wait_send()
+
+
+def attend_back(slots, back, queries, keys, values, lse, segments, rows, heads_rows, gates, collective_id):
+    experts = lax.axis_size("expert")
+    choices, (count, width), span = queries.shape[0], back.shape, keys.shape[0]
+    blocks = choices // TOPK // Q_ROWS
+    f, share = heads_rows.shape[1], D // experts
+    dma = pltpu.SemaphoreType.DMA
+    return pl.pallas_call(
+        functools.partial(attend_back_kernel, experts),
+        out_shape=[
+            jax.ShapeDtypeStruct((count, width), BF16),
+            jax.ShapeDtypeStruct((span, width), BF16),
+            jax.ShapeDtypeStruct((span, width), BF16),
+            jax.ShapeDtypeStruct((experts, share, f), BF16),
+        ],
+        in_specs=[VMEM] * 10,
+        out_specs=[VMEM] * 4,
+        scratch_shapes=[
+            pltpu.VMEM((count, choices), BF16),
+            pltpu.VMEM((choices, count), BF16),
+            pltpu.VMEM((blocks, WINDOW + Q_ROWS, TOPK * Q_ROWS), F32),
+            pltpu.VMEM((span, HD), F32),
+            pltpu.VMEM((span, HD), F32),
+            pltpu.VMEM((choices, HD), BF16),
+            pltpu.VMEM((choices, HD), BF16),
+            pltpu.VMEM(heads_rows.shape, BF16),
+            pltpu.VMEM((experts, share, f), BF16),
+        ] + [dma((experts,))] * 2,
+        compiler_params=pltpu.CompilerParams(
+            collective_id=collective_id, has_side_effects=True, vmem_limit_bytes=63 * 2**20),
+        cost_estimate=pl.CostEstimate(flops=10**11, bytes_accessed=10**7, transcendentals=0),
+    )(slots, back, queries, keys, values, lse, segments, rows, heads_rows, gates)
+
+
+def fact_column(facts, k):
+    return jnp.concatenate([facts, jnp.zeros((120, 256), F32)], axis=0).T[:CAP, k : k + 1]
+
+
 def front_kernel(experts, bits, *refs):
-    (tokens, gain, slots, wide, routes, routers, w_in, kv_in,
-     rows, back, w, window, kv, keys, values, gates, rivals, x, y, facts, facts_in,
-     f_send, f_recv, z_send, z_recv, t_send, t_recv, y_send, y_recv, w_send, w_recv, k_send, k_recv, n_send, n_recv, own_sem) = refs
+    (tokens, gain, slots, routes, routers, segments, w_in, kv_in, wo_in,
+     rows, w, window, kv, keys, values, gates, facts_in, grouped, queries, lse, wo,
+     back, x, y, facts, spread, gathered, bias, packed, heads,
+     f_send, f_recv, v_send, v_recv, z_send, z_recv, t_send, t_recv, y_send, y_recv, w_send, w_recv, k_send, k_recv, n_send, n_recv, own_sem) = refs
     e, t = lax.axis_index("expert"), lax.axis_index("tensor")
     partner = partners(e, experts, True)
     width = x.shape[1]
@@ -278,10 +448,18 @@
 
     state = tokens[...].astype(F32)
     rate = lax.rsqrt(jnp.mean(state * state, axis=1, keepdims=True) + eps)
-    window[2] = (state * rate * gain[...]).astype(BF16)
-    two_on(1).start()
+    window[2] = (state * rate * gain[...].astype(F32)).astype(BF16)
+
+    @pl.when(e < experts - 2)
+    def _():
+        two_on(1).start()
+
+    @pl.when(e < 2)
+    def _():
+        window[0] = jnp.zeros((here, tensor * width), BF16)
+
     place = lax.broadcasted_iota(jnp.int32, (x.shape[0], here), 0)
-    chosen = (place == slots[:, pl.ds(0, here)]) | (place == slots[:, pl.ds(here, here)])
+    chosen = (place == slots[0:1, pl.ds(0, here)]) | (place == slots[0:1, pl.ds(here, here)])
     x[...] = jnp.dot(chosen.astype(F32).astype(BF16), window[2, :, cols(0)], preferred_element_type=F32).astype(BF16)
 
     @pl.loop(1, experts)
@@ -296,26 +474,24 @@
 
     rows[e, :, cols(0)] = x[x_part(e), :]
 
-    logits = jnp.dot(window[2], routers[...], preferred_element_type=F32)
-    lane = lax.broadcasted_iota(jnp.int32, logits.shape, 1)
-    first, second = (jnp.sum(jnp.where(lane == routes[:, k : k + 1], logits, 0.0), axis=1, keepdims=True) for k in (0, 1))
+    logits = lax.dot_general(routers[...], window[2], (((1,), (1,)), ((), ())), preferred_element_type=F32)
+    row = lax.broadcasted_iota(jnp.int32, logits.shape, 0)
+    first, second = (jnp.sum(jnp.where(row == routes[k : k + 1, :], logits, 0.0), axis=0, keepdims=True) for k in (0, 1))
     top = jnp.maximum(first, second)
     first, second = jnp.exp(first - top), jnp.exp(second - top)
-    gate = jnp.concatenate([first, second], axis=0) / jnp.concatenate([first + second] * 2, axis=0)
-    other = jnp.concatenate([routes[:, 3:4], routes[:, 2:3]], axis=0).astype(F32)
+    gate = jnp.concatenate([first / (first + second), second / (first + second)], axis=1)
+    other = jnp.concatenate([routes[3:4, :], routes[2:3, :]], axis=1).astype(F32)
     high = gate.astype(BF16).astype(F32)
     middle = (gate - high).astype(BF16).astype(F32)
-    lane = lax.broadcasted_iota(jnp.int32, (2 * here, 128), 1)
-    table = jnp.where(lane == 0, high, jnp.where(lane == 1, middle, jnp.where(lane == 2, gate - high - middle, 0.0)))
-    fact = []
-    for k, values_of in enumerate((table, jnp.where(lane == 0, other, 0.0))):
-        spot = lax.broadcasted_iota(jnp.int32, (2 * here, EXPERTS * 256), 1) == wide[:, k : k + 1]
-        fact.append(jnp.dot(values_of.T[:16].astype(BF16), spot.astype(F32).astype(BF16), preferred_element_type=F32))
-    gate_row = fact[0][0:1] + fact[0][1:2] + fact[0][2:3]
-    row = lax.broadcasted_iota(jnp.int32, (8, EXPERTS * 256), 0)
-    fact = jnp.where(row == 0, gate_row, jnp.where(row == 1, fact[1][0:1], 0.0))
+    empty = jnp.zeros((13, 2 * here), F32)
+    tables = [jnp.concatenate([high, middle, gate - high - middle, empty], axis=0).astype(BF16),
+              jnp.concatenate([other, empty, empty[:2]], axis=0).astype(BF16)]
     for q in range(EXPERTS):
-        facts[q] = fact[:, q * 256 : (q + 1) * 256]
+        place = lax.broadcasted_iota(jnp.int32, (256, 2 * here), 0) + q * 256
+        fact = [lax.dot_general(table, (place == slots[2 + k : 3 + k, :]).astype(F32).astype(BF16),
+                                (((1,), (1,)), ((), ())), preferred_element_type=F32) for k, table in enumerate(tables)]
+        row = lax.broadcasted_iota(jnp.int32, (8, 256), 0)
+        facts[q] = jnp.where(row == 0, fact[0][0:1] + fact[0][1:2] + fact[0][2:3], jnp.where(row == 1, fact[1][0:1], 0.0))
 
     @pl.loop(1, experts)
     def _(s):
@@ -324,6 +500,8 @@
 
     facts_in[e] = facts[e // pieces]
     chunks(expert_bits - 1)
+    place_matrices(slots, spread, gathered)
+    mask_bias(segments, bias)
 
     @pl.loop(0, experts + bits)
     def _(i):
@@ -345,7 +523,10 @@
 
         @pl.when(i == experts // 2)
         def _():
-            two_on(-1).wait_recv()
+            @pl.when(e >= 2)
+            def _():
+                two_on(-1).wait_recv()
+
             across().start()
             for b in reversed(range(bits)):
                 pass_on(experts, 0, b).start()
@@ -372,6 +553,18 @@
             remote(y.at[j], back.at[e], y_send.at[j], y_recv.at[e], expert=j).start()
 
     back[e] = y[e]
+
+    def map_from(j):
+        return remote(wo_in.at[j], wo.at[part(j)], v_send.at[j], v_recv.at[j], expert=j)
+
+    own_wo = pltpu.make_async_copy(wo_in.at[e], wo.at[part(e)], own_sem.at[2])
+    own_wo.start()
+
+    @pl.loop(1, experts)
+    def _(s):
+        j = partner(s)
+        remote(wo_in.at[j], wo.at[part(e)], v_send.at[j], v_recv.at[e], expert=j).start()
+
     for k in range(1, bits + 1):
         for q in range(2):
             stage(experts + q, k)
@@ -390,21 +583,30 @@
 
     @pl.loop(0, experts)
     def _(j):
-        column = jnp.concatenate([facts_in[j], jnp.zeros((120, 256), F32)], axis=0).T[:cap]
-        gates[j] = column[:, 0:1]
-        rivals[j] = column[:, 1:2]
+        gates[j] = fact_column(facts_in[j], 0)
+
+    @pl.loop(1, experts)
+    def _(s):
+        handed(partner(s)).wait_recv()
+
+    attend(back, keys, values, grouped, queries, lse, spread, gathered, bias, packed, heads)
+    own_wo.wait()
 
     @pl.loop(1, experts)
     def _(s):
         j = partner(s)
         arrived(j).wait_send()
-        handed(j).wait_recv()
         handed(j).wait_send()
         remote(w_in.at[j], w.at[part(j)], w_send.at[j], w_recv.at[j], expert=j).wait_send()
+        map_from(j).wait_recv()
+        map_from(j).wait_send()
 
     for d in range(1, experts):
         passed_chunk(d).wait_send()
-    two_on(1).wait_send()
+    @pl.when(e < experts - 2)
+    def _():
+        two_on(1).wait_send()
+
     across().wait_send()
     for q in range(2):
         for d in range(1, tensor):
@@ -416,38 +618,47 @@
             passed(j, d).wait_send()
 
 
-def front(tokens, gain, slots, wide, routes, routers, w, kv, collective_id):
+def front(tokens, gain, slots, routes, routers, segments, w, kv, wo, collective_id):
     experts, tensor = lax.axis_size("expert"), lax.axis_size("tensor")
     bits = tensor.bit_length() - 1
     here = tokens.shape[0]
     f, f_kv = w.shape[2], kv.shape[2]
     dma = pltpu.SemaphoreType.DMA
+    outs = [
+        ((experts, CAP, D), BF16),
+        ((D, f), BF16),
+        ((3, here, D), BF16),
+        ((2, D, f_kv), BF16),
+        ((3 * here, f_kv), BF16),
+        ((3 * here, f_kv), BF16),
+        ((experts, CAP, 1), F32),
+        ((experts, 8, 256), F32),
+        ((SLOTS, f_kv), BF16),
+        ((TOPK * here, f_kv), BF16),
+        ((f_kv // HD, 1, TOPK * here), F32),
+        ((D, f), BF16),
+    ]
     return pl.pallas_call(
         functools.partial(front_kernel, experts, bits),
-        out_shape=[
-            jax.ShapeDtypeStruct((experts, CAP, D), BF16),
-            jax.ShapeDtypeStruct((experts, CAP, f), BF16),
-            jax.ShapeDtypeStruct((D, f), BF16),
-            jax.ShapeDtypeStruct((3, here, D), BF16),
-            jax.ShapeDtypeStruct((2, D, f_kv), BF16),
-            jax.ShapeDtypeStruct((3 * here, f_kv), BF16),
-            jax.ShapeDtypeStruct((3 * here, f_kv), BF16),
-            jax.ShapeDtypeStruct((experts, CAP, 1), F32),
-            jax.ShapeDtypeStruct((experts, CAP, 1), F32),
-        ],
-        in_specs=[VMEM] * 6 + [ANY, ANY],
-        out_specs=[VMEM] * 9,
+        out_shape=[jax.ShapeDtypeStruct(*out) for out in outs],
+        in_specs=[VMEM] * 6 + [ANY] * 3,
+        out_specs=[VMEM] * 11 + [ANY],
         scratch_shapes=[
+            pltpu.VMEM((experts, CAP, f), BF16),
             pltpu.VMEM((SLOTS, D // tensor), BF16),
             pltpu.VMEM((experts, CAP, f), BF16),
             pltpu.VMEM((EXPERTS, 8, 256), F32),
-            pltpu.VMEM((experts, 8, 256), F32),
-        ] + [dma((experts,))] * 2 + [dma((experts,))] * 2 + [dma((experts + 2, tensor))] * 2 + [dma((experts,))] * 6
-        + [dma((2,))] * 3,
+            pltpu.VMEM((SLOTS, TOPK * here), BF16),
+            pltpu.VMEM((TOPK * here, SLOTS), BF16),
+            pltpu.VMEM((here // Q_ROWS, WINDOW + Q_ROWS, TOPK * Q_ROWS), F32),
+            pltpu.VMEM((SLOTS, HD), BF16),
+            pltpu.VMEM((TOPK * here, HD), BF16),
+        ] + [dma((experts,))] * 6 + [dma((experts + 2, tensor))] * 2 + [dma((experts,))] * 6
+        + [dma((2,))] * 2 + [dma((3,))],
         compiler_params=pltpu.CompilerParams(
-            collective_id=collective_id, has_side_effects=True, vmem_limit_bytes=56 * 2**20),
+            collective_id=collective_id, has_side_effects=True, vmem_limit_bytes=63 * 2**20),
         cost_estimate=pl.CostEstimate(flops=10**11, bytes_accessed=10**7, transcendentals=0),
-    )(tokens, gain, slots, wide, routes, routers, w, kv)
+    )(tokens, gain, slots, routes, routers, segments, w, kv, wo)
 
 
 def scatter_kernel(experts, bits, depth, near, scale, noted, *refs):
@@ -457,16 +668,17 @@
     gate = refs.pop(0) if scale else None
     notes = refs.pop(0) if noted else None
     if depth:
-        key_grad, value_grad, kv, rows, pair_part = refs[:5]
+        key_grad, value_grad, kv_in, rows_in, window_in = refs[:5]
         refs = refs[5:]
     back, h = refs[:2]
     refs = refs[2:]
     if depth:
-        owed, map_grad, pair_came = refs[:3]
-        refs = refs[3:]
+        owed, map_grad, pair_kept, pair_came = refs[:4]
+        refs = refs[4:]
     keep, sent, got, y, t_send, t_recv, y_send, y_recv, h_send, h_recv = refs[:10]
     if depth:
-        n_keep, n_sent, n_got, n_y, n_in, part_grad, n_send, n_recv, o_send, o_recv, g_send, g_recv, p_sem = refs[10:]
+        (kv, rows, window, n_keep, n_sent, n_got, n_in, n_y, n_back, own, total_grad, pair_away,
+         n_send, n_recv, o_send, o_recv, p_send, p_recv, l_sem) = refs[10:]
     e, t = lax.axis_index("expert"), lax.axis_index("tensor")
     partner = partners(e, experts, near)
     tensor = 1 << bits
@@ -483,49 +695,54 @@
     def give(j, d):
         return remote(sent.at[j, d - 1], got.at[j, d - 1], t_send.at[j, d], t_recv.at[j, d], tensor=t ^ (1 << low_bit(d)))
 
-    def owe(q, d):
-        return remote(n_sent.at[q, d - 1], n_got.at[q, d - 1], n_send.at[q, d], n_recv.at[q, d],
-                      tensor=t ^ (1 << low_bit(d)))
-
-    def grad_to(j):
-        return remote(part_grad.at[j], map_grad.at[e], g_send.at[j], g_recv.at[e], expert=j)
-
-    def grad_from(j):
-        return remote(part_grad.at[j], map_grad.at[j], g_send.at[j], g_recv.at[j], expert=j)
-
-    def across():
-        return remote(n_y.at[1], n_in, o_send.at[1], o_recv.at[1], expert=e ^ 1)
+    def owe(d):
+        return remote(n_sent.at[d - 1], n_got.at[d - 1], n_send.at[d], n_recv.at[d], tensor=t ^ (1 << low_bit(d)))
+
+    def across(c):
+        grad = (key_grad, value_grad)[c]
+        here = grad.shape[0] // 3
+        return remote(grad.at[pl.ds(here, here)], n_in.at[c], o_send.at[c], o_recv.at[c], expert=e ^ 1)
 
     def two_back(way):
-        return remote(n_y.at[0], owed.at[1], o_send.at[0], o_recv.at[0],
-                      expert=lax.rem(e + experts - 2 * way, experts))
-
-    def window_stage(k):
-        for q in WINDOW_ORDER:
-            for d in range(tensor - 1, -1, -1):
-                if d % (1 << k) == 0:
-                    came = d | (1 << (k - 1))
-                    owe(q, came).wait_recv()
-                    total = n_keep[q, d // 2] + n_got[q, came - 1].astype(F32)
-                    if k == bits:
-                        if q == 1:
-                            n_y[1] = total.astype(BF16)
-                            across().start()
-                        else:
-                            n_keep[q, 0] = total
-                    elif d & (1 << k):
-                        n_sent[q, d - 1] = total.astype(BF16)
-                        owe(q, d).start()
-                    else:
-                        n_keep[q, d // 2] = total
-
-    def pair_half():
-        half = pair_part.shape[0] // 2
-        return remote(pair_part.at[pl.ds(half, half)], pair_came, p_sem.at[0], p_sem.at[1], expert=e ^ 1)
+        return remote(n_y, n_back, o_send.at[2], o_recv.at[2], expert=lax.rem(e + experts - 2 * way, experts))
+
+    def own_stage(k):
+        for d in range(tensor - 1, -1, -1):
+            if d % (1 << k) == 0:
+                came = d | (1 << (k - 1))
+                owe(came).wait_recv()
+                total = n_keep[d // 2] + n_got[came - 1].astype(F32)
+                if k == bits:
+                    owed[...] = total.astype(BF16)
+                elif d & (1 << k):
+                    n_sent[d - 1] = total.astype(BF16)
+                    owe(d).start()
+                else:
+                    n_keep[d // 2] = total
+
+    def pair_product(p, c):
+        distance = 0
+        for b in range(experts.bit_length() - 1):
+            distance += ((p >> b) & 1) * ((experts // 2) >> b)
+        some = window[:, shares(e ^ distance)]
+        return lax.dot_general(some, (key_grad, value_grad)[c][...], (((0,), (0,)), ((), ())),
+                               preferred_element_type=F32).astype(BF16)
+
+    def pair_chunk(p):
+        return remote(pair_away.at[shares(p)], pair_came.at[shares(p)], p_send.at[p], p_recv.at[p], expert=e ^ 1)
+
+    def shares(q):
+        share = map_grad.shape[1]
+        return pl.ds(pl.multiple_of(q * share, share), share)
 
     def row_from(j):
         return remote(h_in.at[j], h.at[j], h_send.at[j], h_recv.at[j], expert=j)
 
+    if depth:
+        loads = [pltpu.make_async_copy(a, b, l_sem.at[i])
+                 for i, (a, b) in enumerate(((window_in, window), (rows_in, rows), (kv_in, kv)))]
+        for load in loads:
+            load.start()
     meet(experts, bits)
 
     @pl.loop(1, experts)
@@ -535,21 +752,38 @@
 
     h[e] = h_in[e]
     if depth:
-        pair_half().start()
-        here = key_grad.shape[0] // 3
-        for q in WINDOW_ORDER:
-            place = pl.ds(q * here, here)
-            for d in range(tensor - 1, -1, -1):
-                part = lax.dot_general(
-                    key_grad[place, :], kv[0, slice_at(d), :], (((1,), (1,)), ((), ())), preferred_element_type=F32)
-                part += lax.dot_general(
-                    value_grad[place, :], kv[1, slice_at(d), :], (((1,), (1,)), ((), ())), preferred_element_type=F32)
-                if d & 1:
-                    n_sent[q, d - 1] = part.astype(BF16)
-                    owe(q, d).start()
-                else:
-                    n_keep[q, d // 2] = part
-        window_stage(1)
+        here = n_in.shape[1]
+        f = key_grad.shape[1]
+        for c in range(2):
+            across(c).start()
+        loads[0].wait()
+
+        @pl.loop(0, experts // 2)
+        def _(p):
+            for c in range(2):
+                pair_away[shares(p), pl.ds(c * f, f)] = pair_product(p + experts // 2, c)
+            pair_chunk(p).start()
+
+        passing = (e & 1).astype(F32)
+        for c, grad in enumerate((key_grad, value_grad)):
+            across(c).wait_recv()
+            came = n_in[c].astype(F32)
+            n_y[c] = (grad[pl.ds(0, here), :].astype(F32) + passing * came).astype(BF16)
+            own[c] = grad[pl.ds(2 * here, here), :].astype(F32) + (1.0 - passing) * came
+        @pl.when(e >= 2)
+        def _():
+            two_back(1).start()
+
+        @pl.when(e >= experts - 2)
+        def _():
+            n_back[...] = jnp.zeros_like(n_back)
+
+        @pl.loop(0, experts // 2)
+        def _(p):
+            for c in range(2):
+                pair_kept[shares(p), pl.ds(c * f, f)] = pair_product(p, c)
+
+        loads[1].wait()
 
         @pl.loop(1, experts)
         def _(s):
@@ -557,18 +791,9 @@
 
         @pl.loop(0, experts)
         def _(i):
-            j = partner(lax.rem(i + 1, experts))
-            share = part_grad.shape[1]
-            some = rows[:, pl.ds(pl.multiple_of(j * share, share), share)]
-            part_grad[j] = lax.dot_general(
-                some, h[...].reshape(experts * cap, h.shape[2]), (((0,), (0,)), ((), ())),
+            map_grad[i] = lax.dot_general(
+                rows[:, shares(i)], h[...].reshape(experts * cap, h.shape[2]), (((0,), (0,)), ((), ())),
                 preferred_element_type=F32).astype(BF16)
-
-            @pl.when(i < experts - 1)
-            def _():
-                grad_to(j).start()
-
-        map_grad[e] = part_grad[e]
 
     @pl.loop(0, experts + bits)
     def _(i):
@@ -623,19 +848,30 @@
                         remote(y.at[j], back.at[e], y_send.at[j], y_recv.at[e], expert=j).start()
 
         if depth:
-            for k in range(2, bits + 1):
-                @pl.when(i == 2 * (k - 1))
+            @pl.when(i == experts - 1)
+            def _():
+                @pl.when(e < experts - 2)
                 def _():
-                    window_stage(k)
-
-            @pl.when(i == 2 * bits)
+                    two_back(-1).wait_recv()
+
+                loads[2].wait()
+                for c in range(2):
+                    total_grad[c] = (own[c] + n_back[c].astype(F32)).astype(BF16)
+                for d in range(tensor - 1, -1, -1):
+                    part = None
+                    for c in range(2):
+                        term = lax.dot_general(total_grad[c], kv[c, slice_at(d), :], (((1,), (1,)), ((), ())),
+                                               preferred_element_type=F32)
+                        part = term if part is None else part + term
+                    if d & 1:
+                        n_sent[d - 1] = part.astype(BF16)
+                        owe(d).start()
+                    else:
+                        n_keep[d // 2] = part
+
+            @pl.when(i == experts)
             def _():
-                across().wait_recv()
-                passing = (e & 1).astype(F32)
-                came = n_in[...].astype(F32)
-                n_y[0] = (n_keep[0, 0] + passing * came).astype(BF16)
-                owed[0] = (n_keep[2, 0] + (1.0 - passing) * came).astype(BF16)
-                two_back(1).start()
+                own_stage(1)
 
     @pl.loop(1, experts)
     def _(s):
@@ -643,9 +879,6 @@
         row_from(j).wait_send()
         handed(j).wait_recv()
         handed(j).wait_send()
-        if depth:
-            grad_from(j).wait_recv()
-            grad_from(j).wait_send()
 
     @pl.loop(0, experts)
     def _(j):
@@ -653,14 +886,21 @@
             give(j, d).wait_send()
 
     if depth:
-        for q in range(3):
-            for d in range(1, tensor):
-                owe(q, d).wait_send()
-        pair_half().wait_recv()
-        pair_half().wait_send()
-        across().wait_send()
-        two_back(-1).wait_recv()
-        two_back(1).wait_send()
+        for k in range(2, bits + 1):
+            own_stage(k)
+        for d in range(1, tensor):
+            owe(d).wait_send()
+        for c in range(2):
+            across(c).wait_send()
+
+        @pl.when(e >= 2)
+        def _():
+            two_back(1).wait_send()
+
+        @pl.loop(0, experts // 2)
+        def _(p):
+            pair_chunk(p).wait_recv()
+            pair_chunk(p).wait_send()
 
 
 def scatter_rows(h, w, gate=None, notes=None, windows=None, near=True, collective_id=0):
@@ -680,21 +920,28 @@
     if windows is not None:
         ins += windows
         here = windows[0].shape[0] // 3
-        outs.append(jax.ShapeDtypeStruct((2, here, width), BF16))
+        outs.append(jax.ShapeDtypeStruct((here, width), BF16))
         outs.append(jax.ShapeDtypeStruct((experts, D // experts, f), BF16))
-        outs.append(jax.ShapeDtypeStruct((windows[4].shape[0] // 2, windows[4].shape[1]), BF16))
+        outs += [jax.ShapeDtypeStruct((D // 2, 2 * windows[0].shape[1]), BF16)] * 2
+        pair = (2, here, windows[0].shape[1])
         scratch += [
-            pltpu.VMEM((3, tensor // 2, here, width), F32),
-            pltpu.VMEM((3, tensor - 1, here, width), BF16),
-            pltpu.VMEM((3, tensor - 1, here, width), BF16),
-            pltpu.VMEM((2, here, width), BF16),
-            pltpu.VMEM((here, width), BF16),
-            pltpu.VMEM((experts, D // experts, f), BF16),
-        ] + [dma((3, tensor))] * 2 + [dma((2,))] * 2 + [dma((experts,))] * 2 + [dma((2,))]
+            pltpu.VMEM(windows[2].shape, BF16),
+            pltpu.VMEM(windows[3].shape, BF16),
+            pltpu.VMEM(windows[4].shape, BF16),
+            pltpu.VMEM((tensor // 2, here, width), F32),
+            pltpu.VMEM((tensor - 1, here, width), BF16),
+            pltpu.VMEM((tensor - 1, here, width), BF16),
+            pltpu.VMEM(pair, BF16),
+            pltpu.VMEM(pair, BF16),
+            pltpu.VMEM(pair, BF16),
+            pltpu.VMEM(pair, F32),
+            pltpu.VMEM(pair, BF16),
+            pltpu.VMEM((D // 2, 2 * windows[0].shape[1]), BF16),
+        ] + [dma((tensor,))] * 2 + [dma((3,))] * 2 + [dma((experts,))] * 2 + [dma((3,))]
     return pl.pallas_call(
         functools.partial(scatter_kernel, experts, bits, windows is not None, near, gate is not None, notes is not None),
         out_shape=outs,
-        in_specs=[VMEM] * (len(ins) - 1) + [VMEM if windows is None else ANY],
+        in_specs=[VMEM] * (len(ins) - 3) + [VMEM if windows is None else ANY] * 3,
         out_specs=[VMEM] * (len(outs) - 1) + [VMEM if windows is None else ANY],
         scratch_shapes=scratch,
         compiler_params=pltpu.CompilerParams(
@@ -704,9 +951,9 @@
 
 
 def ffn_kernel(experts, bits, pieces, *refs):
-    (x_cols, dy_cols, slots, others, routers, gate_in, up_in, down_in,
+    (x_cols, dy_all, slots, facts, routers, gate_in, up_in, down_in,
      back, rows_out, dys_out, hidden_out, gate_out, up_out,
-     x, dy, land, gate_map, up_map, down_map, gate_pre, up_pre, hidden_grad, gates, pulls, low, sent, got, keep, y,
+     x, dy, dy_near, land, gate_map, up_map, down_map, gate_pre, up_pre, hidden_grad, gates, pulls, low, sent, got, keep,
      z_send, z_recv, t_send, t_recv, r_send, r_recv, y_send, y_recv, w_sem, o_sem) = refs
     e, t = lax.axis_index("expert"), lax.axis_index("tensor")
     tensor = 1 << bits
@@ -717,7 +964,8 @@
     results = ((low.at[0], hidden_out), (low.at[1], gate_out), (low.at[2], up_out))
 
     def first_block(u):
-        return ((e >> 1) ^ u) * 2
+        s = (lax.rem(u, pairs - 1) + 1) * lax.div(u + pairs - 1, pairs)
+        return ((e >> 1) ^ s) * 2
 
     def block(j):
         return pl.ds(pl.multiple_of(j * CAP, CAP), CAP)
@@ -744,9 +992,9 @@
         place = land.at[a, block(j), cols(d)]
         return remote(place, place, t_send.at[a, j, d], t_recv.at[a, j, d], tensor=t ^ (1 << low_bit(d)))
 
-    def stage(j, k):
+    def stage(j, k, arrays=(0, 1)):
         for q in range(2):
-            for a in range(2):
+            for a in arrays:
                 for d in range(1, tensor):
                     if low_bit(d) == bits - k:
                         passed(a, j + q, d).wait_recv()
@@ -761,11 +1009,13 @@
         return remote(sent.at[place_of(u, q), d - 1], got.at[j, d - 1], r_send.at[place_of(u, q), d - 1],
                       r_recv.at[j, d - 1], tensor=t ^ (1 << low_bit(d)))
 
+    final = tensor // 2 - 1
+
     def hand_back(j):
-        return remote(y.at[j], back.at[e], y_send.at[j], y_recv.at[e], expert=j)
+        return remote(got.at[j, final], back.at[e], y_send.at[j], y_recv.at[e], expert=j)
 
     def handed(j):
-        return remote(y.at[j], back.at[j], y_send.at[j], y_recv.at[j], expert=j)
+        return remote(got.at[j, final], back.at[j], y_send.at[j], y_recv.at[j], expert=j)
 
     def sum_stage(u, k):
         j = first_block(u)
@@ -776,7 +1026,7 @@
                     give(u, q, came).wait_recv()
                     total = keep[q, d // 2] + got[j + q, came - 1].astype(F32)
                     if k == bits:
-                        y[j + q] = total.astype(BF16)
+                        got[j + q, final] = total.astype(BF16)
                     elif d & (1 << k):
                         sent[place_of(u, q), d - 1] = total.astype(BF16)
                         give(u, q, d).start()
@@ -790,7 +1040,7 @@
         for q in range(2):
             @pl.when(j + q == e)
             def _():
-                back[e] = y[e]
+                back[e] = got[e, final]
 
             @pl.when(j + q != e)
             def _():
@@ -814,10 +1064,36 @@
     chosen = (place == slots[:, pl.ds(0, here)]) | (place == slots[:, pl.ds(here, here)])
     chosen = chosen.astype(F32).astype(BF16)
     x[...] = jnp.dot(chosen, x_cols[...], preferred_element_type=F32).astype(BF16)
-    dy[...] = jnp.dot(chosen, dy_cols[...], preferred_element_type=F32).astype(BF16)
+    dy[...] = jnp.dot(chosen, dy_all[:, cols(0)], preferred_element_type=F32).astype(BF16)
+
+    even = [d for d in range(2, tensor, 2)]
+
+    def near_block(n):
+        return first_block((n // 2) * (pairs - 1)) + n % 2
+
+    for n in range(4):
+        place = lax.broadcasted_iota(jnp.int32, (CAP, here), 0) + (near_block(n) // pieces) * CAP
+        mine = (place == slots[:, pl.ds(0, here)]) | (place == slots[:, pl.ds(here, here)])
+        mine = mine.astype(F32).astype(BF16)
+        for i, d in enumerate(even):
+            dy_near[n, i] = jnp.dot(mine, dy_all[:, cols(d)], preferred_element_type=F32).astype(BF16)
+
+    def straight(n, i):
+        j, d = near_block(n), even[i]
+        return remote(dy_near.at[n, i], land.at[1, block(e), cols(d)], t_send.at[1, j, d], t_recv.at[1, e, d], expert=j)
+
+    def came_straight(j, d):
+        return remote(land.at[1, block(j), cols(d)], land.at[1, block(j), cols(d)], t_send.at[1, j, d], t_recv.at[1, j, d],
+                      expert=j)
+
     meet(experts, bits)
     for a in range(2):
         arrive(a, e ^ 1).start()
+    for n in range(2):
+        @pl.when(near_block(n) != e)
+        def _():
+            for i in range(len(even)):
+                straight(n, i).start()
 
     def send_pair(u):
         for q in range(2):
@@ -831,14 +1107,24 @@
                 for b in reversed(range(bits)):
                     pass_on(a, first_block(u) + q, 0, b).start()
 
+    def forward_near(j):
+        for a in range(2):
+            arrived(a, j).wait_recv()
+            for b in reversed(range(1 if a else bits)):
+                pass_on(a, j, 0, b).start()
+        for d in even:
+            came_straight(j, d).wait_recv()
+            pass_on(1, j, d, 0).start()
+
     send_pair(1)
-    if pairs > 2:
-        send_pair(2)
     own = first_block(0)
     for a in range(2):
         land[a, block(e), cols(0)] = sources[a][block(e // pieces), :]
-        for b in reversed(range(bits)):
+        for b in reversed(range(1 if a else bits)):
             pass_on(a, e, 0, b).start()
+    for i, d in enumerate(even):
+        land[1, block(e), cols(d)] = dy_near[e & 1, i]
+        pass_on(1, e, d, 0).start()
     foot = pl.ds(pair_rows, NOTES)
     for d in range(tensor):
         for q in range(4):
@@ -847,13 +1133,9 @@
         for q in range(2):
             if d % 2 == 0:
                 keep[q, d // 2, foot, :] = jnp.zeros((NOTES, width), F32)
-    for a in range(2):
-        arrived(a, e ^ 1).wait_recv()
-        for b in reversed(range(bits)):
-            pass_on(a, e ^ 1, 0, b).start()
+    forward_near(e ^ 1)
     for k in range(1, bits):
-        stage(own, k)
-    forward_pair(1)
+        stage(own, k, (0,))
     for copy in weights:
         copy.wait()
 
@@ -866,19 +1148,30 @@
         rows = land[0, pair(j), :]
         gate_pre[...] = jnp.dot(rows, gate_map[...], preferred_element_type=F32)
         up_pre[...] = jnp.dot(rows, up_map[...], preferred_element_type=F32)
-        logits = jnp.dot(rows, routers[...], preferred_element_type=F32)
+        logits = lax.dot_general(rows, routers[...], (((1,), (1,)), ((), ())), preferred_element_type=F32)
         lane = lax.broadcasted_iota(jnp.int32, logits.shape, 1)
         mine = jnp.sum(jnp.where(lane == EXPERTS + e // pieces, logits, 0.0), axis=1, keepdims=True)
-        other = others[pair(j), :] + EXPERTS
+        other = jnp.concatenate([fact_column(facts[j + q], 1) for q in range(2)], axis=0) + EXPERTS
         rival = jnp.sum(jnp.where(lane.astype(F32) == other, logits, 0.0), axis=1, keepdims=True)
         top = jnp.maximum(mine, rival)
         mine, rival = jnp.exp(mine - top), jnp.exp(rival - top)
         gates[...] = mine / (mine + rival)
 
-        @pl.when(u < pairs - 1)
-        def _():
-            for k in range(1, bits):
-                stage(first_block(u + 1), k)
+        @pl.when(u < pairs - 2)
+        def _():
+            forward_pair(u + 1)
+            send_pair(u + 2)
+
+        @pl.when(u == pairs - 3)
+        def _():
+            for n in range(2, 4):
+                for i in range(len(even)):
+                    straight(n, i).start()
+
+        @pl.when(u == pairs - 2)
+        def _():
+            for q in range(2):
+                forward_near(first_block(u + 1) + q)
 
         hidden_grad[...] = lax.dot_general(
             land[1, pair(j), :], down_map[...], (((1,), (1,)), ((), ())), preferred_element_type=F32)
@@ -905,14 +1198,6 @@
 
         for copy in results_to_memory(j):
             copy.start()
-
-        @pl.when(u < pairs - 2)
-        def _():
-            forward_pair(u + 2)
-
-            @pl.when(u < pairs - 3)
-            def _():
-                send_pair(u + 3)
 
         @pl.when(u > 0)
         def _():
@@ -948,6 +1233,16 @@
                 if d & 1:
                     give(u, q, d).start()
         sum_stage(u, 1)
+
+        @pl.when(u < pairs - 1)
+        def _():
+            for k in range(1, bits):
+                stage(first_block(u + 1), k, (0,))
+
+                @pl.when(u < pairs - 2)
+                def _():
+                    stage(first_block(u + 1), k, (1,))
+
         for copy in to_memory(j):
             copy.wait()
 
@@ -971,10 +1266,16 @@
     def _(j):
         for a in range(2):
             for d in range(1, tensor):
-                passed(a, j, d).wait_send()
-
-
-def feed_forward(x, dy, slots, others, routers, gate_map, up_map, down_map, collective_id):
+                if a == 0 or d & 1:
+                    passed(a, j, d).wait_send()
+
+        @pl.when(j != e)
+        def _():
+            for d in even:
+                passed(1, j, d).wait_send()
+
+
+def feed_forward(x, dy, slots, facts, routers, gate_map, up_map, down_map, collective_id):
     experts, tensor = lax.axis_size("expert"), lax.axis_size("tensor")
     bits = tensor.bit_length() - 1
     width, hidden = x.shape[1], gate_map.shape[1]
@@ -990,6 +1291,7 @@
         scratch_shapes=[
             pltpu.VMEM((SLOTS, width), BF16),
             pltpu.VMEM((SLOTS, width), BF16),
+            pltpu.VMEM((4, tensor // 2 - 1, CAP, width), BF16),
             pltpu.VMEM((2, count, D), BF16),
             pltpu.VMEM((D, hidden), BF16),
             pltpu.VMEM((D, hidden), BF16),
@@ -1003,44 +1305,12 @@
             pltpu.VMEM((4, tensor - 1, high, width), BF16),
             pltpu.VMEM((experts, tensor - 1, high, width), BF16),
             pltpu.VMEM((2, tensor // 2, high, width), F32),
-            pltpu.VMEM((experts, high, width), BF16),
         ] + [dma((2, experts))] * 2 + [dma((2, experts, tensor))] * 2
         + [dma((4, tensor - 1)), dma((experts, tensor - 1))] + [dma((experts,))] * 2 + [dma((3,)), dma((5,))],
         compiler_params=pltpu.CompilerParams(
             collective_id=collective_id, has_side_effects=True, vmem_limit_bytes=63 * 2**20),
         cost_estimate=pl.CostEstimate(flops=10**11, bytes_accessed=10**7, transcendentals=0),
-    )(x, dy, slots, others, routers, gate_map, up_map, down_map)
-
-
-def share_kernel(me, left_ref, right_ref, out_ref):
-    out_ref[...] = lax.dot_general(
-        left_ref[...], right_ref[...], (((0,), (0,)), ((), ())), preferred_element_type=F32).astype(BF16)
-
-
-def share_products(left, right, expert_index, experts):
-    share, f = D // experts, right.shape[1]
-
-    def share_at(p, me):
-        distance, last = 0, experts // 2
-        for b in range(experts.bit_length() - 1):
-            distance += ((p >> b) & 1) * (last >> b)
-        return me[0] ^ distance
-
-    return pl.pallas_call(
-        share_kernel,
-        grid_spec=pltpu.PrefetchScalarGridSpec(
-            num_scalar_prefetch=1,
-            grid=(experts,),
-            in_specs=[
-                pl.BlockSpec((left.shape[0], share), lambda p, me: (0, share_at(p, me))),
-                pl.BlockSpec(right.shape, lambda p, me: (0, 0)),
-            ],
-            out_specs=pl.BlockSpec((share, f), lambda p, me: (p, 0)),
-        ),
-        out_shape=jax.ShapeDtypeStruct((D, f), BF16),
-        compiler_params=pltpu.CompilerParams(vmem_limit_bytes=32 * 2**20),
-        cost_estimate=pl.CostEstimate(flops=10**10, bytes_accessed=2 * 10**7, transcendentals=0),
-    )(expert_index[None], left, right)
+    )(x, dy, slots, facts, routers, gate_map, up_map, down_map)
 
 
 def small_kernel(experts, tensor, part, out, came, s_send, s_recv, b_send, b_recv):
@@ -1194,148 +1464,6 @@
     inner_sum = gating * (pulled - jnp.sum(gating * pulled, axis=1, keepdims=True))
     one_hot = (routes[:, :, None] == jnp.arange(EXPERTS, dtype=jnp.int32)[None, None, :]).astype(F32)
     return jnp.sum(one_hot * inner_sum[:, :, None], axis=1).astype(BF16)
-
-
-def place_matrices(slots_ref, spread, gathered):
-    count, choices = spread.shape
-    spread[...] = (lax.broadcasted_iota(jnp.int32, (count, choices), 0) == slots_ref[...]).astype(F32).astype(BF16)
-    gathered[...] = spread[...].T
-
-
-def mask_bias(query_ids, key_ids, bias):
-    blocks, span, _ = bias.shape
-
-    for block in range(blocks):
-        first = block * Q_ROWS
-        query_place = lax.broadcasted_iota(jnp.int32, (span, Q_ROWS), 1) + WINDOW
-        distance = query_place - lax.broadcasted_iota(jnp.int32, (span, Q_ROWS), 0)
-        same = key_ids[pl.ds(first, span), :] == query_ids[:, pl.ds(first, Q_ROWS)]
-        allowed = (distance >= 0) & (distance < WINDOW) & same
-        part = jnp.where(allowed, 0.0, masked_value)
-        for k in range(TOPK):
-            bias[block, :, pl.ds(k * Q_ROWS, Q_ROWS)] = part
-
-
-def of_block(choices, block):
-    rows = choices.shape[0] // TOPK
-    return jnp.concatenate([choices[pl.ds(k * rows + block * Q_ROWS, Q_ROWS), :] for k in range(TOPK)], axis=0)
-
-
-def attend_kernel(slots_ref, back_ref, key_ref, value_ref, query_ids, key_ids, grouped_ref, query_ref, lse_ref,
-                  spread, gathered, bias, heads):
-    @pl.when(pl.program_id(0) == 0)
-    def _():
-        place_matrices(slots_ref, spread, gathered)
-        mask_bias(query_ids, key_ids, bias)
-
-    query_ref[...] = jnp.dot(gathered[...], back_ref[...], preferred_element_type=F32).astype(BF16)
-    blocks, span, _ = bias.shape
-    rows = query_ref.shape[0] // TOPK
-    for block in range(blocks):
-        queries = of_block(query_ref, block)
-        keys = key_ref[pl.ds(block * Q_ROWS, span), :]
-        values = value_ref[pl.ds(block * Q_ROWS, span), :]
-        scores = lax.dot_general(keys, queries, (((1,), (1,)), ((), ())), preferred_element_type=F32)
-        scores = scores * (SCALE * LOG2E) + bias[block]
-        top = jnp.max(scores, axis=0, keepdims=True)
-        probs = jnp.exp2(scores - top)
-        total = jnp.sum(probs, axis=0, keepdims=True)
-        out = lax.dot_general(values, probs.astype(BF16), (((0,), (0,)), ((), ())), preferred_element_type=F32)
-        out = (out * (1.0 / total)).T.astype(BF16)
-        for k in range(TOPK):
-            heads[pl.ds(k * rows + block * Q_ROWS, Q_ROWS), :] = out[k * Q_ROWS : (k + 1) * Q_ROWS]
-        lse_ref[0, :, pl.ds(block * TOPK * Q_ROWS, TOPK * Q_ROWS)] = top + jnp.log2(total)
-    grouped_ref[...] = jnp.dot(spread[...], heads[...], preferred_element_type=F32).astype(BF16)
-
-
-def attend(slots, back, keys, values, query_ids, key_ids):
-    choices, (count, width), span = slots.shape[1], back.shape, keys.shape[0]
-    blocks = choices // TOPK // Q_ROWS
-    head = lambda rows: pl.BlockSpec((rows, HD), lambda h: (0, h))
-    whole = lambda a: pl.BlockSpec(a.shape, lambda h: (0, 0))
-    return pl.pallas_call(
-        attend_kernel,
-        grid=(width // HD,),
-        out_shape=[
-            jax.ShapeDtypeStruct((count, width), BF16),
-            jax.ShapeDtypeStruct((choices, width), BF16),
-            jax.ShapeDtypeStruct((width // HD, 1, choices), F32),
-        ],
-        in_specs=[whole(slots), head(count), head(span), head(span), whole(query_ids), whole(key_ids)],
-        out_specs=[head(count), head(choices), pl.BlockSpec((1, 1, choices), lambda h: (h, 0, 0))],
-        scratch_shapes=[
-            pltpu.VMEM((count, choices), BF16),
-            pltpu.VMEM((choices, count), BF16),
-            pltpu.VMEM((blocks, WINDOW + Q_ROWS, TOPK * Q_ROWS), F32),
-            pltpu.VMEM((choices, HD), BF16),
-        ],
-        compiler_params=pltpu.CompilerParams(vmem_limit_bytes=48 * 2**20),
-        cost_estimate=pl.CostEstimate(flops=16 * 10**9, bytes_accessed=10**7, transcendentals=10**7),
-    )(slots, back, keys, values, query_ids, key_ids)
-
-
-def attend_back_kernel(slots_ref, back_ref, query_ref, key_ref, value_ref, lse_ref, query_ids, key_ids,
-                       grouped_ref, key_grad_ref, value_grad_ref,
-                       spread, gathered, bias, key_acc, value_acc, query_grad, head_grad):
-    @pl.when(pl.program_id(0) == 0)
-    def _():
-        place_matrices(slots_ref, spread, gathered)
-        mask_bias(query_ids, key_ids, bias)
-
-    head_grad[...] = jnp.dot(gathered[...], back_ref[...], preferred_element_type=F32).astype(BF16)
-    key_acc[...] = jnp.zeros_like(key_acc)
-    value_acc[...] = jnp.zeros_like(value_acc)
-    blocks, span, _ = bias.shape
-    rows = query_ref.shape[0] // TOPK
-    for block in range(blocks):
-        queries = of_block(query_ref, block)
-        grads = of_block(head_grad, block)
-        place = pl.ds(block * Q_ROWS, span)
-        keys, values = key_ref[place, :], value_ref[place, :]
-        scores = lax.dot_general(keys, queries, (((1,), (1,)), ((), ())), preferred_element_type=F32)
-        lse = lse_ref[0, :, pl.ds(block * TOPK * Q_ROWS, TOPK * Q_ROWS)]
-        probs = jnp.exp2(scores * (SCALE * LOG2E) + bias[block] - lse)
-        pulled = lax.dot_general(values, grads, (((1,), (1,)), ((), ())), preferred_element_type=F32)
-        pulled = probs * pulled
-        inner = jnp.sum(pulled, axis=0, keepdims=True)
-        score_grad = (pulled - probs * inner).astype(BF16)
-        value_acc[place, :] += jnp.dot(probs.astype(BF16), grads, preferred_element_type=F32)
-        key_acc[place, :] += jnp.dot(score_grad, queries, preferred_element_type=F32)
-        out = lax.dot_general(keys, score_grad, (((0,), (0,)), ((), ())), preferred_element_type=F32)
-        out = (out * SCALE).T.astype(BF16)
-        for k in range(TOPK):
-            query_grad[pl.ds(k * rows + block * Q_ROWS, Q_ROWS), :] = out[k * Q_ROWS : (k + 1) * Q_ROWS]
-    grouped_ref[...] = jnp.dot(spread[...], query_grad[...], preferred_element_type=F32).astype(BF16)
-    key_grad_ref[...] = (key_acc[...] * SCALE).astype(BF16)
-    value_grad_ref[...] = value_acc[...].astype(BF16)
-
-
-def attend_back(slots, back, queries, keys, values, lse, query_ids, key_ids):
-    choices, (count, width), span = slots.shape[1], back.shape, keys.shape[0]
-    blocks = choices // TOPK // Q_ROWS
-    head = lambda rows: pl.BlockSpec((rows, HD), lambda h: (0, h))
-    whole = lambda a: pl.BlockSpec(a.shape, lambda h: (0, 0))
-    return pl.pallas_call(
-        attend_back_kernel,
-        grid=(width // HD,),
-        out_shape=[jax.ShapeDtypeStruct((count, width), BF16)] + [jax.ShapeDtypeStruct((span, width), BF16)] * 2,
-        in_specs=[
-            whole(slots), head(count), head(choices), head(span), head(span),
-            pl.BlockSpec((1, 1, choices), lambda h: (h, 0, 0)), whole(query_ids), whole(key_ids),
-        ],
-        out_specs=[head(count), head(span), head(span)],
-        scratch_shapes=[
-            pltpu.VMEM((count, choices), BF16),
-            pltpu.VMEM((choices, count), BF16),
-            pltpu.VMEM((blocks, WINDOW + Q_ROWS, TOPK * Q_ROWS), F32),
-            pltpu.VMEM((span, HD), F32),
-            pltpu.VMEM((span, HD), F32),
-            pltpu.VMEM((choices, HD), BF16),
-            pltpu.VMEM((choices, HD), BF16),
-        ],
-        compiler_params=pltpu.CompilerParams(vmem_limit_bytes=56 * 2**20),
-        cost_estimate=pl.CostEstimate(flops=30 * 10**9, bytes_accessed=10**7, transcendentals=10**7),
-    )(slots, back, queries, keys, values, lse, query_ids, key_ids)
 
 
 def per_device(
@@ -1398,32 +1526,26 @@
     def exchange(away, b):
         return lax.ppermute(away, "expert", [(i, i ^ (1 << b)) for i in range(expert_count)])
 
+    attn_slots, ffn_slots = slot_numbers(attn_routes), slot_numbers(ffn_routes)
+
+    slots = jnp.stack([attn_slots, ffn_slots, spaced(attn_slots, 256), spaced(ffn_slots, 256)])
+    segments = jnp.concatenate([jnp.full((WINDOW,), -1, jnp.int32), segment_ids])[None]
+    (rows_one, query_map, window, pair_map, keys, values, attn_gate_blocks, facts, heads, queries, log_total,
+     output_map) = front(
+        tokens, attn_gain[None], slots, jnp.concatenate([attn_routes.T, ffn_routes.T]), routers.T, segments,
+        to_pieces(query_weight, pieces), key_value_weight, to_pieces(output_weight, pieces), collective_id=0)
+    rows_one, attn_slots, ffn_slots, tokens, attn_gain, ffn_gain, routers, cotangent = lax.optimization_barrier(
+        (rows_one, attn_slots, ffn_slots, tokens, attn_gain, ffn_gain, routers, cotangent))
+    routers_one, routers_two = routers[:, :EXPERTS], routers[:, EXPERTS:]
     state_in = tokens.astype(F32)
     gain_one = attn_gain.astype(F32)
     gain_two = cols(ffn_gain.astype(F32))
-    routers_one, routers_two = routers[:, :EXPERTS], routers[:, EXPERTS:]
     dy_cols = cols(cotangent)
     token_cols = cols(tokens).astype(F32)
-
-    attn_slots, ffn_slots = slot_numbers(attn_routes), slot_numbers(ffn_routes)
     attn_places, ffn_places = place_matrix(attn_slots), place_matrix(ffn_slots)
-
-
-    wide_slots = jnp.stack([spaced(attn_slots, 256), spaced(ffn_slots, 256)], axis=1)
-    rows_one, query_rows, query_map, window, pair_map, keys, values, attn_gate_blocks, rivals = front(
-        tokens, gain_one[None], attn_slots[None], wide_slots, jnp.concatenate([attn_routes, ffn_routes], axis=1), routers,
-        to_pieces(query_weight, pieces), key_value_weight, collective_id=0)
-    output_weight, keys = lax.optimization_barrier((output_weight, keys))
     rows_one = rows_one.reshape(-1, D)
-    output_map = swap(to_pieces(output_weight, pieces)).reshape(D, -1)
     normed_one = window[2]
     window = window.reshape(-1, D)
-    padded_segments = jnp.concatenate([jnp.full((WINDOW,), -1, jnp.int32), segment_ids])
-    key_ids = lax.dynamic_slice_in_dim(padded_segments, expert_index * rows_here, WINDOW + rows_here)
-    query_ids = key_ids[None, WINDOW:]
-    key_ids = key_ids[:, None]
-    heads, queries, log_total = attend(
-        attn_slots[None], from_pieces(query_rows, pieces).reshape(SLOTS, -1), keys, values, query_ids, key_ids)
     attn_back, heads_rows = scatter_rows(
         to_pieces(heads.reshape(EXPERTS, CAP, -1), pieces), output_map, attn_gate_blocks, collective_id=1)
     heads_rows = heads_rows.reshape(expert_count * CAP, -1)
@@ -1434,7 +1556,7 @@
     normed_two = (state * rate_two * gain_two).astype(BF16)
     gate_map, up_map, down_map = gate_weight[0], up_weight[0], down_weight[0]
     ffn_back, rows_two, rows_dy, hidden, gate_low, up_low = feed_forward(
-        normed_two, dy_cols, ffn_slots[None], rivals.reshape(-1, 1), routers, gate_map, up_map, down_map, collective_id=2)
+        normed_two, cotangent, ffn_slots[None], facts, routers.T, gate_map, up_map, down_map, collective_id=2)
     normed_two_grad = sums_of(ffn_back, token_matrix(ffn_slots, 2 * CAP + NOTES))
     noted = read_notes(ffn_back, ffn_places, 2, 2 * CAP)
     ffn_pull, ffn_gates = noted[:, :, 0].T, noted[:, :, 1].T
@@ -1452,22 +1574,23 @@
     rows_state = rows_state.reshape(-1, D)
     heads_grad_rows = heads_grad_rows.reshape(expert_count * CAP, -1)
     attn_notes = notes_of(jnp.sum(heads_grad_rows.astype(F32) * heads_rows.astype(F32), axis=1))
-    output_part = mm_tn((rows_state.astype(F32) * attn_gate_blocks.reshape(-1, 1)).astype(BF16), heads_rows).astype(BF16)
-    heads_grad, output_part = lax.optimization_barrier((heads_grad, output_part))
-
-    query_back, key_back, value_back = attend_back(
+    query_back, key_back, value_back, output_grad = attend_back(
         attn_slots[None], from_pieces(heads_grad, pieces).reshape(SLOTS, -1), queries, keys, values, log_total,
-        query_ids, key_ids)
-    output_grad = swap(output_part.reshape(expert_count, D // expert_count, -1))
-    pair_part = share_products(window, jnp.concatenate([key_back, value_back], axis=1), expert_index, expert_count)
-    query_back, output_grad = lax.optimization_barrier((query_back, output_grad))
+        segments, rows_state, heads_rows, attn_gate_blocks.reshape(-1, 1), collective_id=6)
     output_grad = from_pieces(output_grad, pieces).astype(F32)
-    normed_back, unused_rows, owed, query_grad, pair_came = scatter_rows(
+    normed_back, unused_rows, owed, query_grad, pair_part, pair_came = scatter_rows(
         to_pieces(query_back.reshape(EXPERTS, CAP, -1), pieces), query_map, notes=attn_notes,
-        windows=[key_back, value_back, pair_map, rows_one, pair_part], collective_id=5)
-    query_grad = from_pieces(query_grad, pieces).astype(F32)
-    normed_grad = sums_of(normed_back, token_matrix(attn_slots, CAP + NOTES)) + jnp.sum(owed.astype(F32), axis=0)
-    rows_two, rows_dy, normed_back = lax.optimization_barrier((rows_two, rows_dy, normed_back))
+        windows=[key_back, value_back, pair_map, rows_one, window], collective_id=5)
+    pair_part = (pair_part.astype(F32) + pair_came.astype(F32)).astype(BF16)
+    pair_part, query_grad, rows_two, hidden = lax.optimization_barrier((pair_part, query_grad, rows_two, hidden))
+    pair_came = exchange(pair_part[pair_part.shape[0] // 2 :], 1)
+    query_grad = swap(query_grad)
+    gate_grad = mm_tn(rows_two, gate_low)
+    up_grad = mm_tn(rows_two, up_low)
+    down_grad = mm_tn(hidden, rows_dy)
+    normed_back, owed, gate_grad, up_grad, down_grad, pair_came = lax.optimization_barrier(
+        (normed_back, owed, gate_grad, up_grad, down_grad, pair_came))
+    normed_grad = sums_of(normed_back, token_matrix(attn_slots, CAP + NOTES)) + owed.astype(F32)
     attn_pull = read_notes(normed_back, attn_places, 1)[:, :, 0].T
     attn_gates = pick_gates(mm(normed_one, routers_one), attn_routes)
     attn_logit_grad = gate_back(attn_gates, attn_pull, attn_routes)
@@ -1485,18 +1608,14 @@
         [attn_router_cols.T, ffn_router_cols.T, attn_gain_cols[None], ffn_gain_cols[None],
          jnp.zeros((6, column_count), F32)], axis=0)
     small = small_sums(small, collective_id=3)
-    small, pair_came = lax.optimization_barrier((small, pair_came))
     small = small.T
-    for b in range(1, expert_count.bit_length()):
+    query_grad = from_pieces(query_grad, pieces).astype(F32)
+    for b in range(2, expert_count.bit_length() - 1):
         pair_part = pair_part[: pair_came.shape[0]].astype(F32) + pair_came.astype(F32)
-        if b < expert_count.bit_length() - 1:
-            pair_part = pair_part.astype(BF16)
-            pair_came = exchange(pair_part[pair_part.shape[0] // 2 :], b)
+        pair_part = pair_part.astype(BF16)
+        pair_came = exchange(pair_part[pair_part.shape[0] // 2 :], b)
+    pair_part = pair_part[: pair_came.shape[0]].astype(F32) + pair_came.astype(F32)
     key_value_grad = pair_part.reshape(D // expert_count, 2, -1).transpose(1, 0, 2)
-
-    gate_grad = mm_tn(rows_two, gate_low)
-    up_grad = mm_tn(rows_two, up_low)
-    down_grad = mm_tn(hidden, rows_dy)
     ffn_out = sums_of(ffn_back, token_matrix(ffn_slots, 2 * CAP + NOTES, CAP))
     mixed = (state + ffn_out).astype(BF16)
     return (

time: 887 us -> 858 us (0.967)
  waiting for transfers between devices: 11.1 us -> 0.03 us
  Pallas kernels: 684 us -> 694 us
    pallas_call x1, Pallas kernels: 153 us -> 191 us  [front(): pl.pallas_call(functools.partial(front_kernel, experts, bits), out_shape=...]
    pallas_call x2, Pallas kernels: 203 us -> 186 us  [scatter_rows(): pl.pallas_call(functools.partial(scatter_kernel, experts, bits, windows i...]
    all_to_all x2 -> x1, starting transfers between devices: 17.5 us -> 4.36 us  [swap(): lax.all_to_all(blocks, 'expert', split_axis=0, concat_axis=0, tiled=True)]
    pallas_call x1, Pallas kernels: 15.4 us -> 26.7 us  [small_sums(): pl.pallas_call(functools.partial(small_kernel, experts, tensor), out_shap...]
    pallas_call x1, Pallas kernels: 175 us -> 165 us  [feed_forward(): pl.pallas_call(functools.partial(ffn_kernel, experts, bits, experts // EX...]
    pallas_call x3 -> x1, Pallas kernels: 60.1 us -> 54.4 us  [attend_back(): pl.pallas_call(functools.partial(attend_back_kernel, experts), out_shape=...]
    dot_general x16 -> x15, matrix products: 67.1 us -> 61.7 us  [dot(): lax.dot_general(left, right, ((dims[0], dims[1]), ((), ())), preferred_el...]
  transfers between devices with their start and end apart: 5 -> 4, of which waited for: 3 -> 0; matrix products, arithmetic and copies ran while one was open for 9% -> 9% of each run, Pallas kernels for 9% -> 3%
where the time goes in v4:
time: 858 us; the launch traced here: 849 us
  Pallas kernels  694 us (81%)
  matrix products  61.7 us (7%)
  other arithmetic  30.6 us (4%)
  local copies, waits for them, and re-layouts  16.9 us (2%)
  blocking collectives  16.9 us (2%)
  between operations  14.8 us (2%)
  starting transfers between devices  13.7 us (2%)
    pallas_call x1, Pallas kernels, front(): pl.pallas_call(functools.partial(front_kernel, experts, bits), out_shape=...  191 us
    pallas_call x2, Pallas kernels, scatter_rows(): pl.pallas_call(functools.partial(scatter_kernel, experts, bits, windows i...  186 us
    pallas_call x1, Pallas kernels, feed_forward(): pl.pallas_call(functools.partial(ffn_kernel, experts, bits, experts // EX...  165 us
    pallas_call x1, Pallas kernels, gather_rows(): pl.pallas_call(functools.partial(gather_kernel, experts, bits, near, mult...  70.7 us
    dot_general x15, matrix products, dot(): lax.dot_general(left, right, ((dims[0], dims[1]), ((), ())), preferred_el...  61.7 us
    pallas_call x1, Pallas kernels, attend_back(): pl.pallas_call(functools.partial(attend_back_kernel, experts), out_shape=...  54.4 us
    pallas_call x1, Pallas kernels, small_sums(): pl.pallas_call(functools.partial(small_kernel, experts, tensor), out_shap...  26.7 us
  transfers between devices with their start and end apart: 4, of which 0 were waited for; matrix products, arithmetic and copies ran while one was open for 9% of the time, Pallas kernels for 3%

profile of v4, /device:TPU:0, one launch (start us, length us, event | category | flops | bytes accessed | tf_op | source)
XLA Modules:
  0.0 848.9 jit_solution(14834242091648982744)
XLA Ops:
  7.2 0.7 multiply_bitcast_fusion.1
  7.9 0.7 copy.50
  8.6 0.5 convert_reduce_fusion.1
  9.1 0.7 multiply_bitcast_fusion
  9.8 0.7 copy.52
  10.5 0.5 convert_reduce_fusion
  11.0 1.3 broadcast_in_dim.26.refs_1_
  12.3 1.3 concatenate.10
  13.6 1.3 pad_add_fusion.1.refs_3_
  15.0 0.6 pad_add_fusion.refs_2_
  15.7 191.1 %shard_map.221 = (bf16[8,160,2048]{2,1,0:T(8,128)(2,1)}, bf16[2048,512]{1,0:T(8,128)(2,1)}, bf16[3,512,2048]{2,1,0:T(8,128)(2,1)}, bf16[2,2048,512]{2,1,0:T(8,12...) custom-call(bf16[512,2048]{1,0:T(8,128)(2,1)} %refs_0_.1, ...), custom_call_target="tpu_custom_call" | custom-call | flops 99999997952 | bytes 10000000 | tf_op jit(solution)/shard_map/pallas_call | solution.py:641
  206.8 1.9 iota_compare_fusion.7
  208.6 0.6 broadcast_add_fusion
  209.3 70.0 %shard_map.222 = (bf16[8,160,512]{2,1,0:T(8,128)(2,1)}, bf16[8,160,512]{2,1,0:T(8,128)(2,1)}) custom-call(bf16[8,160,512]{2,1,0:T(8,128)(2,1)} %bitcast.170, bf16[2048,512]{1,0:T(8,128)(2,1)} %get-tuple-element.65.refs_1_, f32[8,160,1]{2,1,0:T(8,128)} %get-tuple-element.66.refs_2_), custom_call_target="tpu_custom_call" | custom-call | flops 99999997952 | bytes 10000000 | tf_op jit(solution)/shard_map/pallas_call | solution.py:941
  279.3 2.4 multiply_reduce_fusion.4
  281.7 5.7 psum.21
  287.4 0.8 dynamic-slice_convert_fusion.1
  288.2 0.6 fusion.80
  288.8 0.9 multiply_convert_fusion.refs_0_
  289.8 165.5 %shard_map.223 = (bf16[8,336,512]{2,1,0:T(8,128)(2,1)}, bf16[1280,2048]{1,0:T(8,128)(2,1)}, bf16[1280,2048]{1,0:T(8,128)(2,1)}, bf16[1280,1408]{1,0:T(8,128)(2,1...) custom-call(bf16[512,512]{1,0:T(8,128)(2,1)} %multiply_convert_fusion.refs_0_, bf16[512,2048]{1,0:T(8,128)(2,1)} %refs_1_, ...), custom_call_target="tpu_custom_call" | custom-call | flops 99999997952 | bytes 10000000 | tf_op jit(solution)/shard_map/pallas_call | solution.py:1285
  455.2 0.8 slice_bitcast_fusion
  456.1 2.1 fusion.87
  458.3 3.6 fusion.4
  461.9 1.1 multiply_reduce_fusion.2
  463.0 5.6 psum.22
  468.7 2.2 convolution_convert_fusion
  470.9 70.7 %shard_map.224 = (bf16[8,160,2048]{2,1,0:T(8,128)(2,1)}, bf16[8,160,512]{2,1,0:T(8,128)(2,1)S(1)}, bf16[8,160,512]{2,1,0:T(8,128)(2,1)S(1)}) custom-call(bf16[8,160,512]{2,1,0:T(8,128)(2,1)S(1)} %bitcast.117, bf16[2048,512]{1,0:T(8,128)(2,1)} %get-tuple-element.65.refs_1_, f32[8,160,1]{2,1,0:T(8,128)S(1)} %copy-done.1), custom_call_target="tpu_custom_call" | custom-call | flops 99999997952 | bytes 10000000 | tf_op jit(solution)/shard_map/pallas_call | solution.py:185
  541.7 0.4 multiply_reduce_fusion.1
  542.1 0.6 copy-done
  542.7 0.7 pad.5.refs_2_
  543.5 54.4 %shard_map.225 = (bf16[1280,512]{1,0:T(8,128)(2,1)}, bf16[1536,512]{1,0:T(8,128)(2,1)}, bf16[1536,512]{1,0:T(8,128)(2,1)}, bf16[8,256,512]{2,1,0:T(8,128)(2,1)}) custom-call(s32[1,1024]{1,0:T(1,128)} %bitcast.127, bf16[1280,512]{1,0:T(8,128)(2,1)} %bitcast.116, bf16[1024,512]{1,0:T(8,128)(2,1)} %get-tuple-element.75.refs_2_, ...), custom_call_target="tpu_custom_call" | custom-call | flops 99999997952 | bytes 10000000 | tf_op jit(solution)/shard_map/pallas_call | solution.py:336
  597.8 115.9 %shard_map.226 = (bf16[8,176,512]{2,1,0:T(8,128)(2,1)}, bf16[8,160,512]{2,1,0:T(8,128)(2,1)}, bf16[512,512]{1,0:T(8,128)(2,1)}, bf16[8,256,512]{2,1,0:T(8,128)(2...) custom-call(bf16[8,160,512]{2,1,0:T(8,128)(2,1)} %bitcast.171, bf16[2048,512]{1,0:T(8,128)(2,1)} %get-tuple-element.82.refs_1_, ...), custom_call_target="tpu_custom_call" | custom-call | flops 99999997952 | bytes 10000000 | tf_op jit(solution)/shard_map/pallas_call | solution.py:941
  713.8 3.2 add_convert_fusion
  717.0 1.0 slice.88
  718.0 6.5 collective-permute-start
  724.5 4.4 all-to-all-start
  729.0 2.4 fusion.16
  731.4 0.5 multiply_reduce_fusion
  731.9 14.5 %fusion.89 = f32[2048,1408]{1,0:T(8,128)} fusion(bf16[1280,2048]{1,0:T(8,128)(2,1)} %get-tuple-element.96, bf16[1280,1408]{1,0:T(8,128)(2,1)} %get-tuple-element.98), kind=kOutput, calls=%fused_computation.138 | convolution fusion | flops 7381975040 | bytes 20381696 | tf_op jit(solution)/shard_map/dot_general | solution.py:1392
  746.5 11.3 %fusion.88 = f32[2048,1408]{1,0:T(8,128)} fusion(bf16[1280,2048]{1,0:T(8,128)(2,1)S(1)} %bitcast.174, bf16[1280,1408]{1,0:T(8,128)(2,1)S(1)} %copy-done.29), kind=kOutput, calls=%fused_computation.137 | convolution fusion | flops 7381975040 | bytes 20381696 | tf_op jit(solution)/shard_map/dot_general | solution.py:1392
  757.9 13.4 %fusion.90 = f32[1408,2048]{1,0:T(8,128)} fusion(bf16[1280,1408]{1,0:T(8,128)(2,1)} %get-tuple-element.99, bf16[1280,2048]{1,0:T(8,128)(2,1)} %get-tuple-element.100), kind=kOutput, calls=%fused_computation.139 | convolution fusion | flops 7381975040 | bytes 20381696 | tf_op jit(solution)/shard_map/dot_general | solution.py:1392
  771.3 0.8 dynamic-slice_convert_fusion
  772.1 0.8 iota_compare_fusion.6
  772.9 0.8 slice_reduce_fusion
  773.8 0.8 fusion.91
  774.7 1.0 fusion.53
  775.8 4.0 fusion.48
  779.7 5.6 psum.23
  785.4 3.3 fusion.45
  788.8 1.9 slice.89
  790.6 0.3 copy-done.7
  791.0 2.6 convert_element_type.143
  793.8 0.2 copy-done.28
  793.9 2.5 fusion.38
  796.4 1.7 add_convert_fusion.1
  798.2 2.8 collective-permute-start.1
  801.0 0.2 fusion.49
  801.2 1.8 concatenate.11.part
  803.0 26.7 %shard_map.227 = f32[24,256]{1,0:T(8,128)} custom-call(f32[24,512]{1,0:T(8,128)} %concatenate.11.part), custom_call_target="tpu_custom_call" | custom-call | flops 10000000000 | bytes 100000 | tf_op jit(solution)/shard_map/pallas_call | solution.py:1379
  829.7 1.3 slice.102
  831.0 1.3 fusion.81
  832.5 1.1 copy.63
  833.6 4.2 convert_element_type.142
  837.8 4.1 convert_element_type.141
  (99 shorter events, 1.1 us)
Async XLA Ops:
  15.0 193.7 %copy-start.18 = (s32[1024]{0:T(1024)}, s32[1024]{0:T(1024)S(1)}, u32[]{:S(2)}) copy-start(s32[1024]{0:T(1024)S(1)} %get-tuple-element.68) | copy-start | bytes 12292
  15.0 194.3 %copy-start.13 = (s32[1024]{0:T(1024)}, s32[1024]{0:T(1024)S(1)}, u32[]{:S(2)}) copy-start(s32[1024]{0:T(1024)S(1)} %get-tuple-element.63) | copy-start | bytes 12292
  279.3 8.9 %copy-start.15 = (bf16[2048,16]{0,1:T(8,128)(2,1)S(1)}, bf16[2048,16]{0,1:T(8,128)(2,1)}, u32[]{:S(2)}) copy-start(bf16[2048,16]{0,1:T(8,128)(2,1)} %param.20) | copy-start | bytes 196612
  281.7 7.1 copy-start.2
  287.4 181.3 %copy-start.21 = (f32[512,1]{0,1:T(1,128)}, f32[512,1]{0,1:T(1,128)S(1)}, u32[]{:S(2)}) copy-start(f32[512,1]{0,1:T(1,128)S(1)} %add_rsqrt_fusion.1) | copy-start | bytes 6148
  288.2 180.5 %copy-start.19 = (f32[512]{0:T(512)}, f32[512]{0:T(512)S(1)}, u32[]{:S(2)}) copy-start(f32[512]{0:T(512)S(1)} %dynamic-slice_convert_fusion.1) | copy-start | bytes 6148
  289.8 168.5 %copy-start.17 = (s32[512,2]{0,1:T(2,128)S(1)}, s32[512,2]{0,1:T(2,128)}, u32[]{:S(2)}) copy-start(s32[512,2]{0,1:T(2,128)} %param.17) | copy-start | bytes 12292
  289.8 168.6 %copy-start.24 = (s32[1024]{0:T(1024)S(1)}, s32[1024]{0:T(1024)}, u32[]{:S(2)}) copy-start(s32[1024]{0:T(1024)} %get-tuple-element.118) | copy-start | bytes 12292
  458.3 3.6 copy-start.11
  458.3 3.6 copy-start.3
  463.0 7.9 copy-start.5
  468.7 2.3 copy-start.25
  468.7 2.3 copy-start.1
  470.9 70.8 %copy-start.9 = (bf16[8,160,512]{2,1,0:T(8,128)(2,1)S(1)}, bf16[8,160,512]{2,1,0:T(8,128)(2,1)}, u32[]{:S(2)}) copy-start(bf16[8,160,512]{2,1,0:T(8,128)(2,1)} %get-tuple-element.80) | copy-start | bytes 3932164
  541.7 1.1 copy-start
  717.0 12.0 %copy-start.16 = (bf16[2048,16]{0,1:T(8,128)(2,1)S(1)}, bf16[2048,16]{0,1:T(8,128)(2,1)}, u32[]{:S(2)}) copy-start(bf16[2048,16]{0,1:T(8,128)(2,1)} %param.20) | copy-start | bytes 196612
  718.0 54.9 %collective-permute-start = (bf16[512,1024]{1,0:T(8,128)(2,1)}, bf16[512,1024]{1,0:T(8,128)(2,1)}, u32[]{:S(2)}, u32[]{:S(2)}) collective-permute-start(bf16[512,1024]{1,0:T(8,128)(2,1)} %slice.88), channel_id=1, source_target_pairs={{0,8},{4,12},{8,0},{12,4},{16,24},{20,28},{24,16},{28,20},{1,9},{5... | collective-permute-start | bytes 3145736 | tf_op jit(solution)/shard_map/ppermute | solution.py:1527
  724.5 109.0 %all-to-all-start = ((bf16[8,256,512]{2,1,0:T(8,128)(2,1)}), bf16[8,256,512]{2,1,0:T(8,128)(2,1)}, u32[]{:S(2)}, u32[]{:S(2)}) async-start(bf16[8,256,512]{2,1,0:T(8,128)(2,1)} %get-tuple-element.105), calls=%async_computation | async-start | bytes 4194304 | tf_op jit(solution)/shard_map/all_to_all | solution.py:1408
  728.9 108.9 %all-gather.2.cloned.1.call-start = ((), (), s32[]{:S(2)}) async-start(), calls=%async_computation.1 | async-start | bytes 2621440 | tf_op jit(solution)/shard_map/all_gather | solution.py:1412
  729.0 2.4 copy-start.6
  729.0 17.5 %slice-start = ((s8[5242880]{0:T(1024)(128)(4,1)}), s8[4194304]{0:T(1024)(128)(4,1)S(1)}, s32[]{:S(2)}) async-start(s8[5242880]{0:T(1024)(128)(4,1)} %bitcast.173), calls=%async_computation.2 | async-start | bytes 8388608
  731.9 14.6 %slice-start.1 = ((s8[5242880]{0:T(1024)(128)(4,1)}), s8[1048576]{0:T(1024)(128)(4,1)S(1)}, s32[]{:S(2)}) async-start(s8[5242880]{0:T(1024)(128)(4,1)} %bitcast.173), calls=%async_computation.3 | async-start | bytes 2097152
  731.9 14.6 %copy-start.29 = (bf16[1280,1408]{1,0:T(8,128)(2,1)S(1)}, bf16[1280,1408]{1,0:T(8,128)(2,1)}, u32[]{:S(2)}) copy-start(bf16[1280,1408]{1,0:T(8,128)(2,1)} %get-tuple-element.97) | copy-start | bytes 10813444
  746.5 11.4 %copy-start.10 = (s32[512,2]{0,1:T(2,128)S(1)}, s32[512,2]{0,1:T(2,128)}, u32[]{:S(2)}) copy-start(s32[512,2]{0,1:T(2,128)} %param.16) | copy-start | bytes 12292
  757.9 14.2 %copy-start.14 = (s32[1024]{0:T(1024)S(1)}, s32[1024]{0:T(1024)}, u32[]{:S(2)}) copy-start(s32[1024]{0:T(1024)} %copy-done.13) | copy-start | bytes 12292
  775.7 9.6 %copy-start.4 = (f32[512,512]{1,0:T(8,128)S(1)}, f32[512,512]{1,0:T(8,128)}, u32[]{:S(2)}) copy-start(f32[512,512]{1,0:T(8,128)} %copy-done.2) | copy-start | bytes 3145732
  775.7 9.6 %copy-start.20 = (f32[512]{0:T(512)S(1)}, f32[512]{0:T(512)}, u32[]{:S(2)}) copy-start(f32[512]{0:T(512)} %copy-done.19) | copy-start | bytes 6148
  775.8 9.6 %copy-start.22 = (f32[512,1]{0,1:T(1,128)S(1)}, f32[512,1]{0,1:T(1,128)}, u32[]{:S(2)}) copy-start(f32[512,1]{0,1:T(1,128)} %copy-done.21) | copy-start | bytes 6148
  775.8 9.6 %copy-start.26 = (f32[512,1]{0,1:T(1,128)S(1)}, f32[512,1]{0,1:T(1,128)}, u32[]{:S(2)}) copy-start(f32[512,1]{0,1:T(1,128)} %copy-done.25) | copy-start | bytes 6148
  788.8 2.2 copy-start.7
  791.0 2.6 copy-start.23
  791.0 2.6 copy-start.8
  791.0 2.6 copy-start.12
  791.0 3.0 copy-start.28
  796.4 4.7 copy-start.27
  798.2 34.2 %collective-permute-start.1 = (bf16[256,1024]{1,0:T(8,128)(2,1)S(1)}, bf16[256,1024]{1,0:T(8,128)(2,1)S(1)}, u32[]{:S(2)}, u32[]{:S(2)}) collective-permute-start(bf16[256,1024]{1,0:T(8,128)(2,1)S(1)} %slice.104), channel_id=1, source_target_pairs={{0,16},{4,20},{8,24},{12,28},{16,0},{20,4},{24,8},{28,12},{1,17},{... | collective-permute-start | bytes 1572872 | tf_op jit(solution)/shard_map/ppermute | solution.py:1527
Sparse Core Ops, SparseCore 0:
  788.9 23.1 all-gather.1

commit v5 on v4

--- a/solution.py
+++ b/solution.py
@@ -62,9 +62,11 @@
     x = refs.pop(0)
     w = refs.pop(0) if multiply else None
     gate = refs.pop(0) if scale else None
+    others = refs.pop(0) if scale else None
     rows = refs.pop(0)
     back = refs.pop(0) if multiply else None
     product = refs.pop(0) if scale else None
+    map_grad = refs.pop(0) if scale else None
     y = refs.pop(0) if multiply else None
     z_send, z_recv, t_send, t_recv = refs[:4]
     refs = refs[4:]
@@ -146,6 +148,17 @@
                     def _():
                         hand_back(j).start()
 
+    if scale:
+        cap, f = others.shape[1], others.shape[2]
+        share = map_grad.shape[1]
+        scaled = (others[...].astype(F32) * gate[...]).astype(BF16).reshape(experts * cap, f)
+
+        @pl.loop(0, experts)
+        def _(j):
+            some = rows[:, :, pl.ds(pl.multiple_of(j * share, share), share)].reshape(experts * cap, share)
+            map_grad[j] = lax.dot_general(
+                some, scaled, (((0,), (0,)), ((), ())), preferred_element_type=F32).astype(BF16)
+
     @pl.loop(1, experts)
     def _(s):
         j = partner(s)
@@ -160,7 +173,7 @@
             passed(j, d).wait_send()
 
 
-def gather_rows(x, w=None, gate=None, near=True, collective_id=0):
+def gather_rows(x, w=None, gate=None, others=None, near=True, collective_id=0):
     experts, tensor = lax.axis_size("expert"), lax.axis_size("tensor")
     bits = tensor.bit_length() - 1
     cap, width = x.shape[1], x.shape[2]
@@ -174,9 +187,10 @@
         specs.append(VMEM)
         outs.append(jax.ShapeDtypeStruct((experts, cap, f), BF16))
     if gate is not None:
-        ins.append(gate)
-        specs.append(VMEM)
+        ins += [gate, others]
+        specs += [VMEM, VMEM]
         outs.append(jax.ShapeDtypeStruct((experts, cap, f), BF16))
+        outs.append(jax.ShapeDtypeStruct((experts, D // experts, f), BF16))
     if multiply:
         scratch.append(pltpu.VMEM((experts, cap, f), BF16))
     scratch += [pltpu.SemaphoreType.DMA((experts,))] * 2 + [pltpu.SemaphoreType.DMA((experts, tensor))] * 2
@@ -255,18 +269,13 @@
 
 
 def attend_back_kernel(experts, *refs):
-    (slots, back, queries_ref, keys_ref, values_ref, lse, segments, rows, heads_rows, gates,
+    (slots, back, queries_ref, keys_ref, values_ref, lse, segments, part_grad,
      grouped, key_grad, value_grad, map_grad,
-     spread, gathered, bias, key_acc, value_acc, query_grad, head_grad, scaled, part_grad,
-     g_send, g_recv) = refs
+     spread, gathered, bias, key_acc, value_acc, query_grad, head_grad,
+     g_send, g_recv, own_sem) = refs
     e = lax.axis_index("expert")
     blocks, span, _ = bias.shape
     here = queries_ref.shape[0] // TOPK
-    share = part_grad.shape[1]
-
-    def shares(q):
-        return pl.ds(pl.multiple_of(q * share, share), share)
-
     def grad_from(j):
         return remote(part_grad.at[j], map_grad.at[j], g_send.at[j], g_recv.at[j], expert=j)
 
@@ -276,20 +285,15 @@
     def _(s):
         pl.semaphore_signal(barrier, inc=1, device_id={"expert": e ^ s}, device_id_type=MESH)
 
-    scaled[...] = (heads_rows[...].astype(F32) * gates[...]).astype(BF16)
+    own = pltpu.make_async_copy(part_grad.at[e], map_grad.at[e], own_sem)
+    own.start()
     pl.semaphore_wait(barrier, experts - 1)
 
-    @pl.loop(0, experts)
-    def _(s):
-        j = e ^ lax.rem(s + 1, experts)
-        part_grad[j] = lax.dot_general(
-            rows[:, shares(j)], scaled[...], (((0,), (0,)), ((), ())), preferred_element_type=F32).astype(BF16)
-
-        @pl.when(s < experts - 1)
-        def _():
-            remote(part_grad.at[j], map_grad.at[e], g_send.at[j], g_recv.at[e], expert=j).start()
-
-    map_grad[e] = part_grad[e]
+    @pl.loop(1, experts)
+    def _(s):
+        j = e ^ s
+        remote(part_grad.at[j], map_grad.at[e], g_send.at[j], g_recv.at[e], expert=j).start()
+
     place_matrices(slots, spread, gathered)
     mask_bias(segments, bias)
 
@@ -321,17 +325,18 @@
         key_grad[:, lanes] = (key_acc[...] * SCALE).astype(BF16)
         value_grad[:, lanes] = value_acc[...].astype(BF16)
 
+    own.wait()
+
     @pl.loop(1, experts)
     def _(s):
         grad_from(e ^ s).wait_recv()
         grad_from(e ^ s).wait_send()
 
 
-def attend_back(slots, back, queries, keys, values, lse, segments, rows, heads_rows, gates, collective_id):
+def attend_back(slots, back, queries, keys, values, lse, segments, map_grad, collective_id):
     experts = lax.axis_size("expert")
     choices, (count, width), span = queries.shape[0], back.shape, keys.shape[0]
     blocks = choices // TOPK // Q_ROWS
-    f, share = heads_rows.shape[1], D // experts
     dma = pltpu.SemaphoreType.DMA
     return pl.pallas_call(
         functools.partial(attend_back_kernel, experts),
@@ -339,10 +344,10 @@
             jax.ShapeDtypeStruct((count, width), BF16),
             jax.ShapeDtypeStruct((span, width), BF16),
             jax.ShapeDtypeStruct((span, width), BF16),
-            jax.ShapeDtypeStruct((experts, share, f), BF16),
+            jax.ShapeDtypeStruct(map_grad.shape, BF16),
         ],
-        in_specs=[VMEM] * 10,
-        out_specs=[VMEM] * 4,
+        in_specs=[VMEM] * 7 + [ANY],
+        out_specs=[VMEM] * 3 + [ANY],
         scratch_shapes=[
             pltpu.VMEM((count, choices), BF16),
             pltpu.VMEM((choices, count), BF16),
@@ -351,13 +356,11 @@
             pltpu.VMEM((span, HD), F32),
             pltpu.VMEM((choices, HD), BF16),
             pltpu.VMEM((choices, HD), BF16),
-            pltpu.VMEM(heads_rows.shape, BF16),
-            pltpu.VMEM((experts, share, f), BF16),
-        ] + [dma((experts,))] * 2,
+        ] + [dma((experts,))] * 2 + [dma],
         compiler_params=pltpu.CompilerParams(
-            collective_id=collective_id, has_side_effects=True, vmem_limit_bytes=63 * 2**20),
+            collective_id=collective_id, has_side_effects=True, vmem_limit_bytes=56 * 2**20),
         cost_estimate=pl.CostEstimate(flops=10**11, bytes_accessed=10**7, transcendentals=0),
-    )(slots, back, queries, keys, values, lse, segments, rows, heads_rows, gates)
+    )(slots, back, queries, keys, values, lse, segments, map_grad)
 
 
 def fact_column(facts, k):
@@ -720,16 +723,22 @@
                 else:
                     n_keep[d // 2] = total
 
+    order = [list(range(experts.bit_length() - 1)) for _ in range(2)]
+    order[1][:2] = [1, 0]
+
     def pair_product(p, c):
         distance = 0
-        for b in range(experts.bit_length() - 1):
-            distance += ((p >> b) & 1) * ((experts // 2) >> b)
+        for i, b in enumerate(reversed(order[c])):
+            distance += ((p >> i) & 1) * (1 << b)
         some = window[:, shares(e ^ distance)]
         return lax.dot_general(some, (key_grad, value_grad)[c][...], (((0,), (0,)), ((), ())),
                                preferred_element_type=F32).astype(BF16)
 
-    def pair_chunk(p):
-        return remote(pair_away.at[shares(p)], pair_came.at[shares(p)], p_send.at[p], p_recv.at[p], expert=e ^ 1)
+    def pair_chunk(p, c):
+        f = key_grad.shape[1]
+        place, lanes = shares(p), pl.ds(c * f, f)
+        return remote(pair_away.at[place, lanes], pair_came.at[place, lanes], p_send.at[c, p], p_recv.at[c, p],
+                      expert=e ^ (1 << order[c][0]))
 
     def shares(q):
         share = map_grad.shape[1]
@@ -762,7 +771,7 @@
         def _(p):
             for c in range(2):
                 pair_away[shares(p), pl.ds(c * f, f)] = pair_product(p + experts // 2, c)
-            pair_chunk(p).start()
+                pair_chunk(p, c).start()
 
         passing = (e & 1).astype(F32)
         for c, grad in enumerate((key_grad, value_grad)):
@@ -783,28 +792,17 @@
             for c in range(2):
                 pair_kept[shares(p), pl.ds(c * f, f)] = pair_product(p, c)
 
-        loads[1].wait()
-
-        @pl.loop(1, experts)
-        def _(s):
-            row_from(partner(s)).wait_recv()
-
-        @pl.loop(0, experts)
-        def _(i):
-            map_grad[i] = lax.dot_general(
-                rows[:, shares(i)], h[...].reshape(experts * cap, h.shape[2]), (((0,), (0,)), ((), ())),
-                preferred_element_type=F32).astype(BF16)
-
     @pl.loop(0, experts + bits)
     def _(i):
         @pl.when(i < experts)
         def _():
             j = partner(i)
             slot = lax.rem(i, bits + 1)
-            if not depth:
-                @pl.when(i > 0)
-                def _():
-                    row_from(j).wait_recv()
+
+            @pl.when(i > 0)
+            def _():
+                row_from(j).wait_recv()
+
             for d in range(tensor - 1, -1, -1):
                 part = lax.dot_general(
                     h[j], w[slice_at(d), :], (((1,), (1,)), ((), ())), preferred_element_type=F32)
@@ -873,6 +871,17 @@
             def _():
                 own_stage(1)
 
+    if depth:
+        for k in range(2, bits + 1):
+            own_stage(k)
+        loads[1].wait()
+
+        @pl.loop(0, experts)
+        def _(i):
+            map_grad[i] = lax.dot_general(
+                rows[:, shares(i)], h[...].reshape(experts * cap, h.shape[2]), (((0,), (0,)), ((), ())),
+                preferred_element_type=F32).astype(BF16)
+
     @pl.loop(1, experts)
     def _(s):
         j = partner(s)
@@ -886,8 +895,6 @@
             give(j, d).wait_send()
 
     if depth:
-        for k in range(2, bits + 1):
-            own_stage(k)
         for d in range(1, tensor):
             owe(d).wait_send()
         for c in range(2):
@@ -899,8 +906,9 @@
 
         @pl.loop(0, experts // 2)
         def _(p):
-            pair_chunk(p).wait_recv()
-            pair_chunk(p).wait_send()
+            for c in range(2):
+                pair_chunk(p, c).wait_recv()
+                pair_chunk(p, c).wait_send()
 
 
 def scatter_rows(h, w, gate=None, notes=None, windows=None, near=True, collective_id=0):
@@ -937,7 +945,7 @@
             pltpu.VMEM(pair, F32),
             pltpu.VMEM(pair, BF16),
             pltpu.VMEM((D // 2, 2 * windows[0].shape[1]), BF16),
-        ] + [dma((tensor,))] * 2 + [dma((3,))] * 2 + [dma((experts,))] * 2 + [dma((3,))]
+        ] + [dma((tensor,))] * 2 + [dma((3,))] * 2 + [dma((2, experts))] * 2 + [dma((3,))]
     return pl.pallas_call(
         functools.partial(scatter_kernel, experts, bits, windows is not None, near, gate is not None, notes is not None),
         out_shape=outs,
@@ -953,7 +961,7 @@
 def ffn_kernel(experts, bits, pieces, *refs):
     (x_cols, dy_all, slots, facts, routers, gate_in, up_in, down_in,
      back, rows_out, dys_out, hidden_out, gate_out, up_out,
-     x, dy, dy_near, land, gate_map, up_map, down_map, gate_pre, up_pre, hidden_grad, gates, pulls, low, sent, got, keep,
+     x, dy, dy_near, land, gate_map, up_map, down_map, gate_pre, up_pre, hidden_grad, gates, pulls, moments, own_logits, low, sent, got, keep,
      z_send, z_recv, t_send, t_recv, r_send, r_recv, y_send, y_recv, w_sem, o_sem) = refs
     e, t = lax.axis_index("expert"), lax.axis_index("tensor")
     tensor = 1 << bits
@@ -1153,6 +1161,7 @@
         mine = jnp.sum(jnp.where(lane == EXPERTS + e // pieces, logits, 0.0), axis=1, keepdims=True)
         other = jnp.concatenate([fact_column(facts[j + q], 1) for q in range(2)], axis=0) + EXPERTS
         rival = jnp.sum(jnp.where(lane.astype(F32) == other, logits, 0.0), axis=1, keepdims=True)
+        own_logits[...] = mine
         top = jnp.maximum(mine, rival)
         mine, rival = jnp.exp(mine - top), jnp.exp(rival - top)
         gates[...] = mine / (mine + rival)
@@ -1181,9 +1190,9 @@
             for copy in results_to_memory(j):
                 copy.wait()
 
-        @pl.loop(0, pair_rows // 16)
+        @pl.loop(0, pair_rows // 32)
         def _(r):
-            some = pl.ds(pl.multiple_of(r * 16, 16), 16)
+            some = pl.ds(pl.multiple_of(r * 32, 32), 32)
             gate_here, up_here = gate_pre[some, :], up_pre[some, :]
             weight = gates[some, :]
             sigma = 1.0 / (1.0 + jnp.exp(-gate_here))
@@ -1193,8 +1202,12 @@
             pulls[some, :] = jnp.sum(hidden * grad, axis=1, keepdims=True)
             grad = grad * weight
             low[0, some, :] = (hidden * weight).astype(BF16)
-            low[1, some, :] = (grad * up_here * (sigma * (1.0 + gate_here * (1.0 - sigma)))).astype(BF16)
-            low[2, some, :] = (grad * silu).astype(BF16)
+            gate_low = (grad * up_here * (sigma * (1.0 + gate_here * (1.0 - sigma)))).astype(BF16)
+            up_low = (grad * silu).astype(BF16)
+            low[1, some, :] = gate_low
+            low[2, some, :] = up_low
+            moments[some, :] = jnp.sum(
+                gate_low.astype(F32) * gate_here + up_low.astype(F32) * up_here, axis=1, keepdims=True)
 
         for copy in results_to_memory(j):
             copy.start()
@@ -1213,7 +1226,9 @@
         for q in range(2):
             some = pl.ds(q * CAP, CAP)
             lane = lax.broadcasted_iota(jnp.int32, (CAP, 128), 1)
-            column = jnp.where(lane == 0, pulls[some, :], jnp.where(lane == 1, gates[some, :] / (tensor * pieces), 0.0))
+            shared = tensor * pieces
+            column = jnp.where(lane == 0, pulls[some, :], jnp.where(lane == 1, gates[some, :] / shared, 0.0))
+            column = jnp.where(lane == 2, moments[some, :], jnp.where(lane == 3, own_logits[some, :] / shared, column))
             column = jnp.concatenate([column, jnp.zeros((256 - CAP, 128), F32)], axis=0)
             noted.append(column.T[:NOTES])
         for d in range(tensor - 1, -1, -1):
@@ -1301,6 +1316,8 @@
             pltpu.VMEM((2 * CAP, hidden), F32),
             pltpu.VMEM((2 * CAP, 1), F32),
             pltpu.VMEM((2 * CAP, 1), F32),
+            pltpu.VMEM((2 * CAP, 1), F32),
+            pltpu.VMEM((2 * CAP, 1), F32),
             pltpu.VMEM((3, 2 * CAP, hidden), BF16),
             pltpu.VMEM((4, tensor - 1, high, width), BF16),
             pltpu.VMEM((experts, tensor - 1, high, width), BF16),
@@ -1558,38 +1575,50 @@
     ffn_back, rows_two, rows_dy, hidden, gate_low, up_low = feed_forward(
         normed_two, cotangent, ffn_slots[None], facts, routers.T, gate_map, up_map, down_map, collective_id=2)
     normed_two_grad = sums_of(ffn_back, token_matrix(ffn_slots, 2 * CAP + NOTES))
-    noted = read_notes(ffn_back, ffn_places, 2, 2 * CAP)
-    ffn_pull, ffn_gates = noted[:, :, 0].T, noted[:, :, 1].T
+    ffn_pull, ffn_gates, moments, own_logits = (
+        note.T for note in jnp.moveaxis(read_notes(ffn_back, ffn_places, 4, 2 * CAP), 2, 0))
     ffn_logit_grad = gate_back(ffn_gates, ffn_pull, ffn_routes)
     normed_two_grad = normed_two_grad + mm_nt(
         ffn_logit_grad, lax.dynamic_slice_in_dim(routers_two, tensor_index * column_count, column_count, 0))
     ffn_router_cols = mm_tn(normed_two, ffn_logit_grad)
     ffn_gain_cols = jnp.sum(normed_two_grad * state * rate_two, axis=0)
     ahead = normed_two_grad * gain_two
-    centre = lax.psum(jnp.sum(ahead * state, axis=1, keepdims=True), "tensor") / D
+    chosen_grad = jnp.sum(
+        jnp.where(ffn_routes[:, :, None] == jnp.arange(EXPERTS, dtype=jnp.int32), ffn_logit_grad[:, None].astype(F32), 0.0),
+        axis=2)
+    centre = jnp.sum(moments + chosen_grad * own_logits, axis=1, keepdims=True) / (rate_two * D)
     state_grad = dy_cols.astype(F32) + rate_two * ahead - state * rate_two * rate_two * rate_two * centre
 
-    rows_state, heads_grad, heads_grad_rows = gather_rows(
-        group_tokens(state_grad.astype(BF16), token_matrix(attn_slots)), output_map, gate=attn_gate_blocks, collective_id=4)
-    rows_state = rows_state.reshape(-1, D)
+    unused_rows, heads_grad, heads_grad_rows, output_grad = gather_rows(
+        group_tokens(state_grad.astype(BF16), token_matrix(attn_slots)), output_map, gate=attn_gate_blocks,
+        others=heads_rows.reshape(expert_count, CAP, -1), collective_id=4)
     heads_grad_rows = heads_grad_rows.reshape(expert_count * CAP, -1)
     attn_notes = notes_of(jnp.sum(heads_grad_rows.astype(F32) * heads_rows.astype(F32), axis=1))
     query_back, key_back, value_back, output_grad = attend_back(
         attn_slots[None], from_pieces(heads_grad, pieces).reshape(SLOTS, -1), queries, keys, values, log_total,
-        segments, rows_state, heads_rows, attn_gate_blocks.reshape(-1, 1), collective_id=6)
+        segments, output_grad, collective_id=6)
     output_grad = from_pieces(output_grad, pieces).astype(F32)
     normed_back, unused_rows, owed, query_grad, pair_part, pair_came = scatter_rows(
         to_pieces(query_back.reshape(EXPERTS, CAP, -1), pieces), query_map, notes=attn_notes,
         windows=[key_back, value_back, pair_map, rows_one, window], collective_id=5)
     pair_part = (pair_part.astype(F32) + pair_came.astype(F32)).astype(BF16)
     pair_part, query_grad, rows_two, hidden = lax.optimization_barrier((pair_part, query_grad, rows_two, hidden))
-    pair_came = exchange(pair_part[pair_part.shape[0] // 2 :], 1)
+    quarter = D // 4
+    pair_came = jnp.concatenate(
+        [exchange(pair_part[quarter:, :head_width], 1), exchange(pair_part[quarter:, head_width:], 0)], axis=1)
     query_grad = swap(query_grad)
     gate_grad = mm_tn(rows_two, gate_low)
     up_grad = mm_tn(rows_two, up_low)
+    pair_came, hidden, gate_grad, up_grad = lax.optimization_barrier((pair_came, hidden, gate_grad, up_grad))
+    pair_part = pair_part[:quarter].astype(F32) + pair_came.astype(F32)
+    for b in range(2, expert_count.bit_length() - 1):
+        rest = pair_part.shape[0] // 2
+        pair_part = pair_part.astype(BF16)
+        if b == 2:
+            pair_part, hidden = lax.optimization_barrier((pair_part, hidden))
+        pair_part = pair_part[:rest].astype(F32) + exchange(pair_part[rest:], b).astype(F32)
     down_grad = mm_tn(hidden, rows_dy)
-    normed_back, owed, gate_grad, up_grad, down_grad, pair_came = lax.optimization_barrier(
-        (normed_back, owed, gate_grad, up_grad, down_grad, pair_came))
+    normed_back, owed, down_grad = lax.optimization_barrier((normed_back, owed, down_grad))
     normed_grad = sums_of(normed_back, token_matrix(attn_slots, CAP + NOTES)) + owed.astype(F32)
     attn_pull = read_notes(normed_back, attn_places, 1)[:, :, 0].T
     attn_gates = pick_gates(mm(normed_one, routers_one), attn_routes)
@@ -1600,21 +1629,17 @@
     rate_one = lax.rsqrt(jnp.mean(state_in * state_in, axis=1, keepdims=True) + eps)
     attn_gain_cols = jnp.sum(normed_grad * token_cols * rate_one, axis=0)
     ahead_one = normed_grad * cols(gain_one)
-    centre_one = lax.psum(jnp.sum(ahead_one * token_cols, axis=1, keepdims=True), "tensor") / D
+    centre_one = jnp.sum(ahead_one * token_cols, axis=1, keepdims=True)
+    centre_one = lax.psum(centre_one, "tensor") / D
     tokens_grad = state_grad + rate_one * ahead_one - token_cols * rate_one * rate_one * rate_one * centre_one
     tokens_grad = columns_together(tokens_grad.astype(BF16)).astype(F32)
 
     small = jnp.concatenate(
         [attn_router_cols.T, ffn_router_cols.T, attn_gain_cols[None], ffn_gain_cols[None],
          jnp.zeros((6, column_count), F32)], axis=0)
-    small = small_sums(small, collective_id=3)
-    small = small.T
+    small, pair_part = lax.optimization_barrier((small, pair_part))
+    small = small_sums(small, collective_id=3).T
     query_grad = from_pieces(query_grad, pieces).astype(F32)
-    for b in range(2, expert_count.bit_length() - 1):
-        pair_part = pair_part[: pair_came.shape[0]].astype(F32) + pair_came.astype(F32)
-        pair_part = pair_part.astype(BF16)
-        pair_came = exchange(pair_part[pair_part.shape[0] // 2 :], b)
-    pair_part = pair_part[: pair_came.shape[0]].astype(F32) + pair_came.astype(F32)
     key_value_grad = pair_part.reshape(D // expert_count, 2, -1).transpose(1, 0, 2)
     ffn_out = sums_of(ffn_back, token_matrix(ffn_slots, 2 * CAP + NOTES, CAP))
     mixed = (state + ffn_out).astype(BF16)

time: 858 us -> 844 us (0.984)
  Pallas kernels: 694 us -> 670 us
  waiting for transfers between devices: 0.03 us -> 11 us
    pallas_call x1, Pallas kernels: 26.7 us -> 11.2 us  [small_sums(): pl.pallas_call(functools.partial(small_kernel, experts, tensor), out_shap...]
    ppermute x2 -> x3, waiting for transfers between devices: 0.01 us -> 10.9 us  [exchange(): lax.ppermute(away, 'expert', [(i, i ^ 1 << b) for i in range(expert_count)])]
  transfers between devices with their start and end apart: 4 -> 5, of which waited for: 0 -> 1; matrix products, arithmetic and copies ran while one was open for 9% -> 9% of each run, Pallas kernels for 3% -> 1%
where the time goes in v5:
time: 844 us; the launch traced here: 835 us
  Pallas kernels  670 us (79%)
  matrix products  61.6 us (7%)
  other arithmetic  33.9 us (4%)
  local copies, waits for them, and re-layouts  17.1 us (2%)
  between operations  14.8 us (2%)
  starting transfers between devices  14.3 us (2%)
  blocking collectives  11.6 us (1%)
  waiting for transfers between devices  11 us (1%)
    pallas_call x1, Pallas kernels, front(): pl.pallas_call(functools.partial(front_kernel, experts, bits), out_shape=...  191 us
    pallas_call x2, Pallas kernels, scatter_rows(): pl.pallas_call(functools.partial(scatter_kernel, experts, bits, windows i...  184 us
    pallas_call x1, Pallas kernels, feed_forward(): pl.pallas_call(functools.partial(ffn_kernel, experts, bits, experts // EX...  165 us
    pallas_call x1, Pallas kernels, gather_rows(): pl.pallas_call(functools.partial(gather_kernel, experts, bits, near, mult...  70.4 us
    dot_general x15, matrix products, dot(): lax.dot_general(left, right, ((dims[0], dims[1]), ((), ())), preferred_el...  61.6 us
    pallas_call x1, Pallas kernels, attend_back(): pl.pallas_call(functools.partial(attend_back_kernel, experts), out_shape=...  48.7 us
  transfers between devices with their start and end apart: 5, of which 1 were waited for; matrix products, arithmetic and copies ran while one was open for 9% of the time, Pallas kernels for 1%

profile of v5, /device:TPU:0, one launch (start us, length us, event | category | flops | bytes accessed | tf_op | source)
XLA Modules:
  0.0 834.8 jit_solution(2001108253810356826)
XLA Ops:
  7.2 1.3 broadcast_in_dim.36.refs_1_
  8.5 0.7 multiply_bitcast_fusion
  9.2 0.7 copy.53
  9.9 0.5 convert_reduce_fusion
  10.4 0.7 multiply_bitcast_fusion.1
  11.1 0.7 copy.51
  11.8 0.5 convert_reduce_fusion.1
  12.3 1.3 pad_add_fusion.1.refs_3_
  13.6 1.3 concatenate.13
  15.0 0.6 pad_add_fusion.refs_2_
  15.6 191.1 %shard_map.221 = (bf16[8,160,2048]{2,1,0:T(8,128)(2,1)}, bf16[2048,512]{1,0:T(8,128)(2,1)}, bf16[3,512,2048]{2,1,0:T(8,128)(2,1)}, bf16[2,2048,512]{2,1,0:T(8,12...) custom-call(bf16[512,2048]{1,0:T(8,128)(2,1)} %refs_0_.1, ...), custom_call_target="tpu_custom_call" | custom-call | flops 99999997952 | bytes 10000000 | tf_op jit(solution)/shard_map/pallas_call | solution.py:644
  206.8 0.6 broadcast_add_fusion
  207.4 1.9 iota_compare_fusion.7
  209.3 0.8 dynamic-slice_convert_fusion.1
  210.0 70.1 %shard_map.222 = (bf16[8,160,512]{2,1,0:T(8,128)(2,1)}, bf16[8,160,512]{2,1,0:T(8,128)(2,1)}) custom-call(bf16[8,160,512]{2,1,0:T(8,128)(2,1)} %bitcast.177, bf16[2048,512]{1,0:T(8,128)(2,1)} %get-tuple-element.70.refs_1_, f32[8,160,1]{2,1,0:T(8,128)} %get-tuple-element.71.refs_2_), custom_call_target="tpu_custom_call" | custom-call | flops 99999997952 | bytes 10000000 | tf_op jit(solution)/shard_map/pallas_call | solution.py:949
  280.1 2.4 multiply_reduce_fusion.3
  282.6 5.7 psum.14
  288.3 0.6 fusion.79
  288.9 1.0 multiply_convert_fusion.refs_0_
  289.9 165.0 %shard_map.223 = (bf16[8,336,512]{2,1,0:T(8,128)(2,1)}, bf16[1280,2048]{1,0:T(8,128)(2,1)}, bf16[1280,2048]{1,0:T(8,128)(2,1)}, bf16[1280,1408]{1,0:T(8,128)(2,1...) custom-call(bf16[512,512]{1,0:T(8,128)(2,1)} %multiply_convert_fusion.refs_0_, bf16[512,2048]{1,0:T(8,128)(2,1)} %refs_1_, ...), custom_call_target="tpu_custom_call" | custom-call | flops 99999997952 | bytes 10000000 | tf_op jit(solution)/shard_map/pallas_call | solution.py:1300
  454.9 0.8 slice_bitcast_fusion
  455.8 2.1 fusion.86
  458.1 3.6 fusion.4
  461.7 0.3 convolution_add_fusion.1
  462.1 2.5 convolution_convert_fusion
  464.7 70.4 %shard_map.224 = (bf16[8,160,2048]{2,1,0:T(8,128)(2,1)}, bf16[8,160,512]{2,1,0:T(8,128)(2,1)S(1)}, bf16[8,160,512]{2,1,0:T(8,128)(2,1)S(1)}, bf16[8,256,512]{2,1,0:T(8,128)(2,1)}) custom-call(bf16[8,160,512]{2,1,0:T(8,128)(2,1)S(1)} %bitcast.128, bf16[2048,512]{1,0:T(8,128)(2,1)} %get-tuple-element.70.refs_1_, f32[8,160,1]{2,1,0:T(8,128)S(1)} %copy-done.2, ...), custom_call_target="tpu_custom_call" | custom-call | flops 99999997952 | bytes 10000000 | tf_op jit(solution)/shard_map/pallas_call | solution.py:199
  535.1 0.4 multiply_reduce_fusion.1
  535.6 0.6 copy-done.1
  536.2 0.7 pad.5.refs_2_
  536.9 48.7 %shard_map.225 = (bf16[1280,512]{1,0:T(8,128)(2,1)}, bf16[1536,512]{1,0:T(8,128)(2,1)}, bf16[1536,512]{1,0:T(8,128)(2,1)}, bf16[8,256,512]{2,1,0:T(8,128)(2,1)}) custom-call(s32[1,1024]{1,0:T(1,128)} %bitcast.138, bf16[1280,512]{1,0:T(8,128)(2,1)} %bitcast.127, bf16[1024,512]{1,0:T(8,128)(2,1)} %get-tuple-element.81.refs_2_, ...), custom_call_target="tpu_custom_call" | custom-call | flops 99999997952 | bytes 10000000 | tf_op jit(solution)/shard_map/pallas_call | solution.py:341
  585.6 114.0 %shard_map.226 = (bf16[8,176,512]{2,1,0:T(8,128)(2,1)}, bf16[8,160,512]{2,1,0:T(8,128)(2,1)}, bf16[512,512]{1,0:T(8,128)(2,1)}, bf16[8,256,512]{2,1,0:T(8,128)(2...) custom-call(bf16[8,160,512]{2,1,0:T(8,128)(2,1)} %bitcast.178, bf16[2048,512]{1,0:T(8,128)(2,1)} %get-tuple-element.87.refs_1_, ...), custom_call_target="tpu_custom_call" | custom-call | flops 99999997952 | bytes 10000000 | tf_op jit(solution)/shard_map/pallas_call | solution.py:949
  699.6 3.2 add_convert_fusion
  702.8 1.0 fusion.78
  703.8 0.7 collective-permute-start.1
  704.5 6.1 collective-permute-start
  710.5 4.7 all-to-all-start
  715.4 2.2 multiply_reduce_fusion
  717.6 2.2 fusion.16
  719.9 0.8 dynamic-slice_convert_fusion
  720.6 14.1 %fusion.87 = f32[2048,1408]{1,0:T(8,128)} fusion(bf16[1280,2048]{1,0:T(8,128)(2,1)} %get-tuple-element.103, bf16[1280,1408]{1,0:T(8,128)(2,1)} %get-tuple-element.104), kind=kOutput, calls=%fused_computation.143 | convolution fusion | flops 7381975040 | bytes 20381696 | tf_op jit(solution)/shard_map/dot_general | solution.py:1409
  734.7 11.4 %fusion.88 = f32[2048,1408]{1,0:T(8,128)} fusion(bf16[1280,2048]{1,0:T(8,128)(2,1)S(1)} %bitcast.181, bf16[1280,1408]{1,0:T(8,128)(2,1)S(1)} %copy-done.28), kind=kOutput, calls=%fused_computation.144 | convolution fusion | flops 7381975040 | bytes 20381696 | tf_op jit(solution)/shard_map/dot_general | solution.py:1409
  746.2 0.8 iota_compare_fusion.6
  747.0 1.4 pad_maximum_fusion
  748.5 1.4 add_convert_fusion.1
  749.9 12.5 %fusion.89 = f32[1408,2048]{1,0:T(8,128)} fusion(bf16[1280,1408]{1,0:T(8,128)(2,1)S(1)} %copy-done.26, bf16[1280,2048]{1,0:T(8,128)(2,1)} %get-tuple-element.109), kind=kOutput, calls=%fused_computation.145 | convolution fusion | flops 7381975040 | bytes 20381696 | tf_op jit(solution)/shard_map/dot_general | solution.py:1409
  762.4 0.8 slice_reduce_fusion
  763.2 0.8 fusion.90
  764.1 2.5 fusion.25
  766.7 2.2 fusion.45
  768.9 6.0 psum.15
  774.9 3.7 multiply_reduce_fusion.2
  778.7 2.8 collective-permute-start.2
  781.5 4.6 fusion.35
  786.1 2.2 slice.86
  788.3 0.3 copy-done.8
  788.7 2.6 convert_element_type.161
  791.6 1.8 concatenate.15.part
  793.5 10.9 %collective-permute-done.2 = bf16[256,1024]{1,0:T(8,128)(2,1)S(1)} collective-permute-done((bf16[256,1024]{1,0:T(8,128)(2,1)S(1)}, bf16[256,1024]{1,0:T(8,128)(2,1)S(1)}, u32[]{:S(2)}, u32[]{:S(2)}) %collective-permute-start.2) | collective-permute-done | bytes 524320 | tf_op jit(solution)/shard_map/ppermute | solution.py:1544
  804.6 11.2 %shard_map.227 = f32[24,256]{1,0:T(8,128)} custom-call(f32[24,512]{1,0:T(8,128)} %concatenate.15.part), custom_call_target="tpu_custom_call" | custom-call | flops 10000000000 | bytes 100000 | tf_op jit(solution)/shard_map/pallas_call | solution.py:1396
  815.8 1.3 slice.96
  817.1 1.1 copy.68
  818.1 1.3 fusion.80
  819.5 4.1 convert_element_type.157
  823.6 4.2 convert_element_type.160
  (102 shorter events, 1.4 us)
Async XLA Ops:
  14.9 192.5 %copy-start.18 = (s32[1024]{0:T(1024)}, s32[1024]{0:T(1024)S(1)}, u32[]{:S(2)}) copy-start(s32[1024]{0:T(1024)S(1)} %get-tuple-element.73) | copy-start | bytes 12292
  14.9 194.3 %copy-start.14 = (s32[1024]{0:T(1024)}, s32[1024]{0:T(1024)S(1)}, u32[]{:S(2)}) copy-start(s32[1024]{0:T(1024)S(1)} %get-tuple-element.68) | copy-start | bytes 12292
  210.0 252.0 %copy-start.19 = (f32[512]{0:T(512)}, f32[512]{0:T(512)S(1)}, u32[]{:S(2)}) copy-start(f32[512]{0:T(512)S(1)} %dynamic-slice_convert_fusion.1) | copy-start | bytes 6148
  280.1 8.2 copy-start.16
  282.5 6.3 copy-start.6
  288.2 173.8 %copy-start.21 = (f32[512,1]{0,1:T(1,128)}, f32[512,1]{0,1:T(1,128)S(1)}, u32[]{:S(2)}) copy-start(f32[512,1]{0,1:T(1,128)S(1)} %add_rsqrt_fusion.1) | copy-start | bytes 6148
  289.9 168.1 %copy-start.12 = (s32[512,2]{0,1:T(2,128)S(1)}, s32[512,2]{0,1:T(2,128)}, u32[]{:S(2)}) copy-start(s32[512,2]{0,1:T(2,128)} %param.17) | copy-start | bytes 12292
  458.0 3.7 copy-start.10
  458.1 4.0 copy-start.24
  458.1 4.0 copy-start.7
  462.1 2.6 copy-start.5
  462.1 2.6 copy-start
  462.1 2.6 copy-start.2
  535.1 1.1 copy-start.1
  703.8 43.2 %collective-permute-start.1 = (bf16[512,512]{1,0:T(8,128)(2,1)}, bf16[512,512]{1,0:T(8,128)(2,1)}, u32[]{:S(2)}, u32[]{:S(2)}) collective-permute-start(bf16[512,512]{1,0:T(8,128)(2,1)} %get-tuple-element.134), channel_id=1, source_target_pairs={{0,4},{4,0},{8,12},{12,8},{16,20},{20,16},{24,28},{28,24},{1,5},{5... | collective-permute-start | bytes 1572872 | tf_op jit(solution)/shard_map/ppermute | solution.py:1544
  704.5 13.1 %copy-start.15 = (s32[1024]{0:T(1024)S(1)}, s32[1024]{0:T(1024)}, u32[]{:S(2)}) copy-start(s32[1024]{0:T(1024)} %copy-done.14) | copy-start | bytes 12292
  704.5 13.1 %copy-start.17 = (bf16[2048,16]{0,1:T(8,128)(2,1)S(1)}, bf16[2048,16]{0,1:T(8,128)(2,1)}, u32[]{:S(2)}) copy-start(bf16[2048,16]{0,1:T(8,128)(2,1)} %param.20) | copy-start | bytes 196612
  704.5 42.5 %collective-permute-start = (bf16[512,512]{1,0:T(8,128)(2,1)}, bf16[512,512]{1,0:T(8,128)(2,1)}, u32[]{:S(2)}, u32[]{:S(2)}) collective-permute-start(bf16[512,512]{1,0:T(8,128)(2,1)} %get-tuple-element.133), channel_id=1, source_target_pairs={{0,8},{4,12},{8,0},{12,4},{16,24},{20,28},{24,16},{28,20},{1,9},{5... | collective-permute-start | bytes 1572872 | tf_op jit(solution)/shard_map/ppermute | solution.py:1544
  710.5 113.1 %all-to-all-start = ((bf16[8,256,512]{2,1,0:T(8,128)(2,1)}), bf16[8,256,512]{2,1,0:T(8,128)(2,1)}, u32[]{:S(2)}, u32[]{:S(2)}) async-start(bf16[8,256,512]{2,1,0:T(8,128)(2,1)} %get-tuple-element.115), calls=%async_computation | async-start | bytes 4194304 | tf_op jit(solution)/shard_map/all_to_all | solution.py:1425
  715.3 104.2 %all-gather.2.cloned.1.call-start = ((), (), s32[]{:S(2)}) async-start(), calls=%async_computation.1 | async-start | bytes 2621440 | tf_op jit(solution)/shard_map/all_gather | solution.py:1429
  715.3 19.4 %slice-start = ((s8[5242880]{0:T(1024)(128)(4,1)}), s8[4194304]{0:T(1024)(128)(4,1)S(1)}, s32[]{:S(2)}) async-start(s8[5242880]{0:T(1024)(128)(4,1)} %bitcast.180), calls=%async_computation.2 | async-start | bytes 8388608
  720.6 14.1 %slice-start.1 = ((s8[5242880]{0:T(1024)(128)(4,1)}), s8[1048576]{0:T(1024)(128)(4,1)S(1)}, s32[]{:S(2)}) async-start(s8[5242880]{0:T(1024)(128)(4,1)} %bitcast.180), calls=%async_computation.3 | async-start | bytes 2097152
  720.6 14.1 %copy-start.28 = (bf16[1280,1408]{1,0:T(8,128)(2,1)S(1)}, bf16[1280,1408]{1,0:T(8,128)(2,1)}, u32[]{:S(2)}) copy-start(bf16[1280,1408]{1,0:T(8,128)(2,1)} %get-tuple-element.105) | copy-start | bytes 10813444
  734.7 11.4 %copy-start.13 = (s32[512,2]{0,1:T(2,128)S(1)}, s32[512,2]{0,1:T(2,128)}, u32[]{:S(2)}) copy-start(s32[512,2]{0,1:T(2,128)} %param.16) | copy-start | bytes 12292
  747.0 2.9 copy-start.26
  749.9 14.3 %copy-start.27 = (bf16[512,512]{1,0:T(8,128)(2,1)S(1)}, bf16[512,512]{1,0:T(8,128)(2,1)}, u32[]{:S(2)}) copy-start(bf16[512,512]{1,0:T(8,128)(2,1)} %get-tuple-element.111) | copy-start | bytes 1572868
  764.1 2.6 copy-start.3
  766.7 8.2 copy-start.20
  766.7 8.2 copy-start.22
  766.7 8.2 copy-start.25
  774.9 3.8 copy-start.23
  774.9 3.8 copy-start.4
  778.7 25.7 %collective-permute-start.2 = (bf16[256,1024]{1,0:T(8,128)(2,1)S(1)}, bf16[256,1024]{1,0:T(8,128)(2,1)S(1)}, u32[]{:S(2)}, u32[]{:S(2)}) collective-permute-start(bf16[256,1024]{1,0:T(8,128)(2,1)S(1)} %slice.90), channel_id=1, source_target_pairs={{0,16},{4,20},{8,24},{12,28},{16,0},{20,4},{24,8},{28,12},{1,17},{... | collective-permute-start | bytes 1572872 | tf_op jit(solution)/shard_map/ppermute | solution.py:1544
  786.1 2.6 copy-start.8
  788.7 2.6 copy-start.9
  788.7 2.6 copy-start.11
Sparse Core Ops, SparseCore 0:
  778.8 22.9 all-gather.1

commit v6 on v5

--- a/solution.py
+++ b/solution.py
@@ -217,9 +217,14 @@
 def mask_bias(segments, bias):
     blocks, span, _ = bias.shape
     here = blocks * Q_ROWS
-    e = lax.axis_index("expert")
-    query_ids = segments[:, pl.ds(pl.multiple_of(e * here + WINDOW, 128), here)]
-    key_row = segments[:, pl.ds(pl.multiple_of(e * here, 128), WINDOW + here)].astype(F32)
+    e, experts = lax.axis_index("expert"), lax.axis_size("expert")
+    parts = []
+    for back in range(WINDOW // here, -1, -1):
+        device = lax.rem(e + experts - back, experts)
+        part = segments[:, pl.ds(pl.multiple_of(device * here, 128), here)]
+        parts.append(jnp.where(e >= back, part, -1))
+    query_ids = parts[-1]
+    key_row = jnp.concatenate(parts, axis=1).astype(F32)
     key_ids = jnp.concatenate([key_row, jnp.zeros((7, WINDOW + here), F32)], axis=0).T[:, 0:1].astype(jnp.int32)
 
     for block in range(blocks):
@@ -368,8 +373,8 @@
 
 
 def front_kernel(experts, bits, *refs):
-    (tokens, gain, slots, routes, routers, segments, w_in, kv_in, wo_in,
-     rows, w, window, kv, keys, values, gates, facts_in, grouped, queries, lse, wo,
+    (tokens, gain, slots, routes, next_routes, routers, segments, w_in, kv_in, wo_in,
+     rows, w, window, kv, keys, values, gates, facts_in, grouped, queries, lse, gate_row, rate_out, wo,
      back, x, y, facts, spread, gathered, bias, packed, heads,
      f_send, f_recv, v_send, v_recv, z_send, z_recv, t_send, t_recv, y_send, y_recv, w_send, w_recv, k_send, k_recv, n_send, n_recv, own_sem) = refs
     e, t = lax.axis_index("expert"), lax.axis_index("tensor")
@@ -451,6 +456,7 @@
 
     state = tokens[...].astype(F32)
     rate = lax.rsqrt(jnp.mean(state * state, axis=1, keepdims=True) + eps)
+    rate_out[...] = rate
     window[2] = (state * rate * gain[...].astype(F32)).astype(BF16)
 
     @pl.when(e < experts - 2)
@@ -483,7 +489,8 @@
     top = jnp.maximum(first, second)
     first, second = jnp.exp(first - top), jnp.exp(second - top)
     gate = jnp.concatenate([first / (first + second), second / (first + second)], axis=1)
-    other = jnp.concatenate([routes[3:4, :], routes[2:3, :]], axis=1).astype(F32)
+    gate_row[...] = gate
+    other = jnp.concatenate([next_routes[1:2, :], next_routes[0:1, :]], axis=1).astype(F32)
     high = gate.astype(BF16).astype(F32)
     middle = (gate - high).astype(BF16).astype(F32)
     empty = jnp.zeros((13, 2 * here), F32)
@@ -621,7 +628,7 @@
             passed(j, d).wait_send()
 
 
-def front(tokens, gain, slots, routes, routers, segments, w, kv, wo, collective_id):
+def front(tokens, gain, slots, routes, next_routes, routers, segments, w, kv, wo, collective_id):
     experts, tensor = lax.axis_size("expert"), lax.axis_size("tensor")
     bits = tensor.bit_length() - 1
     here = tokens.shape[0]
@@ -639,13 +646,15 @@
         ((SLOTS, f_kv), BF16),
         ((TOPK * here, f_kv), BF16),
         ((f_kv // HD, 1, TOPK * here), F32),
+        ((1, TOPK * here), F32),
+        ((here, 1), F32),
         ((D, f), BF16),
     ]
     return pl.pallas_call(
         functools.partial(front_kernel, experts, bits),
         out_shape=[jax.ShapeDtypeStruct(*out) for out in outs],
-        in_specs=[VMEM] * 6 + [ANY] * 3,
-        out_specs=[VMEM] * 11 + [ANY],
+        in_specs=[VMEM] * 7 + [ANY] * 3,
+        out_specs=[VMEM] * 13 + [ANY],
         scratch_shapes=[
             pltpu.VMEM((experts, CAP, f), BF16),
             pltpu.VMEM((SLOTS, D // tensor), BF16),
@@ -661,7 +670,7 @@
         compiler_params=pltpu.CompilerParams(
             collective_id=collective_id, has_side_effects=True, vmem_limit_bytes=63 * 2**20),
         cost_estimate=pl.CostEstimate(flops=10**11, bytes_accessed=10**7, transcendentals=0),
-    )(tokens, gain, slots, routes, routers, segments, w, kv, wo)
+    )(tokens, gain, slots, routes, next_routes, routers, segments, w, kv, wo)
 
 
 def scatter_kernel(experts, bits, depth, near, scale, noted, *refs):
@@ -1472,11 +1481,6 @@
     return jnp.repeat(rows, pieces, axis=0) if pieces > 1 else rows
 
 
-def pick_gates(logits, routes):
-    one_hot = (routes[:, :, None] == jnp.arange(EXPERTS, dtype=jnp.int32)[None, None, :]).astype(F32)
-    return jax.nn.softmax(jnp.sum(one_hot * logits[:, None, :], axis=2), axis=-1)
-
-
 def gate_back(gating, pulled, routes):
     inner_sum = gating * (pulled - jnp.sum(gating * pulled, axis=1, keepdims=True))
     one_hot = (routes[:, :, None] == jnp.arange(EXPERTS, dtype=jnp.int32)[None, None, :]).astype(F32)
@@ -1546,22 +1550,22 @@
     attn_slots, ffn_slots = slot_numbers(attn_routes), slot_numbers(ffn_routes)
 
     slots = jnp.stack([attn_slots, ffn_slots, spaced(attn_slots, 256), spaced(ffn_slots, 256)])
-    segments = jnp.concatenate([jnp.full((WINDOW,), -1, jnp.int32), segment_ids])[None]
+    segments = segment_ids[None]
     (rows_one, query_map, window, pair_map, keys, values, attn_gate_blocks, facts, heads, queries, log_total,
-     output_map) = front(
-        tokens, attn_gain[None], slots, jnp.concatenate([attn_routes.T, ffn_routes.T]), routers.T, segments,
+     gate_row, rate_one, output_map) = front(
+        tokens, attn_gain[None], slots, attn_routes.T, ffn_routes.T, routers.T, segments,
         to_pieces(query_weight, pieces), key_value_weight, to_pieces(output_weight, pieces), collective_id=0)
     rows_one, attn_slots, ffn_slots, tokens, attn_gain, ffn_gain, routers, cotangent = lax.optimization_barrier(
         (rows_one, attn_slots, ffn_slots, tokens, attn_gain, ffn_gain, routers, cotangent))
     routers_one, routers_two = routers[:, :EXPERTS], routers[:, EXPERTS:]
-    state_in = tokens.astype(F32)
     gain_one = attn_gain.astype(F32)
     gain_two = cols(ffn_gain.astype(F32))
     dy_cols = cols(cotangent)
     token_cols = cols(tokens).astype(F32)
     attn_places, ffn_places = place_matrix(attn_slots), place_matrix(ffn_slots)
     rows_one = rows_one.reshape(-1, D)
-    normed_one = window[2]
+    normed_cols = lax.dynamic_slice(
+        window, (2, 0, tensor_index * column_count), (1, rows_here, column_count)).reshape(rows_here, column_count)
     window = window.reshape(-1, D)
     attn_back, heads_rows = scatter_rows(
         to_pieces(heads.reshape(EXPERTS, CAP, -1), pieces), output_map, attn_gate_blocks, collective_id=1)
@@ -1621,12 +1625,11 @@
     normed_back, owed, down_grad = lax.optimization_barrier((normed_back, owed, down_grad))
     normed_grad = sums_of(normed_back, token_matrix(attn_slots, CAP + NOTES)) + owed.astype(F32)
     attn_pull = read_notes(normed_back, attn_places, 1)[:, :, 0].T
-    attn_gates = pick_gates(mm(normed_one, routers_one), attn_routes)
+    attn_gates = gate_row.reshape(TOPK, rows_here).T
     attn_logit_grad = gate_back(attn_gates, attn_pull, attn_routes)
     normed_grad = normed_grad + mm_nt(
         attn_logit_grad, lax.dynamic_slice_in_dim(routers_one, tensor_index * column_count, column_count, 0))
-    attn_router_cols = mm_tn(cols(normed_one), attn_logit_grad)
-    rate_one = lax.rsqrt(jnp.mean(state_in * state_in, axis=1, keepdims=True) + eps)
+    attn_router_cols = mm_tn(normed_cols, attn_logit_grad)
     attn_gain_cols = jnp.sum(normed_grad * token_cols * rate_one, axis=0)
     ahead_one = normed_grad * cols(gain_one)
     centre_one = jnp.sum(ahead_one * token_cols, axis=1, keepdims=True)
@@ -1637,9 +1640,9 @@
     small = jnp.concatenate(
         [attn_router_cols.T, ffn_router_cols.T, attn_gain_cols[None], ffn_gain_cols[None],
          jnp.zeros((6, column_count), F32)], axis=0)
-    small, pair_part = lax.optimization_barrier((small, pair_part))
+    query_grad = from_pieces(query_grad, pieces).astype(F32)
+    small, pair_part, query_grad, tokens_grad = lax.optimization_barrier((small, pair_part, query_grad, tokens_grad))
     small = small_sums(small, collective_id=3).T
-    query_grad = from_pieces(query_grad, pieces).astype(F32)
     key_value_grad = pair_part.reshape(D // expert_count, 2, -1).transpose(1, 0, 2)
     ffn_out = sums_of(ffn_back, token_matrix(ffn_slots, 2 * CAP + NOTES, CAP))
     mixed = (state + ffn_out).astype(BF16)

time: 844 us -> 837 us (level)
    dot_general x15 -> x14, matrix products: 61.6 us -> 60.5 us  [dot(): lax.dot_general(left, right, ((dims[0], dims[1]), ((), ())), preferred_el...]
  transfers between devices with their start and end apart: 5 -> 5, of which waited for: 1 -> 1; matrix products, arithmetic and copies ran while one was open for 9% -> 8% of each run, Pallas kernels for 1% -> 0%
where the time goes in v6:
time: 837 us; the launch traced here: 827 us
  Pallas kernels  670 us (80%)
  matrix products  60.5 us (7%)
  other arithmetic  30.6 us (4%)
  between operations  14.9 us (2%)
  starting transfers between devices  14.2 us (2%)
  local copies, waits for them, and re-layouts  13 us (2%)
  waiting for transfers between devices  12.7 us (2%)
  blocking collectives  11.3 us (1%)
    pallas_call x1, Pallas kernels, front(): pl.pallas_call(functools.partial(front_kernel, experts, bits), out_shape=...  191 us
    pallas_call x2, Pallas kernels, scatter_rows(): pl.pallas_call(functools.partial(scatter_kernel, experts, bits, windows i...  184 us
    pallas_call x1, Pallas kernels, feed_forward(): pl.pallas_call(functools.partial(ffn_kernel, experts, bits, experts // EX...  165 us
    pallas_call x1, Pallas kernels, gather_rows(): pl.pallas_call(functools.partial(gather_kernel, experts, bits, near, mult...  70.5 us
    dot_general x14, matrix products, dot(): lax.dot_general(left, right, ((dims[0], dims[1]), ((), ())), preferred_el...  60.5 us
    pallas_call x1, Pallas kernels, attend_back(): pl.pallas_call(functools.partial(attend_back_kernel, experts), out_shape=...  48.7 us
  transfers between devices with their start and end apart: 5, of which 1 were waited for; matrix products, arithmetic and copies ran while one was open for 8% of the time, Pallas kernels for 0%

profile of v6, /device:TPU:0, one launch (start us, length us, event | category | flops | bytes accessed | tf_op | source)
XLA Modules:
  0.0 827.4 jit_solution(2447667115712101008)
XLA Ops:
  7.2 1.3 broadcast_in_dim.36.refs_1_
  8.5 0.7 multiply_bitcast_fusion
  9.2 0.7 copy.53
  9.9 0.5 convert_reduce_fusion
  10.4 0.7 multiply_bitcast_fusion.1
  11.1 0.7 copy.51
  11.8 0.5 convert_reduce_fusion.1
  12.4 0.6 pad_add_fusion.refs_2_
  13.0 191.0 %shard_map.221 = (bf16[8,160,2048]{2,1,0:T(8,128)(2,1)}, bf16[2048,512]{1,0:T(8,128)(2,1)}, bf16[3,512,2048]{2,1,0:T(8,128)(2,1)}, bf16[2,2048,512]{2,1,0:T(8,12...) custom-call(bf16[512,2048]{1,0:T(8,128)(2,1)} %refs_0_.1, ...), custom_call_target="tpu_custom_call" | custom-call | flops 99999997952 | bytes 10000000 | tf_op jit(solution)/shard_map/pallas_call | solution.py:653
  204.0 0.6 broadcast_add_fusion
  204.6 1.9 iota_compare_fusion.6
  206.5 0.8 dynamic-slice_convert_fusion.1
  207.3 70.1 %shard_map.222 = (bf16[8,160,512]{2,1,0:T(8,128)(2,1)}, bf16[8,160,512]{2,1,0:T(8,128)(2,1)}) custom-call(bf16[8,160,512]{2,1,0:T(8,128)(2,1)} %bitcast.177, bf16[2048,512]{1,0:T(8,128)(2,1)} %get-tuple-element.74.refs_1_, f32[8,160,1]{2,1,0:T(8,128)} %get-tuple-element.75.refs_2_), custom_call_target="tpu_custom_call" | custom-call | flops 99999997952 | bytes 10000000 | tf_op jit(solution)/shard_map/pallas_call | solution.py:958
  277.4 2.4 multiply_reduce_fusion.2
  279.8 5.7 psum.14
  285.5 0.6 fusion.73
  286.1 0.9 multiply_convert_fusion.refs_0_
  287.1 164.9 %shard_map.223 = (bf16[8,336,512]{2,1,0:T(8,128)(2,1)}, bf16[1280,2048]{1,0:T(8,128)(2,1)}, bf16[1280,2048]{1,0:T(8,128)(2,1)}, bf16[1280,1408]{1,0:T(8,128)(2,1...) custom-call(bf16[512,512]{1,0:T(8,128)(2,1)} %multiply_convert_fusion.refs_0_, bf16[512,2048]{1,0:T(8,128)(2,1)} %refs_1_, ...), custom_call_target="tpu_custom_call" | custom-call | flops 99999997952 | bytes 10000000 | tf_op jit(solution)/shard_map/pallas_call | solution.py:1309
  452.0 0.8 slice_bitcast_fusion
  452.8 0.1 reshape.290
  452.9 2.1 fusion.80
  455.2 3.6 fusion.4
  458.8 0.3 convolution_add_fusion.1
  459.2 2.5 convolution_convert_fusion
  461.8 70.5 %shard_map.224 = (bf16[8,160,2048]{2,1,0:T(8,128)(2,1)}, bf16[8,160,512]{2,1,0:T(8,128)(2,1)S(1)}, bf16[8,160,512]{2,1,0:T(8,128)(2,1)S(1)}, bf16[8,256,512]{2,1,0:T(8,128)(2,1)}) custom-call(bf16[8,160,512]{2,1,0:T(8,128)(2,1)S(1)} %bitcast.128, bf16[2048,512]{1,0:T(8,128)(2,1)} %get-tuple-element.74.refs_1_, f32[8,160,1]{2,1,0:T(8,128)S(1)} %copy-done.2, ...), custom_call_target="tpu_custom_call" | custom-call | flops 99999997952 | bytes 10000000 | tf_op jit(solution)/shard_map/pallas_call | solution.py:199
  532.3 0.4 multiply_reduce_fusion
  532.7 0.6 copy-done.1
  533.3 0.7 pad.4.refs_2_
  534.1 48.7 %shard_map.225 = (bf16[1280,512]{1,0:T(8,128)(2,1)}, bf16[1536,512]{1,0:T(8,128)(2,1)}, bf16[1536,512]{1,0:T(8,128)(2,1)}, bf16[8,256,512]{2,1,0:T(8,128)(2,1)}) custom-call(s32[1,1024]{1,0:T(1,128)} %bitcast.133, bf16[1280,512]{1,0:T(8,128)(2,1)} %bitcast.127, bf16[1024,512]{1,0:T(8,128)(2,1)} %get-tuple-element.86.refs_2_, ...), custom_call_target="tpu_custom_call" | custom-call | flops 99999997952 | bytes 10000000 | tf_op jit(solution)/shard_map/pallas_call | solution.py:346
  582.8 113.9 %shard_map.226 = (bf16[8,176,512]{2,1,0:T(8,128)(2,1)}, bf16[8,160,512]{2,1,0:T(8,128)(2,1)}, bf16[512,512]{1,0:T(8,128)(2,1)}, bf16[8,256,512]{2,1,0:T(8,128)(2...) custom-call(bf16[8,160,512]{2,1,0:T(8,128)(2,1)} %bitcast.178, bf16[2048,512]{1,0:T(8,128)(2,1)} %get-tuple-element.92.refs_1_, ...), custom_call_target="tpu_custom_call" | custom-call | flops 99999997952 | bytes 10000000 | tf_op jit(solution)/shard_map/pallas_call | solution.py:958
  696.7 3.2 add_convert_fusion
  699.9 1.0 fusion.72
  700.9 0.7 collective-permute-start.1
  701.6 6.1 collective-permute-start
  707.7 4.6 all-to-all-start
  712.3 0.5 broadcast.216
  712.8 0.7 reduce.7
  713.5 14.1 %fusion.81 = f32[2048,1408]{1,0:T(8,128)} fusion(bf16[1280,2048]{1,0:T(8,128)(2,1)} %get-tuple-element.108, bf16[1280,1408]{1,0:T(8,128)(2,1)} %get-tuple-element.109), kind=kOutput, calls=%fused_computation.133 | convolution fusion | flops 7381975040 | bytes 20381696 | tf_op jit(solution)/shard_map/dot_general | solution.py:1418
  727.6 13.1 %fusion.82 = f32[2048,1408]{1,0:T(8,128)} fusion(bf16[1280,2048]{1,0:T(8,128)(2,1)} %get-tuple-element.108, bf16[1280,1408]{1,0:T(8,128)(2,1)S(1)} %copy-done.30), kind=kOutput, calls=%fused_computation.134 | convolution fusion | flops 7381975040 | bytes 20381696 | tf_op jit(solution)/shard_map/dot_general | solution.py:1418
  740.7 0.8 dynamic-slice_convert_fusion
  741.4 0.1 reduce.3
  741.6 0.8 iota_compare_fusion.7
  742.4 1.4 pad_maximum_fusion
  743.9 1.4 add_convert_fusion.1
  745.3 12.8 %fusion.83 = f32[1408,2048]{1,0:T(8,128)} fusion(bf16[1280,1408]{1,0:T(8,128)(2,1)S(1)} %copy-done.28, bf16[1280,2048]{1,0:T(8,128)(2,1)} %get-tuple-element.114), kind=kOutput, calls=%fused_computation.135 | convolution fusion | flops 7381975040 | bytes 20381696 | tf_op jit(solution)/shard_map/dot_general | solution.py:1418
  758.2 0.8 fusion.84
  759.0 1.0 fusion.23
  760.1 1.7 fusion.43
  761.8 5.7 psum.15
  767.5 3.3 fusion.42
  770.9 2.8 collective-permute-start.2
  773.7 4.7 fusion.33
  778.4 2.6 convert_element_type.156
  781.0 0.2 fusion.85
  781.2 1.2 fusion.44
  782.4 1.8 concatenate.7.part
  784.3 12.6 %collective-permute-done.2 = bf16[256,1024]{1,0:T(8,128)(2,1)S(1)} collective-permute-done((bf16[256,1024]{1,0:T(8,128)(2,1)S(1)}, bf16[256,1024]{1,0:T(8,128)(2,1)S(1)}, u32[]{:S(2)}, u32[]{:S(2)}) %collective-permute-start.2) | collective-permute-done | bytes 524320 | tf_op jit(solution)/shard_map/ppermute | solution.py:1548
  796.9 0.2 convert_add_fusion.1
  797.1 4.2 convert_element_type.152
  801.3 4.1 convert_element_type.155
  805.4 11.2 %shard_map.227 = f32[24,256]{1,0:T(8,128)} custom-call(f32[24,512]{1,0:T(8,128)} %concatenate.7.part), custom_call_target="tpu_custom_call" | custom-call | flops 10000000000 | bytes 100000 | tf_op jit(solution)/shard_map/pallas_call | solution.py:1405
  816.6 1.3 fusion.74
  817.9 1.3 slice.92
  819.3 1.1 copy.68
  (96 shorter events, 0.7 us)
Async XLA Ops:
  12.3 192.3 %copy-start.17 = (s32[1024]{0:T(1024)}, s32[1024]{0:T(1024)S(1)}, u32[]{:S(2)}) copy-start(s32[1024]{0:T(1024)S(1)} %get-tuple-element.77) | copy-start | bytes 12292
  12.3 194.2 %copy-start.13 = (s32[1024]{0:T(1024)}, s32[1024]{0:T(1024)S(1)}, u32[]{:S(2)}) copy-start(s32[1024]{0:T(1024)S(1)} %get-tuple-element.72) | copy-start | bytes 12292
  207.3 251.9 %copy-start.19 = (f32[512]{0:T(512)}, f32[512]{0:T(512)S(1)}, u32[]{:S(2)}) copy-start(f32[512]{0:T(512)S(1)} %dynamic-slice_convert_fusion.1) | copy-start | bytes 6148
  277.3 8.2 copy-start.15
  279.8 6.3 copy-start.6
  285.5 173.7 %copy-start.21 = (f32[512,1]{0,1:T(1,128)}, f32[512,1]{0,1:T(1,128)S(1)}, u32[]{:S(2)}) copy-start(f32[512,1]{0,1:T(1,128)S(1)} %add_rsqrt_fusion) | copy-start | bytes 6148
  287.1 168.0 %copy-start.16 = (s32[512,2]{0,1:T(2,128)S(1)}, s32[512,2]{0,1:T(2,128)}, u32[]{:S(2)}) copy-start(s32[512,2]{0,1:T(2,128)} %param.17) | copy-start | bytes 12292
  455.1 3.7 copy-start.11
  455.2 4.0 copy-start.24
  455.2 4.0 copy-start.7
  459.2 2.6 copy-start.4
  459.2 2.6 copy-start
  459.2 2.6 copy-start.2
  532.3 1.1 copy-start.1
  700.9 11.4 %copy-start.14 = (s32[1024]{0:T(1024)S(1)}, s32[1024]{0:T(1024)}, u32[]{:S(2)}) copy-start(s32[1024]{0:T(1024)} %copy-done.13) | copy-start | bytes 12292
  700.9 11.9 %copy-start.26 = (f32[1,1024]{1,0:T(1,128)S(1)}, f32[1,1024]{1,0:T(1,128)}, u32[]{:S(2)}) copy-start(f32[1,1024]{1,0:T(1,128)} %get-tuple-element.83) | copy-start | bytes 12292
  700.9 41.5 %collective-permute-start.1 = (bf16[512,512]{1,0:T(8,128)(2,1)}, bf16[512,512]{1,0:T(8,128)(2,1)}, u32[]{:S(2)}, u32[]{:S(2)}) collective-permute-start(bf16[512,512]{1,0:T(8,128)(2,1)} %get-tuple-element.140), channel_id=1, source_target_pairs={{0,4},{4,0},{8,12},{12,8},{16,20},{20,16},{24,28},{28,24},{1,5},{5... | collective-permute-start | bytes 1572872 | tf_op jit(solution)/shard_map/ppermute | solution.py:1548
  701.6 40.8 %collective-permute-start = (bf16[512,512]{1,0:T(8,128)(2,1)}, bf16[512,512]{1,0:T(8,128)(2,1)}, u32[]{:S(2)}, u32[]{:S(2)}) collective-permute-start(bf16[512,512]{1,0:T(8,128)(2,1)} %get-tuple-element.139), channel_id=1, source_target_pairs={{0,8},{4,12},{8,0},{12,4},{16,24},{20,28},{24,16},{28,20},{1,9},{5... | collective-permute-start | bytes 1572872 | tf_op jit(solution)/shard_map/ppermute | solution.py:1548
  707.7 89.4 %all-to-all-start = ((bf16[8,256,512]{2,1,0:T(8,128)(2,1)}), bf16[8,256,512]{2,1,0:T(8,128)(2,1)}, u32[]{:S(2)}, u32[]{:S(2)}) async-start(bf16[8,256,512]{2,1,0:T(8,128)(2,1)} %get-tuple-element.119), calls=%async_computation | async-start | bytes 4194304 | tf_op jit(solution)/shard_map/all_to_all | solution.py:1434
  712.2 89.0 %all-gather.2.cloned.1.call-start = ((), (), s32[]{:S(2)}) async-start(), calls=%async_computation.1 | async-start | bytes 2621440 | tf_op jit(solution)/shard_map/all_gather | solution.py:1438
  713.5 14.1 %copy-start.30 = (bf16[1280,1408]{1,0:T(8,128)(2,1)S(1)}, bf16[1280,1408]{1,0:T(8,128)(2,1)}, u32[]{:S(2)}) copy-start(bf16[1280,1408]{1,0:T(8,128)(2,1)} %get-tuple-element.110) | copy-start | bytes 10813444
  727.6 13.8 %copy-start.10 = (f32[512,1]{1,0:T(8,128)S(1)}, f32[512,1]{1,0:T(8,128)}, u32[]{:S(2)}) copy-start(f32[512,1]{1,0:T(8,128)} %get-tuple-element.117) | copy-start | bytes 6148
  742.4 2.9 copy-start.28
  745.3 12.8 %copy-start.27 = (bf16[8,176,512]{2,1,0:T(8,128)(2,1)S(1)}, bf16[8,176,512]{2,1,0:T(8,128)(2,1)}, u32[]{:S(2)}) copy-start(bf16[8,176,512]{2,1,0:T(8,128)(2,1)} %get-tuple-element.115) | copy-start | bytes 4325380
  745.3 13.7 %copy-start.18 = (s32[512,2]{0,1:T(2,128)S(1)}, s32[512,2]{0,1:T(2,128)}, u32[]{:S(2)}) copy-start(s32[512,2]{0,1:T(2,128)} %param.16) | copy-start | bytes 12292
  745.3 13.7 %copy-start.29 = (bf16[512,512]{1,0:T(8,128)(2,1)S(1)}, bf16[512,512]{1,0:T(8,128)(2,1)}, u32[]{:S(2)}) copy-start(bf16[512,512]{1,0:T(8,128)(2,1)} %get-tuple-element.116) | copy-start | bytes 1572868
  760.1 7.4 copy-start.5
  760.1 7.4 copy-start.20
  760.1 7.4 copy-start.22
  760.1 7.4 copy-start.25
  767.5 3.3 copy-start.23
  767.5 3.3 copy-start.3
  770.9 26.0 %collective-permute-start.2 = (bf16[256,1024]{1,0:T(8,128)(2,1)S(1)}, bf16[256,1024]{1,0:T(8,128)(2,1)S(1)}, u32[]{:S(2)}, u32[]{:S(2)}) collective-permute-start(bf16[256,1024]{1,0:T(8,128)(2,1)S(1)} %slice.86), channel_id=1, source_target_pairs={{0,16},{4,20},{8,24},{12,28},{16,0},{20,4},{24,8},{28,12},{1,17},{... | collective-permute-start | bytes 1572872 | tf_op jit(solution)/shard_map/ppermute | solution.py:1548
  773.7 4.7 copy-start.8
  778.4 2.6 copy-start.9
  778.4 2.6 copy-start.12
Sparse Core Ops, SparseCore 0:
  770.9 22.9 all-gather.1

commit v7 on v6

--- a/solution.py
+++ b/solution.py
@@ -1034,9 +1034,9 @@
     def handed(j):
         return remote(got.at[j, final], back.at[j], y_send.at[j], y_recv.at[j], expert=j)
 
-    def sum_stage(u, k):
+    def sum_stage(u, k, blocks=(0, 1)):
         j = first_block(u)
-        for q in range(2):
+        for q in blocks:
             for d in range(tensor - 1, -1, -1):
                 if d % (1 << k) == 0:
                     came = d | (1 << (k - 1))
@@ -1052,9 +1052,11 @@
 
     def finish(u):
         j = first_block(u)
-        for k in range(2, bits + 1):
+        for k in range(2, bits):
             sum_stage(u, k)
         for q in range(2):
+            sum_stage(u, bits, (q,))
+
             @pl.when(j + q == e)
             def _():
                 back[e] = got[e, final]

time: 837 us -> 834 us (level)
  no operation moved by 1% of the time
where the time goes in v7:
time: 834 us; the launch traced here: 824 us
  Pallas kernels  667 us (80%)
  matrix products  60.5 us (7%)
  other arithmetic  30.6 us (4%)
  between operations  14.9 us (2%)
  starting transfers between devices  13.3 us (2%)
  local copies, waits for them, and re-layouts  13 us (2%)
  waiting for transfers between devices  12.7 us (2%)
  blocking collectives  11.3 us (1%)
    pallas_call x1, Pallas kernels, front(): pl.pallas_call(functools.partial(front_kernel, experts, bits), out_shape=...  191 us
    pallas_call x2, Pallas kernels, scatter_rows(): pl.pallas_call(functools.partial(scatter_kernel, experts, bits, windows i...  184 us
    pallas_call x1, Pallas kernels, feed_forward(): pl.pallas_call(functools.partial(ffn_kernel, experts, bits, experts // EX...  163 us
    pallas_call x1, Pallas kernels, gather_rows(): pl.pallas_call(functools.partial(gather_kernel, experts, bits, near, mult...  69.5 us
    dot_general x14, matrix products, dot(): lax.dot_general(left, right, ((dims[0], dims[1]), ((), ())), preferred_el...  60.5 us
    pallas_call x1, Pallas kernels, attend_back(): pl.pallas_call(functools.partial(attend_back_kernel, experts), out_shape=...  48.7 us
  transfers between devices with their start and end apart: 5, of which 1 were waited for; matrix products, arithmetic and copies ran while one was open for 8% of the time, Pallas kernels for 0%

profile of v7, /device:TPU:0, one launch (start us, length us, event | category | flops | bytes accessed | tf_op | source)
XLA Modules:
  0.0 823.6 jit_solution(6310688731974252591)
XLA Ops:
  7.2 1.3 broadcast_in_dim.36.refs_1_
  8.5 0.7 multiply_bitcast_fusion
  9.2 0.7 copy.53
  9.9 0.5 convert_reduce_fusion
  10.4 0.7 multiply_bitcast_fusion.1
  11.1 0.7 copy.51
  11.8 0.5 convert_reduce_fusion.1
  12.4 0.6 pad_add_fusion.refs_2_
  13.0 191.0 %shard_map.221 = (bf16[8,160,2048]{2,1,0:T(8,128)(2,1)}, bf16[2048,512]{1,0:T(8,128)(2,1)}, bf16[3,512,2048]{2,1,0:T(8,128)(2,1)}, bf16[2,2048,512]{2,1,0:T(8,12...) custom-call(bf16[512,2048]{1,0:T(8,128)(2,1)} %refs_0_.1, ...), custom_call_target="tpu_custom_call" | custom-call | flops 99999997952 | bytes 10000000 | tf_op jit(solution)/shard_map/pallas_call | solution.py:653
  204.0 0.6 broadcast_add_fusion
  204.6 1.9 iota_compare_fusion.6
  206.5 0.8 dynamic-slice_convert_fusion.1
  207.3 70.1 %shard_map.222 = (bf16[8,160,512]{2,1,0:T(8,128)(2,1)}, bf16[8,160,512]{2,1,0:T(8,128)(2,1)}) custom-call(bf16[8,160,512]{2,1,0:T(8,128)(2,1)} %bitcast.177, bf16[2048,512]{1,0:T(8,128)(2,1)} %get-tuple-element.74.refs_1_, f32[8,160,1]{2,1,0:T(8,128)} %get-tuple-element.75.refs_2_), custom_call_target="tpu_custom_call" | custom-call | flops 99999997952 | bytes 10000000 | tf_op jit(solution)/shard_map/pallas_call | solution.py:958
  277.4 2.4 multiply_reduce_fusion.2
  279.8 5.7 psum.14
  285.5 0.6 fusion.73
  286.1 0.9 multiply_convert_fusion.refs_0_
  287.1 163.2 %shard_map.223 = (bf16[8,336,512]{2,1,0:T(8,128)(2,1)}, bf16[1280,2048]{1,0:T(8,128)(2,1)}, bf16[1280,2048]{1,0:T(8,128)(2,1)}, bf16[1280,1408]{1,0:T(8,128)(2,1...) custom-call(bf16[512,512]{1,0:T(8,128)(2,1)} %multiply_convert_fusion.refs_0_, bf16[512,2048]{1,0:T(8,128)(2,1)} %refs_1_, ...), custom_call_target="tpu_custom_call" | custom-call | flops 99999997952 | bytes 10000000 | tf_op jit(solution)/shard_map/pallas_call | solution.py:1311
  450.3 0.8 slice_bitcast_fusion
  451.1 0.1 reshape.290
  451.2 2.1 fusion.80
  453.5 3.6 fusion.4
  457.1 0.3 convolution_add_fusion.1
  457.5 2.5 convolution_convert_fusion
  460.0 69.5 %shard_map.224 = (bf16[8,160,2048]{2,1,0:T(8,128)(2,1)}, bf16[8,160,512]{2,1,0:T(8,128)(2,1)S(1)}, bf16[8,160,512]{2,1,0:T(8,128)(2,1)S(1)}, bf16[8,256,512]{2,1,0:T(8,128)(2,1)}) custom-call(bf16[8,160,512]{2,1,0:T(8,128)(2,1)S(1)} %bitcast.128, bf16[2048,512]{1,0:T(8,128)(2,1)} %get-tuple-element.74.refs_1_, f32[8,160,1]{2,1,0:T(8,128)S(1)} %copy-done.2, ...), custom_call_target="tpu_custom_call" | custom-call | flops 99999997952 | bytes 10000000 | tf_op jit(solution)/shard_map/pallas_call | solution.py:199
  529.6 0.4 multiply_reduce_fusion
  530.0 0.6 copy-done.1
  530.6 0.7 pad.4.refs_2_
  531.3 48.7 %shard_map.225 = (bf16[1280,512]{1,0:T(8,128)(2,1)}, bf16[1536,512]{1,0:T(8,128)(2,1)}, bf16[1536,512]{1,0:T(8,128)(2,1)}, bf16[8,256,512]{2,1,0:T(8,128)(2,1)}) custom-call(s32[1,1024]{1,0:T(1,128)} %bitcast.133, bf16[1280,512]{1,0:T(8,128)(2,1)} %bitcast.127, bf16[1024,512]{1,0:T(8,128)(2,1)} %get-tuple-element.86.refs_2_, ...), custom_call_target="tpu_custom_call" | custom-call | flops 99999997952 | bytes 10000000 | tf_op jit(solution)/shard_map/pallas_call | solution.py:346
  580.0 113.6 %shard_map.226 = (bf16[8,176,512]{2,1,0:T(8,128)(2,1)}, bf16[8,160,512]{2,1,0:T(8,128)(2,1)}, bf16[512,512]{1,0:T(8,128)(2,1)}, bf16[8,256,512]{2,1,0:T(8,128)(2...) custom-call(bf16[8,160,512]{2,1,0:T(8,128)(2,1)} %bitcast.178, bf16[2048,512]{1,0:T(8,128)(2,1)} %get-tuple-element.92.refs_1_, ...), custom_call_target="tpu_custom_call" | custom-call | flops 99999997952 | bytes 10000000 | tf_op jit(solution)/shard_map/pallas_call | solution.py:958
  693.7 3.2 add_convert_fusion
  696.8 1.0 fusion.72
  697.9 0.7 collective-permute-start.1
  698.6 5.2 collective-permute-start
  703.8 4.6 all-to-all-start
  708.5 0.5 broadcast.216
  709.0 0.7 reduce.7
  709.7 14.1 %fusion.81 = f32[2048,1408]{1,0:T(8,128)} fusion(bf16[1280,2048]{1,0:T(8,128)(2,1)} %get-tuple-element.108, bf16[1280,1408]{1,0:T(8,128)(2,1)} %get-tuple-element.109), kind=kOutput, calls=%fused_computation.133 | convolution fusion | flops 7381975040 | bytes 20381696 | tf_op jit(solution)/shard_map/dot_general | solution.py:1420
  723.8 13.1 %fusion.82 = f32[2048,1408]{1,0:T(8,128)} fusion(bf16[1280,2048]{1,0:T(8,128)(2,1)} %get-tuple-element.108, bf16[1280,1408]{1,0:T(8,128)(2,1)S(1)} %copy-done.30), kind=kOutput, calls=%fused_computation.134 | convolution fusion | flops 7381975040 | bytes 20381696 | tf_op jit(solution)/shard_map/dot_general | solution.py:1420
  736.8 0.8 dynamic-slice_convert_fusion
  737.6 0.1 reduce.3
  737.7 0.8 iota_compare_fusion.7
  738.6 1.4 pad_maximum_fusion
  740.0 1.4 add_convert_fusion.1
  741.4 12.7 %fusion.83 = f32[1408,2048]{1,0:T(8,128)} fusion(bf16[1280,1408]{1,0:T(8,128)(2,1)S(1)} %copy-done.28, bf16[1280,2048]{1,0:T(8,128)(2,1)} %get-tuple-element.114), kind=kOutput, calls=%fused_computation.135 | convolution fusion | flops 7381975040 | bytes 20381696 | tf_op jit(solution)/shard_map/dot_general | solution.py:1420
  754.3 0.8 fusion.84
  755.1 1.0 fusion.23
  756.2 1.7 fusion.43
  758.0 5.7 psum.15
  763.7 3.3 fusion.42
  767.0 2.8 collective-permute-start.2
  769.9 4.7 fusion.33
  774.6 2.6 convert_element_type.156
  777.2 0.2 fusion.85
  777.3 1.2 fusion.44
  778.6 1.8 concatenate.7.part
  780.4 12.6 %collective-permute-done.2 = bf16[256,1024]{1,0:T(8,128)(2,1)S(1)} collective-permute-done((bf16[256,1024]{1,0:T(8,128)(2,1)S(1)}, bf16[256,1024]{1,0:T(8,128)(2,1)S(1)}, u32[]{:S(2)}, u32[]{:S(2)}) %collective-permute-start.2) | collective-permute-done | bytes 524320 | tf_op jit(solution)/shard_map/ppermute | solution.py:1550
  793.1 0.2 convert_add_fusion.1
  793.2 4.2 convert_element_type.152
  797.4 4.1 convert_element_type.155
  801.6 11.2 %shard_map.227 = f32[24,256]{1,0:T(8,128)} custom-call(f32[24,512]{1,0:T(8,128)} %concatenate.7.part), custom_call_target="tpu_custom_call" | custom-call | flops 10000000000 | bytes 100000 | tf_op jit(solution)/shard_map/pallas_call | solution.py:1407
  812.7 1.3 fusion.74
  814.1 1.3 slice.92
  815.4 1.1 copy.68
  (96 shorter events, 0.7 us)
Async XLA Ops:
  12.3 192.3 %copy-start.17 = (s32[1024]{0:T(1024)}, s32[1024]{0:T(1024)S(1)}, u32[]{:S(2)}) copy-start(s32[1024]{0:T(1024)S(1)} %get-tuple-element.77) | copy-start | bytes 12292
  12.3 194.2 %copy-start.13 = (s32[1024]{0:T(1024)}, s32[1024]{0:T(1024)S(1)}, u32[]{:S(2)}) copy-start(s32[1024]{0:T(1024)S(1)} %get-tuple-element.72) | copy-start | bytes 12292
  207.3 250.2 %copy-start.19 = (f32[512]{0:T(512)}, f32[512]{0:T(512)S(1)}, u32[]{:S(2)}) copy-start(f32[512]{0:T(512)S(1)} %dynamic-slice_convert_fusion.1) | copy-start | bytes 6148
  277.3 8.2 copy-start.15
  279.8 6.3 copy-start.6
  285.5 171.9 %copy-start.21 = (f32[512,1]{0,1:T(1,128)}, f32[512,1]{0,1:T(1,128)S(1)}, u32[]{:S(2)}) copy-start(f32[512,1]{0,1:T(1,128)S(1)} %add_rsqrt_fusion) | copy-start | bytes 6148
  287.1 166.3 %copy-start.16 = (s32[512,2]{0,1:T(2,128)S(1)}, s32[512,2]{0,1:T(2,128)}, u32[]{:S(2)}) copy-start(s32[512,2]{0,1:T(2,128)} %param.17) | copy-start | bytes 12292
  453.4 3.7 copy-start.11
  453.5 4.0 copy-start.24
  453.5 4.0 copy-start.7
  457.4 2.6 copy-start.4
  457.5 2.6 copy-start
  457.5 2.6 copy-start.2
  529.6 1.1 copy-start.1
  697.9 10.5 %copy-start.14 = (s32[1024]{0:T(1024)S(1)}, s32[1024]{0:T(1024)}, u32[]{:S(2)}) copy-start(s32[1024]{0:T(1024)} %copy-done.13) | copy-start | bytes 12292
  697.9 11.1 %copy-start.26 = (f32[1,1024]{1,0:T(1,128)S(1)}, f32[1,1024]{1,0:T(1,128)}, u32[]{:S(2)}) copy-start(f32[1,1024]{1,0:T(1,128)} %get-tuple-element.83) | copy-start | bytes 12292
  697.9 40.6 %collective-permute-start.1 = (bf16[512,512]{1,0:T(8,128)(2,1)}, bf16[512,512]{1,0:T(8,128)(2,1)}, u32[]{:S(2)}, u32[]{:S(2)}) collective-permute-start(bf16[512,512]{1,0:T(8,128)(2,1)} %get-tuple-element.140), channel_id=1, source_target_pairs={{0,4},{4,0},{8,12},{12,8},{16,20},{20,16},{24,28},{28,24},{1,5},{5... | collective-permute-start | bytes 1572872 | tf_op jit(solution)/shard_map/ppermute | solution.py:1550
  698.6 40.0 %collective-permute-start = (bf16[512,512]{1,0:T(8,128)(2,1)}, bf16[512,512]{1,0:T(8,128)(2,1)}, u32[]{:S(2)}, u32[]{:S(2)}) collective-permute-start(bf16[512,512]{1,0:T(8,128)(2,1)} %get-tuple-element.139), channel_id=1, source_target_pairs={{0,8},{4,12},{8,0},{12,4},{16,24},{20,28},{24,16},{28,20},{1,9},{5... | collective-permute-start | bytes 1572872 | tf_op jit(solution)/shard_map/ppermute | solution.py:1550
  703.8 89.4 %all-to-all-start = ((bf16[8,256,512]{2,1,0:T(8,128)(2,1)}), bf16[8,256,512]{2,1,0:T(8,128)(2,1)}, u32[]{:S(2)}, u32[]{:S(2)}) async-start(bf16[8,256,512]{2,1,0:T(8,128)(2,1)} %get-tuple-element.119), calls=%async_computation | async-start | bytes 4194304 | tf_op jit(solution)/shard_map/all_to_all | solution.py:1436
  708.4 89.1 %all-gather.2.cloned.1.call-start = ((), (), s32[]{:S(2)}) async-start(), calls=%async_computation.1 | async-start | bytes 2621440 | tf_op jit(solution)/shard_map/all_gather | solution.py:1440
  709.6 14.1 %copy-start.30 = (bf16[1280,1408]{1,0:T(8,128)(2,1)S(1)}, bf16[1280,1408]{1,0:T(8,128)(2,1)}, u32[]{:S(2)}) copy-start(bf16[1280,1408]{1,0:T(8,128)(2,1)} %get-tuple-element.110) | copy-start | bytes 10813444
  723.8 13.8 %copy-start.10 = (f32[512,1]{1,0:T(8,128)S(1)}, f32[512,1]{1,0:T(8,128)}, u32[]{:S(2)}) copy-start(f32[512,1]{1,0:T(8,128)} %get-tuple-element.117) | copy-start | bytes 6148
  738.5 2.9 copy-start.28
  741.4 12.8 %copy-start.27 = (bf16[8,176,512]{2,1,0:T(8,128)(2,1)S(1)}, bf16[8,176,512]{2,1,0:T(8,128)(2,1)}, u32[]{:S(2)}) copy-start(bf16[8,176,512]{2,1,0:T(8,128)(2,1)} %get-tuple-element.115) | copy-start | bytes 4325380
  741.4 13.7 %copy-start.18 = (s32[512,2]{0,1:T(2,128)S(1)}, s32[512,2]{0,1:T(2,128)}, u32[]{:S(2)}) copy-start(s32[512,2]{0,1:T(2,128)} %param.16) | copy-start | bytes 12292
  741.4 13.7 %copy-start.29 = (bf16[512,512]{1,0:T(8,128)(2,1)S(1)}, bf16[512,512]{1,0:T(8,128)(2,1)}, u32[]{:S(2)}) copy-start(bf16[512,512]{1,0:T(8,128)(2,1)} %get-tuple-element.116) | copy-start | bytes 1572868
  756.2 7.4 copy-start.5
  756.2 7.4 copy-start.20
  756.2 7.4 copy-start.22
  756.2 7.4 copy-start.25
  763.7 3.3 copy-start.23
  763.7 3.3 copy-start.3
  767.0 26.0 %collective-permute-start.2 = (bf16[256,1024]{1,0:T(8,128)(2,1)S(1)}, bf16[256,1024]{1,0:T(8,128)(2,1)S(1)}, u32[]{:S(2)}, u32[]{:S(2)}) collective-permute-start(bf16[256,1024]{1,0:T(8,128)(2,1)S(1)} %slice.86), channel_id=1, source_target_pairs={{0,16},{4,20},{8,24},{12,28},{16,0},{20,4},{24,8},{28,12},{1,17},{... | collective-permute-start | bytes 1572872 | tf_op jit(solution)/shard_map/ppermute | solution.py:1550
  769.9 4.7 copy-start.8
  774.6 2.6 copy-start.9
  774.6 2.6 copy-start.12
Sparse Core Ops, SparseCore 0:
  767.1 24.0 all-gather.1
